TPU v7x, 128 devices: a whole 4x4x4 slice. The times are simulated.
128 devices in a mesh: batch: 4 (over y_lo, core), frames: 4 (over x), chan: 8 (over z, y_hi).
Axes of the slice: x: 4, y: 4 (y_hi: 2, y_lo: 2; y = y_hi * 2 + y_lo), z: 4, core: 2. Of those that a mesh axis runs over, the one named last changes fastest.
Arguments:
- tokens: bfloat16 [8, 2048, 1536], P('batch', 'frames'), may hold values from -6 to 6
- cotangent: bfloat16 [8, 2048, 1536], P('batch', 'frames'), may hold values from -6 to 6
- norm_gain: float32 [1536], replicated, may hold values from 0.5 to 1.5
- norm_bias: float32 [1536], replicated, may hold values from -3 to 3
- qkv_weight: bfloat16 [1536, 3, 1536], P(None, None, 'chan'), may hold values from -2 to 2
- out_weight: bfloat16 [1536, 1536], P('chan'), may hold values from -0.625 to 0.625
- lengths: int32 [8], P('batch'), may hold values from 1024 to 2048, as said below
- segments: int32 [8, 2048], P('batch'), may hold values from 0 to 15, never falling along the last dimension, each value on 1 to 256 neighbouring positions
Outputs:
- output: bfloat16 [8, 2048, 1536], P('batch', 'frames')
- grad_tokens: bfloat16 [8, 2048, 1536], P('batch', 'frames')
- grad_proj: float32 [1536, 4, 1536], P(('batch', 'frames'), None, 'chan')
Inputs may be any that keep to these rules, and one draw needn't show every extreme that they name: `lengths`: some recording has all 2048 frames valid and some has exactly 1024. `segments`: along a recording stretch numbers never fall; each stretch has 1 to 256 frames.
All inputs are finite; a program needn't handle non-finite values.
Results may differ from a plain program's by a relative error of at most 0.0067.
Values may be sent and summed in bfloat16 or wider, within the bound.
No kernel may reach another device: no remote copies, remote signals or barrier semaphores. Data moves between devices by JAX's collectives and lax.ppermute only.
A program may use at most 128 MiB of HBM per device.

v0:
```python
import jax
import jax.numpy as jnp
from jax import lax
from jax.sharding import PartitionSpec as P

HEAD = 64
CTX = 256


EPS = 1e-05
NEG = -1e30


def extended_2(array, sides, width):
    for axis, dim in sides:
        size, length = (lax.axis_size(axis), array.shape[dim])
        up = [(i, (i + 1) % size) for i in range(size - 1)]
        down = [(j, i) for i, j in up]
        last = lax.slice_in_dim(array, length - width, length, axis=dim)
        initial = lax.slice_in_dim(array, 0, width, axis=dim)
        before = lax.ppermute(last, axis, up)
        after = lax.ppermute(initial, axis, down)
        array = jnp.concatenate([before, array, after], axis=dim)
    return array


def normalize(tokens, norm_gain, norm_bias):
    values = tokens.astype(jnp.float32)
    centered = values - jnp.mean(values, axis=-1, keepdims=True)
    inverse = lax.rsqrt(jnp.mean(centered * centered, axis=-1, keepdims=True) + EPS)
    scaled = centered * inverse
    return (scaled, inverse, (scaled * norm_gain + norm_bias).astype(jnp.bfloat16))


def shards(tokens, cotangent, norm_gain, norm_bias, qkv_weight, out_weight, lengths, segments):
    rec_count, frame_rows, model_width = tokens.shape
    local_width = qkv_weight.shape[2]
    local_heads = local_width // HEAD
    key_span = frame_rows + 2 * CTX
    seg_start = lax.axis_index("frames") * frame_rows
    position = seg_start + jnp.arange(frame_rows, dtype=jnp.int32)
    reach = seg_start - CTX + jnp.arange(key_span, dtype=jnp.int32)
    padded_segs = jnp.pad(segments, ((0, 0), (CTX, CTX)), constant_values=-10)
    seg_keys = lax.dynamic_slice_in_dim(padded_segs, seg_start, key_span, 1)
    seg_rows = lax.dynamic_slice_in_dim(segments, seg_start, frame_rows, 1)
    near = jnp.abs(position[:, None] - reach[None, :]) <= CTX
    live_keys = (reach[None, None, :] < lengths[:, None, None]) | (
        position[:, None] == reach[None, :]
    )[None]
    stretch = jnp.abs(seg_rows[:, :, None] - seg_keys[:, None, :]) <= 1
    visible = (near[None] & live_keys & stretch)[:, None]
    live_rows = (position[None, :] < lengths[:, None]).astype(jnp.float32)
    scaled, inverse, normed = normalize(tokens, norm_gain, norm_bias)
    qkv = jnp.einsum(
        "rfc,ckd->rfkd", normed, qkv_weight, preferred_element_type=jnp.float32
    ).astype(jnp.bfloat16)
    query = qkv[:, :, 0].reshape(rec_count, frame_rows, local_heads, HEAD)
    extended = extended_2(qkv[:, :, 1:], (("frames", 1),), CTX)
    keys = extended[:, :, 0].reshape(rec_count, key_span, local_heads, HEAD)
    values = extended[:, :, 1].reshape(rec_count, key_span, local_heads, HEAD)
    grad_mixed = jnp.einsum(
        "rfc,ac->rfa", cotangent, out_weight, preferred_element_type=jnp.float32
    )
    grad_mixed = (grad_mixed * live_rows[:, :, None]).astype(jnp.bfloat16)
    grad_mixed = grad_mixed.reshape(rec_count, frame_rows, local_heads, HEAD)
    score_scale = HEAD ** (-0.5)
    scores = (
        jnp.einsum("rqhd,rkhd->rhqk", query, keys, preferred_element_type=jnp.float32) * score_scale
    )
    scores = jnp.where(visible, scores, NEG)
    highest = jnp.max(scores, axis=-1, keepdims=True)
    weights = jnp.exp(scores - highest)
    weights = weights / jnp.sum(weights, axis=-1, keepdims=True)
    rounded = weights.astype(jnp.bfloat16)
    mixed = jnp.einsum("rhqk,rkhd->rqhd", rounded, values, preferred_element_type=jnp.float32)
    mixed = (mixed * live_rows[:, :, None, None]).astype(jnp.bfloat16)
    mixed_flat = mixed.reshape(rec_count, frame_rows, local_width)
    grad_weights = jnp.einsum(
        "rqhd,rkhd->rhqk", grad_mixed, values, preferred_element_type=jnp.float32
    )
    grad_values = jnp.einsum(
        "rhqk,rqhd->rkhd", rounded, grad_mixed, preferred_element_type=jnp.float32
    )
    grad_scores = (
        weights
        * (grad_weights - jnp.sum(weights * grad_weights, axis=-1, keepdims=True))
        * score_scale
    )
    grad_scores = grad_scores.astype(jnp.bfloat16)
    grad_query = jnp.einsum(
        "rhqk,rkhd->rqhd", grad_scores, keys, preferred_element_type=jnp.float32
    )
    grad_keys = jnp.einsum(
        "rhqk,rqhd->rkhd", grad_scores, query, preferred_element_type=jnp.float32
    )
    partial_sum = jnp.einsum(
        "rfa,ac->rfc", mixed_flat, out_weight, preferred_element_type=jnp.float32
    )
    attended = lax.psum(partial_sum, "chan")
    output = (tokens.astype(jnp.float32) + attended).astype(jnp.bfloat16)
    key_value_grads = jnp.stack([grad_keys, grad_values], axis=2).reshape(
        rec_count, key_span, 2, local_width
    )
    edges = jnp.concatenate(
        [key_value_grads[:, :CTX], key_value_grads[:, CTX + frame_rows :]], axis=1
    )
    beside_all = extended_2(edges, (("frames", 1),), CTX)
    own_grads = key_value_grads[:, CTX : CTX + frame_rows]
    own_grads = own_grads.at[:, :CTX].add(beside_all[:, :CTX])
    own_grads = own_grads.at[:, frame_rows - CTX :].add(beside_all[:, 3 * CTX :])
    own_grads = own_grads.astype(jnp.bfloat16)
    grad_qkv = jnp.concatenate(
        [grad_query.astype(jnp.bfloat16).reshape(rec_count, frame_rows, 1, local_width), own_grads],
        axis=2,
    )
    back = jnp.einsum("rfkd,ckd->rfc", grad_qkv, qkv_weight, preferred_element_type=jnp.float32)
    full_back = lax.psum(back, "chan")
    weighted = full_back * norm_gain
    first_mean = jnp.mean(weighted, axis=-1, keepdims=True)
    second_mean = jnp.mean(weighted * scaled, axis=-1, keepdims=True)
    grad_tokens = (
        inverse * (weighted - first_mean - scaled * second_mean) + cotangent.astype(jnp.float32)
    ).astype(jnp.bfloat16)
    inner = jnp.einsum("rfc,rfkd->ckd", normed, grad_qkv, preferred_element_type=jnp.float32)
    outer = jnp.einsum("rfc,rfa->ca", cotangent, mixed_flat, preferred_element_type=jnp.float32)
    grad_proj = lax.psum_scatter(
        jnp.concatenate([inner, outer[:, None, :]], axis=1),
        ("batch", "frames"),
        scatter_dimension=0,
        tiled=True,
    )
    return (output, grad_tokens, grad_proj)


def solution(mesh):
    return jax.shard_map(
        shards,
        mesh=mesh,
        in_specs=(
            P("batch", "frames", None),
            P("batch", "frames", None),
            P(),
            P(),
            P(None, None, "chan"),
            P("chan", None),
            P("batch"),
            P("batch", None),
        ),
        out_specs=(
            P("batch", "frames", None),
            P("batch", "frames", None),
            P(("batch", "frames"), None, "chan"),
        ),
        check_vma=False,
    )
```

profile of v0, /device:TPU:18, one launch (start us, length us, event | category | flops | bytes accessed | tf_op | source)
XLA Modules:
  0.0 715.1 jit_solution(8379501826565858999)
XLA Ops:
  8.1 2.5 convert_reduce_fusion
  10.6 2.8 fusion.20
  13.5 2.3 fusion.41
  16.8 3.4 collective-permute-start
  20.2 3.2 collective-permute-start.1
  23.9 1.3 pad_dynamic-slice_fusion
  26.5 1.5 abs_compare_fusion.1
  28.8 3.5 fusion.31
  33.8 3.1 fusion.50
  36.9 1.4 pad_maximum_fusion.1
  39.4 6.3 fusion.75
  45.7 10.1 %fusion.74 = (f32[2,3,512]{2,1,0:T(4,128)S(1)}, f32[2,3,512,1024]{3,2,1,0:T(8,128)}) fusion(bf16[2,512,3,64]{1,3,2,0:T(8,128)(2,1)S(1)} %bitcast.89, bf16[2,1024,3,64]{1,3,2,0:T(8,128)(2,1)} %bitcast.86, pred[2,512,1024]{2,1,0:T(8,128)(4,1)S(1)} %copy-done.11), kind=kOutput, calls=%fused_computation.94 | convolution fusion | flops 415237120 | bytes 14823424 | tf_op jit(solution)/shard_map/sub | solution.py:72
  55.8 6.0 fusion.33
  61.8 27.1 %fusion.26 = f32[2,3,64,1024]{3,2,1,0:T(8,128)} fusion(bf16[2,512,3,64]{1,3,2,0:T(8,128)(2,1)} %bitcast.88, f32[2,3,512,1024]{3,2,1,0:T(8,128)} %fusion.75, f32[2,3,512,1024]{3,2,1,0:T(8,128)} %get-tuple-element.48, f32[2,3,512]{2,1,0:T(4,128)S(1)} %get-tuple-element.47), kind=kOutput, calls=%fused_computation.31 | convolution fusion | flops 424677376 | bytes 27144192 | tf_op jit(solution)/shard_map/rhqk,rqhd->rkhd/dot_general | solution.py:93
  90.2 2.9 collective-permute-start.2
  93.1 1.3 fusion.40
  94.4 16.4 %collective-permute-done.2 = f32[2,256,2,192]{1,3,2,0:T(8,128)S(1)} collective-permute-done((f32[2,256,2,192]{1,3,2,0:T(8,128)S(1)}, f32[2,256,2,192]{1,3,2,0:T(8,128)S(1)}, u32[]{:S(2)}, u32[]{:S(2)}) %collective-permute-start.2) | collective-permute-done | bytes 786464 | tf_op jit(solution)/shard_map/ppermute | solution.py:21
  113.0 1.9 collective-permute-start.3
  114.9 7.4 %fusion.47 = bf16[2,3,64,512]{3,2,1,0:T(8,128)(2,1)} fusion(bf16[2,1024,3,64]{1,3,2,0:T(8,128)(2,1)S(1)} %bitcast.82, f32[2,512]{1,0:T(2,128)S(1)} %copy-done.20, f32[2,3,512,1024]{3,2,1,0:T(8,128)} %get-tuple-element.48, f32[2,3,512]{2,1,0:T(4,128)S(1)} %get-tuple-element.47), kind=kOutput, calls=%fused_computation.59 | convolution fusion | flops 409337856 | bytes 13778944 | tf_op jit(solution)/shard_map/rhqk,rkhd->rqhd/dot_general | solution.py:75
  122.3 26.2 %fusion.51 = bf16[2,3,64,512]{3,2,1,0:T(8,128)(2,1)} fusion(bf16[2,1024,3,64]{1,3,2,0:T(8,128)(2,1)} %bitcast.87, f32[2,3,512,1024]{3,2,1,0:T(8,128)} %fusion.75, f32[2,3,512,1024]{3,2,1,0:T(8,128)} %get-tuple-element.48, f32[2,3,512]{2,1,0:T(4,128)S(1)} %get-tuple-element.47), kind=kOutput, calls=%fused_computation.61 | convolution fusion | flops 424873984 | bytes 26357760 | tf_op jit(solution)/shard_map/rhqk,rkhd->rqhd/dot_general | solution.py:90
  148.6 2.9 convolution_bitcast_fusion.2
  151.5 1.3 fusion.60
  153.0 2.4 convolution_bitcast_fusion.1
  155.5 2.4 pad_maximum_fusion
  157.9 6.2 copy.26
  164.5 3.7 fusion.62
  168.2 4.5 convolution_bitcast_fusion
  172.7 66.2 %reduce-scatter.4.cloned.1.call-done = f32[96,768]{1,0:T(8,128)} async-done(((f32[1536,768]{1,0:T(8,128)}), f32[96,768]{1,0:T(8,128)}) %reduce-scatter.4.cloned.1.call-update) | async-done | bytes 294928
  241.0 453.2 %all-reduce.4.cloned.1.call-done = (f32[2,512,1536]{2,1,0:T(8,128)}, f32[2,512,1536]{2,1,0:T(8,128)}) async-done(((f32[2,512,1536]{2,1,0:T(8,128)}, f32[2,512,1536]{2,1,0:T(8,128)}), (f32[2,512,1536]{2,1,0:T(8,128)}, f32[2,512,1536]{2,1,0:T(8,128)})) %all-reduce.4.cloned.1.call-update) | async-done | bytes 12582928 | tf_op jit(solution)/shard_map/psum | solution.py:99
  694.3 4.8 multiply_reduce_fusion.1
  699.1 1.7 copy-done.4
  700.8 6.9 fusion.19
  (73 shorter events, 12.1 us)
Async XLA Ops:
  8.0 5.5 copy-start
  8.0 5.5 copy-start.18
  8.0 5.5 copy-start.21
  8.0 230.9 %reduce-scatter.4.cloned.1.call-start = ((), (), s32[]{:S(2)}) async-start(), calls=%async_computation.1 | async-start | bytes 5013504
  8.1 5.4 copy-start.1
  15.8 18.0 %copy-start.14 = (bf16[192,1536]{1,0:T(8,128)(2,1)S(1)}, bf16[192,1536]{1,0:T(8,128)(2,1)}, u32[]{:S(2)}) copy-start(bf16[192,1536]{1,0:T(8,128)(2,1)} %param.17) | copy-start | bytes 1769476
  16.8 20.1 %collective-permute-start = (bf16[2,256,2,192]{1,3,2,0:T(8,128)(2,1)}, bf16[2,256,2,192]{1,3,2,0:T(8,128)(2,1)}, u32[]{:S(2)}, u32[]{:S(2)}) collective-permute-start(bf16[2,256,2,192]{1,3,2,0:T(8,128)(2,1)} %get-tuple-element.43), channel_id=1, source_target_pairs={{0,8},{8,16},{16,24},{1,9},{9,17},{17,25},{2,10},{10,18},{18,26},{... | collective-permute-start | bytes 1179656 | tf_op jit(solution)/shard_map/ppermute | solution.py:21
  20.2 16.7 %collective-permute-start.1 = (bf16[2,256,2,192]{1,3,2,0:T(8,128)(2,1)}, bf16[2,256,2,192]{1,3,2,0:T(8,128)(2,1)}, u32[]{:S(2)}, u32[]{:S(2)}) collective-permute-start(bf16[2,256,2,192]{1,3,2,0:T(8,128)(2,1)} %get-tuple-element.44), channel_id=1, source_target_pairs={{8,0},{16,8},{24,16},{9,1},{17,9},{25,17},{10,2},{18,10},{26,18},{... | collective-permute-start | bytes 1179656 | tf_op jit(solution)/shard_map/ppermute | solution.py:22
  33.0 6.4 copy-start.19
  36.9 8.8 %copy-start.17 = (bf16[2,512,192]{1,2,0:T(8,128)(2,1)}, bf16[2,512,192]{1,2,0:T(8,128)(2,1)S(1)}, u32[]{:S(2)}) copy-start(bf16[2,512,192]{1,2,0:T(8,128)(2,1)S(1)} %fusion.50) | copy-start | bytes 1179652
  39.3 6.3 copy-start.8
  39.4 6.3 copy-start.11
  39.4 6.3 copy-start.16
  88.9 21.9 %copy-start.5 = (f32[2,3,64,1024]{3,2,1,0:T(8,128)S(1)}, f32[2,3,64,1024]{3,2,1,0:T(8,128)}, u32[]{:S(2)}) copy-start(f32[2,3,64,1024]{3,2,1,0:T(8,128)} %fusion.26) | copy-start | bytes 4718596
  88.9 26.0 %copy-start.9 = (bf16[2,1024,1,192]{1,3,2,0:T(8,128)(2,1)S(1)}, bf16[2,1024,1,192]{1,3,2,0:T(8,128)(2,1)}, u32[]{:S(2)}) copy-start(bf16[2,1024,1,192]{1,3,2,0:T(8,128)(2,1)} %copy-done.8) | copy-start | bytes 2359300
  88.9 26.0 %copy-start.20 = (f32[2,512]{1,0:T(2,128)S(1)}, f32[2,512]{1,0:T(2,128)}, u32[]{:S(2)}) copy-start(f32[2,512]{1,0:T(2,128)} %copy-done.19) | copy-start | bytes 12292
  90.2 20.6 %collective-permute-start.2 = (f32[2,256,2,192]{1,3,2,0:T(8,128)S(1)}, f32[2,256,2,192]{1,3,2,0:T(8,128)S(1)}, u32[]{:S(2)}, u32[]{:S(2)}) collective-permute-start(f32[2,256,2,192]{1,3,2,0:T(8,128)S(1)} %fusion.56), channel_id=1, source_target_pairs={{0,8},{8,16},{16,24},{1,9},{9,17},{17,25},{2,10},{10,18},{18,26},{... | collective-permute-start | bytes 2359304 | tf_op jit(solution)/shard_map/ppermute | solution.py:21
  111.8 1.1 copy-start.6
  113.0 38.5 %collective-permute-start.3 = (f32[2,256,2,192]{1,3,2,0:T(8,128)}, f32[2,256,2,192]{1,3,2,0:T(8,128)}, u32[]{:S(2)}, u32[]{:S(2)}) collective-permute-start(f32[2,256,2,192]{1,3,2,0:T(8,128)} %get-tuple-element.39), channel_id=1, source_target_pairs={{8,0},{16,8},{24,16},{9,1},{17,9},{25,17},{10,2},{18,10},{26,18},{... | collective-permute-start | bytes 2359304 | tf_op jit(solution)/shard_map/ppermute | solution.py:22
  122.3 29.2 %copy-start.7 = (f32[2,512,2,192]{1,3,2,0:T(8,128)S(1)}, f32[2,512,2,192]{1,3,2,0:T(8,128)}, u32[]{:S(2)}) copy-start(f32[2,512,2,192]{1,3,2,0:T(8,128)} %copy-done.6) | copy-start | bytes 4718596
  148.6 4.4 copy-start.2
  148.6 4.4 copy-start.22
  148.6 4.4 copy-start.23
  152.9 2.5 copy-start.12
  157.9 6.6 copy-start.10
  157.9 6.6 copy-start.15
  164.1 4.1 copy-start.13
  164.2 530.1 %all-reduce.4.cloned.1.call-start = ((), (), s32[]{:S(2)}) async-start(), calls=%async_computation.2 | async-start | bytes 25165824 | tf_op jit(solution)/shard_map/psum | solution.py:99
  164.5 3.7 copy-start.24
  694.3 4.8 copy-start.3
  694.3 6.5 copy-start.4
Sparse Core Ops, SparseCore 0:
  164.3 74.6 reduce-scatter.3
Sparse Core Ops, SparseCore 1:
  172.8 521.4 all-reduce.3
where the time goes:
time: 718 us; the launch traced here: 715 us
  waiting for transfers between devices  536 us (75%)
  matrix products  102 us (14%)
  other arithmetic  33 us (5%)
  local copies, waits for them, and re-layouts  16.5 us (2%)
  between operations  15.8 us (2%)
  starting transfers between devices  11.7 us (2%)
    psum x1, waiting for transfers between devices, shards(): attended = lax.psum(partial_sum, 'chan')  453 us
    unnamed x3, waiting for transfers between devices  66.3 us
    dot_general x1, matrix products, shards(): jnp.einsum('rhqk,rqhd->rkhd', grad_scores, query, preferred_element_type=...  27.1 us
    dot_general x1, matrix products, shards(): jnp.einsum('rhqk,rkhd->rqhd', grad_scores, keys, preferred_element_type=j...  26.2 us
    ppermute x2, waiting for transfers between devices, extended_2(): before = lax.ppermute(last, axis, up)  16.4 us
  transfers between devices with their start and end apart: 6, of which 3 were waited for; matrix products, arithmetic and copies ran while one was open for 9% of the time, Pallas kernels for 0%

commit v1 on v0

v1 whole, which is shorter than its diff:
```python
import jax
import jax.numpy as jnp
from jax import lax
from jax.experimental import pallas as pl
from jax.experimental.pallas import tpu as pltpu
from jax.sharding import PartitionSpec as P

HEAD = 64
CTX = 256
EPS = 1e-05
NEG = -1e30
VMEM_LIMIT = 50 * 1024 * 1024
SHIFTS = ((1, 0), (3, 0), (0, 1), (1, 1), (3, 1), (2, 0), (2, 1))

F32 = jnp.float32
BF16 = jnp.bfloat16


def params():
    return pltpu.CompilerParams(vmem_limit_bytes=VMEM_LIMIT)


def dot_nn(a, b):
    return lax.dot_general(a, b, (((1,), (0,)), ((), ())), preferred_element_type=F32)


def dot_nt(a, b):
    return lax.dot_general(a, b, (((1,), (1,)), ((), ())), preferred_element_type=F32)


def dot_tn(a, b):
    return lax.dot_general(a, b, (((0,), (0,)), ((), ())), preferred_element_type=F32)


def norm_stats(tokens):
    values = tokens.astype(F32)
    centered = values - jnp.mean(values, axis=-1, keepdims=True)
    inverse = lax.rsqrt(jnp.mean(centered * centered, axis=-1, keepdims=True) + EPS)
    return centered * inverse, inverse


def project_body(tok, cot, gain, bias, weight, out_w, live, normed, q, kv, g, kv_first, kv_last):
    width = q.shape[0]
    scaled, _ = norm_stats(tok[...])
    rows = (scaled * gain[...] + bias[...]).astype(BF16)
    normed[...] = rows
    qkv = dot_nt(weight[...], rows).astype(BF16)
    q[...] = qkv[:width]
    kv[...] = qkv[width:]
    step = pl.program_id(0)

    @pl.when(step % 2 == 0)
    def _():
        kv_first[...] = qkv[width:]

    @pl.when(step % 2 == 1)
    def _():
        kv_last[...] = qkv[width:]

    g[...] = (dot_nt(out_w[...], cot[...]) * live[...]).astype(BF16)


def project(tokens, cotangent, gain, bias, weight, out_w, live):
    rows, model = tokens.shape
    width = out_w.shape[0]
    full = lambda shape: pl.BlockSpec(shape, lambda i: (0, 0))
    by_row = pl.BlockSpec((CTX, model), lambda i: (i, 0))
    by_col = lambda n: pl.BlockSpec((n, CTX), lambda i: (0, i))
    by_half = pl.BlockSpec((2 * width, CTX), lambda i: (0, i // 2))
    return pl.pallas_call(
        project_body,
        grid=(rows // CTX,),
        in_specs=[
            by_row,
            by_row,
            full((1, model)),
            full((1, model)),
            full((3 * width, model)),
            full((width, model)),
            by_col(1),
        ],
        out_specs=[by_row, by_col(width), by_col(2 * width), by_col(width), by_half, by_half],
        out_shape=[
            jax.ShapeDtypeStruct((rows, model), BF16),
            jax.ShapeDtypeStruct((width, rows), BF16),
            jax.ShapeDtypeStruct((2 * width, rows), BF16),
            jax.ShapeDtypeStruct((width, rows), BF16),
            jax.ShapeDtypeStruct((2 * width, rows // 2), BF16),
            jax.ShapeDtypeStruct((2 * width, rows // 2), BF16),
        ],
        compiler_params=params(),
        name="project",
    )(tokens, cotangent, gain, bias, weight, out_w, live)


def attention_body(
    q, kv, before, after, g, seg_keys, seg_rows, live, mixed, dq, dkv, dbefore, dafter, acc, mask
):
    width = q.shape[0]
    span = 3 * CTX
    kv_all = jnp.concatenate([before[...], kv[...], after[...]], axis=1)
    q_small = q[...] * jnp.asarray(HEAD**-0.5, BF16)
    grads = g[...]
    acc[...] = jnp.zeros_like(acc)
    for tile in range(2):
        cols = slice(tile * CTX, (tile + 1) * CTX)
        keys = slice(tile * CTX, tile * CTX + span)
        away = (
            lax.broadcasted_iota(jnp.int32, (span, CTX), 0)
            - CTX
            - lax.broadcasted_iota(jnp.int32, (span, CTX), 1)
        )
        near = jnp.abs(away) <= CTX
        stretch = jnp.abs(seg_keys[0, keys, :] - seg_rows[0, :, cols]) <= 1
        visible = (near & stretch) | (away == 0)
        mask[...] = jnp.where(visible, 0.0, NEG)
        for head in range(width // HEAD):
            d = slice(head * HEAD, (head + 1) * HEAD)
            dv = slice(width + head * HEAD, width + (head + 1) * HEAD)
            k_t, v_t = kv_all[d, keys], kv_all[dv, keys]
            q_t, g_t = q_small[d, cols], grads[d, cols]
            scores = dot_tn(k_t, q_t) + mask[...]
            weights = jnp.exp(scores - jnp.max(scores, axis=0, keepdims=True))
            weights = weights * (1.0 / jnp.sum(weights, axis=0, keepdims=True))
            rounded = weights.astype(BF16)
            mixed[d, cols] = (dot_nn(v_t, rounded) * live[:, cols]).astype(BF16)
            grad_w = dot_tn(v_t, g_t)
            total = jnp.sum(weights * grad_w, axis=0, keepdims=True)
            grad_s = (weights * (grad_w - total)).astype(BF16)
            dq[d, cols] = (dot_nn(k_t, grad_s) * (HEAD**-0.5)).astype(BF16)
            acc[d, keys] += dot_nt(q_t, grad_s)
            acc[dv, keys] += dot_nt(g_t, rounded)
    frames = q.shape[1]
    dkv[...] = acc[:, CTX : CTX + frames]
    dbefore[...] = acc[:, :CTX].astype(BF16)
    dafter[...] = acc[:, CTX + frames :].astype(BF16)


def attention(q, kv, before, after, g, seg_keys, seg_rows, live):
    width, rows = q.shape
    recs, span, _ = seg_keys.shape
    frames = rows // recs
    by_rec = lambda n, m: pl.BlockSpec((n, m), lambda r: (0, r))
    return pl.pallas_call(
        attention_body,
        grid=(recs,),
        in_specs=[
            by_rec(width, frames),
            by_rec(2 * width, frames),
            by_rec(2 * width, CTX),
            by_rec(2 * width, CTX),
            by_rec(width, frames),
            pl.BlockSpec((1, span, 1), lambda r: (r, 0, 0)),
            pl.BlockSpec((1, 1, frames), lambda r: (r, 0, 0)),
            by_rec(1, frames),
        ],
        out_specs=[
            by_rec(width, frames),
            by_rec(width, frames),
            by_rec(2 * width, frames),
            by_rec(2 * width, CTX),
            by_rec(2 * width, CTX),
        ],
        out_shape=[
            jax.ShapeDtypeStruct((width, rows), BF16),
            jax.ShapeDtypeStruct((width, rows), BF16),
            jax.ShapeDtypeStruct((2 * width, rows), F32),
            jax.ShapeDtypeStruct((2 * width, recs * CTX), BF16),
            jax.ShapeDtypeStruct((2 * width, recs * CTX), BF16),
        ],
        scratch_shapes=[pltpu.VMEM((2 * width, span), F32), pltpu.VMEM((3 * CTX, CTX), F32)],
        compiler_params=params(),
        name="attention",
    )(q, kv, before, after, g, seg_keys, seg_rows, live)


def back_body(order, dq, own, left, right, weight, gkv, mine, *parts):
    step = pl.program_id(0)
    chunk = own.shape[1]
    half = CTX // chunk
    place = order[step] % (2 * half)
    beside = jnp.where(place < half, left[...].astype(F32), right[...].astype(F32))
    kv_grads = (own[...] + beside).astype(BF16)
    gkv[...] = kv_grads
    grads = jnp.concatenate([dq[...], kv_grads], axis=0)
    back = dot_tn(grads, weight[...])

    @pl.when(step == 0)
    def _():
        mine[...] = back

    for index, part in enumerate(parts):

        @pl.when(step == index + 1)
        def _(part=part):
            part[...] = back.astype(BF16)


def back_parts(order, dq, own, left, right, weight):
    width, rows = dq.shape
    model = weight.shape[1]
    count = len(SHIFTS) + 1
    chunk = rows // count
    half = CTX // chunk
    by_order = lambda n: pl.BlockSpec((n, chunk), lambda i, o: (0, o[i]))
    whole = pl.BlockSpec((chunk, model), lambda i, o: (0, 0))

    def edge(i, o):
        return (0, (o[i] // (2 * half)) * half + o[i] % half)

    return pl.pallas_call(
        back_body,
        grid_spec=pltpu.PrefetchScalarGridSpec(
            num_scalar_prefetch=1,
            grid=(count,),
            in_specs=[
                by_order(width),
                by_order(2 * width),
                pl.BlockSpec((2 * width, chunk), edge),
                pl.BlockSpec((2 * width, chunk), edge),
                pl.BlockSpec((3 * width, model), lambda i, o: (0, 0)),
            ],
            out_specs=[by_order(2 * width)] + [whole] * count,
        ),
        out_shape=[
            jax.ShapeDtypeStruct((2 * width, rows), BF16),
            jax.ShapeDtypeStruct((chunk, model), F32),
        ]
        + [jax.ShapeDtypeStruct((chunk, model), BF16)] * (count - 1),
        compiler_params=params(),
        name="back",
    )(order, dq, own, left, right, weight)


def finish_body(place, tok, cot, gain, mine, *rest):
    parts, out = rest[:-1], rest[-1]
    back = mine[...]
    for part in parts:
        back = back + part[...].astype(F32)
    scaled, inverse = norm_stats(tok[...])
    weighted = back * gain[...]
    first = jnp.mean(weighted, axis=-1, keepdims=True)
    second = jnp.mean(weighted * scaled, axis=-1, keepdims=True)
    grad = inverse * (weighted - first - scaled * second) + cot[...].astype(F32)
    out[...] = grad.astype(BF16)


def finish(place, tokens, cotangent, gain, mine, parts):
    chunk, model = mine.shape
    here = pl.BlockSpec((chunk, model), lambda i, p: (p[0], 0))
    whole = pl.BlockSpec((chunk, model), lambda i, p: (0, 0))
    return pl.pallas_call(
        finish_body,
        grid_spec=pltpu.PrefetchScalarGridSpec(
            num_scalar_prefetch=1,
            grid=(1,),
            in_specs=[here, here, pl.BlockSpec((1, model), lambda i, p: (0, 0))]
            + [whole] * (1 + len(parts)),
            out_specs=whole,
        ),
        out_shape=jax.ShapeDtypeStruct((chunk, model), BF16),
        compiler_params=params(),
        name="finish",
    )(place, tokens, cotangent, gain, mine, *parts)


def to_peer(array, shift):
    dz, dy = shift
    pairs = [
        (z * 2 + y, ((z + dz) % 4) * 2 + (y + dy) % 2) for z in range(4) for y in range(2)
    ]
    return lax.ppermute(array, "chan", pairs)


def peer_index(me, shift, sign):
    dz, dy = shift
    return ((me // 2 + sign * dz) % 4) * 2 + (me % 2 + dy) % 2


def scatter_grads(grads):
    batch, frame = lax.axis_index("batch"), lax.axis_index("frames")
    core, row = batch % 2, batch // 2
    grads = grads.reshape(2, 2, 4, -1, grads.shape[-1])
    pick = lambda array, index, axis: lax.dynamic_index_in_dim(array, index, axis, keepdims=False)
    sent = pick(grads, 1 - core, 1).astype(BF16)
    got = lax.ppermute(sent, "batch", [(0, 1), (1, 0), (2, 3), (3, 2)])
    pair = pick(grads, core, 1) + got.astype(F32)
    sums = pick(pair, frame, 1)
    for shift in (1, 3, 2):
        sent = pick(pair, (frame + shift) % 4, 1).astype(BF16)
        got = lax.ppermute(sent, "frames", [(i, (i + shift) % 4) for i in range(4)])
        sums = sums + got.astype(F32)
    sent = pick(sums, 1 - row, 0).astype(BF16)
    got = lax.ppermute(sent, "batch", [(0, 2), (1, 3), (2, 0), (3, 1)])
    return pick(sums, row, 0) + got.astype(F32)


def shards(tokens, cotangent, norm_gain, norm_bias, qkv_weight, out_weight, lengths, segments):
    recs, frames, model = tokens.shape
    rows = recs * frames
    width = out_weight.shape[0]
    me = lax.axis_index("chan")
    start = lax.axis_index("frames") * frames

    full_out = lax.all_gather(out_weight, "chan", tiled=True)

    flat_tokens = tokens.reshape(rows, model)
    flat_cot = cotangent.reshape(rows, model)
    gain = norm_gain.reshape(1, model)
    weight = qkv_weight.transpose(1, 2, 0).reshape(3 * width, model)
    position = start + jnp.arange(frames, dtype=jnp.int32)
    reach = start - CTX + jnp.arange(frames + 2 * CTX, dtype=jnp.int32)
    live = (position[None, :] < lengths[:, None]).astype(F32).reshape(1, rows)
    padded = jnp.pad(segments, ((0, 0), (CTX, CTX)), constant_values=-10)
    seg_keys = lax.dynamic_slice_in_dim(padded, start, frames + 2 * CTX, 1)
    seg_keys = jnp.where(reach[None, :] < lengths[:, None], seg_keys, -10)[:, :, None]
    seg_rows = lax.dynamic_slice_in_dim(segments, start, frames, 1)[:, None, :]

    normed, q, kv, g, kv_first, kv_last = project(
        flat_tokens, flat_cot, gain, norm_bias.reshape(1, model), weight, out_weight, live
    )
    size = lax.axis_size("frames")
    up = [(i, i + 1) for i in range(size - 1)]
    down = [(i + 1, i) for i in range(size - 1)]
    before = lax.ppermute(kv_last, "frames", up)
    after = lax.ppermute(kv_first, "frames", down)
    mixed, dq, dkv, dbefore, dafter = attention(
        q, kv, before, after, g, seg_keys, seg_rows, live
    )
    from_right = lax.ppermute(dbefore, "frames", down)
    from_left = lax.ppermute(dafter, "frames", up)

    full_mixed = lax.all_gather(mixed, "chan", tiled=True)

    order = jnp.stack([me] + [peer_index(me, shift, 1) for shift in SHIFTS]).astype(jnp.int32)
    gkv, mine, *parts = back_parts(order, dq, dkv, from_left, from_right, weight)
    got = [to_peer(part, shift) for part, shift in zip(parts, SHIFTS)]
    piece = finish(me.reshape(1).astype(jnp.int32), flat_tokens, flat_cot, gain, mine, got)

    chunk = piece.shape[0]
    grad_tokens = jnp.zeros((rows, model), BF16)
    grad_tokens = lax.dynamic_update_slice_in_dim(grad_tokens, piece, me * chunk, 0)
    for shift in SHIFTS:
        other = to_peer(piece, shift)
        place = peer_index(me, shift, -1) * chunk
        grad_tokens = lax.dynamic_update_slice_in_dim(grad_tokens, other, place, 0)

    inner = lax.dot_general(
        normed,
        jnp.concatenate([dq, gkv], axis=0),
        (((0,), (1,)), ((), ())),
        preferred_element_type=F32,
    )
    outer = lax.dot_general(
        flat_cot, mixed, (((0,), (1,)), ((), ())), preferred_element_type=F32
    )
    grad_proj = scatter_grads(jnp.concatenate([inner, outer], axis=1))
    grad_proj = grad_proj.reshape(-1, 4, width)

    output = (flat_tokens.astype(F32) + dot_tn(full_mixed, full_out)).astype(BF16)
    shape = (recs, frames, model)
    return (output.reshape(shape), grad_tokens.reshape(shape), grad_proj)


def solution(mesh):
    return jax.shard_map(
        shards,
        mesh=mesh,
        in_specs=(
            P("batch", "frames", None),
            P("batch", "frames", None),
            P(),
            P(),
            P(None, None, "chan"),
            P("chan", None),
            P("batch"),
            P("batch", None),
        ),
        out_specs=(
            P("batch", "frames", None),
            P("batch", "frames", None),
            P(("batch", "frames"), None, "chan"),
        ),
        check_vma=False,
    )
```

time: 718 us -> 264 us (0.37)
  waiting for transfers between devices: 536 us -> 128 us
  matrix products: 102 us -> 14.2 us
  Pallas kernels: 0 us -> 39.7 us
  other arithmetic: 33 us -> 3.73 us
  starting transfers between devices: 11.7 us -> 40 us
    psum x1 -> x0, waiting for transfers between devices: 453 us -> none  [shards(): attended = lax.psum(partial_sum, 'chan')]
    dot_general x11 -> x3, matrix products: 92 us -> 14.2 us  [the longest x1 9.32 us: dot_tn(): lax.dot_general(a, b, (((0,), (0,)), ((), ())), preferred_element_type=F32)]
    ppermute x4 -> x23, waiting for transfers between devices: 16.4 us -> 88.2 us  [the longest x14 68.3 us: to_peer(): return lax.ppermute(array, 'chan', pairs)]
    unnamed x3 -> x2, waiting for transfers between devices: 66.3 us -> 0.71 us
    pallas_call x0 -> x4, Pallas kernels: none -> 39.7 us  [the longest x1 17.8 us: attention(): pl.pallas_call(attention_body, grid=(recs,), in_specs=[by_rec(width, fram...]
    all_gather x0 -> x2, waiting for transfers between devices: none -> 38.7 us  [the longest x1 38.7 us: shards(): full_out = lax.all_gather(out_weight, 'chan', tiled=True)]
    ppermute x4 -> x23, starting transfers between devices: 11.4 us -> 39.9 us  [the longest x14 24.2 us: to_peer(): return lax.ppermute(array, 'chan', pairs)]
    reduce_sum x3 -> x0, other arithmetic: 10.2 us -> none  [the longest x1 4.79 us: shards(): first_mean = jnp.mean(weighted, axis=-1, keepdims=True)]
  transfers between devices with their start and end apart: 6 -> 25, of which waited for: 3 -> 17; matrix products, arithmetic and copies ran while one was open for 9% -> 10% of each run, Pallas kernels for 0% -> 4%
where the time goes in v1:
time: 264 us; the launch traced here: 261 us
  waiting for transfers between devices  128 us (48%)
  starting transfers between devices  40 us (15%)
  Pallas kernels  39.7 us (15%)
  local copies, waits for them, and re-layouts  21 us (8%)
  between operations  14.4 us (5%)
  matrix products  14.2 us (5%)
  other arithmetic  3.73 us (1%)
    ppermute x14, waiting for transfers between devices, to_peer(): return lax.ppermute(array, 'chan', pairs)  68.3 us
    all_gather x1, waiting for transfers between devices, shards(): full_out = lax.all_gather(out_weight, 'chan', tiled=True)  38.7 us
    ppermute x14, starting transfers between devices, to_peer(): return lax.ppermute(array, 'chan', pairs)  24.2 us
    pallas_call x1, Pallas kernels, attention(): pl.pallas_call(attention_body, grid=(recs,), in_specs=[by_rec(width, fram...  17.8 us
    pallas_call x1, Pallas kernels, project(): pl.pallas_call(project_body, grid=(rows // CTX,), in_specs=[by_row, by_ro...  10.3 us
    pallas_call x1, Pallas kernels, back_parts(): pl.pallas_call(back_body, grid_spec=pltpu.PrefetchScalarGridSpec(num_scal...  9.52 us
    dot_general x1, matrix products, dot_tn(): lax.dot_general(a, b, (((0,), (0,)), ((), ())), preferred_element_type=F32)  9.32 us
    concatenate x1, local copies, waits for them, and re-layouts, shards(): grad_proj = scatter_grads(jnp.concatenate([inner, outer], axis=1))  6.04 us
  transfers between devices with their start and end apart: 25, of which 17 were waited for; matrix products, arithmetic and copies ran while one was open for 10% of the time, Pallas kernels for 4%

profile of v1, /device:TPU:18, one launch (start us, length us, event | category | flops | bytes accessed | tf_op | source)
XLA Modules:
  0.0 260.7 jit_solution(1953469754566296210)
XLA Ops:
  10.4 10.3 %project.1 = (bf16[1024,1536]{1,0:T(8,128)(2,1)}, bf16[192,1024]{1,0:T(8,128)(2,1)S(1)}, bf16[384,1024]{1,0:T(8,128)(2,1)S(1)}, bf16[192,1024]{1,0:T(8,128)(2,1)...) custom-call(bf16[1024,1536]{1,0:T(8,128)(2,1)} %bitcast.60, bf16[1024,1536]{1,0:T(8,128)(2,1)} %bitcast.55, ...), custom_call_target="tpu_custom_call" | custom-call | tf_op jit(solution)/shard_map/project/pallas_call | solution.py:70
  20.8 3.4 %collective-permute-start = (bf16[384,512]{1,0:T(8,128)(2,1)S(1)}, bf16[384,512]{1,0:T(8,128)(2,1)S(1)}, u32[]{:S(2)}, u32[]{:S(2)}) collective-permute-start(bf16[384,512]{1,0:T(8,128)(2,1)S(1)} %get-tuple-element.25), channel_id=1, source_target_pairs={{0,8},{8,16},{16,24},{1,9},{9,17},{17,25},{2,10},{10,18},{18,26},{... | collective-permute-start | bytes 1179656 | tf_op jit(solution)/shard_map/ppermute | solution.py:325
  24.2 2.5 collective-permute-start.1
  28.1 5.4 %collective-permute-done.before = bf16[384,512]{1,0:T(8,128)(2,1)S(1)} collective-permute-done((bf16[384,512]{1,0:T(8,128)(2,1)S(1)}, bf16[384,512]{1,0:T(8,128)(2,1)S(1)}, u32[]{:S(2)}, u32[]{:S(2)}) %collective-permute-start) | collective-permute-done | bytes 393248 | tf_op jit(solution)/shard_map/ppermute | solution.py:325
  33.5 3.1 %collective-permute-done.1.after = bf16[384,512]{1,0:T(8,128)(2,1)S(1)} collective-permute-done((bf16[384,512]{1,0:T(8,128)(2,1)S(1)}, bf16[384,512]{1,0:T(8,128)(2,1)S(1)}, u32[]{:S(2)}, u32[]{:S(2)}) %collective-permute-start.1) | collective-permute-done | bytes 393248 | tf_op jit(solution)/shard_map/ppermute | solution.py:326
  36.6 17.8 %attention.1 = (bf16[192,1024]{1,0:T(8,128)(2,1)}, bf16[192,1024]{1,0:T(8,128)(2,1)S(1)}, f32[384,1024]{1,0:T(8,128)}, bf16[384,512]{1,0:T(8,128)(2,1)S(1)}, bf16[384,512]{1,0:T(8,128)(2,1)S(1)}) custom-call(bf16[192,1024]{1,0:T(8,128)(2,1)S(1)} %get-tuple-element.23.q, bf16[384,1024]{1,0:T(8,128)(2,1)S(1)} %get-tuple-element.24.kv, ...), custom_call_target="tpu_custom_call" | custom-call | tf_op jit(solution)/shard_map/attention/pallas_call | solution.py:144
  55.2 3.1 %collective-permute-start.2 = (bf16[384,512]{1,0:T(8,128)(2,1)S(1)}, bf16[384,512]{1,0:T(8,128)(2,1)S(1)}, u32[]{:S(2)}, u32[]{:S(2)}) collective-permute-start(bf16[384,512]{1,0:T(8,128)(2,1)S(1)} %get-tuple-element.31), channel_id=1, source_target_pairs={{0,8},{8,16},{16,24},{1,9},{9,17},{17,25},{2,10},{10,18},{18,26},{... | collective-permute-start | bytes 1179656 | tf_op jit(solution)/shard_map/ppermute | solution.py:331
  58.4 2.8 %collective-permute-start.3 = (bf16[384,512]{1,0:T(8,128)(2,1)S(1)}, bf16[384,512]{1,0:T(8,128)(2,1)S(1)}, u32[]{:S(2)}, u32[]{:S(2)}) collective-permute-start(bf16[384,512]{1,0:T(8,128)(2,1)S(1)} %get-tuple-element.32), channel_id=1, source_target_pairs={{8,0},{16,8},{24,16},{9,1},{17,9},{25,17},{10,2},{18,10},{26,18},{... | collective-permute-start | bytes 1179656 | tf_op jit(solution)/shard_map/ppermute | solution.py:330
  61.3 5.5 %collective-permute-done.2.left = bf16[384,512]{1,0:T(8,128)(2,1)S(1)} collective-permute-done((bf16[384,512]{1,0:T(8,128)(2,1)S(1)}, bf16[384,512]{1,0:T(8,128)(2,1)S(1)}, u32[]{:S(2)}, u32[]{:S(2)}) %collective-permute-start.2) | collective-permute-done | bytes 393248 | tf_op jit(solution)/shard_map/ppermute | solution.py:331
  66.8 2.8 %collective-permute-done.3.right = bf16[384,512]{1,0:T(8,128)(2,1)S(1)} collective-permute-done((bf16[384,512]{1,0:T(8,128)(2,1)S(1)}, bf16[384,512]{1,0:T(8,128)(2,1)S(1)}, u32[]{:S(2)}, u32[]{:S(2)}) %collective-permute-start.3) | collective-permute-done | bytes 393248 | tf_op jit(solution)/shard_map/ppermute | solution.py:330
  69.6 9.5 %back.1 = (bf16[384,1024]{1,0:T(8,128)(2,1)}, f32[128,1536]{1,0:T(8,128)}, bf16[128,1536]{1,0:T(8,128)(2,1)}, bf16[128,1536]{1,0:T(8,128)(2,1)S(1)}, bf16[128,15...) custom-call(s32[8]{0:T(128)S(1)} %stack.32.order, ...), custom_call_target="tpu_custom_call" | custom-call | tf_op jit(solution)/shard_map/back/pallas_call | solution.py:211
  79.2 3.6 %collective-permute-start.10 = (bf16[128,1536]{1,0:T(8,128)(2,1)}, bf16[128,1536]{1,0:T(8,128)(2,1)S(1)}, u32[]{:S(2)}, u32[]{:S(2)}) collective-permute-start(bf16[128,1536]{1,0:T(8,128)(2,1)} %get-tuple-element.40), channel_id=1, source_target_pairs={{0,5},{1,4},{2,7},{3,6},{4,1},{5,0},{6,3},{7,2},{8,13},{9,12},{10,... | collective-permute-start | bytes 1179656 | tf_op jit(solution)/shard_map/ppermute | solution.py:272
  83.8 2.9 %convolution_bitcast_fusion = f32[1536,192]{0,1:T(8,128)S(1)} fusion(bf16[192,1024]{1,0:T(8,128)(2,1)} %get-tuple-element.28, bf16[1024,1536]{1,0:T(8,128)(2,1)} %bitcast.56), kind=kOutput, calls=%fused_computation.2 | convolution fusion | flops 603979776 | bytes 4718592 | tf_op jit(solution)/shard_map/dot_general | solution.py:354
  86.8 2.3 collective-permute-start.5
  89.1 3.2 %collective-permute-start.6 = (bf16[128,1536]{1,0:T(8,128)(2,1)S(1)}, bf16[128,1536]{1,0:T(8,128)(2,1)S(1)}, u32[]{:S(2)}, u32[]{:S(2)}) collective-permute-start(bf16[128,1536]{1,0:T(8,128)(2,1)S(1)} %get-tuple-element.36), channel_id=1, source_target_pairs={{0,1},{1,0},{2,3},{3,2},{4,5},{5,4},{6,7},{7,6},{8,9},{9,8},{10,11... | collective-permute-start | bytes 1179656 | tf_op jit(solution)/shard_map/ppermute | solution.py:272
  94.2 3.7 %collective-permute-start.8 = (bf16[128,1536]{1,0:T(8,128)(2,1)S(1)}, bf16[128,1536]{1,0:T(8,128)(2,1)S(1)}, u32[]{:S(2)}, u32[]{:S(2)}) collective-permute-start(bf16[128,1536]{1,0:T(8,128)(2,1)S(1)} %get-tuple-element.38), channel_id=1, source_target_pairs={{0,7},{1,6},{2,1},{3,0},{4,3},{5,2},{6,5},{7,4},{8,15},{9,14},{10,... | collective-permute-start | bytes 1179656 | tf_op jit(solution)/shard_map/ppermute | solution.py:272
  97.9 5.2 %collective-permute-done.4.rest_0_ = bf16[128,1536]{1,0:T(8,128)(2,1)S(1)} collective-permute-done((bf16[128,1536]{1,0:T(8,128)(2,1)}, bf16[128,1536]{1,0:T(8,128)(2,1)S(1)}, u32[]{:S(2)}, u32[]{:S(2)}) %collective-permute-start.4) | collective-permute-done | bytes 393248 | tf_op jit(solution)/shard_map/ppermute | solution.py:272
  105.5 4.1 %collective-permute-done.6.rest_2_ = bf16[128,1536]{1,0:T(8,128)(2,1)S(1)} collective-permute-done((bf16[128,1536]{1,0:T(8,128)(2,1)S(1)}, bf16[128,1536]{1,0:T(8,128)(2,1)S(1)}, u32[]{:S(2)}, u32[]{:S(2)}) %collective-permute-start.6) | collective-permute-done | bytes 393248 | tf_op jit(solution)/shard_map/ppermute | solution.py:272
  109.7 15.5 %collective-permute-done.7.rest_3_ = bf16[128,1536]{1,0:T(8,128)(2,1)S(1)} collective-permute-done((bf16[128,1536]{1,0:T(8,128)(2,1)S(1)}, bf16[128,1536]{1,0:T(8,128)(2,1)S(1)}, u32[]{:S(2)}, u32[]{:S(2)}) %collective-permute-start.7) | collective-permute-done | bytes 393248 | tf_op jit(solution)/shard_map/ppermute | solution.py:272
  125.1 10.2 %collective-permute-done.8.rest_4_ = bf16[128,1536]{1,0:T(8,128)(2,1)S(1)} collective-permute-done((bf16[128,1536]{1,0:T(8,128)(2,1)S(1)}, bf16[128,1536]{1,0:T(8,128)(2,1)S(1)}, u32[]{:S(2)}, u32[]{:S(2)}) %collective-permute-start.8) | collective-permute-done | bytes 393248 | tf_op jit(solution)/shard_map/ppermute | solution.py:272
  137.5 2.5 pad_maximum_fusion
  140.0 6.0 %copy.15 = f32[1536,768]{1,0:T(8,128)} copy(f32[1536,768]{0,1:T(8,128)} %pad_maximum_fusion) | data formatting | bytes 9437184 | tf_op jit(solution)/shard_map/concatenate | solution.py:357
  147.9 3.3 %collective-permute-start.12 = (bf16[128,1536]{1,0:T(8,128)(2,1)S(1)}, bf16[128,1536]{1,0:T(8,128)(2,1)S(1)}, u32[]{:S(2)}, u32[]{:S(2)}) collective-permute-start(bf16[128,1536]{1,0:T(8,128)(2,1)S(1)} %finish.1), channel_id=1, source_target_pairs={{0,6},{1,7},{2,0},{3,1},{4,2},{5,3},{6,4},{7,5},{8,14},{9,15},{10,... | collective-permute-start | bytes 1179656 | tf_op jit(solution)/shard_map/ppermute | solution.py:272
  155.6 4.1 %collective-permute-start.15 = (bf16[128,1536]{1,0:T(8,128)(2,1)S(1)}, bf16[128,1536]{1,0:T(8,128)(2,1)S(1)}, u32[]{:S(2)}, u32[]{:S(2)}) collective-permute-start(bf16[128,1536]{1,0:T(8,128)(2,1)S(1)} %finish.1), channel_id=1, source_target_pairs={{0,7},{1,6},{2,1},{3,0},{4,3},{5,2},{6,5},{7,4},{8,15},{9,14},{10,... | collective-permute-start | bytes 1179656 | tf_op jit(solution)/shard_map/ppermute | solution.py:272
  160.5 4.5 %collective-permute-done.12 = bf16[128,1536]{1,0:T(8,128)(2,1)S(1)} collective-permute-done((bf16[128,1536]{1,0:T(8,128)(2,1)S(1)}, bf16[128,1536]{1,0:T(8,128)(2,1)S(1)}, u32[]{:S(2)}, u32[]{:S(2)}) %collective-permute-start.12) | collective-permute-done | bytes 393248 | tf_op jit(solution)/shard_map/ppermute | solution.py:272
  166.8 3.9 %collective-permute-done.13 = bf16[128,1536]{1,0:T(8,128)(2,1)S(1)} collective-permute-done((bf16[128,1536]{1,0:T(8,128)(2,1)S(1)}, bf16[128,1536]{1,0:T(8,128)(2,1)S(1)}, u32[]{:S(2)}, u32[]{:S(2)}) %collective-permute-start.13) | collective-permute-done | bytes 393248 | tf_op jit(solution)/shard_map/ppermute | solution.py:272
  171.5 8.4 %collective-permute-done.14 = bf16[128,1536]{1,0:T(8,128)(2,1)S(1)} collective-permute-done((bf16[128,1536]{1,0:T(8,128)(2,1)S(1)}, bf16[128,1536]{1,0:T(8,128)(2,1)S(1)}, u32[]{:S(2)}, u32[]{:S(2)}) %collective-permute-start.14) | collective-permute-done | bytes 393248 | tf_op jit(solution)/shard_map/ppermute | solution.py:272
  183.1 4.6 %collective-permute-done.15 = bf16[128,1536]{1,0:T(8,128)(2,1)S(1)} collective-permute-done((bf16[128,1536]{1,0:T(8,128)(2,1)S(1)}, bf16[128,1536]{1,0:T(8,128)(2,1)S(1)}, u32[]{:S(2)}, u32[]{:S(2)}) %collective-permute-start.15) | collective-permute-done | bytes 393248 | tf_op jit(solution)/shard_map/ppermute | solution.py:272
  188.5 9.6 %collective-permute-done.16 = bf16[128,1536]{1,0:T(8,128)(2,1)S(1)} collective-permute-done((bf16[128,1536]{1,0:T(8,128)(2,1)S(1)}, bf16[128,1536]{1,0:T(8,128)(2,1)S(1)}, u32[]{:S(2)}, u32[]{:S(2)}) %collective-permute-start.16) | collective-permute-done | bytes 393248 | tf_op jit(solution)/shard_map/ppermute | solution.py:272
  201.7 3.1 %collective-permute-done.22 = bf16[96,768]{1,0:T(8,128)(2,1)S(1)} collective-permute-done((bf16[96,768]{1,0:T(8,128)(2,1)S(1)}, bf16[96,768]{1,0:T(8,128)(2,1)S(1)}, u32[]{:S(2)}, u32[]{:S(2)}) %collective-permute-start.22) | collective-permute-done | bytes 147488 | tf_op jit(solution)/shard_map/ppermute | solution.py:294
  205.8 38.7 %all-gather.5.cloned.1.call-done = bf16[1536,1536]{1,0:T(8,128)(2,1)} async-done(((bf16[192,1536]{1,0:T(8,128)(2,1)}), bf16[1536,1536]{1,0:T(8,128)(2,1)}) %all-gather.5.cloned.1.call-update) | async-done | bytes 4718608 | tf_op jit(solution)/shard_map/all_gather | solution.py:305
  244.5 9.3 %add_convert_fusion = bf16[1024,1536]{1,0:T(8,128)(2,1)} fusion(bf16[1024,1536]{1,0:T(8,128)(2,1)S(1)} %bitcast.62, bf16[1536,1024]{1,0:T(8,128)(2,1)} %all-gather.3.cloned.1.call-done, bf16[1536,1536]{1,0:T(8,128)(2,1)} %all-gather.5.cloned.1.call-done), kind=kOutput, calls=%fused_computation | convolution fusion | flops 4836556800 | bytes 14155776 | tf_op jit(solution)/shard_map/dot_general | solution.py:32
  (72 shorter events, 31.4 us)
Async XLA Ops:
  7.2 198.6 %all-gather.3.cloned.1.call-start = ((), (), s32[]{:S(2)}) async-start(), calls=%async_computation | async-start | bytes 3538944 | tf_op jit(solution)/shard_map/all_gather | solution.py:333
  10.4 16.2 %copy-start.4 = (s32[2,2048]{1,0:T(2,128)S(1)}, s32[2,2048]{1,0:T(2,128)}, u32[]{:S(2)}) copy-start(s32[2,2048]{1,0:T(2,128)} %param.15) | copy-start | bytes 49156
  10.4 16.2 %copy-start.5 = (s32[2]{0:T(128)S(1)}, s32[2]{0:T(128)}, u32[]{:S(2)}) copy-start(s32[2]{0:T(128)} %param.14) | copy-start | bytes 28
  20.8 12.7 %collective-permute-start = (bf16[384,512]{1,0:T(8,128)(2,1)S(1)}, bf16[384,512]{1,0:T(8,128)(2,1)S(1)}, u32[]{:S(2)}, u32[]{:S(2)}) collective-permute-start(bf16[384,512]{1,0:T(8,128)(2,1)S(1)} %get-tuple-element.25), channel_id=1, source_target_pairs={{0,8},{8,16},{16,24},{1,9},{9,17},{17,25},{2,10},{10,18},{18,26},{... | collective-permute-start | bytes 1179656 | tf_op jit(solution)/shard_map/ppermute | solution.py:325
  24.2 12.5 %collective-permute-start.1 = (bf16[384,512]{1,0:T(8,128)(2,1)S(1)}, bf16[384,512]{1,0:T(8,128)(2,1)S(1)}, u32[]{:S(2)}, u32[]{:S(2)}) collective-permute-start(bf16[384,512]{1,0:T(8,128)(2,1)S(1)} %get-tuple-element.26), channel_id=1, source_target_pairs={{8,0},{16,8},{24,16},{9,1},{17,9},{25,17},{10,2},{18,10},{26,18},{... | collective-permute-start | bytes 1179656 | tf_op jit(solution)/shard_map/ppermute | solution.py:326
  54.5 190.0 %all-gather.5.cloned.1.call-start = ((), (), s32[]{:S(2)}) async-start(), calls=%async_computation.1 | async-start | bytes 5308416 | tf_op jit(solution)/shard_map/all_gather | solution.py:305
  55.2 11.6 %collective-permute-start.2 = (bf16[384,512]{1,0:T(8,128)(2,1)S(1)}, bf16[384,512]{1,0:T(8,128)(2,1)S(1)}, u32[]{:S(2)}, u32[]{:S(2)}) collective-permute-start(bf16[384,512]{1,0:T(8,128)(2,1)S(1)} %get-tuple-element.31), channel_id=1, source_target_pairs={{0,8},{8,16},{16,24},{1,9},{9,17},{17,25},{2,10},{10,18},{18,26},{... | collective-permute-start | bytes 1179656 | tf_op jit(solution)/shard_map/ppermute | solution.py:331
  58.4 11.3 %collective-permute-start.3 = (bf16[384,512]{1,0:T(8,128)(2,1)S(1)}, bf16[384,512]{1,0:T(8,128)(2,1)S(1)}, u32[]{:S(2)}, u32[]{:S(2)}) collective-permute-start(bf16[384,512]{1,0:T(8,128)(2,1)S(1)} %get-tuple-element.32), channel_id=1, source_target_pairs={{8,0},{16,8},{24,16},{9,1},{17,9},{25,17},{10,2},{18,10},{26,18},{... | collective-permute-start | bytes 1179656 | tf_op jit(solution)/shard_map/ppermute | solution.py:330
  79.2 15.0 %collective-permute-start.10 = (bf16[128,1536]{1,0:T(8,128)(2,1)}, bf16[128,1536]{1,0:T(8,128)(2,1)S(1)}, u32[]{:S(2)}, u32[]{:S(2)}) collective-permute-start(bf16[128,1536]{1,0:T(8,128)(2,1)} %get-tuple-element.40), channel_id=1, source_target_pairs={{0,5},{1,4},{2,7},{3,6},{4,1},{5,0},{6,3},{7,2},{8,13},{9,12},{10,... | collective-permute-start | bytes 1179656 | tf_op jit(solution)/shard_map/ppermute | solution.py:272
  82.8 20.3 %collective-permute-start.4 = (bf16[128,1536]{1,0:T(8,128)(2,1)}, bf16[128,1536]{1,0:T(8,128)(2,1)S(1)}, u32[]{:S(2)}, u32[]{:S(2)}) collective-permute-start(bf16[128,1536]{1,0:T(8,128)(2,1)} %get-tuple-element.34), channel_id=1, source_target_pairs={{0,2},{1,3},{2,4},{3,5},{4,6},{5,7},{6,0},{7,1},{8,10},{9,11},{10,... | collective-permute-start | bytes 1179656 | tf_op jit(solution)/shard_map/ppermute | solution.py:272
  83.8 19.3 %copy-start.6 = (bf16[1024,1536]{1,0:T(8,128)(2,1)S(1)}, bf16[1024,1536]{1,0:T(8,128)(2,1)}, u32[]{:S(2)}) copy-start(bf16[1024,1536]{1,0:T(8,128)(2,1)} %get-tuple-element.41) | copy-start | bytes 9437188
  83.8 19.3 %copy-start.7 = (bf16[384,1024]{1,0:T(8,128)(2,1)S(1)}, bf16[384,1024]{1,0:T(8,128)(2,1)}, u32[]{:S(2)}) copy-start(bf16[384,1024]{1,0:T(8,128)(2,1)} %get-tuple-element.42) | copy-start | bytes 2359300
  86.8 18.8 %collective-permute-start.5 = (bf16[128,1536]{1,0:T(8,128)(2,1)S(1)}, bf16[128,1536]{1,0:T(8,128)(2,1)S(1)}, u32[]{:S(2)}, u32[]{:S(2)}) collective-permute-start(bf16[128,1536]{1,0:T(8,128)(2,1)S(1)} %get-tuple-element.35), channel_id=1, source_target_pairs={{0,6},{1,7},{2,0},{3,1},{4,2},{5,3},{6,4},{7,5},{8,14},{9,15},{10,... | collective-permute-start | bytes 1179656 | tf_op jit(solution)/shard_map/ppermute | solution.py:272
  89.1 20.6 %collective-permute-start.6 = (bf16[128,1536]{1,0:T(8,128)(2,1)S(1)}, bf16[128,1536]{1,0:T(8,128)(2,1)S(1)}, u32[]{:S(2)}, u32[]{:S(2)}) collective-permute-start(bf16[128,1536]{1,0:T(8,128)(2,1)S(1)} %get-tuple-element.36), channel_id=1, source_target_pairs={{0,1},{1,0},{2,3},{3,2},{4,5},{5,4},{6,7},{7,6},{8,9},{9,8},{10,11... | collective-permute-start | bytes 1179656 | tf_op jit(solution)/shard_map/ppermute | solution.py:272
  92.3 32.9 %collective-permute-start.7 = (bf16[128,1536]{1,0:T(8,128)(2,1)S(1)}, bf16[128,1536]{1,0:T(8,128)(2,1)S(1)}, u32[]{:S(2)}, u32[]{:S(2)}) collective-permute-start(bf16[128,1536]{1,0:T(8,128)(2,1)S(1)} %get-tuple-element.37), channel_id=1, source_target_pairs={{0,3},{1,2},{2,5},{3,4},{4,7},{5,6},{6,1},{7,0},{8,11},{9,10},{10,... | collective-permute-start | bytes 1179656 | tf_op jit(solution)/shard_map/ppermute | solution.py:272
  94.2 41.2 %collective-permute-start.8 = (bf16[128,1536]{1,0:T(8,128)(2,1)S(1)}, bf16[128,1536]{1,0:T(8,128)(2,1)S(1)}, u32[]{:S(2)}, u32[]{:S(2)}) collective-permute-start(bf16[128,1536]{1,0:T(8,128)(2,1)S(1)} %get-tuple-element.38), channel_id=1, source_target_pairs={{0,7},{1,6},{2,1},{3,0},{4,3},{5,2},{6,5},{7,4},{8,15},{9,14},{10,... | collective-permute-start | bytes 1179656 | tf_op jit(solution)/shard_map/ppermute | solution.py:272
  103.1 32.3 %collective-permute-start.9 = (bf16[128,1536]{1,0:T(8,128)(2,1)S(1)}, bf16[128,1536]{1,0:T(8,128)(2,1)S(1)}, u32[]{:S(2)}, u32[]{:S(2)}) collective-permute-start(bf16[128,1536]{1,0:T(8,128)(2,1)S(1)} %get-tuple-element.39), channel_id=1, source_target_pairs={{0,4},{1,5},{2,6},{3,7},{4,0},{5,1},{6,2},{7,3},{8,12},{9,13},{10,... | collective-permute-start | bytes 1179656 | tf_op jit(solution)/shard_map/ppermute | solution.py:272
  103.1 32.3 %copy-start.1 = (f32[128,1536]{1,0:T(8,128)S(1)}, f32[128,1536]{1,0:T(8,128)}, u32[]{:S(2)}) copy-start(f32[128,1536]{1,0:T(8,128)} %get-tuple-element.33.mine) | copy-start | bytes 2359300
  137.4 18.2 %collective-permute-start.11 = (bf16[128,1536]{1,0:T(8,128)(2,1)S(1)}, bf16[128,1536]{1,0:T(8,128)(2,1)S(1)}, u32[]{:S(2)}, u32[]{:S(2)}) collective-permute-start(bf16[128,1536]{1,0:T(8,128)(2,1)S(1)} %finish.1), channel_id=1, source_target_pairs={{0,2},{1,3},{2,4},{3,5},{4,6},{5,7},{6,0},{7,1},{8,10},{9,11},{10,... | collective-permute-start | bytes 1179656 | tf_op jit(solution)/shard_map/ppermute | solution.py:272
  147.8 32.9 %copy-start.2 = (f32[1536,768]{1,0:T(8,128)S(1)}, f32[1536,768]{1,0:T(8,128)}, u32[]{:S(2)}) copy-start(f32[1536,768]{1,0:T(8,128)} %copy.15) | copy-start | bytes 14155780
  147.8 32.8 %collective-permute-start.18 = (bf16[2,4,96,768]{3,2,1,0:T(8,128)(2,1)S(1)}, bf16[2,4,96,768]{3,2,1,0:T(8,128)(2,1)S(1)}, u32[]{:S(2)}, u32[]{:S(2)}) collective-permute-start(bf16[2,4,96,768]{3,2,1,0:T(8,128)(2,1)S(1)} %fusion), channel_id=1, source_target_pairs={{0,32},{32,0},{64,96},{96,64},{1,33},{33,1},{65,97},{97,65},{2,34}... | collective-permute-start | bytes 3538952 | tf_op jit(solution)/shard_map/ppermute | solution.py:286
  147.9 17.0 %collective-permute-start.12 = (bf16[128,1536]{1,0:T(8,128)(2,1)S(1)}, bf16[128,1536]{1,0:T(8,128)(2,1)S(1)}, u32[]{:S(2)}, u32[]{:S(2)}) collective-permute-start(bf16[128,1536]{1,0:T(8,128)(2,1)S(1)} %finish.1), channel_id=1, source_target_pairs={{0,6},{1,7},{2,0},{3,1},{4,2},{5,3},{6,4},{7,5},{8,14},{9,15},{10,... | collective-permute-start | bytes 1179656 | tf_op jit(solution)/shard_map/ppermute | solution.py:272
  151.2 19.5 %collective-permute-start.13 = (bf16[128,1536]{1,0:T(8,128)(2,1)S(1)}, bf16[128,1536]{1,0:T(8,128)(2,1)S(1)}, u32[]{:S(2)}, u32[]{:S(2)}) collective-permute-start(bf16[128,1536]{1,0:T(8,128)(2,1)S(1)} %finish.1), channel_id=1, source_target_pairs={{0,1},{1,0},{2,3},{3,2},{4,5},{5,4},{6,7},{7,6},{8,9},{9,8},{10,11... | collective-permute-start | bytes 1179656 | tf_op jit(solution)/shard_map/ppermute | solution.py:272
  151.4 28.5 %collective-permute-start.14 = (bf16[128,1536]{1,0:T(8,128)(2,1)S(1)}, bf16[128,1536]{1,0:T(8,128)(2,1)S(1)}, u32[]{:S(2)}, u32[]{:S(2)}) collective-permute-start(bf16[128,1536]{1,0:T(8,128)(2,1)S(1)} %finish.1), channel_id=1, source_target_pairs={{0,3},{1,2},{2,5},{3,4},{4,7},{5,6},{6,1},{7,0},{8,11},{9,10},{10,... | collective-permute-start | bytes 1179656 | tf_op jit(solution)/shard_map/ppermute | solution.py:272
  155.6 32.1 %collective-permute-start.15 = (bf16[128,1536]{1,0:T(8,128)(2,1)S(1)}, bf16[128,1536]{1,0:T(8,128)(2,1)S(1)}, u32[]{:S(2)}, u32[]{:S(2)}) collective-permute-start(bf16[128,1536]{1,0:T(8,128)(2,1)S(1)} %finish.1), channel_id=1, source_target_pairs={{0,7},{1,6},{2,1},{3,0},{4,3},{5,2},{6,5},{7,4},{8,15},{9,14},{10,... | collective-permute-start | bytes 1179656 | tf_op jit(solution)/shard_map/ppermute | solution.py:272
  165.0 33.1 %collective-permute-start.16 = (bf16[128,1536]{1,0:T(8,128)(2,1)S(1)}, bf16[128,1536]{1,0:T(8,128)(2,1)S(1)}, u32[]{:S(2)}, u32[]{:S(2)}) collective-permute-start(bf16[128,1536]{1,0:T(8,128)(2,1)S(1)} %finish.1), channel_id=1, source_target_pairs={{0,4},{1,5},{2,6},{3,7},{4,0},{5,1},{6,2},{7,3},{8,12},{9,13},{10,... | collective-permute-start | bytes 1179656 | tf_op jit(solution)/shard_map/ppermute | solution.py:272
  170.7 30.1 %collective-permute-start.17 = (bf16[128,1536]{1,0:T(8,128)(2,1)S(1)}, bf16[128,1536]{1,0:T(8,128)(2,1)S(1)}, u32[]{:S(2)}, u32[]{:S(2)}) collective-permute-start(bf16[128,1536]{1,0:T(8,128)(2,1)S(1)} %finish.1), channel_id=1, source_target_pairs={{0,5},{1,4},{2,7},{3,6},{4,1},{5,0},{6,3},{7,2},{8,13},{9,12},{10,... | collective-permute-start | bytes 1179656 | tf_op jit(solution)/shard_map/ppermute | solution.py:272
  181.0 63.5 %copy-start.3 = (bf16[2,512,1536]{2,1,0:T(8,128)(2,1)S(1)}, bf16[2,512,1536]{2,1,0:T(8,128)(2,1)}, u32[]{:S(2)}) copy-start(bf16[2,512,1536]{2,1,0:T(8,128)(2,1)} %param.8) | copy-start | bytes 9437188
  181.0 17.8 %collective-permute-start.19 = (bf16[2,96,768]{2,1,0:T(8,128)(2,1)S(1)}, bf16[2,96,768]{2,1,0:T(8,128)(2,1)S(1)}, u32[]{:S(2)}, u32[]{:S(2)}) collective-permute-start(bf16[2,96,768]{2,1,0:T(8,128)(2,1)S(1)} %get-tuple-element.43), channel_id=1, source_target_pairs={{0,8},{8,16},{16,24},{24,0},{1,9},{9,17},{17,25},{25,1},{2,10},{10... | collective-permute-start | bytes 884744 | tf_op jit(solution)/shard_map/ppermute | solution.py:291
  181.7 17.1 %collective-permute-start.20 = (bf16[2,96,768]{2,1,0:T(8,128)(2,1)S(1)}, bf16[2,96,768]{2,1,0:T(8,128)(2,1)S(1)}, u32[]{:S(2)}, u32[]{:S(2)}) collective-permute-start(bf16[2,96,768]{2,1,0:T(8,128)(2,1)S(1)} %get-tuple-element.45), channel_id=1, source_target_pairs={{0,24},{8,0},{16,8},{24,16},{1,25},{9,1},{17,9},{25,17},{2,26},{10... | collective-permute-start | bytes 884744 | tf_op jit(solution)/shard_map/ppermute | solution.py:291
  187.7 11.1 %collective-permute-start.21 = (bf16[2,96,768]{2,1,0:T(8,128)(2,1)S(1)}, bf16[2,96,768]{2,1,0:T(8,128)(2,1)S(1)}, u32[]{:S(2)}, u32[]{:S(2)}) collective-permute-start(bf16[2,96,768]{2,1,0:T(8,128)(2,1)S(1)} %get-tuple-element.44), channel_id=1, source_target_pairs={{0,16},{8,24},{16,0},{24,8},{1,17},{9,25},{17,1},{25,9},{2,18},{10... | collective-permute-start | bytes 884744 | tf_op jit(solution)/shard_map/ppermute | solution.py:291
  199.0 5.7 %collective-permute-start.22 = (bf16[96,768]{1,0:T(8,128)(2,1)S(1)}, bf16[96,768]{1,0:T(8,128)(2,1)S(1)}, u32[]{:S(2)}, u32[]{:S(2)}) collective-permute-start(bf16[96,768]{1,0:T(8,128)(2,1)S(1)} %fusion.10), channel_id=1, source_target_pairs={{0,64},{32,96},{64,0},{96,32},{1,65},{33,97},{65,1},{97,33},{2,66}... | collective-permute-start | bytes 442376 | tf_op jit(solution)/shard_map/ppermute | solution.py:294
  (1 other events, 1.1 us)
Sparse Core Ops, SparseCore 0:
  54.6 85.9 all-gather.2
  142.9 101.5 all-gather.4

commit v2 on v1

v2 whole, which is shorter than its diff:
```python
import jax
import jax.numpy as jnp
from jax import lax
from jax.experimental import pallas as pl
from jax.experimental.pallas import tpu as pltpu
from jax.sharding import PartitionSpec as P

HEAD = 64
CTX = 256
EPS = 1e-05
NEG = -1e30
VMEM_LIMIT = 50 * 1024 * 1024
SHIFTS = ((1, 0), (3, 0), (0, 1), (1, 1), (3, 1), (2, 0), (2, 1))
SPREAD = (0, 1, 2, 3)

F32 = jnp.float32
BF16 = jnp.bfloat16


def params():
    return pltpu.CompilerParams(vmem_limit_bytes=VMEM_LIMIT)


def dot_nn(a, b):
    return lax.dot_general(a, b, (((1,), (0,)), ((), ())), preferred_element_type=F32)


def dot_nt(a, b):
    return lax.dot_general(a, b, (((1,), (1,)), ((), ())), preferred_element_type=F32)


def dot_tn(a, b):
    return lax.dot_general(a, b, (((0,), (0,)), ((), ())), preferred_element_type=F32)


def norm_stats(tokens):
    values = tokens.astype(F32)
    centered = values - jnp.mean(values, axis=-1, keepdims=True)
    inverse = lax.rsqrt(jnp.mean(centered * centered, axis=-1, keepdims=True) + EPS)
    return centered * inverse, inverse


def project_body(
    lengths, tok, cot, gain, bias, weight, out_w, normed, q, kv, g, kv_first, kv_last, live
):
    width = q.shape[0]
    scaled, _ = norm_stats(tok[...])
    rows = (scaled * gain[...][None, :] + bias[...][None, :]).astype(BF16)
    normed[...] = rows
    qkv = dot_nt(weight[...], rows).astype(BF16)
    q[...] = qkv[:width]
    kv[...] = qkv[width:]
    step = pl.program_id(0)

    @pl.when(step % 2 == 0)
    def _():
        kv_first[...] = qkv[width:]

    @pl.when(step % 2 == 1)
    def _():
        kv_last[...] = qkv[width:]

    start = lax.axis_index("frames") * (2 * CTX) + (step % 2) * CTX
    position = start + lax.broadcasted_iota(jnp.int32, (1, CTX), 1)
    alive = jnp.where(position < lengths[step // 2], 1.0, 0.0)
    live[...] = alive
    g[...] = (dot_nt(out_w[...], cot[...]) * alive).astype(BF16)


def project(lengths, tokens, cotangent, gain, bias, weight, out_w):
    rows, model = tokens.shape
    width = out_w.shape[0]
    full = lambda shape: pl.BlockSpec(shape, lambda i: (0,) * len(shape))
    by_row = pl.BlockSpec((CTX, model), lambda i: (i, 0))
    by_col = lambda n: pl.BlockSpec((n, CTX), lambda i: (0, i))
    by_half = pl.BlockSpec((2 * width, CTX), lambda i: (0, i // 2))
    return pl.pallas_call(
        project_body,
        grid=(rows // CTX,),
        in_specs=[
            pl.BlockSpec(memory_space=pltpu.SMEM),
            by_row,
            by_row,
            full((model,)),
            full((model,)),
            full((3 * width, model)),
            full((width, model)),
        ],
        out_specs=[
            by_row,
            by_col(width),
            by_col(2 * width),
            by_col(width),
            by_half,
            by_half,
            by_col(1),
        ],
        out_shape=[
            jax.ShapeDtypeStruct((rows, model), BF16),
            jax.ShapeDtypeStruct((width, rows), BF16),
            jax.ShapeDtypeStruct((2 * width, rows), BF16),
            jax.ShapeDtypeStruct((width, rows), BF16),
            jax.ShapeDtypeStruct((2 * width, rows // 2), BF16),
            jax.ShapeDtypeStruct((2 * width, rows // 2), BF16),
            jax.ShapeDtypeStruct((1, rows), F32),
        ],
        compiler_params=params(),
        cost_estimate=pl.CostEstimate(flops=2400000000, bytes_accessed=15000000, transcendentals=0),
        name="project",
    )(lengths, tokens, cotangent, gain, bias, weight, out_w)


def attention_body(
    q,
    kv,
    before,
    after,
    g,
    seg_keys,
    seg_rows,
    live,
    mixed,
    dq,
    dkv,
    dbefore,
    dafter,
    peer_grads,
    peer_before,
    peer_after,
    acc,
    mask,
):
    width = q.shape[0]
    span = 3 * CTX
    kv_all = jnp.concatenate([before[...], kv[...], after[...]], axis=1)
    q_small = q[...] * jnp.asarray(HEAD**-0.5, BF16)
    grads = g[...]
    acc[...] = jnp.zeros_like(acc)
    for tile in range(2):
        cols = slice(tile * CTX, (tile + 1) * CTX)
        keys = slice(tile * CTX, tile * CTX + span)
        away = (
            lax.broadcasted_iota(jnp.int32, (span, CTX), 0)
            - CTX
            - lax.broadcasted_iota(jnp.int32, (span, CTX), 1)
        )
        near = jnp.abs(away) <= CTX
        stretch = jnp.abs(seg_keys[0, keys, :] - seg_rows[0, :, cols]) <= 1
        visible = (near & stretch) | (away == 0)
        mask[...] = jnp.where(visible, 0.0, NEG)
        for head in range(width // HEAD):
            d = slice(head * HEAD, (head + 1) * HEAD)
            dv = slice(width + head * HEAD, width + (head + 1) * HEAD)
            k_t, v_t = kv_all[d, keys], kv_all[dv, keys]
            q_t, g_t = q_small[d, cols], grads[d, cols]
            scores = dot_tn(k_t, q_t) + mask[...]
            weights = jnp.exp(scores - jnp.max(scores, axis=0, keepdims=True))
            weights = weights * (1.0 / jnp.sum(weights, axis=0, keepdims=True))
            rounded = weights.astype(BF16)
            mixed[d, cols] = (dot_nn(v_t, rounded) * live[:, cols]).astype(BF16)
            grad_w = dot_tn(v_t, g_t)
            total = jnp.sum(weights * grad_w, axis=0, keepdims=True)
            grad_s = (weights * (grad_w - total)).astype(BF16)
            dq[d, cols] = (dot_nn(k_t, grad_s) * (HEAD**-0.5)).astype(BF16)
            acc[d, keys] += dot_nt(q_t, grad_s)
            acc[dv, keys] += dot_nt(g_t, rounded)
    frames = q.shape[1]
    dkv[...] = acc[:, CTX : CTX + frames]
    dbefore[...] = acc[:, :CTX].astype(BF16)
    dafter[...] = acc[:, CTX + frames :].astype(BF16)

    @pl.when(pl.program_id(0) != lax.axis_index("chan") % 2)
    def _():
        peer_grads[:width, :] = dq[...]
        peer_grads[width:, :] = acc[:, CTX : CTX + frames].astype(BF16)
        peer_before[...] = dbefore[...]
        peer_after[...] = dafter[...]


def attention(q, kv, before, after, g, seg_keys, seg_rows, live):
    width, rows = q.shape
    recs, span, _ = seg_keys.shape
    frames = rows // recs
    by_rec = lambda n, m: pl.BlockSpec((n, m), lambda r: (0, r))
    fixed = lambda n, m: pl.BlockSpec((n, m), lambda r: (0, 0))
    return pl.pallas_call(
        attention_body,
        grid=(recs,),
        in_specs=[
            by_rec(width, frames),
            by_rec(2 * width, frames),
            by_rec(2 * width, CTX),
            by_rec(2 * width, CTX),
            by_rec(width, frames),
            pl.BlockSpec((1, span, 1), lambda r: (r, 0, 0)),
            pl.BlockSpec((1, 1, frames), lambda r: (r, 0, 0)),
            by_rec(1, frames),
        ],
        out_specs=[
            by_rec(width, frames),
            by_rec(width, frames),
            by_rec(2 * width, frames),
            by_rec(2 * width, CTX),
            by_rec(2 * width, CTX),
            fixed(3 * width, frames),
            fixed(2 * width, CTX),
            fixed(2 * width, CTX),
        ],
        out_shape=[
            jax.ShapeDtypeStruct((width, rows), BF16),
            jax.ShapeDtypeStruct((width, rows), BF16),
            jax.ShapeDtypeStruct((2 * width, rows), F32),
            jax.ShapeDtypeStruct((2 * width, recs * CTX), BF16),
            jax.ShapeDtypeStruct((2 * width, recs * CTX), BF16),
            jax.ShapeDtypeStruct((3 * width, frames), BF16),
            jax.ShapeDtypeStruct((2 * width, CTX), BF16),
            jax.ShapeDtypeStruct((2 * width, CTX), BF16),
        ],
        scratch_shapes=[pltpu.VMEM((2 * width, span), F32), pltpu.VMEM((3 * CTX, CTX), F32)],
        compiler_params=params(),
        cost_estimate=pl.CostEstimate(flops=2400000000, bytes_accessed=8000000, transcendentals=0),
        name="attention",
    )(q, kv, before, after, g, seg_keys, seg_rows, live)


def back_body(
    here, dq, own, left, right, peer, peer_left, peer_right, weight, peer_weight, mine, *rest
):
    parts, (flipped, sums) = rest[:-2], rest[-2:]
    width = dq.shape[0]
    chunk = mine.shape[0]

    @pl.when(pl.program_id(0) == 0)
    def _():
        beside = jnp.concatenate([left[...], right[...]], axis=1).astype(F32)
        peer_beside = jnp.concatenate([peer_left[...], peer_right[...]], axis=1).astype(F32)
        flipped[:, :width] = dq[...].T
        flipped[:, width : 3 * width] = (own[...] + beside).astype(BF16).T
        flipped[:, 3 * width : 4 * width] = peer[:width, :].T
        flipped[:, 4 * width :] = (peer[width:, :].astype(F32) + peer_beside).astype(BF16).T

    sums[...] = dot_nn(flipped[:, : 3 * width], weight[...]) + dot_nn(
        flipped[:, 3 * width :], peer_weight[...]
    )
    z = here[0] >> 1
    for index, part in enumerate((mine,) + parts):
        rows = pl.ds(pl.multiple_of(((z + index) & 3) * chunk, chunk), chunk)
        part[...] = sums[rows, :].astype(part.dtype)


def back_parts(here, dq, own, left, right, peer, peer_left, peer_right, weight, peer_weight):
    width = dq.shape[0]
    frames = peer.shape[1]
    model = weight.shape[1]
    chunk = frames // 4
    tile = 256
    full = lambda n, m: pl.BlockSpec((n, m), lambda i, h: (0, 0))
    by_rec = lambda n, m: pl.BlockSpec((n, m), lambda i, h: (0, h[0] & 1))
    by_col = lambda n: pl.BlockSpec((n, tile), lambda i, h: (0, i))
    return pl.pallas_call(
        back_body,
        grid_spec=pltpu.PrefetchScalarGridSpec(
            num_scalar_prefetch=1,
            grid=(model // tile,),
            in_specs=[
                by_rec(width, frames),
                by_rec(2 * width, frames),
                by_rec(2 * width, CTX),
                by_rec(2 * width, CTX),
                full(3 * width, frames),
                full(2 * width, CTX),
                full(2 * width, CTX),
                by_col(3 * width),
                by_col(3 * width),
            ],
            out_specs=[by_col(chunk)] * 4,
            scratch_shapes=[
                pltpu.VMEM((frames, 6 * width), BF16),
                pltpu.VMEM((frames, tile), F32),
            ],
        ),
        out_shape=[jax.ShapeDtypeStruct((chunk, model), F32)]
        + [jax.ShapeDtypeStruct((chunk, model), BF16)] * 3,
        compiler_params=params(),
        cost_estimate=pl.CostEstimate(flops=1800000000, bytes_accessed=8000000, transcendentals=0),
        name="back",
    )(here, dq, own, left, right, peer, peer_left, peer_right, weight, peer_weight)


def weight_grads_body(normed, cot, dq, own, left, right, mixed, sent, kept, gkv):
    width = dq.shape[0]

    @pl.when(pl.program_id(0) == 0)
    def _():
        beside = []
        for rec in range(own.shape[1] // (2 * CTX)):
            cols = slice(rec * CTX, (rec + 1) * CTX)
            beside += [left[:, cols], right[:, cols]]
        gkv[...] = (own[...] + jnp.concatenate(beside, axis=1).astype(F32)).astype(BF16)

    turned = normed[...].T
    sums = [
        dot_nt(turned, dq[...]),
        dot_nt(turned, gkv[...]),
        dot_nt(cot[...].T, mixed[...]),
    ]
    offsets = (0, width, 3 * width)

    @pl.when(pl.program_id(0) < 2)
    def _():
        for part, offset in zip(sums, offsets):
            sent[0, :, offset : offset + part.shape[1]] = part.astype(BF16)

    @pl.when(pl.program_id(0) >= 2)
    def _():
        for part, offset in zip(sums, offsets):
            kept[0, :, offset : offset + part.shape[1]] = part


def weight_grads(core, normed, cotangent, dq, own, left, right, mixed):
    rows, model = normed.shape
    width = dq.shape[0]
    block = model // 4

    def by_step(i, c):
        return (0, (i % 2) * 2 + jnp.where(i < 2, 1 - c[0], c[0]))

    full = lambda n: pl.BlockSpec((n, rows), lambda i, c: (0, 0))
    half = pl.BlockSpec((2 * width, rows // 2), lambda i, c: (0, 0))
    return pl.pallas_call(
        lambda c, *refs: weight_grads_body(*refs),
        grid_spec=pltpu.PrefetchScalarGridSpec(
            num_scalar_prefetch=1,
            grid=(4,),
            in_specs=[
                pl.BlockSpec((rows, block), by_step),
                pl.BlockSpec((rows, block), by_step),
                full(width),
                full(2 * width),
                half,
                half,
                full(width),
            ],
            out_specs=[
                pl.BlockSpec((1, block, 4 * width), lambda i, c: (jnp.minimum(i, 1), 0, 0)),
                pl.BlockSpec((1, block, 4 * width), lambda i, c: (jnp.maximum(i, 2) - 2, 0, 0)),
            ],
            scratch_shapes=[pltpu.VMEM((2 * width, rows), BF16)],
        ),
        out_shape=[
            jax.ShapeDtypeStruct((2, block, 4 * width), BF16),
            jax.ShapeDtypeStruct((2, block, 4 * width), F32),
        ],
        compiler_params=params(),
        cost_estimate=pl.CostEstimate(flops=2400000000, bytes_accessed=12000000, transcendentals=0),
        name="weight_grads",
    )(core, normed, cotangent, dq, own, left, right, mixed)


def output_body(tok, near, far, weight, out, stacked):
    me = lax.axis_index("chan")
    depth = weight.shape[0]
    width = depth // (2 * len(SPREAD))
    for index, dz in enumerate(SPREAD):
        rows = slice(index * width, (index + 1) * width)
        for side, source in ((0, near), (1, far)):
            chan = (((me >> 1) - dz) & 3) * 2 + ((me & 1) ^ side)
            place = pl.ds(pl.multiple_of(chan * width, width), width)
            stacked[place, :] = source[rows, :]
    total = tok[...].astype(F32) + dot_nn(stacked[...].T, weight[...])
    out[...] = total.astype(BF16)


def output_rows(tokens, near, far, weight):
    rows, model = tokens.shape
    by_row = pl.BlockSpec((CTX, model), lambda i: (i, 0))
    by_col = pl.BlockSpec((near.shape[0], CTX), lambda i: (0, i))
    return pl.pallas_call(
        output_body,
        grid=(rows // CTX,),
        in_specs=[by_row, by_col, by_col, pl.BlockSpec(weight.shape, lambda i: (0, 0))],
        out_specs=by_row,
        out_shape=jax.ShapeDtypeStruct((rows, model), BF16),
        scratch_shapes=[pltpu.VMEM((weight.shape[0], CTX), BF16)],
        compiler_params=params(),
        cost_estimate=pl.CostEstimate(flops=4800000000, bytes_accessed=14000000, transcendentals=0),
        name="output",
    )(tokens, near, far, weight)


def finish_body(place, tok, cot, gain, mine, *rest):
    parts, out = rest[:-1], rest[-1]
    back = mine[...]
    for part in parts:
        back = back + part[...].astype(F32)
    scaled, inverse = norm_stats(tok[...])
    weighted = back * gain[...][None, :]
    first = jnp.mean(weighted, axis=-1, keepdims=True)
    second = jnp.mean(weighted * scaled, axis=-1, keepdims=True)
    grad = inverse * (weighted - first - scaled * second) + cot[...].astype(F32)
    out[...] = grad.astype(BF16)


def finish(place, tokens, cotangent, gain, mine, parts):
    chunk, model = mine.shape
    here = pl.BlockSpec((chunk, model), lambda i, p: (p[0], 0))
    whole = pl.BlockSpec((chunk, model), lambda i, p: (0, 0))
    return pl.pallas_call(
        finish_body,
        grid_spec=pltpu.PrefetchScalarGridSpec(
            num_scalar_prefetch=1,
            grid=(1,),
            in_specs=[here, here, pl.BlockSpec((model,), lambda i, p: (0,))]
            + [whole] * (1 + len(parts)),
            out_specs=whole,
        ),
        out_shape=jax.ShapeDtypeStruct((chunk, model), BF16),
        compiler_params=params(),
        cost_estimate=pl.CostEstimate(flops=10000000, bytes_accessed=5000000, transcendentals=0),
        name="finish",
    )(place, tokens, cotangent, gain, mine, *parts)


def assemble_body(places, *refs):
    pieces, out, sems = refs[:-2], refs[-2], refs[-1]
    chunk = pieces[0].shape[0]
    copies = []
    for index, piece in enumerate(pieces):
        rows = pl.ds(pl.multiple_of(places[index] * chunk, chunk), chunk)
        copies.append(pltpu.make_async_copy(piece, out.at[rows, :], sems.at[index]))
    for copy in copies:
        copy.start()
    for copy in copies:
        copy.wait()


def assemble(places, pieces):
    chunk, model = pieces[0].shape
    count = len(pieces)
    anywhere = pl.BlockSpec(memory_space=pl.ANY)
    return pl.pallas_call(
        assemble_body,
        in_specs=[pl.BlockSpec(memory_space=pltpu.SMEM)] + [anywhere] * count,
        out_specs=anywhere,
        out_shape=jax.ShapeDtypeStruct((count * chunk, model), BF16),
        scratch_shapes=[pltpu.SemaphoreType.DMA((count,))],
        compiler_params=params(),
        cost_estimate=pl.CostEstimate(flops=0, bytes_accessed=6000000, transcendentals=0),
        name="assemble",
    )(places, *pieces)


def to_peer(array, shift):
    dz, dy = shift
    pairs = [
        (z * 2 + y, ((z + dz) % 4) * 2 + (y + dy) % 2) for z in range(4) for y in range(2)
    ]
    return lax.ppermute(array, "chan", pairs)


def piece_index(me, shift):
    dz, dy = shift
    return ((me & 1) ^ dy) * 4 + (((me >> 1) - dz) & 3)


def pick(array, index, axis):
    return lax.dynamic_index_in_dim(array, index, axis, keepdims=False)


def pair_sums(got, kept):
    frame = lax.axis_index("frames")
    pair = (kept + got.astype(F32)).reshape(2, 4, -1, kept.shape[-1])
    sums = pick(pair, frame, 1)
    for shift in (1, 3, 2):
        sent = pick(pair, (frame + shift) & 3, 1).astype(BF16)
        got = lax.ppermute(sent, "frames", [(i, (i + shift) % 4) for i in range(4)])
        sums = sums + got.astype(F32)
    return sums


def row_sums(sums):
    row = lax.axis_index("batch") >> 1
    sent = pick(sums, 1 - row, 0).astype(BF16)
    got = lax.ppermute(sent, "batch", [(0, 2), (1, 3), (2, 0), (3, 1)])
    return pick(sums, row, 0) + got.astype(F32)


def shards(tokens, cotangent, norm_gain, norm_bias, qkv_weight, out_weight, lengths, segments):
    recs, frames, model = tokens.shape
    rows = recs * frames
    width = out_weight.shape[0]
    me = lax.axis_index("chan")
    start = lax.axis_index("frames") * frames
    scalar = lambda value: value.reshape(1).astype(jnp.int32)

    weight = qkv_weight.transpose(1, 2, 0).reshape(3 * width, model)
    peer_weight = to_peer(weight, (0, 1))
    full_out = lax.all_gather(out_weight, "chan", tiled=True)

    flat_tokens = tokens.reshape(rows, model)
    flat_cot = cotangent.reshape(rows, model)
    reach = start - CTX + jnp.arange(frames + 2 * CTX, dtype=jnp.int32)
    padded = jnp.pad(segments, ((0, 0), (CTX, CTX)), constant_values=-10)
    seg_keys = lax.dynamic_slice_in_dim(padded, start, frames + 2 * CTX, 1)
    seg_keys = jnp.where(reach[None, :] < lengths[:, None], seg_keys, -10)[:, :, None]
    seg_rows = lax.dynamic_slice_in_dim(segments, start, frames, 1)[:, None, :]

    normed, q, kv, g, kv_first, kv_last, live = project(
        lengths, flat_tokens, flat_cot, norm_gain, norm_bias, weight, out_weight
    )
    size = lax.axis_size("frames")
    up = [(i, i + 1) for i in range(size - 1)]
    down = [(i + 1, i) for i in range(size - 1)]
    before = lax.ppermute(kv_last, "frames", up)
    after = lax.ppermute(kv_first, "frames", down)
    mixed, dq, dkv, dbefore, dafter, peer_grads, peer_before, peer_after = attention(
        q, kv, before, after, g, seg_keys, seg_rows, live
    )
    tie = lax.optimization_barrier
    dbefore, dafter, peer_grads, peer_before, peer_after, peer_weight = tie(
        (dbefore, dafter, peer_grads, peer_before, peer_after, peer_weight)
    )
    cross = lambda pairs: [(a * 8 + c, b * 8 + (c ^ 1)) for a, b in pairs for c in range(8)]
    both = ("frames", "chan")
    peer_grads = to_peer(peer_grads, (0, 1))
    peer_right = lax.ppermute(peer_before, both, cross(down))
    peer_left = lax.ppermute(peer_after, both, cross(up))
    from_right = lax.ppermute(dbefore, "frames", down)
    from_left = lax.ppermute(dafter, "frames", up)

    late_mixed, from_left, from_right = tie((mixed, from_left, from_right))
    core = scalar(lax.axis_index("batch") & 1)
    sent, kept = weight_grads(core, normed, flat_cot, dq, dkv, from_left, from_right, mixed)
    sent, peer_grads, peer_left, peer_right = tie((sent, peer_grads, peer_left, peer_right))

    mine, *parts = back_parts(
        scalar(me),
        dq,
        dkv,
        from_left,
        from_right,
        peer_grads,
        peer_left,
        peer_right,
        weight,
        peer_weight,
    )
    near = [to_peer(late_mixed, (dz, 0)) for dz in SPREAD[1:]]
    got = [to_peer(part, (dz, 0)) for part, dz in zip(parts, SPREAD[1:])]
    pair = lax.ppermute(sent, "batch", [(0, 1), (1, 0), (2, 3), (3, 2)])
    near, pair, got[0] = tie((near, pair, got[0]))
    near_mixed = jnp.concatenate([mixed] + near, axis=0)
    sums = pair_sums(pair, kept)
    far_mixed = to_peer(near_mixed, (0, 1))
    sums, full_out = tie((sums, full_out))

    here = piece_index(me, (0, 0))
    piece = finish(scalar(here), flat_tokens, flat_cot, norm_gain, mine, got)

    places = jnp.stack([here] + [piece_index(me, shift) for shift in SHIFTS]).astype(jnp.int32)
    grad_tokens = assemble(places, [piece] + [to_peer(piece, shift) for shift in SHIFTS])
    grad_proj = row_sums(sums).reshape(-1, 4, width)
    output = output_rows(flat_tokens, near_mixed, far_mixed, full_out)
    shape = (recs, frames, model)
    return (output.reshape(shape), grad_tokens.reshape(shape), grad_proj)


def solution(mesh):
    return jax.shard_map(
        shards,
        mesh=mesh,
        in_specs=(
            P("batch", "frames", None),
            P("batch", "frames", None),
            P(),
            P(),
            P(None, None, "chan"),
            P("chan", None),
            P("batch"),
            P("batch", None),
        ),
        out_specs=(
            P("batch", "frames", None),
            P("batch", "frames", None),
            P(("batch", "frames"), None, "chan"),
        ),
        check_vma=False,
    )
```

time: 264 us -> 251 us (0.951)
  waiting for transfers between devices: 128 us -> 101 us
  Pallas kernels: 39.7 us -> 59.5 us
  matrix products: 14.2 us -> 0 us
  starting transfers between devices: 40 us -> 47.6 us
    all_gather x1, waiting for transfers between devices: 38.7 us -> 0.02 us  [shards(): full_out = lax.all_gather(out_weight, 'chan', tiled=True)]
    pallas_call x1 -> x4, Pallas kernels: 10.3 us -> 31.6 us  [the longest x1 10.4 us: project(): pl.pallas_call(project_body, grid=(rows // CTX,), in_specs=[pl.BlockSpec(...]
    dot_general x3 -> x0, matrix products: 14.2 us -> none  [the longest x1 9.32 us: dot_tn(): lax.dot_general(a, b, (((0,), (0,)), ((), ())), preferred_element_type=F32)]
    ppermute x14 -> x16, waiting for transfers between devices: 68.3 us -> 82 us  [to_peer(): return lax.ppermute(array, 'chan', pairs)]
    unnamed x17 -> x35, local copies, waits for them, and re-layouts: 1.1 us -> 11.9 us
    ppermute x5 -> x7, starting transfers between devices: 4.03 us -> 12.3 us  [the longest x1 6.33 us: shards(): peer_left = lax.ppermute(peer_after, both, cross(up))]
    ppermute x5 -> x7, waiting for transfers between devices: 3.11 us -> 9.65 us  [the longest x3 9.64 us: pair_sums(): got = lax.ppermute(sent, 'frames', [(i, (i + shift) % 4) for i in range(4)])]
    dynamic_update_slice x8 -> x0, local copies, waits for them, and re-layouts: 6.17 us -> none  [the longest x7 5.4 us: shards(): grad_tokens = lax.dynamic_update_slice_in_dim(grad_tokens, other, place, 0)]
  transfers between devices with their start and end apart: 25 -> 28, of which waited for: 17 -> 11; matrix products, arithmetic and copies ran while one was open for 10% -> 7% of each run, Pallas kernels for 4% -> 24%
where the time goes in v2:
time: 251 us; the launch traced here: 247 us
  waiting for transfers between devices  101 us (40%)
  Pallas kernels  59.5 us (24%)
  starting transfers between devices  47.6 us (19%)
  local copies, waits for them, and re-layouts  19.6 us (8%)
  between operations  14.2 us (6%)
  other arithmetic  5.39 us (2%)
    ppermute x16, waiting for transfers between devices, to_peer(): return lax.ppermute(array, 'chan', pairs)  82 us
    ppermute x16, starting transfers between devices, to_peer(): return lax.ppermute(array, 'chan', pairs)  23.6 us
    pallas_call x1, Pallas kernels, attention(): pl.pallas_call(attention_body, grid=(recs,), in_specs=[by_rec(width, fram...  18.3 us
    unnamed x35, local copies, waits for them, and re-layouts  11.9 us
    pallas_call x1, Pallas kernels, project(): pl.pallas_call(project_body, grid=(rows // CTX,), in_specs=[pl.BlockSpec(...  10.4 us
    pallas_call x1, Pallas kernels, output_rows(): pl.pallas_call(output_body, grid=(rows // CTX,), in_specs=[by_row, by_col...  10 us
    ppermute x3, waiting for transfers between devices, pair_sums(): got = lax.ppermute(sent, 'frames', [(i, (i + shift) % 4) for i in range(4)])  9.64 us
    pallas_call x1, Pallas kernels, weight_grads(): pl.pallas_call(lambda c, *refs: weight_grads_body(*refs), grid_spec=pltpu...  8.89 us
  transfers between devices with their start and end apart: 28, of which 11 were waited for; matrix products, arithmetic and copies ran while one was open for 7% of the time, Pallas kernels for 24%

profile of v2, /device:TPU:18, one launch (start us, length us, event | category | flops | bytes accessed | tf_op | source)
XLA Modules:
  0.0 246.9 jit_solution(7001427714019040861)
XLA Ops:
  11.4 10.4 %project.1 = (bf16[1024,1536]{1,0:T(8,128)(2,1)}, bf16[192,1024]{1,0:T(8,128)(2,1)S(1)}, bf16[384,1024]{1,0:T(8,128)(2,1)S(1)}, bf16[192,1024]{1,0:T(8,128)(2,1)...) custom-call(s32[2]{0:T(128)S(1)} %copy-done.4, ...), custom_call_target="tpu_custom_call" | custom-call | flops 2400000000 | bytes 15000000 | tf_op jit(solution)/shard_map/project/pallas_call | solution.py:77
  24.3 3.4 %collective-permute-start = (bf16[384,512]{1,0:T(8,128)(2,1)S(1)}, bf16[384,512]{1,0:T(8,128)(2,1)S(1)}, u32[]{:S(2)}, u32[]{:S(2)}) collective-permute-start(bf16[384,512]{1,0:T(8,128)(2,1)S(1)} %get-tuple-element.46), channel_id=1, source_target_pairs={{0,8},{8,16},{16,24},{1,9},{9,17},{17,25},{2,10},{10,18},{18,26},{... | collective-permute-start | bytes 1179656 | tf_op jit(solution)/shard_map/ppermute | solution.py:514
  27.7 2.5 collective-permute-start.1
  31.6 5.1 %collective-permute-done.before = bf16[384,512]{1,0:T(8,128)(2,1)S(1)} collective-permute-done((bf16[384,512]{1,0:T(8,128)(2,1)S(1)}, bf16[384,512]{1,0:T(8,128)(2,1)S(1)}, u32[]{:S(2)}, u32[]{:S(2)}) %collective-permute-start) | collective-permute-done | bytes 393248 | tf_op jit(solution)/shard_map/ppermute | solution.py:514
  36.8 3.1 %collective-permute-done.1.after = bf16[384,512]{1,0:T(8,128)(2,1)S(1)} collective-permute-done((bf16[384,512]{1,0:T(8,128)(2,1)S(1)}, bf16[384,512]{1,0:T(8,128)(2,1)S(1)}, u32[]{:S(2)}, u32[]{:S(2)}) %collective-permute-start.1) | collective-permute-done | bytes 393248 | tf_op jit(solution)/shard_map/ppermute | solution.py:515
  41.9 18.3 %attention.1 = (bf16[192,1024]{1,0:T(8,128)(2,1)S(1)}, bf16[192,1024]{1,0:T(8,128)(2,1)S(1)}, f32[384,1024]{1,0:T(8,128)}, bf16[384,512]{1,0:T(8,128)(2,1)S(1)},...) custom-call(bf16[192,1024]{1,0:T(8,128)(2,1)S(1)} %copy-done.9, ...), custom_call_target="tpu_custom_call" | custom-call | flops 2400000000 | bytes 8000000 | tf_op jit(solution)/shard_map/attention/pallas_call | solution.py:186
  60.2 3.1 %collective-permute-start.3 = (bf16[384,512]{1,0:T(8,128)(2,1)S(1)}, bf16[384,512]{1,0:T(8,128)(2,1)S(1)}, u32[]{:S(2)}, u32[]{:S(2)}) collective-permute-start(bf16[384,512]{1,0:T(8,128)(2,1)S(1)} %get-tuple-element.56), channel_id=1, source_target_pairs={{0,8},{8,16},{16,24},{1,9},{9,17},{17,25},{2,10},{10,18},{18,26},{... | collective-permute-start | bytes 1179656 | tf_op jit(solution)/shard_map/ppermute | solution.py:529
  63.3 2.8 %collective-permute-start.4 = (bf16[384,512]{1,0:T(8,128)(2,1)S(1)}, bf16[384,512]{1,0:T(8,128)(2,1)S(1)}, u32[]{:S(2)}, u32[]{:S(2)}) collective-permute-start(bf16[384,512]{1,0:T(8,128)(2,1)S(1)} %get-tuple-element.57), channel_id=1, source_target_pairs={{8,0},{16,8},{24,16},{9,1},{17,9},{25,17},{10,2},{18,10},{26,18},{... | collective-permute-start | bytes 1179656 | tf_op jit(solution)/shard_map/ppermute | solution.py:528
  66.0 3.3 %collective-permute-start.8 = (bf16[576,512]{1,0:T(8,128)(2,1)}, bf16[576,512]{1,0:T(8,128)(2,1)S(1)}, u32[]{:S(2)}, u32[]{:S(2)}) collective-permute-start(bf16[576,512]{1,0:T(8,128)(2,1)} %get-tuple-element.65), channel_id=1, source_target_pairs={{0,1},{1,0},{2,3},{3,2},{4,5},{5,4},{6,7},{7,6},{8,9},{9,8},{10,11... | collective-permute-start | bytes 1769480 | tf_op jit(solution)/shard_map/ppermute | solution.py:458
  69.3 1.9 collective-permute-start.10
  71.2 6.3 %collective-permute-start.9 = (bf16[384,256]{1,0:T(8,128)(2,1)S(1)}, bf16[384,256]{1,0:T(8,128)(2,1)S(1)}, u32[]{:S(2)}, u32[]{:S(2)}) collective-permute-start(bf16[384,256]{1,0:T(8,128)(2,1)S(1)} %get-tuple-element.66), channel_id=1, source_target_pairs={{0,9},{1,8},{2,11},{3,10},{4,13},{5,12},{6,15},{7,14},{8,17},{9,16... | collective-permute-start | bytes 589832 | tf_op jit(solution)/shard_map/ppermute | solution.py:527
  77.6 8.9 %weight_grads.1 = (bf16[2,384,768]{2,1,0:T(8,128)(2,1)}, f32[2,384,768]{2,1,0:T(8,128)}) custom-call(s32[1]{0:T(128)} %bitcast.6.c, bf16[1024,1536]{1,0:T(8,128)(2,1)} %get-tuple-element.59.refs_0_, bf16[1024,1536]{1,0:T(8,128)(2,1)} %bitcast.45, bf16[192,1024]{1,0:T(8,128)(2,1)S(1)} %get-tuple-element.60.refs_2_.dq, ...), custom_call_target="tpu_custom_call" | custom-call | flops 2400000000 | bytes 12000000 | tf_op jit(solution)/shard_map/weight_grads/pallas_call | solution.py:330
  86.5 16.2 %collective-permute-done.8.peer = bf16[576,512]{1,0:T(8,128)(2,1)S(1)} collective-permute-done((bf16[576,512]{1,0:T(8,128)(2,1)}, bf16[576,512]{1,0:T(8,128)(2,1)S(1)}, u32[]{:S(2)}, u32[]{:S(2)}) %collective-permute-start.8) | collective-permute-done | bytes 589856 | tf_op jit(solution)/shard_map/ppermute | solution.py:458
  102.7 1.9 collective-permute-start.5
  104.6 3.6 %collective-permute-start.6 = (bf16[192,1024]{1,0:T(8,128)(2,1)S(1)}, bf16[192,1024]{1,0:T(8,128)(2,1)}, u32[]{:S(2)}, u32[]{:S(2)}) collective-permute-start(bf16[192,1024]{1,0:T(8,128)(2,1)S(1)} %get-tuple-element.58.refs_6_), channel_id=1, source_target_pairs={{0,4},{1,5},{2,6},{3,7},{4,0},{5,1},{6,2},{7,3},{8,12},{9,13},{10,... | collective-permute-start | bytes 1179656 | tf_op jit(solution)/shard_map/ppermute | solution.py:458
  109.2 7.8 %back.1 = (f32[128,1536]{1,0:T(8,128)}, bf16[128,1536]{1,0:T(8,128)(2,1)}, bf16[128,1536]{1,0:T(8,128)(2,1)S(1)}, bf16[128,1536]{1,0:T(8,128)(2,1)S(1)}) custom-call(s32[1]{0:T(128)} %bitcast.7.here, bf16[192,1024]{1,0:T(8,128)(2,1)S(1)} %get-tuple-element.60.refs_2_.dq, f32[384,1024]{1,0:T(8,128)} %get-tuple-element.61.refs_3_.own, ...), custom_call_target="tpu_custom_call" | custom-call | flops 1800000000 | bytes 8000000 | tf_op jit(solution)/shard_map/back/pallas_call | solution.py:260
  118.9 11.8 %collective-permute-done.5 = bf16[192,1024]{1,0:T(8,128)(2,1)} collective-permute-done((bf16[192,1024]{1,0:T(8,128)(2,1)S(1)}, bf16[192,1024]{1,0:T(8,128)(2,1)}, u32[]{:S(2)}, u32[]{:S(2)}) %collective-permute-start.5) | collective-permute-done | bytes 393248 | tf_op jit(solution)/shard_map/ppermute | solution.py:458
  130.8 16.6 %collective-permute-done.12.rest_0_ = bf16[128,1536]{1,0:T(8,128)(2,1)S(1)} collective-permute-done((bf16[128,1536]{1,0:T(8,128)(2,1)}, bf16[128,1536]{1,0:T(8,128)(2,1)S(1)}, u32[]{:S(2)}, u32[]{:S(2)}) %collective-permute-start.12) | collective-permute-done | bytes 393248 | tf_op jit(solution)/shard_map/ppermute | solution.py:458
  152.8 3.0 %convert_add_fusion = f32[2,384,768]{2,1,0:T(8,128)} fusion(f32[2,384,768]{2,1,0:T(8,128)S(1)} %copy-done.12, bf16[2,384,768]{2,1,0:T(8,128)(2,1)} %collective-permute-done.11), kind=kLoop, calls=%fused_computation | loop fusion | flops 1179648 | bytes 5898240 | tf_op jit(solution)/shard_map/add | solution.py:472
  155.8 2.4 fusion.3
  162.2 3.2 %collective-permute-start.20 = (bf16[128,1536]{1,0:T(8,128)(2,1)S(1)}, bf16[128,1536]{1,0:T(8,128)(2,1)S(1)}, u32[]{:S(2)}, u32[]{:S(2)}) collective-permute-start(bf16[128,1536]{1,0:T(8,128)(2,1)S(1)} %finish.1.refs_0_), channel_id=1, source_target_pairs={{0,6},{1,7},{2,0},{3,1},{4,2},{5,3},{6,4},{7,5},{8,14},{9,15},{10,... | collective-permute-start | bytes 1179656 | tf_op jit(solution)/shard_map/ppermute | solution.py:458
  165.4 1.9 collective-permute-done.14
  167.3 3.2 %collective-permute-start.21 = (bf16[128,1536]{1,0:T(8,128)(2,1)S(1)}, bf16[128,1536]{1,0:T(8,128)(2,1)S(1)}, u32[]{:S(2)}, u32[]{:S(2)}) collective-permute-start(bf16[128,1536]{1,0:T(8,128)(2,1)S(1)} %finish.1.refs_0_), channel_id=1, source_target_pairs={{0,1},{1,0},{2,3},{3,2},{4,5},{5,4},{6,7},{7,6},{8,9},{9,8},{10,11... | collective-permute-start | bytes 1179656 | tf_op jit(solution)/shard_map/ppermute | solution.py:458
  171.9 7.7 %collective-permute-done.16 = bf16[2,96,768]{2,1,0:T(8,128)(2,1)S(1)} collective-permute-done((bf16[2,96,768]{2,1,0:T(8,128)(2,1)S(1)}, bf16[2,96,768]{2,1,0:T(8,128)(2,1)S(1)}, u32[]{:S(2)}, u32[]{:S(2)}) %collective-permute-start.16) | collective-permute-done | bytes 294944 | tf_op jit(solution)/shard_map/ppermute | solution.py:476
  179.7 5.6 %collective-permute-start.23 = (bf16[128,1536]{1,0:T(8,128)(2,1)S(1)}, bf16[128,1536]{1,0:T(8,128)(2,1)S(1)}, u32[]{:S(2)}, u32[]{:S(2)}) collective-permute-start(bf16[128,1536]{1,0:T(8,128)(2,1)S(1)} %finish.1.refs_0_), channel_id=1, source_target_pairs={{0,7},{1,6},{2,1},{3,0},{4,3},{5,2},{6,5},{7,4},{8,15},{9,14},{10,... | collective-permute-start | bytes 1179656 | tf_op jit(solution)/shard_map/ppermute | solution.py:458
  185.3 14.8 %collective-permute-done.21.refs_3_ = bf16[128,1536]{1,0:T(8,128)(2,1)S(1)} collective-permute-done((bf16[128,1536]{1,0:T(8,128)(2,1)S(1)}, bf16[128,1536]{1,0:T(8,128)(2,1)S(1)}, u32[]{:S(2)}, u32[]{:S(2)}) %collective-permute-start.21) | collective-permute-done | bytes 393248 | tf_op jit(solution)/shard_map/ppermute | solution.py:458
  200.3 2.3 fusion.1
  202.5 2.1 collective-permute-done.22.refs_4_
  204.6 10.4 %collective-permute-done.23.refs_5_ = bf16[128,1536]{1,0:T(8,128)(2,1)S(1)} collective-permute-done((bf16[128,1536]{1,0:T(8,128)(2,1)S(1)}, bf16[128,1536]{1,0:T(8,128)(2,1)S(1)}, u32[]{:S(2)}, u32[]{:S(2)}) %collective-permute-start.23) | collective-permute-done | bytes 393248 | tf_op jit(solution)/shard_map/ppermute | solution.py:458
  215.1 9.9 %collective-permute-done.25.refs_7_ = bf16[128,1536]{1,0:T(8,128)(2,1)S(1)} collective-permute-done((bf16[128,1536]{1,0:T(8,128)(2,1)S(1)}, bf16[128,1536]{1,0:T(8,128)(2,1)S(1)}, u32[]{:S(2)}, u32[]{:S(2)}) %collective-permute-start.25) | collective-permute-done | bytes 393248 | tf_op jit(solution)/shard_map/ppermute | solution.py:458
  225.0 2.3 assemble.1
  229.0 10.0 %output.1 = bf16[1024,1536]{1,0:T(8,128)(2,1)} custom-call(bf16[1024,1536]{1,0:T(8,128)(2,1)} %bitcast.49, bf16[768,1024]{1,0:T(8,128)(2,1)} %constant_dynamic-update-slice_fusion.near, bf16[768,1024]{1,0:T(8,128)(2,1)} %collective-permute-done.13.far, bf16[1536,1536]{1,0:T(8,128)(2,1)} %all-gather.2.cloned.1.call-done.weight), custom_call_target="tpu_custom_call" | custom-call | flops 4800000000 | bytes 14000000 | tf_op jit(solution)/shard_map/output/pallas_call | solution.py:378
  (80 shorter events, 26.7 us)
Async XLA Ops:
  7.2 220.1 %all-gather.2.cloned.1.call-start = ((), (), s32[]{:S(2)}) async-start(), calls=%async_computation | async-start | bytes 5308416 | tf_op jit(solution)/shard_map/all_gather | solution.py:498
  7.9 52.3 %collective-permute-start.2 = (bf16[576,1536]{1,0:T(8,128)(2,1)}, bf16[576,1536]{1,0:T(8,128)(2,1)}, u32[]{:S(2)}, u32[]{:S(2)}) collective-permute-start(bf16[576,1536]{1,0:T(8,128)(2,1)} %bitcast.51), channel_id=1, source_target_pairs={{0,1},{1,0},{2,3},{3,2},{4,5},{5,4},{6,7},{7,6},{8,9},{9,8},{10,11... | collective-permute-start | bytes 5308424 | tf_op jit(solution)/shard_map/ppermute | solution.py:458
  11.4 18.8 %copy-start.5 = (s32[2]{0:T(128)S(1)}, s32[2]{0:T(128)}, u32[]{:S(2)}) copy-start(s32[2]{0:T(128)} %lengths.1) | copy-start | bytes 28
  11.4 18.8 %copy-start.15 = (s32[2,2048]{1,0:T(2,128)S(1)}, s32[2,2048]{1,0:T(2,128)}, u32[]{:S(2)}) copy-start(s32[2,2048]{1,0:T(2,128)} %param.15) | copy-start | bytes 49156
  24.3 12.5 %collective-permute-start = (bf16[384,512]{1,0:T(8,128)(2,1)S(1)}, bf16[384,512]{1,0:T(8,128)(2,1)S(1)}, u32[]{:S(2)}, u32[]{:S(2)}) collective-permute-start(bf16[384,512]{1,0:T(8,128)(2,1)S(1)} %get-tuple-element.46), channel_id=1, source_target_pairs={{0,8},{8,16},{16,24},{1,9},{9,17},{17,25},{2,10},{10,18},{18,26},{... | collective-permute-start | bytes 1179656 | tf_op jit(solution)/shard_map/ppermute | solution.py:514
  27.7 12.2 %collective-permute-start.1 = (bf16[384,512]{1,0:T(8,128)(2,1)S(1)}, bf16[384,512]{1,0:T(8,128)(2,1)S(1)}, u32[]{:S(2)}, u32[]{:S(2)}) collective-permute-start(bf16[384,512]{1,0:T(8,128)(2,1)S(1)} %get-tuple-element.47), channel_id=1, source_target_pairs={{8,0},{16,8},{24,16},{9,1},{17,9},{25,17},{10,2},{18,10},{26,18},{... | collective-permute-start | bytes 1179656 | tf_op jit(solution)/shard_map/ppermute | solution.py:515
  60.2 17.4 %collective-permute-start.3 = (bf16[384,512]{1,0:T(8,128)(2,1)S(1)}, bf16[384,512]{1,0:T(8,128)(2,1)S(1)}, u32[]{:S(2)}, u32[]{:S(2)}) collective-permute-start(bf16[384,512]{1,0:T(8,128)(2,1)S(1)} %get-tuple-element.56), channel_id=1, source_target_pairs={{0,8},{8,16},{16,24},{1,9},{9,17},{17,25},{2,10},{10,18},{18,26},{... | collective-permute-start | bytes 1179656 | tf_op jit(solution)/shard_map/ppermute | solution.py:529
  63.3 14.3 %collective-permute-start.4 = (bf16[384,512]{1,0:T(8,128)(2,1)S(1)}, bf16[384,512]{1,0:T(8,128)(2,1)S(1)}, u32[]{:S(2)}, u32[]{:S(2)}) collective-permute-start(bf16[384,512]{1,0:T(8,128)(2,1)S(1)} %get-tuple-element.57), channel_id=1, source_target_pairs={{8,0},{16,8},{24,16},{9,1},{17,9},{25,17},{10,2},{18,10},{26,18},{... | collective-permute-start | bytes 1179656 | tf_op jit(solution)/shard_map/ppermute | solution.py:528
  66.0 36.7 %collective-permute-start.8 = (bf16[576,512]{1,0:T(8,128)(2,1)}, bf16[576,512]{1,0:T(8,128)(2,1)S(1)}, u32[]{:S(2)}, u32[]{:S(2)}) collective-permute-start(bf16[576,512]{1,0:T(8,128)(2,1)} %get-tuple-element.65), channel_id=1, source_target_pairs={{0,1},{1,0},{2,3},{3,2},{4,5},{5,4},{6,7},{7,6},{8,9},{9,8},{10,11... | collective-permute-start | bytes 1769480 | tf_op jit(solution)/shard_map/ppermute | solution.py:458
  69.3 17.2 %collective-permute-start.10 = (bf16[384,256]{1,0:T(8,128)(2,1)}, bf16[384,256]{1,0:T(8,128)(2,1)S(1)}, u32[]{:S(2)}, u32[]{:S(2)}) collective-permute-start(bf16[384,256]{1,0:T(8,128)(2,1)} %get-tuple-element.67), channel_id=1, source_target_pairs={{8,1},{9,0},{10,3},{11,2},{12,5},{13,4},{14,7},{15,6},{16,9},{17,8... | collective-permute-start | bytes 589832 | tf_op jit(solution)/shard_map/ppermute | solution.py:526
  71.2 15.3 %collective-permute-start.9 = (bf16[384,256]{1,0:T(8,128)(2,1)S(1)}, bf16[384,256]{1,0:T(8,128)(2,1)S(1)}, u32[]{:S(2)}, u32[]{:S(2)}) collective-permute-start(bf16[384,256]{1,0:T(8,128)(2,1)S(1)} %get-tuple-element.66), channel_id=1, source_target_pairs={{0,9},{1,8},{2,11},{3,10},{4,13},{5,12},{6,15},{7,14},{8,17},{9,16... | collective-permute-start | bytes 589832 | tf_op jit(solution)/shard_map/ppermute | solution.py:527
  102.7 44.8 %collective-permute-start.11 = (bf16[2,384,768]{2,1,0:T(8,128)(2,1)}, bf16[2,384,768]{2,1,0:T(8,128)(2,1)}, u32[]{:S(2)}, u32[]{:S(2)}) collective-permute-start(bf16[2,384,768]{2,1,0:T(8,128)(2,1)} %get-tuple-element.68), channel_id=1, source_target_pairs={{0,32},{32,0},{64,96},{96,64},{1,33},{33,1},{65,97},{97,65},{2,34}... | collective-permute-start | bytes 3538952 | tf_op jit(solution)/shard_map/ppermute | solution.py:550
  102.7 27.9 %collective-permute-start.5 = (bf16[192,1024]{1,0:T(8,128)(2,1)S(1)}, bf16[192,1024]{1,0:T(8,128)(2,1)}, u32[]{:S(2)}, u32[]{:S(2)}) collective-permute-start(bf16[192,1024]{1,0:T(8,128)(2,1)S(1)} %get-tuple-element.58.refs_6_), channel_id=1, source_target_pairs={{0,2},{1,3},{2,4},{3,5},{4,6},{5,7},{6,0},{7,1},{8,10},{9,11},{10,... | collective-permute-start | bytes 1179656 | tf_op jit(solution)/shard_map/ppermute | solution.py:458
  104.6 26.2 %collective-permute-start.6 = (bf16[192,1024]{1,0:T(8,128)(2,1)S(1)}, bf16[192,1024]{1,0:T(8,128)(2,1)}, u32[]{:S(2)}, u32[]{:S(2)}) collective-permute-start(bf16[192,1024]{1,0:T(8,128)(2,1)S(1)} %get-tuple-element.58.refs_6_), channel_id=1, source_target_pairs={{0,4},{1,5},{2,6},{3,7},{4,0},{5,1},{6,2},{7,3},{8,12},{9,13},{10,... | collective-permute-start | bytes 1179656 | tf_op jit(solution)/shard_map/ppermute | solution.py:458
  108.2 22.6 %collective-permute-start.7 = (bf16[192,1024]{1,0:T(8,128)(2,1)S(1)}, bf16[192,1024]{1,0:T(8,128)(2,1)}, u32[]{:S(2)}, u32[]{:S(2)}) collective-permute-start(bf16[192,1024]{1,0:T(8,128)(2,1)S(1)} %get-tuple-element.58.refs_6_), channel_id=1, source_target_pairs={{0,6},{1,7},{2,0},{3,1},{4,2},{5,3},{6,4},{7,5},{8,14},{9,15},{10,... | collective-permute-start | bytes 1179656 | tf_op jit(solution)/shard_map/ppermute | solution.py:458
  117.1 30.4 %collective-permute-start.12 = (bf16[128,1536]{1,0:T(8,128)(2,1)}, bf16[128,1536]{1,0:T(8,128)(2,1)S(1)}, u32[]{:S(2)}, u32[]{:S(2)}) collective-permute-start(bf16[128,1536]{1,0:T(8,128)(2,1)} %get-tuple-element.73), channel_id=1, source_target_pairs={{0,2},{1,3},{2,4},{3,5},{4,6},{5,7},{6,0},{7,1},{8,10},{9,11},{10,... | collective-permute-start | bytes 1179656 | tf_op jit(solution)/shard_map/ppermute | solution.py:458
  118.1 34.7 %copy-start.12 = (f32[2,384,768]{2,1,0:T(8,128)S(1)}, f32[2,384,768]{2,1,0:T(8,128)}, u32[]{:S(2)}) copy-start(f32[2,384,768]{2,1,0:T(8,128)} %get-tuple-element.77) | copy-start | bytes 7077892
  130.7 29.6 %collective-permute-start.17 = (bf16[128,1536]{1,0:T(8,128)(2,1)S(1)}, bf16[128,1536]{1,0:T(8,128)(2,1)S(1)}, u32[]{:S(2)}, u32[]{:S(2)}) collective-permute-start(bf16[128,1536]{1,0:T(8,128)(2,1)S(1)} %get-tuple-element.82), channel_id=1, source_target_pairs={{0,4},{1,5},{2,6},{3,7},{4,0},{5,1},{6,2},{7,3},{8,12},{9,13},{10,... | collective-permute-start | bytes 1179656 | tf_op jit(solution)/shard_map/ppermute | solution.py:458
  130.8 29.4 %collective-permute-start.18 = (bf16[128,1536]{1,0:T(8,128)(2,1)S(1)}, bf16[128,1536]{1,0:T(8,128)(2,1)S(1)}, u32[]{:S(2)}, u32[]{:S(2)}) collective-permute-start(bf16[128,1536]{1,0:T(8,128)(2,1)S(1)} %get-tuple-element.83), channel_id=1, source_target_pairs={{0,6},{1,7},{2,0},{3,1},{4,2},{5,3},{6,4},{7,5},{8,14},{9,15},{10,... | collective-permute-start | bytes 1179656 | tf_op jit(solution)/shard_map/ppermute | solution.py:458
  152.8 76.2 %collective-permute-start.13 = (bf16[768,1024]{1,0:T(8,128)(2,1)}, bf16[768,1024]{1,0:T(8,128)(2,1)}, u32[]{:S(2)}, u32[]{:S(2)}) collective-permute-start(bf16[768,1024]{1,0:T(8,128)(2,1)} %constant_dynamic-update-slice_fusion.near), channel_id=1, source_target_pairs={{0,1},{1,0},{2,3},{3,2},{4,5},{5,4},{6,7},{7,6},{8,9},{9,8},{10,11... | collective-permute-start | bytes 4718600 | tf_op jit(solution)/shard_map/ppermute | solution.py:458
  158.2 9.1 %collective-permute-start.14 = (bf16[2,96,768]{2,1,0:T(8,128)(2,1)S(1)}, bf16[2,96,768]{2,1,0:T(8,128)(2,1)}, u32[]{:S(2)}, u32[]{:S(2)}) collective-permute-start(bf16[2,96,768]{2,1,0:T(8,128)(2,1)S(1)} %get-tuple-element.85), channel_id=1, source_target_pairs={{0,8},{8,16},{16,24},{24,0},{1,9},{9,17},{17,25},{25,1},{2,10},{10... | collective-permute-start | bytes 884744 | tf_op jit(solution)/shard_map/ppermute | solution.py:476
  159.8 10.7 %collective-permute-start.15 = (bf16[2,96,768]{2,1,0:T(8,128)(2,1)}, bf16[2,96,768]{2,1,0:T(8,128)(2,1)}, u32[]{:S(2)}, u32[]{:S(2)}) collective-permute-start(bf16[2,96,768]{2,1,0:T(8,128)(2,1)} %get-tuple-element.87), channel_id=1, source_target_pairs={{0,24},{8,0},{16,8},{24,16},{1,25},{9,1},{17,9},{25,17},{2,26},{10... | collective-permute-start | bytes 884744 | tf_op jit(solution)/shard_map/ppermute | solution.py:476
  162.1 17.6 %collective-permute-start.19 = (bf16[128,1536]{1,0:T(8,128)(2,1)S(1)}, bf16[128,1536]{1,0:T(8,128)(2,1)S(1)}, u32[]{:S(2)}, u32[]{:S(2)}) collective-permute-start(bf16[128,1536]{1,0:T(8,128)(2,1)S(1)} %finish.1.refs_0_), channel_id=1, source_target_pairs={{0,2},{1,3},{2,4},{3,5},{4,6},{5,7},{6,0},{7,1},{8,10},{9,11},{10,... | collective-permute-start | bytes 1179656 | tf_op jit(solution)/shard_map/ppermute | solution.py:458
  162.2 23.1 %collective-permute-start.20 = (bf16[128,1536]{1,0:T(8,128)(2,1)S(1)}, bf16[128,1536]{1,0:T(8,128)(2,1)S(1)}, u32[]{:S(2)}, u32[]{:S(2)}) collective-permute-start(bf16[128,1536]{1,0:T(8,128)(2,1)S(1)} %finish.1.refs_0_), channel_id=1, source_target_pairs={{0,6},{1,7},{2,0},{3,1},{4,2},{5,3},{6,4},{7,5},{8,14},{9,15},{10,... | collective-permute-start | bytes 1179656 | tf_op jit(solution)/shard_map/ppermute | solution.py:458
  167.3 32.8 %collective-permute-start.21 = (bf16[128,1536]{1,0:T(8,128)(2,1)S(1)}, bf16[128,1536]{1,0:T(8,128)(2,1)S(1)}, u32[]{:S(2)}, u32[]{:S(2)}) collective-permute-start(bf16[128,1536]{1,0:T(8,128)(2,1)S(1)} %finish.1.refs_0_), channel_id=1, source_target_pairs={{0,1},{1,0},{2,3},{3,2},{4,5},{5,4},{6,7},{7,6},{8,9},{9,8},{10,11... | collective-permute-start | bytes 1179656 | tf_op jit(solution)/shard_map/ppermute | solution.py:458
  170.6 9.1 %collective-permute-start.16 = (bf16[2,96,768]{2,1,0:T(8,128)(2,1)S(1)}, bf16[2,96,768]{2,1,0:T(8,128)(2,1)S(1)}, u32[]{:S(2)}, u32[]{:S(2)}) collective-permute-start(bf16[2,96,768]{2,1,0:T(8,128)(2,1)S(1)} %copy-done.14), channel_id=1, source_target_pairs={{0,16},{8,24},{16,0},{24,8},{1,17},{9,25},{17,1},{25,9},{2,18},{10... | collective-permute-start | bytes 884744 | tf_op jit(solution)/shard_map/ppermute | solution.py:476
  179.7 24.9 %collective-permute-start.22 = (bf16[128,1536]{1,0:T(8,128)(2,1)S(1)}, bf16[128,1536]{1,0:T(8,128)(2,1)S(1)}, u32[]{:S(2)}, u32[]{:S(2)}) collective-permute-start(bf16[128,1536]{1,0:T(8,128)(2,1)S(1)} %finish.1.refs_0_), channel_id=1, source_target_pairs={{0,3},{1,2},{2,5},{3,4},{4,7},{5,6},{6,1},{7,0},{8,11},{9,10},{10,... | collective-permute-start | bytes 1179656 | tf_op jit(solution)/shard_map/ppermute | solution.py:458
  179.7 35.4 %collective-permute-start.23 = (bf16[128,1536]{1,0:T(8,128)(2,1)S(1)}, bf16[128,1536]{1,0:T(8,128)(2,1)S(1)}, u32[]{:S(2)}, u32[]{:S(2)}) collective-permute-start(bf16[128,1536]{1,0:T(8,128)(2,1)S(1)} %finish.1.refs_0_), channel_id=1, source_target_pairs={{0,7},{1,6},{2,1},{3,0},{4,3},{5,2},{6,5},{7,4},{8,15},{9,14},{10,... | collective-permute-start | bytes 1179656 | tf_op jit(solution)/shard_map/ppermute | solution.py:458
  185.3 29.7 %collective-permute-start.24 = (bf16[128,1536]{1,0:T(8,128)(2,1)S(1)}, bf16[128,1536]{1,0:T(8,128)(2,1)S(1)}, u32[]{:S(2)}, u32[]{:S(2)}) collective-permute-start(bf16[128,1536]{1,0:T(8,128)(2,1)S(1)} %finish.1.refs_0_), channel_id=1, source_target_pairs={{0,4},{1,5},{2,6},{3,7},{4,0},{5,1},{6,2},{7,3},{8,12},{9,13},{10,... | collective-permute-start | bytes 1179656 | tf_op jit(solution)/shard_map/ppermute | solution.py:458
  200.2 24.8 %collective-permute-start.25 = (bf16[128,1536]{1,0:T(8,128)(2,1)S(1)}, bf16[128,1536]{1,0:T(8,128)(2,1)S(1)}, u32[]{:S(2)}, u32[]{:S(2)}) collective-permute-start(bf16[128,1536]{1,0:T(8,128)(2,1)S(1)} %finish.1.refs_0_), channel_id=1, source_target_pairs={{0,5},{1,4},{2,7},{3,6},{4,1},{5,0},{6,3},{7,2},{8,13},{9,12},{10,... | collective-permute-start | bytes 1179656 | tf_op jit(solution)/shard_map/ppermute | solution.py:458
  228.3 10.7 %copy-start.13 = (f32[2,96,768]{2,1,0:T(8,128)S(1)}, f32[2,96,768]{2,1,0:T(8,128)}, u32[]{:S(2)}) copy-start(f32[2,96,768]{2,1,0:T(8,128)} %fusion.1) | copy-start | bytes 1769476
  228.3 10.7 %collective-permute-start.26 = (bf16[96,768]{1,0:T(8,128)(2,1)S(1)}, bf16[96,768]{1,0:T(8,128)(2,1)S(1)}, u32[]{:S(2)}, u32[]{:S(2)}) collective-permute-start(bf16[96,768]{1,0:T(8,128)(2,1)S(1)} %fusion.5), channel_id=1, source_target_pairs={{0,64},{32,96},{64,0},{96,32},{1,65},{33,97},{65,1},{97,33},{2,66}... | collective-permute-start | bytes 442376 | tf_op jit(solution)/shard_map/ppermute | solution.py:484
  (12 other events, 26.8 us)
Sparse Core Ops, SparseCore 0:
  10.3 110.2 all-gather.1

commit v3 on v2

--- a/solution.py
+++ b/solution.py
@@ -9,7 +9,7 @@
 CTX = 256
 EPS = 1e-05
 NEG = -1e30
-VMEM_LIMIT = 50 * 1024 * 1024
+VMEM_LIMIT = 60 * 1024 * 1024
 SHIFTS = ((1, 0), (3, 0), (0, 1), (1, 1), (3, 1), (2, 0), (2, 1))
 SPREAD = (0, 1, 2, 3)
 
@@ -309,12 +309,14 @@
     @pl.when(pl.program_id(0) < 2)
     def _():
         for part, offset in zip(sums, offsets):
-            sent[0, :, offset : offset + part.shape[1]] = part.astype(BF16)
+            shape = (sent.shape[0], sent.shape[2], part.shape[1])
+            sent[:, 0, :, offset : offset + part.shape[1]] = part.astype(BF16).reshape(shape)
 
     @pl.when(pl.program_id(0) >= 2)
     def _():
         for part, offset in zip(sums, offsets):
-            kept[0, :, offset : offset + part.shape[1]] = part
+            shape = (kept.shape[0], kept.shape[2], part.shape[1])
+            kept[:, 0, :, offset : offset + part.shape[1]] = part.reshape(shape)
 
 
 def weight_grads(core, normed, cotangent, dq, own, left, right, mixed):
@@ -327,6 +329,7 @@
 
     full = lambda n: pl.BlockSpec((n, rows), lambda i, c: (0, 0))
     half = pl.BlockSpec((2 * width, rows // 2), lambda i, c: (0, 0))
+    part = (4, 1, block // 4, 4 * width)
     return pl.pallas_call(
         lambda c, *refs: weight_grads_body(*refs),
         grid_spec=pltpu.PrefetchScalarGridSpec(
@@ -342,14 +345,14 @@
                 full(width),
             ],
             out_specs=[
-                pl.BlockSpec((1, block, 4 * width), lambda i, c: (jnp.minimum(i, 1), 0, 0)),
-                pl.BlockSpec((1, block, 4 * width), lambda i, c: (jnp.maximum(i, 2) - 2, 0, 0)),
+                pl.BlockSpec(part, lambda i, c: (0, jnp.minimum(i, 1), 0, 0)),
+                pl.BlockSpec(part, lambda i, c: (0, jnp.maximum(i, 2) - 2, 0, 0)),
             ],
             scratch_shapes=[pltpu.VMEM((2 * width, rows), BF16)],
         ),
         out_shape=[
-            jax.ShapeDtypeStruct((2, block, 4 * width), BF16),
-            jax.ShapeDtypeStruct((2, block, 4 * width), F32),
+            jax.ShapeDtypeStruct((4, 2, block // 4, 4 * width), BF16),
+            jax.ShapeDtypeStruct((4, 2, block // 4, 4 * width), F32),
         ],
         compiler_params=params(),
         cost_estimate=pl.CostEstimate(flops=2400000000, bytes_accessed=12000000, transcendentals=0),
@@ -357,35 +360,36 @@
     )(core, normed, cotangent, dq, own, left, right, mixed)
 
 
-def output_body(tok, near, far, weight, out, stacked):
-    me = lax.axis_index("chan")
-    depth = weight.shape[0]
-    width = depth // (2 * len(SPREAD))
+def output_body(tok, near, far, near_weight, far_weight, out, near_stack, far_stack):
+    z = lax.axis_index("chan") >> 1
+    width = near.shape[0] // len(SPREAD)
     for index, dz in enumerate(SPREAD):
         rows = slice(index * width, (index + 1) * width)
-        for side, source in ((0, near), (1, far)):
-            chan = (((me >> 1) - dz) & 3) * 2 + ((me & 1) ^ side)
-            place = pl.ds(pl.multiple_of(chan * width, width), width)
-            stacked[place, :] = source[rows, :]
-    total = tok[...].astype(F32) + dot_nn(stacked[...].T, weight[...])
-    out[...] = total.astype(BF16)
-
-
-def output_rows(tokens, near, far, weight):
+        place = pl.ds(pl.multiple_of(((z - dz) & 3) * width, width), width)
+        near_stack[place, :] = near[rows, :]
+        far_stack[place, :] = far[rows, :]
+    total = dot_nn(near_stack[...].T, near_weight[...])
+    total = total + dot_nn(far_stack[...].T, far_weight[...])
+    out[...] = (tok[...].astype(F32) + total).astype(BF16)
+
+
+def output_rows(tokens, near, far, near_weight, far_weight):
     rows, model = tokens.shape
+    depth = near.shape[0]
     by_row = pl.BlockSpec((CTX, model), lambda i: (i, 0))
-    by_col = pl.BlockSpec((near.shape[0], CTX), lambda i: (0, i))
+    by_col = pl.BlockSpec((depth, CTX), lambda i: (0, i))
+    full = pl.BlockSpec((depth, model), lambda i: (0, 0))
     return pl.pallas_call(
         output_body,
         grid=(rows // CTX,),
-        in_specs=[by_row, by_col, by_col, pl.BlockSpec(weight.shape, lambda i: (0, 0))],
+        in_specs=[by_row, by_col, by_col, full, full],
         out_specs=by_row,
         out_shape=jax.ShapeDtypeStruct((rows, model), BF16),
-        scratch_shapes=[pltpu.VMEM((weight.shape[0], CTX), BF16)],
+        scratch_shapes=[pltpu.VMEM((depth, CTX), BF16)] * 2,
         compiler_params=params(),
         cost_estimate=pl.CostEstimate(flops=4800000000, bytes_accessed=14000000, transcendentals=0),
         name="output",
-    )(tokens, near, far, weight)
+    )(tokens, near, far, near_weight, far_weight)
 
 
 def finish_body(place, tok, cot, gain, mine, *rest):
@@ -421,12 +425,11 @@
     )(place, tokens, cotangent, gain, mine, *parts)
 
 
-def assemble_body(places, *refs):
-    pieces, out, sems = refs[:-2], refs[-2], refs[-1]
+def copy_all(pieces, out, sems, places):
     chunk = pieces[0].shape[0]
     copies = []
-    for index, piece in enumerate(pieces):
-        rows = pl.ds(pl.multiple_of(places[index] * chunk, chunk), chunk)
+    for index, (piece, place) in enumerate(zip(pieces, places)):
+        rows = pl.ds(pl.multiple_of(place * chunk, chunk), chunk)
         copies.append(pltpu.make_async_copy(piece, out.at[rows, :], sems.at[index]))
     for copy in copies:
         copy.start()
@@ -434,20 +437,29 @@
         copy.wait()
 
 
-def assemble(places, pieces):
+def assemble_body(places, *refs):
+    copy_all(refs[:-2], refs[-2], refs[-1], [places[i] for i in range(len(refs) - 2)])
+
+
+def stack_body(*refs):
+    copy_all(refs[:-2], refs[-2], refs[-1], range(len(refs) - 2))
+
+
+def stack(pieces, places=None):
     chunk, model = pieces[0].shape
     count = len(pieces)
     anywhere = pl.BlockSpec(memory_space=pl.ANY)
+    ordered = places is not None
     return pl.pallas_call(
-        assemble_body,
-        in_specs=[pl.BlockSpec(memory_space=pltpu.SMEM)] + [anywhere] * count,
+        assemble_body if ordered else stack_body,
+        in_specs=[pl.BlockSpec(memory_space=pltpu.SMEM)] * ordered + [anywhere] * count,
         out_specs=anywhere,
         out_shape=jax.ShapeDtypeStruct((count * chunk, model), BF16),
         scratch_shapes=[pltpu.SemaphoreType.DMA((count,))],
         compiler_params=params(),
         cost_estimate=pl.CostEstimate(flops=0, bytes_accessed=6000000, transcendentals=0),
-        name="assemble",
-    )(places, *pieces)
+        name="assemble" if ordered else "stack",
+    )(*([places] if ordered else []), *pieces)
 
 
 def to_peer(array, shift):
@@ -468,21 +480,14 @@
 
 
 def pair_sums(got, kept):
-    frame = lax.axis_index("frames")
-    pair = (kept + got.astype(F32)).reshape(2, 4, -1, kept.shape[-1])
-    sums = pick(pair, frame, 1)
-    for shift in (1, 3, 2):
-        sent = pick(pair, (frame + shift) & 3, 1).astype(BF16)
-        got = lax.ppermute(sent, "frames", [(i, (i + shift) % 4) for i in range(4)])
-        sums = sums + got.astype(F32)
-    return sums
+    pair = (kept + got.astype(F32)).astype(BF16)
+    return lax.psum_scatter(pair, "frames", scatter_dimension=0)
 
 
 def row_sums(sums):
     row = lax.axis_index("batch") >> 1
-    sent = pick(sums, 1 - row, 0).astype(BF16)
-    got = lax.ppermute(sent, "batch", [(0, 2), (1, 3), (2, 0), (3, 1)])
-    return pick(sums, row, 0) + got.astype(F32)
+    got = lax.ppermute(pick(sums, 1 - row, 0), "batch", [(0, 2), (1, 3), (2, 0), (3, 1)])
+    return pick(sums, row, 0).astype(F32) + got.astype(F32)
 
 
 def shards(tokens, cotangent, norm_gain, norm_bias, qkv_weight, out_weight, lengths, segments):
@@ -494,8 +499,12 @@
     scalar = lambda value: value.reshape(1).astype(jnp.int32)
 
     weight = qkv_weight.transpose(1, 2, 0).reshape(3 * width, model)
+    over_z = lambda array: lax.all_gather(
+        array, "chan", axis_index_groups=[[0, 2, 4, 6], [1, 3, 5, 7]], tiled=True
+    )
+    near_out = over_z(out_weight)
+    peer_out = to_peer(out_weight, (0, 1))
     peer_weight = to_peer(weight, (0, 1))
-    full_out = lax.all_gather(out_weight, "chan", tiled=True)
 
     flat_tokens = tokens.reshape(rows, model)
     flat_cot = cotangent.reshape(rows, model)
@@ -511,12 +520,14 @@
     size = lax.axis_size("frames")
     up = [(i, i + 1) for i in range(size - 1)]
     down = [(i + 1, i) for i in range(size - 1)]
+    tie = lax.optimization_barrier
+    kv_first, kv_last, peer_out = tie((kv_first, kv_last, peer_out))
+    far_out = over_z(peer_out)
     before = lax.ppermute(kv_last, "frames", up)
     after = lax.ppermute(kv_first, "frames", down)
     mixed, dq, dkv, dbefore, dafter, peer_grads, peer_before, peer_after = attention(
         q, kv, before, after, g, seg_keys, seg_rows, live
     )
-    tie = lax.optimization_barrier
     dbefore, dafter, peer_grads, peer_before, peer_after, peer_weight = tie(
         (dbefore, dafter, peer_grads, peer_before, peer_after, peer_weight)
     )
@@ -528,10 +539,16 @@
     from_right = lax.ppermute(dbefore, "frames", down)
     from_left = lax.ppermute(dafter, "frames", up)
 
-    late_mixed, from_left, from_right = tie((mixed, from_left, from_right))
+    late_mixed, from_left, from_right, peer_left, peer_right = tie(
+        (mixed, from_left, from_right, peer_left, peer_right)
+    )
+    near = [to_peer(late_mixed, (dz, 0)) for dz in SPREAD[1:]]
     core = scalar(lax.axis_index("batch") & 1)
     sent, kept = weight_grads(core, normed, flat_cot, dq, dkv, from_left, from_right, mixed)
-    sent, peer_grads, peer_left, peer_right = tie((sent, peer_grads, peer_left, peer_right))
+    near_mixed = stack([mixed] + near)
+    sent, near_mixed, peer_grads, near_out, far_out = tie(
+        (sent, near_mixed, peer_grads, near_out, far_out)
+    )
 
     mine, *parts = back_parts(
         scalar(me),
@@ -545,22 +562,19 @@
         weight,
         peer_weight,
     )
-    near = [to_peer(late_mixed, (dz, 0)) for dz in SPREAD[1:]]
     got = [to_peer(part, (dz, 0)) for part, dz in zip(parts, SPREAD[1:])]
     pair = lax.ppermute(sent, "batch", [(0, 1), (1, 0), (2, 3), (3, 2)])
-    near, pair, got[0] = tie((near, pair, got[0]))
-    near_mixed = jnp.concatenate([mixed] + near, axis=0)
+    pair, got = tie((pair, got))
     sums = pair_sums(pair, kept)
     far_mixed = to_peer(near_mixed, (0, 1))
-    sums, full_out = tie((sums, full_out))
 
     here = piece_index(me, (0, 0))
     piece = finish(scalar(here), flat_tokens, flat_cot, norm_gain, mine, got)
 
     places = jnp.stack([here] + [piece_index(me, shift) for shift in SHIFTS]).astype(jnp.int32)
-    grad_tokens = assemble(places, [piece] + [to_peer(piece, shift) for shift in SHIFTS])
+    grad_tokens = stack([piece] + [to_peer(piece, shift) for shift in SHIFTS], places)
     grad_proj = row_sums(sums).reshape(-1, 4, width)
-    output = output_rows(flat_tokens, near_mixed, far_mixed, full_out)
+    output = output_rows(flat_tokens, near_mixed, far_mixed, near_out, far_out)
     shape = (recs, frames, model)
     return (output.reshape(shape), grad_tokens.reshape(shape), grad_proj)
 

time: 251 us -> 375 us (1.49)
  Pallas kernels: 59.5 us -> 206 us
  waiting for transfers between devices: 101 us -> 88.7 us
  local copies, waits for them, and re-layouts: 19.6 us -> 8.99 us
    pallas_call x1 -> x2, Pallas kernels: 2.26 us -> 146 us  [stack(): pl.pallas_call(assemble_body if ordered else stack_body, in_specs=[pl.Blo...]
    ppermute x16 -> x17, waiting for transfers between devices: 82 us -> 66.2 us  [to_peer(): return lax.ppermute(array, 'chan', pairs)]
    reduce_scatter x0 -> x1, waiting for transfers between devices: none -> 11.2 us  [pair_sums(): return lax.psum_scatter(pair, 'frames', scatter_dimension=0)]
    ppermute x4 -> x1, waiting for transfers between devices: 9.65 us -> 0.01 us  [row_sums(): lax.ppermute(pick(sums, 1 - row, 0), 'batch', [(0, 2), (1, 3), (2, 0), (3...]
    unnamed x35 -> x46, local copies, waits for them, and re-layouts: 11.9 us -> 3.75 us
    add x3 -> x1, other arithmetic: 5.31 us -> 0.04 us  [row_sums(): return pick(sums, row, 0).astype(F32) + got.astype(F32)]
    ppermute x16 -> x17, starting transfers between devices: 23.6 us -> 26.8 us  [to_peer(): return lax.ppermute(array, 'chan', pairs)]
  transfers between devices with their start and end apart: 28 -> 28, of which waited for: 11 -> 16; matrix products, arithmetic and copies ran while one was open for 7% -> 1% of each run, Pallas kernels for 24% -> 56%
where the time goes in v3:
time: 375 us; the launch traced here: 371 us
  Pallas kernels  206 us (55%)
  waiting for transfers between devices  88.7 us (24%)
  starting transfers between devices  49.6 us (13%)
  between operations  14.1 us (4%)
  local copies, waits for them, and re-layouts  8.99 us (2%)
    pallas_call x2, Pallas kernels, stack(): pl.pallas_call(assemble_body if ordered else stack_body, in_specs=[pl.Blo...  146 us
    ppermute x17, waiting for transfers between devices, to_peer(): return lax.ppermute(array, 'chan', pairs)  66.2 us
    ppermute x17, starting transfers between devices, to_peer(): return lax.ppermute(array, 'chan', pairs)  26.8 us
    pallas_call x1, Pallas kernels, attention(): pl.pallas_call(attention_body, grid=(recs,), in_specs=[by_rec(width, fram...  18.8 us
    reduce_scatter x1, waiting for transfers between devices, pair_sums(): return lax.psum_scatter(pair, 'frames', scatter_dimension=0)  11.2 us
    pallas_call x1, Pallas kernels, project(): pl.pallas_call(project_body, grid=(rows // CTX,), in_specs=[pl.BlockSpec(...  10.7 us
    pallas_call x1, Pallas kernels, output_rows(): pl.pallas_call(output_body, grid=(rows // CTX,), in_specs=[by_row, by_col...  9.99 us
    pallas_call x1, Pallas kernels, weight_grads(): pl.pallas_call(lambda c, *refs: weight_grads_body(*refs), grid_spec=pltpu...  9.3 us
  transfers between devices with their start and end apart: 28, of which 16 were waited for; matrix products, arithmetic and copies ran while one was open for 1% of the time, Pallas kernels for 56%

profile of v3, /device:TPU:18, one launch (start us, length us, event | category | flops | bytes accessed | tf_op | source)
XLA Modules:
  0.0 371.3 jit_solution(3006095743816066920)
XLA Ops:
  8.4 10.7 %project.1 = (bf16[1024,1536]{1,0:T(8,128)(2,1)}, bf16[192,1024]{1,0:T(8,128)(2,1)}, bf16[384,1024]{1,0:T(8,128)(2,1)}, bf16[192,1024]{1,0:T(8,128)(2,1)}, bf16[...) custom-call(s32[2]{0:T(128)} %lengths.1, bf16[1024,1536]{1,0:T(8,128)(2,1)} %bitcast.27, ...), custom_call_target="tpu_custom_call" | custom-call | flops 2400000000 | bytes 15000000 | tf_op jit(solution)/shard_map/project/pallas_call | solution.py:77
  19.1 5.7 %collective-permute-done = bf16[192,1536]{1,0:T(8,128)(2,1)S(1)} collective-permute-done((bf16[192,1536]{1,0:T(8,128)(2,1)}, bf16[192,1536]{1,0:T(8,128)(2,1)S(1)}, u32[]{:S(2)}, u32[]{:S(2)}) %collective-permute-start) | collective-permute-done | bytes 589856 | tf_op jit(solution)/shard_map/ppermute | solution.py:470
  26.1 3.4 collective-permute-start.1
  29.5 3.2 collective-permute-start.2
  38.0 3.1 collective-permute-done.2.after
  41.2 18.8 %attention.1 = (bf16[192,1024]{1,0:T(8,128)(2,1)}, bf16[192,1024]{1,0:T(8,128)(2,1)}, f32[384,1024]{1,0:T(8,128)}, bf16[384,512]{1,0:T(8,128)(2,1)}, bf16[384,51...) custom-call(bf16[192,1024]{1,0:T(8,128)(2,1)} %get-tuple-element.48.q, ...), custom_call_target="tpu_custom_call" | custom-call | flops 2400000000 | bytes 8000000 | tf_op jit(solution)/shard_map/attention/pallas_call | solution.py:186
  60.0 6.8 %collective-permute-done.3.peer_weight = bf16[576,1536]{1,0:T(8,128)(2,1)S(1)} collective-permute-done((bf16[576,1536]{1,0:T(8,128)(2,1)S(1)}, bf16[576,1536]{1,0:T(8,128)(2,1)S(1)}, u32[]{:S(2)}, u32[]{:S(2)}) %collective-permute-start.3) | collective-permute-done | bytes 1769504 | tf_op jit(solution)/shard_map/ppermute | solution.py:470
  66.8 3.4 collective-permute-start.4
  70.2 2.5 collective-permute-start.5
  72.7 3.2 collective-permute-start.6
  75.8 5.1 %collective-permute-start.7 = (bf16[384,256]{1,0:T(8,128)(2,1)}, bf16[384,256]{1,0:T(8,128)(2,1)S(1)}, u32[]{:S(2)}, u32[]{:S(2)}) collective-permute-start(bf16[384,256]{1,0:T(8,128)(2,1)} %get-tuple-element.67), channel_id=1, source_target_pairs={{8,1},{9,0},{10,3},{11,2},{12,5},{13,4},{14,7},{15,6},{16,9},{17,8... | collective-permute-start | bytes 589832 | tf_op jit(solution)/shard_map/ppermute | solution.py:537
  81.3 3.3 collective-permute-done.6.peer_left
  87.6 4.1 %collective-permute-start.10 = (bf16[192,1024]{1,0:T(8,128)(2,1)}, bf16[192,1024]{1,0:T(8,128)(2,1)S(1)}, u32[]{:S(2)}, u32[]{:S(2)}) collective-permute-start(bf16[192,1024]{1,0:T(8,128)(2,1)} %get-tuple-element.71.refs_6_.refs_0_), channel_id=1, source_target_pairs={{0,6},{1,7},{2,0},{3,1},{4,2},{5,3},{6,4},{7,5},{8,14},{9,15},{10,... | collective-permute-start | bytes 1179656 | tf_op jit(solution)/shard_map/ppermute | solution.py:470
  93.5 9.3 %weight_grads.1 = (bf16[4,2,96,768]{3,2,1,0:T(8,128)(2,1)}, f32[4,2,96,768]{3,2,1,0:T(8,128)}) custom-call(s32[1]{0:T(128)} %bitcast.1.c, bf16[1024,1536]{1,0:T(8,128)(2,1)} %get-tuple-element.47.refs_0_, bf16[1024,1536]{1,0:T(8,128)(2,1)} %bitcast.25, bf16[192,1024]{1,0:T(8,128)(2,1)} %get-tuple-element.56.refs_2_.dq, ...), custom_call_target="tpu_custom_call" | custom-call | flops 2400000000 | bytes 12000000 | tf_op jit(solution)/shard_map/weight_grads/pallas_call | solution.py:333
  102.8 3.9 %collective-permute-done.10.refs_3_ = bf16[192,1024]{1,0:T(8,128)(2,1)S(1)} collective-permute-done((bf16[192,1024]{1,0:T(8,128)(2,1)}, bf16[192,1024]{1,0:T(8,128)(2,1)S(1)}, u32[]{:S(2)}, u32[]{:S(2)}) %collective-permute-start.10) | collective-permute-done | bytes 393248 | tf_op jit(solution)/shard_map/ppermute | solution.py:470
  106.7 3.4 collective-permute-done.8.refs_1_
  110.1 48.8 %stack.37.near = bf16[768,1024]{1,0:T(8,128)(2,1)} custom-call(bf16[192,1024]{1,0:T(8,128)(2,1)} %get-tuple-element.71.refs_6_.refs_0_, bf16[192,1024]{1,0:T(8,128)(2,1)} %collective-permute-done.8.refs_1_, bf16[192,1024]{1,0:T(8,128)(2,1)} %collective-permute-done.9.refs_2_, bf16[192,1024]{1,0:T(8,128)(2,1)} %copy-done.17), custom_call_target="tpu_custom_call" | custom-call | bytes 6000000 | tf_op jit(solution)/shard_map/stack/pallas_call | solution.py:453
  159.8 8.6 %back.1 = (f32[128,1536]{1,0:T(8,128)}, bf16[128,1536]{1,0:T(8,128)(2,1)}, bf16[128,1536]{1,0:T(8,128)(2,1)}, bf16[128,1536]{1,0:T(8,128)(2,1)}) custom-call(s32[1]{0:T(128)} %bitcast.16.here, bf16[192,1024]{1,0:T(8,128)(2,1)} %get-tuple-element.56.refs_2_.dq, f32[384,1024]{1,0:T(8,128)} %get-tuple-element.57.refs_3_.own, bf16[384,512]{1,0:T(8,128)(2,1)} %copy-done.3, ...), custom_call_target="tpu_custom_call" | custom-call | flops 1800000000 | bytes 8000000 | tf_op jit(solution)/shard_map/back/pallas_call | solution.py:260
  171.6 17.5 %collective-permute-done.14.rest_0_ = bf16[128,1536]{1,0:T(8,128)(2,1)S(1)} collective-permute-done((bf16[128,1536]{1,0:T(8,128)(2,1)}, bf16[128,1536]{1,0:T(8,128)(2,1)S(1)}, u32[]{:S(2)}, u32[]{:S(2)}) %collective-permute-start.14) | collective-permute-done | bytes 393248 | tf_op jit(solution)/shard_map/ppermute | solution.py:470
  190.5 2.7 add_convert_fusion
  193.2 2.9 collective-permute-start.12
  196.1 3.2 finish.1.refs_0_
  199.5 3.0 collective-permute-start.18
  205.1 11.2 %reduce-scatter.2.cloned.1.call-done = bf16[1,2,96,768]{3,2,1,0:T(8,128)(2,1)} async-done(((bf16[4,2,96,768]{3,2,1,0:T(8,128)(2,1)}), bf16[1,2,96,768]{3,2,1,0:T(8,128)(2,1)}) %reduce-scatter.2.cloned.1.call-update) | async-done | bytes 294928 | tf_op jit(solution)/shard_map/reduce_scatter | solution.py:484
  217.2 15.0 %collective-permute-done.12.far = bf16[768,1024]{1,0:T(8,128)(2,1)} collective-permute-done((bf16[768,1024]{1,0:T(8,128)(2,1)S(1)}, bf16[768,1024]{1,0:T(8,128)(2,1)}, u32[]{:S(2)}, u32[]{:S(2)}) %collective-permute-start.12) | collective-permute-done | bytes 1572896 | tf_op jit(solution)/shard_map/ppermute | solution.py:470
  232.2 4.6 %collective-permute-start.21 = (bf16[128,1536]{1,0:T(8,128)(2,1)}, bf16[128,1536]{1,0:T(8,128)(2,1)S(1)}, u32[]{:S(2)}, u32[]{:S(2)}) collective-permute-start(bf16[128,1536]{1,0:T(8,128)(2,1)} %finish.1.refs_0_), channel_id=1, source_target_pairs={{0,7},{1,6},{2,1},{3,0},{4,3},{5,2},{6,5},{7,4},{8,15},{9,14},{10,... | collective-permute-start | bytes 1179656 | tf_op jit(solution)/shard_map/ppermute | solution.py:470
  236.8 3.7 collective-permute-start.23
  242.4 10.0 %output.1 = bf16[1024,1536]{1,0:T(8,128)(2,1)} custom-call(bf16[1024,1536]{1,0:T(8,128)(2,1)} %bitcast.29, bf16[768,1024]{1,0:T(8,128)(2,1)} %stack.37.near, bf16[768,1024]{1,0:T(8,128)(2,1)} %collective-permute-done.12.far, bf16[768,1536]{1,0:T(8,128)(2,1)} %all-gather.3.cloned.1.call-done.near_weight, bf16[768,1536]{1,0:T(8,128)(2,1)} %all-gather.5.cloned.1.call-done.far_weight), custom_call_target="tpu_custom_call" | custom-call | flops 4800000000 | bytes 14000000 | tf_op jit(solution)/shard_map/output/pallas_call | solution.py:382
  252.5 5.8 %collective-permute-done.21.refs_5_ = bf16[128,1536]{1,0:T(8,128)(2,1)S(1)} collective-permute-done((bf16[128,1536]{1,0:T(8,128)(2,1)}, bf16[128,1536]{1,0:T(8,128)(2,1)S(1)}, u32[]{:S(2)}, u32[]{:S(2)}) %collective-permute-start.21) | collective-permute-done | bytes 393248 | tf_op jit(solution)/shard_map/ppermute | solution.py:470
  258.2 5.2 %collective-permute-done.22.refs_6_ = bf16[128,1536]{1,0:T(8,128)(2,1)S(1)} collective-permute-done((bf16[128,1536]{1,0:T(8,128)(2,1)}, bf16[128,1536]{1,0:T(8,128)(2,1)S(1)}, u32[]{:S(2)}, u32[]{:S(2)}) %collective-permute-start.22) | collective-permute-done | bytes 393248 | tf_op jit(solution)/shard_map/ppermute | solution.py:470
  263.4 2.4 collective-permute-done.23.refs_7_
  266.5 97.1 %assemble.1 = bf16[1024,1536]{1,0:T(8,128)(2,1)} custom-call(s32[8]{0:T(128)} %stack.36.places, bf16[128,1536]{1,0:T(8,128)(2,1)} %finish.1.refs_0_, bf16[128,1536]{1,0:T(8,128)(2,1)} %copy-done.11, bf16[128,1536]{1,0:T(8,128)(2,1)} %copy-done.12, bf16[128,1536]{1,0:T(8,128)(2,1)} %copy-done.13, bf16[128,1536]{1,0:T(8,128)(2,1)} %copy-done.14, ...), custom_call_target="tpu_custom_call" | custom-call | bytes 6000000 | tf_op jit(solution)/shard_map/assemble/pallas_call | solution.py:453
  (91 shorter events, 26.0 us)
Async XLA Ops:
  7.2 151.8 %all-gather.3.cloned.1.call-start = ((), (), s32[]{:S(2)}) async-start(), calls=%async_computation.1 | async-start | bytes 2949120 | tf_op jit(solution)/shard_map/all_gather | solution.py:502
  7.9 151.1 %all-gather.5.cloned.1.call-start = ((), (), s32[]{:S(2)}) async-start(), calls=%async_computation.2 | async-start | bytes 2949120 | tf_op jit(solution)/shard_map/all_gather | solution.py:502
  7.9 16.9 %collective-permute-start = (bf16[192,1536]{1,0:T(8,128)(2,1)}, bf16[192,1536]{1,0:T(8,128)(2,1)S(1)}, u32[]{:S(2)}, u32[]{:S(2)}) collective-permute-start(bf16[192,1536]{1,0:T(8,128)(2,1)} %out_w.1), channel_id=1, source_target_pairs={{0,1},{1,0},{2,3},{3,2},{4,5},{5,4},{6,7},{7,6},{8,9},{9,8},{10,11... | collective-permute-start | bytes 1769480 | tf_op jit(solution)/shard_map/ppermute | solution.py:470
  8.4 24.4 %copy-start.22 = (s32[2]{0:T(128)S(1)}, s32[2]{0:T(128)}, u32[]{:S(2)}) copy-start(s32[2]{0:T(128)} %lengths.1) | copy-start | bytes 28
  25.7 190.6 %reduce-scatter.2.cloned.1.call-start = ((), (), s32[]{:S(2)}) async-start(), calls=%async_computation.3 | async-start | bytes 1474560 | tf_op jit(solution)/shard_map/reduce_scatter | solution.py:484
  25.7 41.1 %collective-permute-start.3 = (bf16[576,1536]{1,0:T(8,128)(2,1)S(1)}, bf16[576,1536]{1,0:T(8,128)(2,1)S(1)}, u32[]{:S(2)}, u32[]{:S(2)}) collective-permute-start(bf16[576,1536]{1,0:T(8,128)(2,1)S(1)} %bitcast.33), channel_id=1, source_target_pairs={{0,1},{1,0},{2,3},{3,2},{4,5},{5,4},{6,7},{7,6},{8,9},{9,8},{10,11... | collective-permute-start | bytes 5308424 | tf_op jit(solution)/shard_map/ppermute | solution.py:470
  26.1 11.9 %collective-permute-start.1 = (bf16[384,512]{1,0:T(8,128)(2,1)}, bf16[384,512]{1,0:T(8,128)(2,1)}, u32[]{:S(2)}, u32[]{:S(2)}) collective-permute-start(bf16[384,512]{1,0:T(8,128)(2,1)} %get-tuple-element.52), channel_id=1, source_target_pairs={{0,8},{8,16},{16,24},{1,9},{9,17},{17,25},{2,10},{10,18},{18,26},{... | collective-permute-start | bytes 1179656 | tf_op jit(solution)/shard_map/ppermute | solution.py:526
  29.5 11.6 %collective-permute-start.2 = (bf16[384,512]{1,0:T(8,128)(2,1)}, bf16[384,512]{1,0:T(8,128)(2,1)}, u32[]{:S(2)}, u32[]{:S(2)}) collective-permute-start(bf16[384,512]{1,0:T(8,128)(2,1)} %get-tuple-element.53), channel_id=1, source_target_pairs={{8,0},{16,8},{24,16},{9,1},{17,9},{25,17},{10,2},{18,10},{26,18},{... | collective-permute-start | bytes 1179656 | tf_op jit(solution)/shard_map/ppermute | solution.py:527
  66.8 36.0 %copy-start.2 = (bf16[576,1536]{1,0:T(8,128)(2,1)}, bf16[576,1536]{1,0:T(8,128)(2,1)S(1)}, u32[]{:S(2)}) copy-start(bf16[576,1536]{1,0:T(8,128)(2,1)S(1)} %collective-permute-done.3.peer_weight) | copy-start | bytes 5308420
  66.8 20.1 %collective-permute-start.4 = (bf16[384,512]{1,0:T(8,128)(2,1)}, bf16[384,512]{1,0:T(8,128)(2,1)S(1)}, u32[]{:S(2)}, u32[]{:S(2)}) collective-permute-start(bf16[384,512]{1,0:T(8,128)(2,1)} %get-tuple-element.64), channel_id=1, source_target_pairs={{0,8},{8,16},{16,24},{1,9},{9,17},{17,25},{2,10},{10,18},{18,26},{... | collective-permute-start | bytes 1179656 | tf_op jit(solution)/shard_map/ppermute | solution.py:540
  70.2 16.7 %collective-permute-start.5 = (bf16[384,512]{1,0:T(8,128)(2,1)}, bf16[384,512]{1,0:T(8,128)(2,1)S(1)}, u32[]{:S(2)}, u32[]{:S(2)}) collective-permute-start(bf16[384,512]{1,0:T(8,128)(2,1)} %get-tuple-element.65), channel_id=1, source_target_pairs={{8,0},{16,8},{24,16},{9,1},{17,9},{25,17},{10,2},{18,10},{26,18},{... | collective-permute-start | bytes 1179656 | tf_op jit(solution)/shard_map/ppermute | solution.py:539
  72.7 12.0 %collective-permute-start.6 = (bf16[384,256]{1,0:T(8,128)(2,1)}, bf16[384,256]{1,0:T(8,128)(2,1)S(1)}, u32[]{:S(2)}, u32[]{:S(2)}) collective-permute-start(bf16[384,256]{1,0:T(8,128)(2,1)} %get-tuple-element.66), channel_id=1, source_target_pairs={{0,9},{1,8},{2,11},{3,10},{4,13},{5,12},{6,15},{7,14},{8,17},{9,16... | collective-permute-start | bytes 589832 | tf_op jit(solution)/shard_map/ppermute | solution.py:538
  75.8 11.1 %collective-permute-start.7 = (bf16[384,256]{1,0:T(8,128)(2,1)}, bf16[384,256]{1,0:T(8,128)(2,1)S(1)}, u32[]{:S(2)}, u32[]{:S(2)}) collective-permute-start(bf16[384,256]{1,0:T(8,128)(2,1)} %get-tuple-element.67), channel_id=1, source_target_pairs={{8,1},{9,0},{10,3},{11,2},{12,5},{13,4},{14,7},{15,6},{16,9},{17,8... | collective-permute-start | bytes 589832 | tf_op jit(solution)/shard_map/ppermute | solution.py:537
  80.9 78.0 %collective-permute-start.11 = (bf16[576,512]{1,0:T(8,128)(2,1)}, bf16[576,512]{1,0:T(8,128)(2,1)S(1)}, u32[]{:S(2)}, u32[]{:S(2)}) collective-permute-start(bf16[576,512]{1,0:T(8,128)(2,1)} %get-tuple-element.72), channel_id=1, source_target_pairs={{0,1},{1,0},{2,3},{3,2},{4,5},{5,4},{6,7},{7,6},{8,9},{9,8},{10,11... | collective-permute-start | bytes 1769480 | tf_op jit(solution)/shard_map/ppermute | solution.py:470
  87.6 19.1 %collective-permute-start.10 = (bf16[192,1024]{1,0:T(8,128)(2,1)}, bf16[192,1024]{1,0:T(8,128)(2,1)S(1)}, u32[]{:S(2)}, u32[]{:S(2)}) collective-permute-start(bf16[192,1024]{1,0:T(8,128)(2,1)} %get-tuple-element.71.refs_6_.refs_0_), channel_id=1, source_target_pairs={{0,6},{1,7},{2,0},{3,1},{4,2},{5,3},{6,4},{7,5},{8,14},{9,15},{10,... | collective-permute-start | bytes 1179656 | tf_op jit(solution)/shard_map/ppermute | solution.py:470
  91.7 18.4 %collective-permute-start.8 = (bf16[192,1024]{1,0:T(8,128)(2,1)}, bf16[192,1024]{1,0:T(8,128)(2,1)}, u32[]{:S(2)}, u32[]{:S(2)}) collective-permute-start(bf16[192,1024]{1,0:T(8,128)(2,1)} %get-tuple-element.71.refs_6_.refs_0_), channel_id=1, source_target_pairs={{0,2},{1,3},{2,4},{3,5},{4,6},{5,7},{6,0},{7,1},{8,10},{9,11},{10,... | collective-permute-start | bytes 1179656 | tf_op jit(solution)/shard_map/ppermute | solution.py:470
  91.7 18.4 %collective-permute-start.9 = (bf16[192,1024]{1,0:T(8,128)(2,1)}, bf16[192,1024]{1,0:T(8,128)(2,1)}, u32[]{:S(2)}, u32[]{:S(2)}) collective-permute-start(bf16[192,1024]{1,0:T(8,128)(2,1)} %get-tuple-element.71.refs_6_.refs_0_), channel_id=1, source_target_pairs={{0,4},{1,5},{2,6},{3,7},{4,0},{5,1},{6,2},{7,3},{8,12},{9,13},{10,... | collective-permute-start | bytes 1179656 | tf_op jit(solution)/shard_map/ppermute | solution.py:470
  159.0 30.7 %collective-permute-start.13 = (bf16[4,2,96,768]{3,2,1,0:T(8,128)(2,1)}, bf16[4,2,96,768]{3,2,1,0:T(8,128)(2,1)}, u32[]{:S(2)}, u32[]{:S(2)}) collective-permute-start(bf16[4,2,96,768]{3,2,1,0:T(8,128)(2,1)} %get-tuple-element.82), channel_id=1, source_target_pairs={{0,32},{32,0},{64,96},{96,64},{1,33},{33,1},{65,97},{97,65},{2,34}... | collective-permute-start | bytes 3538952 | tf_op jit(solution)/shard_map/ppermute | solution.py:566
  159.8 30.7 %copy-start = (f32[4,2,96,768]{3,2,1,0:T(8,128)S(1)}, f32[4,2,96,768]{3,2,1,0:T(8,128)}, u32[]{:S(2)}) copy-start(f32[4,2,96,768]{3,2,1,0:T(8,128)} %get-tuple-element.89) | copy-start | bytes 7077892
  168.3 20.7 %collective-permute-start.14 = (bf16[128,1536]{1,0:T(8,128)(2,1)}, bf16[128,1536]{1,0:T(8,128)(2,1)S(1)}, u32[]{:S(2)}, u32[]{:S(2)}) collective-permute-start(bf16[128,1536]{1,0:T(8,128)(2,1)} %get-tuple-element.83), channel_id=1, source_target_pairs={{0,2},{1,3},{2,4},{3,5},{4,6},{5,7},{6,0},{7,1},{8,10},{9,11},{10,... | collective-permute-start | bytes 1179656 | tf_op jit(solution)/shard_map/ppermute | solution.py:470
  168.4 20.7 %collective-permute-start.15 = (bf16[128,1536]{1,0:T(8,128)(2,1)}, bf16[128,1536]{1,0:T(8,128)(2,1)S(1)}, u32[]{:S(2)}, u32[]{:S(2)}) collective-permute-start(bf16[128,1536]{1,0:T(8,128)(2,1)} %get-tuple-element.84), channel_id=1, source_target_pairs={{0,4},{1,5},{2,6},{3,7},{4,0},{5,1},{6,2},{7,3},{8,12},{9,13},{10,... | collective-permute-start | bytes 1179656 | tf_op jit(solution)/shard_map/ppermute | solution.py:470
  170.8 18.9 %collective-permute-start.16 = (bf16[128,1536]{1,0:T(8,128)(2,1)}, bf16[128,1536]{1,0:T(8,128)(2,1)S(1)}, u32[]{:S(2)}, u32[]{:S(2)}) collective-permute-start(bf16[128,1536]{1,0:T(8,128)(2,1)} %get-tuple-element.85), channel_id=1, source_target_pairs={{0,6},{1,7},{2,0},{3,1},{4,2},{5,3},{6,4},{7,5},{8,14},{9,15},{10,... | collective-permute-start | bytes 1179656 | tf_op jit(solution)/shard_map/ppermute | solution.py:470
  193.2 39.0 %collective-permute-start.12 = (bf16[768,1024]{1,0:T(8,128)(2,1)S(1)}, bf16[768,1024]{1,0:T(8,128)(2,1)}, u32[]{:S(2)}, u32[]{:S(2)}) collective-permute-start(bf16[768,1024]{1,0:T(8,128)(2,1)S(1)} %copy-done.5), channel_id=1, source_target_pairs={{0,1},{1,0},{2,3},{3,2},{4,5},{5,4},{6,7},{7,6},{8,9},{9,8},{10,11... | collective-permute-start | bytes 4718600 | tf_op jit(solution)/shard_map/ppermute | solution.py:470
  199.2 37.5 %collective-permute-start.17 = (bf16[128,1536]{1,0:T(8,128)(2,1)}, bf16[128,1536]{1,0:T(8,128)(2,1)S(1)}, u32[]{:S(2)}, u32[]{:S(2)}) collective-permute-start(bf16[128,1536]{1,0:T(8,128)(2,1)} %finish.1.refs_0_), channel_id=1, source_target_pairs={{0,2},{1,3},{2,4},{3,5},{4,6},{5,7},{6,0},{7,1},{8,10},{9,11},{10,... | collective-permute-start | bytes 1179656 | tf_op jit(solution)/shard_map/ppermute | solution.py:470
  199.5 37.3 %collective-permute-start.18 = (bf16[128,1536]{1,0:T(8,128)(2,1)}, bf16[128,1536]{1,0:T(8,128)(2,1)S(1)}, u32[]{:S(2)}, u32[]{:S(2)}) collective-permute-start(bf16[128,1536]{1,0:T(8,128)(2,1)} %finish.1.refs_0_), channel_id=1, source_target_pairs={{0,6},{1,7},{2,0},{3,1},{4,2},{5,3},{6,4},{7,5},{8,14},{9,15},{10,... | collective-permute-start | bytes 1179656 | tf_op jit(solution)/shard_map/ppermute | solution.py:470
  202.5 38.1 %collective-permute-start.19 = (bf16[128,1536]{1,0:T(8,128)(2,1)}, bf16[128,1536]{1,0:T(8,128)(2,1)S(1)}, u32[]{:S(2)}, u32[]{:S(2)}) collective-permute-start(bf16[128,1536]{1,0:T(8,128)(2,1)} %finish.1.refs_0_), channel_id=1, source_target_pairs={{0,1},{1,0},{2,3},{3,2},{4,5},{5,4},{6,7},{7,6},{8,9},{9,8},{10,11... | collective-permute-start | bytes 1179656 | tf_op jit(solution)/shard_map/ppermute | solution.py:470
  203.8 48.6 %collective-permute-start.20 = (bf16[128,1536]{1,0:T(8,128)(2,1)}, bf16[128,1536]{1,0:T(8,128)(2,1)S(1)}, u32[]{:S(2)}, u32[]{:S(2)}) collective-permute-start(bf16[128,1536]{1,0:T(8,128)(2,1)} %finish.1.refs_0_), channel_id=1, source_target_pairs={{0,3},{1,2},{2,5},{3,4},{4,7},{5,6},{6,1},{7,0},{8,11},{9,10},{10,... | collective-permute-start | bytes 1179656 | tf_op jit(solution)/shard_map/ppermute | solution.py:470
  232.2 26.0 %collective-permute-start.21 = (bf16[128,1536]{1,0:T(8,128)(2,1)}, bf16[128,1536]{1,0:T(8,128)(2,1)S(1)}, u32[]{:S(2)}, u32[]{:S(2)}) collective-permute-start(bf16[128,1536]{1,0:T(8,128)(2,1)} %finish.1.refs_0_), channel_id=1, source_target_pairs={{0,7},{1,6},{2,1},{3,0},{4,3},{5,2},{6,5},{7,4},{8,15},{9,14},{10,... | collective-permute-start | bytes 1179656 | tf_op jit(solution)/shard_map/ppermute | solution.py:470
  236.8 26.6 %collective-permute-start.22 = (bf16[128,1536]{1,0:T(8,128)(2,1)}, bf16[128,1536]{1,0:T(8,128)(2,1)S(1)}, u32[]{:S(2)}, u32[]{:S(2)}) collective-permute-start(bf16[128,1536]{1,0:T(8,128)(2,1)} %finish.1.refs_0_), channel_id=1, source_target_pairs={{0,4},{1,5},{2,6},{3,7},{4,0},{5,1},{6,2},{7,3},{8,12},{9,13},{10,... | collective-permute-start | bytes 1179656 | tf_op jit(solution)/shard_map/ppermute | solution.py:470
  236.8 29.0 %collective-permute-start.23 = (bf16[128,1536]{1,0:T(8,128)(2,1)}, bf16[128,1536]{1,0:T(8,128)(2,1)S(1)}, u32[]{:S(2)}, u32[]{:S(2)}) collective-permute-start(bf16[128,1536]{1,0:T(8,128)(2,1)} %finish.1.refs_0_), channel_id=1, source_target_pairs={{0,5},{1,4},{2,7},{3,6},{4,1},{5,0},{6,3},{7,2},{8,13},{9,12},{10,... | collective-permute-start | bytes 1179656 | tf_op jit(solution)/shard_map/ppermute | solution.py:470
  240.5 123.1 %collective-permute-start.24 = (bf16[96,768]{1,0:T(8,128)(2,1)S(1)}, bf16[96,768]{1,0:T(8,128)(2,1)S(1)}, u32[]{:S(2)}, u32[]{:S(2)}) collective-permute-start(bf16[96,768]{1,0:T(8,128)(2,1)S(1)} %dynamic-slice_bitcast_fusion), channel_id=1, source_target_pairs={{0,64},{32,96},{64,0},{96,32},{1,65},{33,97},{65,1},{97,33},{2,66}... | collective-permute-start | bytes 442376 | tf_op jit(solution)/shard_map/ppermute | solution.py:489
  252.4 111.2 %copy-start.19 = (bf16[1,2,96,768]{3,2,1,0:T(8,128)(2,1)S(1)}, bf16[1,2,96,768]{3,2,1,0:T(8,128)(2,1)}, u32[]{:S(2)}) copy-start(bf16[1,2,96,768]{3,2,1,0:T(8,128)(2,1)} %reduce-scatter.2.cloned.1.call-done) | copy-start | bytes 884740
  (19 other events, 110.9 us)
Sparse Core Ops, SparseCore 0:
  9.7 35.4 all-gather.2
  46.8 33.1 all-gather.4
  193.3 22.9 reduce-scatter.1

commit v4 on v3

--- a/solution.py
+++ b/solution.py
@@ -10,8 +10,6 @@
 EPS = 1e-05
 NEG = -1e30
 VMEM_LIMIT = 60 * 1024 * 1024
-SHIFTS = ((1, 0), (3, 0), (0, 1), (1, 1), (3, 1), (2, 0), (2, 1))
-SPREAD = (0, 1, 2, 3)
 
 F32 = jnp.float32
 BF16 = jnp.bfloat16
@@ -111,24 +109,7 @@
 
 
 def attention_body(
-    q,
-    kv,
-    before,
-    after,
-    g,
-    seg_keys,
-    seg_rows,
-    live,
-    mixed,
-    dq,
-    dkv,
-    dbefore,
-    dafter,
-    peer_grads,
-    peer_before,
-    peer_after,
-    acc,
-    mask,
+    q, kv, before, after, g, seg_keys, seg_rows, live, mixed, dq, dkv, dbefore, dafter, acc, mask
 ):
     width = q.shape[0]
     span = 3 * CTX
@@ -169,20 +150,12 @@
     dbefore[...] = acc[:, :CTX].astype(BF16)
     dafter[...] = acc[:, CTX + frames :].astype(BF16)
 
-    @pl.when(pl.program_id(0) != lax.axis_index("chan") % 2)
-    def _():
-        peer_grads[:width, :] = dq[...]
-        peer_grads[width:, :] = acc[:, CTX : CTX + frames].astype(BF16)
-        peer_before[...] = dbefore[...]
-        peer_after[...] = dafter[...]
-
 
 def attention(q, kv, before, after, g, seg_keys, seg_rows, live):
     width, rows = q.shape
     recs, span, _ = seg_keys.shape
     frames = rows // recs
     by_rec = lambda n, m: pl.BlockSpec((n, m), lambda r: (0, r))
-    fixed = lambda n, m: pl.BlockSpec((n, m), lambda r: (0, 0))
     return pl.pallas_call(
         attention_body,
         grid=(recs,),
@@ -202,9 +175,6 @@
             by_rec(2 * width, frames),
             by_rec(2 * width, CTX),
             by_rec(2 * width, CTX),
-            fixed(3 * width, frames),
-            fixed(2 * width, CTX),
-            fixed(2 * width, CTX),
         ],
         out_shape=[
             jax.ShapeDtypeStruct((width, rows), BF16),
@@ -212,9 +182,6 @@
             jax.ShapeDtypeStruct((2 * width, rows), F32),
             jax.ShapeDtypeStruct((2 * width, recs * CTX), BF16),
             jax.ShapeDtypeStruct((2 * width, recs * CTX), BF16),
-            jax.ShapeDtypeStruct((3 * width, frames), BF16),
-            jax.ShapeDtypeStruct((2 * width, CTX), BF16),
-            jax.ShapeDtypeStruct((2 * width, CTX), BF16),
         ],
         scratch_shapes=[pltpu.VMEM((2 * width, span), F32), pltpu.VMEM((3 * CTX, CTX), F32)],
         compiler_params=params(),
@@ -223,68 +190,45 @@
     )(q, kv, before, after, g, seg_keys, seg_rows, live)
 
 
-def back_body(
-    here, dq, own, left, right, peer, peer_left, peer_right, weight, peer_weight, mine, *rest
-):
-    parts, (flipped, sums) = rest[:-2], rest[-2:]
+def back_body(dq, own, left, right, weight, out, flipped):
     width = dq.shape[0]
-    chunk = mine.shape[0]
 
     @pl.when(pl.program_id(0) == 0)
     def _():
-        beside = jnp.concatenate([left[...], right[...]], axis=1).astype(F32)
-        peer_beside = jnp.concatenate([peer_left[...], peer_right[...]], axis=1).astype(F32)
+        beside = []
+        for rec in range(own.shape[1] // (2 * CTX)):
+            cols = slice(rec * CTX, (rec + 1) * CTX)
+            beside += [left[:, cols], right[:, cols]]
+        beside = jnp.concatenate(beside, axis=1).astype(F32)
         flipped[:, :width] = dq[...].T
-        flipped[:, width : 3 * width] = (own[...] + beside).astype(BF16).T
-        flipped[:, 3 * width : 4 * width] = peer[:width, :].T
-        flipped[:, 4 * width :] = (peer[width:, :].astype(F32) + peer_beside).astype(BF16).T
-
-    sums[...] = dot_nn(flipped[:, : 3 * width], weight[...]) + dot_nn(
-        flipped[:, 3 * width :], peer_weight[...]
-    )
-    z = here[0] >> 1
-    for index, part in enumerate((mine,) + parts):
-        rows = pl.ds(pl.multiple_of(((z + index) & 3) * chunk, chunk), chunk)
-        part[...] = sums[rows, :].astype(part.dtype)
-
-
-def back_parts(here, dq, own, left, right, peer, peer_left, peer_right, weight, peer_weight):
-    width = dq.shape[0]
-    frames = peer.shape[1]
+        flipped[:, width:] = (own[...] + beside).astype(BF16).T
+
+    out[...] = dot_nn(flipped[...], weight[...]).astype(BF16)
+
+
+def back_rows(dq, own, left, right, weight):
+    width, rows = dq.shape
     model = weight.shape[1]
-    chunk = frames // 4
     tile = 256
-    full = lambda n, m: pl.BlockSpec((n, m), lambda i, h: (0, 0))
-    by_rec = lambda n, m: pl.BlockSpec((n, m), lambda i, h: (0, h[0] & 1))
-    by_col = lambda n: pl.BlockSpec((n, tile), lambda i, h: (0, i))
+    full = lambda n, m: pl.BlockSpec((n, m), lambda i: (0, 0))
+    by_col = lambda n: pl.BlockSpec((n, tile), lambda i: (0, i))
     return pl.pallas_call(
         back_body,
-        grid_spec=pltpu.PrefetchScalarGridSpec(
-            num_scalar_prefetch=1,
-            grid=(model // tile,),
-            in_specs=[
-                by_rec(width, frames),
-                by_rec(2 * width, frames),
-                by_rec(2 * width, CTX),
-                by_rec(2 * width, CTX),
-                full(3 * width, frames),
-                full(2 * width, CTX),
-                full(2 * width, CTX),
-                by_col(3 * width),
-                by_col(3 * width),
-            ],
-            out_specs=[by_col(chunk)] * 4,
-            scratch_shapes=[
-                pltpu.VMEM((frames, 6 * width), BF16),
-                pltpu.VMEM((frames, tile), F32),
-            ],
-        ),
-        out_shape=[jax.ShapeDtypeStruct((chunk, model), F32)]
-        + [jax.ShapeDtypeStruct((chunk, model), BF16)] * 3,
+        grid=(model // tile,),
+        in_specs=[
+            full(width, rows),
+            full(2 * width, rows),
+            full(2 * width, rows // 2),
+            full(2 * width, rows // 2),
+            by_col(3 * width),
+        ],
+        out_specs=by_col(rows),
+        out_shape=jax.ShapeDtypeStruct((rows, model), BF16),
+        scratch_shapes=[pltpu.VMEM((rows, 3 * width), BF16)],
         compiler_params=params(),
         cost_estimate=pl.CostEstimate(flops=1800000000, bytes_accessed=8000000, transcendentals=0),
         name="back",
-    )(here, dq, own, left, right, peer, peer_left, peer_right, weight, peer_weight)
+    )(dq, own, left, right, weight)
 
 
 def weight_grads_body(normed, cot, dq, own, left, right, mixed, sent, kept, gkv):
@@ -355,21 +299,13 @@
             jax.ShapeDtypeStruct((4, 2, block // 4, 4 * width), F32),
         ],
         compiler_params=params(),
-        cost_estimate=pl.CostEstimate(flops=2400000000, bytes_accessed=12000000, transcendentals=0),
+        cost_estimate=pl.CostEstimate(flops=1000, bytes_accessed=1000, transcendentals=0),
         name="weight_grads",
     )(core, normed, cotangent, dq, own, left, right, mixed)
 
 
-def output_body(tok, near, far, near_weight, far_weight, out, near_stack, far_stack):
-    z = lax.axis_index("chan") >> 1
-    width = near.shape[0] // len(SPREAD)
-    for index, dz in enumerate(SPREAD):
-        rows = slice(index * width, (index + 1) * width)
-        place = pl.ds(pl.multiple_of(((z - dz) & 3) * width, width), width)
-        near_stack[place, :] = near[rows, :]
-        far_stack[place, :] = far[rows, :]
-    total = dot_nn(near_stack[...].T, near_weight[...])
-    total = total + dot_nn(far_stack[...].T, far_weight[...])
+def output_body(tok, near, far, near_weight, far_weight, out):
+    total = dot_nn(near[...].T, near_weight[...]) + dot_nn(far[...].T, far_weight[...])
     out[...] = (tok[...].astype(F32) + total).astype(BF16)
 
 
@@ -385,81 +321,39 @@
         in_specs=[by_row, by_col, by_col, full, full],
         out_specs=by_row,
         out_shape=jax.ShapeDtypeStruct((rows, model), BF16),
-        scratch_shapes=[pltpu.VMEM((depth, CTX), BF16)] * 2,
-        compiler_params=params(),
-        cost_estimate=pl.CostEstimate(flops=4800000000, bytes_accessed=14000000, transcendentals=0),
+        compiler_params=params(),
+        cost_estimate=pl.CostEstimate(flops=1000, bytes_accessed=1000, transcendentals=0),
         name="output",
     )(tokens, near, far, near_weight, far_weight)
 
 
-def finish_body(place, tok, cot, gain, mine, *rest):
-    parts, out = rest[:-1], rest[-1]
-    back = mine[...]
-    for part in parts:
-        back = back + part[...].astype(F32)
+def finish_body(place, tok, cot, gain, parts, out):
+    back = jnp.sum(parts[...].astype(F32), axis=0)
     scaled, inverse = norm_stats(tok[...])
     weighted = back * gain[...][None, :]
     first = jnp.mean(weighted, axis=-1, keepdims=True)
     second = jnp.mean(weighted * scaled, axis=-1, keepdims=True)
     grad = inverse * (weighted - first - scaled * second) + cot[...].astype(F32)
-    out[...] = grad.astype(BF16)
-
-
-def finish(place, tokens, cotangent, gain, mine, parts):
-    chunk, model = mine.shape
+    out[...] = jnp.broadcast_to(grad.astype(BF16)[None], out.shape)
+
+
+def finish(place, tokens, cotangent, gain, parts):
+    count, chunk, model = parts.shape
     here = pl.BlockSpec((chunk, model), lambda i, p: (p[0], 0))
-    whole = pl.BlockSpec((chunk, model), lambda i, p: (0, 0))
+    whole = pl.BlockSpec((count, chunk, model), lambda i, p: (0, 0, 0))
     return pl.pallas_call(
         finish_body,
         grid_spec=pltpu.PrefetchScalarGridSpec(
             num_scalar_prefetch=1,
             grid=(1,),
-            in_specs=[here, here, pl.BlockSpec((model,), lambda i, p: (0,))]
-            + [whole] * (1 + len(parts)),
+            in_specs=[here, here, pl.BlockSpec((model,), lambda i, p: (0,)), whole],
             out_specs=whole,
         ),
-        out_shape=jax.ShapeDtypeStruct((chunk, model), BF16),
+        out_shape=jax.ShapeDtypeStruct((count, chunk, model), BF16),
         compiler_params=params(),
         cost_estimate=pl.CostEstimate(flops=10000000, bytes_accessed=5000000, transcendentals=0),
         name="finish",
-    )(place, tokens, cotangent, gain, mine, *parts)
-
-
-def copy_all(pieces, out, sems, places):
-    chunk = pieces[0].shape[0]
-    copies = []
-    for index, (piece, place) in enumerate(zip(pieces, places)):
-        rows = pl.ds(pl.multiple_of(place * chunk, chunk), chunk)
-        copies.append(pltpu.make_async_copy(piece, out.at[rows, :], sems.at[index]))
-    for copy in copies:
-        copy.start()
-    for copy in copies:
-        copy.wait()
-
-
-def assemble_body(places, *refs):
-    copy_all(refs[:-2], refs[-2], refs[-1], [places[i] for i in range(len(refs) - 2)])
-
-
-def stack_body(*refs):
-    copy_all(refs[:-2], refs[-2], refs[-1], range(len(refs) - 2))
-
-
-def stack(pieces, places=None):
-    chunk, model = pieces[0].shape
-    count = len(pieces)
-    anywhere = pl.BlockSpec(memory_space=pl.ANY)
-    ordered = places is not None
-    return pl.pallas_call(
-        assemble_body if ordered else stack_body,
-        in_specs=[pl.BlockSpec(memory_space=pltpu.SMEM)] * ordered + [anywhere] * count,
-        out_specs=anywhere,
-        out_shape=jax.ShapeDtypeStruct((count * chunk, model), BF16),
-        scratch_shapes=[pltpu.SemaphoreType.DMA((count,))],
-        compiler_params=params(),
-        cost_estimate=pl.CostEstimate(flops=0, bytes_accessed=6000000, transcendentals=0),
-        name="assemble" if ordered else "stack",
-    )(*([places] if ordered else []), *pieces)
+    )(place, tokens, cotangent, gain, parts)
 
 
 def to_peer(array, shift):
@@ -470,24 +364,13 @@
     return lax.ppermute(array, "chan", pairs)
 
 
-def piece_index(me, shift):
-    dz, dy = shift
-    return ((me & 1) ^ dy) * 4 + (((me >> 1) - dz) & 3)
-
-
-def pick(array, index, axis):
-    return lax.dynamic_index_in_dim(array, index, axis, keepdims=False)
-
-
-def pair_sums(got, kept):
-    pair = (kept + got.astype(F32)).astype(BF16)
-    return lax.psum_scatter(pair, "frames", scatter_dimension=0)
-
-
-def row_sums(sums):
-    row = lax.axis_index("batch") >> 1
-    got = lax.ppermute(pick(sums, 1 - row, 0), "batch", [(0, 2), (1, 3), (2, 0), (3, 1)])
-    return pick(sums, row, 0).astype(F32) + got.astype(F32)
+def to_all(array):
+    return lax.all_to_all(array, "chan", 0, 0, tiled=True)
+
+
+def over_z(array):
+    groups = [[0, 2, 4, 6], [1, 3, 5, 7]]
+    return lax.all_gather(array, "chan", axis_index_groups=groups, tiled=True)
 
 
 def shards(tokens, cotangent, norm_gain, norm_bias, qkv_weight, out_weight, lengths, segments):
@@ -499,12 +382,8 @@
     scalar = lambda value: value.reshape(1).astype(jnp.int32)
 
     weight = qkv_weight.transpose(1, 2, 0).reshape(3 * width, model)
-    over_z = lambda array: lax.all_gather(
-        array, "chan", axis_index_groups=[[0, 2, 4, 6], [1, 3, 5, 7]], tiled=True
-    )
     near_out = over_z(out_weight)
     peer_out = to_peer(out_weight, (0, 1))
-    peer_weight = to_peer(weight, (0, 1))
 
     flat_tokens = tokens.reshape(rows, model)
     flat_cot = cotangent.reshape(rows, model)
@@ -525,55 +404,34 @@
     far_out = over_z(peer_out)
     before = lax.ppermute(kv_last, "frames", up)
     after = lax.ppermute(kv_first, "frames", down)
-    mixed, dq, dkv, dbefore, dafter, peer_grads, peer_before, peer_after = attention(
+    mixed, dq, dkv, dbefore, dafter = attention(
         q, kv, before, after, g, seg_keys, seg_rows, live
     )
-    dbefore, dafter, peer_grads, peer_before, peer_after, peer_weight = tie(
-        (dbefore, dafter, peer_grads, peer_before, peer_after, peer_weight)
-    )
-    cross = lambda pairs: [(a * 8 + c, b * 8 + (c ^ 1)) for a, b in pairs for c in range(8)]
-    both = ("frames", "chan")
-    peer_grads = to_peer(peer_grads, (0, 1))
-    peer_right = lax.ppermute(peer_before, both, cross(down))
-    peer_left = lax.ppermute(peer_after, both, cross(up))
     from_right = lax.ppermute(dbefore, "frames", down)
     from_left = lax.ppermute(dafter, "frames", up)
-
-    late_mixed, from_left, from_right, peer_left, peer_right = tie(
-        (mixed, from_left, from_right, peer_left, peer_right)
+    near_mixed = over_z(mixed)
+    peer_mixed = to_peer(mixed, (0, 1))
+    from_left, from_right, peer_mixed, near_out, far_out = tie(
+        (from_left, from_right, peer_mixed, near_out, far_out)
     )
-    near = [to_peer(late_mixed, (dz, 0)) for dz in SPREAD[1:]]
+    far_mixed = over_z(peer_mixed)
+
+    back = back_rows(dq, dkv, from_left, from_right, weight)
+    parts = to_all(back.reshape(lax.axis_size("chan"), -1, model))
+
     core = scalar(lax.axis_index("batch") & 1)
     sent, kept = weight_grads(core, normed, flat_cot, dq, dkv, from_left, from_right, mixed)
-    near_mixed = stack([mixed] + near)
-    sent, near_mixed, peer_grads, near_out, far_out = tie(
-        (sent, near_mixed, peer_grads, near_out, far_out)
+    pair = lax.ppermute(sent, "batch", [(0, 1), (1, 0), (2, 3), (3, 2)])
+    pair = (kept + pair.astype(F32)).astype(BF16)
+    pair, near_mixed, parts = tie((pair, near_mixed, parts))
+    sums = lax.psum_scatter(pair, "frames", scatter_dimension=0)
+    sums = lax.psum_scatter(
+        sums, "batch", scatter_dimension=0, axis_index_groups=[[0, 2], [1, 3]]
     )
-
-    mine, *parts = back_parts(
-        scalar(me),
-        dq,
-        dkv,
-        from_left,
-        from_right,
-        peer_grads,
-        peer_left,
-        peer_right,
-        weight,
-        peer_weight,
-    )
-    got = [to_peer(part, (dz, 0)) for part, dz in zip(parts, SPREAD[1:])]
-    pair = lax.ppermute(sent, "batch", [(0, 1), (1, 0), (2, 3), (3, 2)])
-    pair, got = tie((pair, got))
-    sums = pair_sums(pair, kept)
-    far_mixed = to_peer(near_mixed, (0, 1))
-
-    here = piece_index(me, (0, 0))
-    piece = finish(scalar(here), flat_tokens, flat_cot, norm_gain, mine, got)
-
-    places = jnp.stack([here] + [piece_index(me, shift) for shift in SHIFTS]).astype(jnp.int32)
-    grad_tokens = stack([piece] + [to_peer(piece, shift) for shift in SHIFTS], places)
-    grad_proj = row_sums(sums).reshape(-1, 4, width)
+    grad_proj = sums.astype(F32).reshape(-1, 4, width)
+
+    pieces = finish(scalar(me), flat_tokens, flat_cot, norm_gain, parts)
+    grad_tokens = to_all(pieces)
     output = output_rows(flat_tokens, near_mixed, far_mixed, near_out, far_out)
     shape = (recs, frames, model)
     return (output.reshape(shape), grad_tokens.reshape(shape), grad_proj)

time: 375 us -> 234 us (0.62)
  Pallas kernels: 206 us -> 60.9 us
  waiting for transfers between devices: 88.7 us -> 121 us
  starting transfers between devices: 49.6 us -> 24.6 us
    pallas_call x3 -> x1, Pallas kernels: 154 us -> 8 us  [back_rows(): pl.pallas_call(back_body, grid=(model // tile,), in_specs=[full(width, ro...]
    all_gather x2 -> x4, waiting for transfers between devices: 0.04 us -> 75.6 us  [over_z(): return lax.all_gather(array, 'chan', axis_index_groups=groups, tiled=True)]
    ppermute x17 -> x2, waiting for transfers between devices: 66.2 us -> 7.98 us  [to_peer(): return lax.ppermute(array, 'chan', pairs)]
    ppermute x17 -> x2, starting transfers between devices: 26.8 us -> 0.83 us  [to_peer(): return lax.ppermute(array, 'chan', pairs)]
    all_to_all x0 -> x2, starting transfers between devices: none -> 11.7 us  [to_all(): return lax.all_to_all(array, 'chan', 0, 0, tiled=True)]
    ppermute x3 -> x0, starting transfers between devices: 10.2 us -> none  [the longest x1 5.1 us: shards(): peer_right = lax.ppermute(peer_before, both, cross(down))]
    reduce_scatter x1 -> x2, waiting for transfers between devices: 11.2 us -> 17.8 us  [the longest x1 11.8 us: shards(): sums = lax.psum_scatter(pair, 'frames', scatter_dimension=0)]
    ppermute x3 -> x0, waiting for transfers between devices: 5.53 us -> none  [the longest x1 3.34 us: shards(): peer_left = lax.ppermute(peer_after, both, cross(up))]
  transfers between devices with their start and end apart: 28 -> 15, of which waited for: 16 -> 12; matrix products, arithmetic and copies ran while one was open for 1% -> 2% of each run, Pallas kernels for 56% -> 23%
where the time goes in v4:
time: 234 us; the launch traced here: 232 us
  waiting for transfers between devices  121 us (52%)
  Pallas kernels  60.9 us (26%)
  starting transfers between devices  24.6 us (11%)
  between operations  14.2 us (6%)
  local copies, waits for them, and re-layouts  8.22 us (4%)
  other arithmetic  3.29 us (1%)
    all_gather x4, waiting for transfers between devices, over_z(): return lax.all_gather(array, 'chan', axis_index_groups=groups, tiled=True)  75.6 us
    pallas_call x1, Pallas kernels, attention(): pl.pallas_call(attention_body, grid=(recs,), in_specs=[by_rec(width, fram...  18.2 us
    reduce_scatter x1, waiting for transfers between devices, shards(): sums = lax.psum_scatter(pair, 'frames', scatter_dimension=0)  11.8 us
    all_to_all x2, starting transfers between devices, to_all(): return lax.all_to_all(array, 'chan', 0, 0, tiled=True)  11.7 us
    pallas_call x1, Pallas kernels, project(): pl.pallas_call(project_body, grid=(rows // CTX,), in_specs=[pl.BlockSpec(...  10.6 us
    pallas_call x1, Pallas kernels, output_rows(): pl.pallas_call(output_body, grid=(rows // CTX,), in_specs=[by_row, by_col...  9.87 us
    pallas_call x1, Pallas kernels, weight_grads(): pl.pallas_call(lambda c, *refs: weight_grads_body(*refs), grid_spec=pltpu...  9.32 us
    pallas_call x1, Pallas kernels, back_rows(): pl.pallas_call(back_body, grid=(model // tile,), in_specs=[full(width, ro...  8 us
  transfers between devices with their start and end apart: 15, of which 12 were waited for; matrix products, arithmetic and copies ran while one was open for 2% of the time, Pallas kernels for 23%

profile of v4, /device:TPU:18, one launch (start us, length us, event | category | flops | bytes accessed | tf_op | source)
XLA Modules:
  0.0 232.5 jit_solution(3976268188681873070)
XLA Ops:
  8.4 10.6 %project.1 = (bf16[1024,1536]{1,0:T(8,128)(2,1)}, bf16[192,1024]{1,0:T(8,128)(2,1)}, bf16[384,1024]{1,0:T(8,128)(2,1)}, bf16[192,1024]{1,0:T(8,128)(2,1)}, bf16[...) custom-call(s32[2]{0:T(128)} %lengths.1, bf16[1024,1536]{1,0:T(8,128)(2,1)} %bitcast.13, ...), custom_call_target="tpu_custom_call" | custom-call | flops 2400000000 | bytes 15000000 | tf_op jit(solution)/shard_map/project/pallas_call | solution.py:75
  19.0 5.8 %collective-permute-done = bf16[192,1536]{1,0:T(8,128)(2,1)S(1)} collective-permute-done((bf16[192,1536]{1,0:T(8,128)(2,1)}, bf16[192,1536]{1,0:T(8,128)(2,1)S(1)}, u32[]{:S(2)}, u32[]{:S(2)}) %collective-permute-start) | collective-permute-done | bytes 589856 | tf_op jit(solution)/shard_map/ppermute | solution.py:364
  24.8 0.8 copy-done.3
  25.7 3.4 %collective-permute-start.1 = (bf16[384,512]{1,0:T(8,128)(2,1)}, bf16[384,512]{1,0:T(8,128)(2,1)S(1)}, u32[]{:S(2)}, u32[]{:S(2)}) collective-permute-start(bf16[384,512]{1,0:T(8,128)(2,1)} %get-tuple-element.33), channel_id=1, source_target_pairs={{0,8},{8,16},{16,24},{1,9},{9,17},{17,25},{2,10},{10,18},{18,26},{... | collective-permute-start | bytes 1179656 | tf_op jit(solution)/shard_map/ppermute | solution.py:405
  29.1 2.5 %collective-permute-start.2 = (bf16[384,512]{1,0:T(8,128)(2,1)}, bf16[384,512]{1,0:T(8,128)(2,1)S(1)}, u32[]{:S(2)}, u32[]{:S(2)}) collective-permute-start(bf16[384,512]{1,0:T(8,128)(2,1)} %get-tuple-element.34), channel_id=1, source_target_pairs={{8,0},{16,8},{24,16},{9,1},{17,9},{25,17},{10,2},{18,10},{26,18},{... | collective-permute-start | bytes 1179656 | tf_op jit(solution)/shard_map/ppermute | solution.py:406
  31.7 1.3 copy.11.seg_keys
  33.6 4.2 %collective-permute-done.1.before = bf16[384,512]{1,0:T(8,128)(2,1)S(1)} collective-permute-done((bf16[384,512]{1,0:T(8,128)(2,1)}, bf16[384,512]{1,0:T(8,128)(2,1)S(1)}, u32[]{:S(2)}, u32[]{:S(2)}) %collective-permute-start.1) | collective-permute-done | bytes 393248 | tf_op jit(solution)/shard_map/ppermute | solution.py:405
  37.8 3.1 %collective-permute-done.2.after = bf16[384,512]{1,0:T(8,128)(2,1)S(1)} collective-permute-done((bf16[384,512]{1,0:T(8,128)(2,1)}, bf16[384,512]{1,0:T(8,128)(2,1)S(1)}, u32[]{:S(2)}, u32[]{:S(2)}) %collective-permute-start.2) | collective-permute-done | bytes 393248 | tf_op jit(solution)/shard_map/ppermute | solution.py:406
  40.9 0.7 copy-done.8
  41.6 18.2 %attention.1 = (bf16[192,1024]{1,0:T(8,128)(2,1)}, bf16[192,1024]{1,0:T(8,128)(2,1)}, f32[384,1024]{1,0:T(8,128)}, bf16[384,512]{1,0:T(8,128)(2,1)}, bf16[384,512]{1,0:T(8,128)(2,1)}) custom-call(bf16[192,1024]{1,0:T(8,128)(2,1)} %get-tuple-element.29.q, bf16[384,1024]{1,0:T(8,128)(2,1)} %get-tuple-element.30.kv, bf16[384,512]{1,0:T(8,128)(2,1)} %copy-done.7, ...), custom_call_target="tpu_custom_call" | custom-call | flops 2400000000 | bytes 8000000 | tf_op jit(solution)/shard_map/attention/pallas_call | solution.py:159
  59.9 3.1 %collective-permute-start.3 = (bf16[384,512]{1,0:T(8,128)(2,1)}, bf16[384,512]{1,0:T(8,128)(2,1)S(1)}, u32[]{:S(2)}, u32[]{:S(2)}) collective-permute-start(bf16[384,512]{1,0:T(8,128)(2,1)} %get-tuple-element.39), channel_id=1, source_target_pairs={{0,8},{8,16},{16,24},{1,9},{9,17},{17,25},{2,10},{10,18},{18,26},{... | collective-permute-start | bytes 1179656 | tf_op jit(solution)/shard_map/ppermute | solution.py:411
  63.0 2.8 %collective-permute-start.4 = (bf16[384,512]{1,0:T(8,128)(2,1)}, bf16[384,512]{1,0:T(8,128)(2,1)S(1)}, u32[]{:S(2)}, u32[]{:S(2)}) collective-permute-start(bf16[384,512]{1,0:T(8,128)(2,1)} %get-tuple-element.40), channel_id=1, source_target_pairs={{8,0},{16,8},{24,16},{9,1},{17,9},{25,17},{10,2},{18,10},{26,18},{... | collective-permute-start | bytes 1179656 | tf_op jit(solution)/shard_map/ppermute | solution.py:410
  66.2 4.7 %collective-permute-done.3.refs_4_.left = bf16[384,512]{1,0:T(8,128)(2,1)S(1)} collective-permute-done((bf16[384,512]{1,0:T(8,128)(2,1)}, bf16[384,512]{1,0:T(8,128)(2,1)S(1)}, u32[]{:S(2)}, u32[]{:S(2)}) %collective-permute-start.3) | collective-permute-done | bytes 393248 | tf_op jit(solution)/shard_map/ppermute | solution.py:411
  70.9 2.8 %collective-permute-done.4.refs_5_.right = bf16[384,512]{1,0:T(8,128)(2,1)S(1)} collective-permute-done((bf16[384,512]{1,0:T(8,128)(2,1)}, bf16[384,512]{1,0:T(8,128)(2,1)S(1)}, u32[]{:S(2)}, u32[]{:S(2)}) %collective-permute-start.4) | collective-permute-done | bytes 393248 | tf_op jit(solution)/shard_map/ppermute | solution.py:410
  73.7 2.2 collective-permute-done.5
  75.9 4.1 %all-gather.7.cloned.1.call-done.far_weight = bf16[768,1536]{1,0:T(8,128)(2,1)} async-done(((bf16[192,1536]{1,0:T(8,128)(2,1)}), bf16[768,1536]{1,0:T(8,128)(2,1)}) %all-gather.7.cloned.1.call-update) | async-done | bytes 2359312 | tf_op jit(solution)/shard_map/all_gather | solution.py:373
  80.0 8.0 %back.1 = bf16[1024,1536]{1,0:T(8,128)(2,1)} custom-call(bf16[192,1024]{1,0:T(8,128)(2,1)} %get-tuple-element.37.refs_2_.dq, f32[384,1024]{1,0:T(8,128)} %get-tuple-element.38.refs_3_.own, bf16[384,512]{1,0:T(8,128)(2,1)} %copy-done.1, bf16[384,512]{1,0:T(8,128)(2,1)} %copy-done.2, bf16[576,1536]{1,0:T(8,128)(2,1)} %bitcast.23), custom_call_target="tpu_custom_call" | custom-call | flops 1800000000 | bytes 8000000 | tf_op jit(solution)/shard_map/back/pallas_call | solution.py:215
  88.0 6.0 %all-to-all-start = ((bf16[8,128,1536]{2,1,0:T(8,128)(2,1)}), bf16[8,128,1536]{2,1,0:T(8,128)(2,1)S(1)}, u32[]{:S(2)}, u32[]{:S(2)}) async-start(bf16[8,128,1536]{2,1,0:T(8,128)(2,1)} %bitcast.17), calls=%async_computation | async-start | bytes 6291456 | tf_op jit(solution)/shard_map/all_to_all | solution.py:368
  94.0 0.7 all-gather.9.cloned.1.call-update
  94.9 9.3 %weight_grads.1 = (bf16[4,2,96,768]{3,2,1,0:T(8,128)(2,1)}, f32[4,2,96,768]{3,2,1,0:T(8,128)}) custom-call(s32[1]{0:T(128)} %bitcast.1.c, bf16[1024,1536]{1,0:T(8,128)(2,1)} %get-tuple-element.28.refs_0_, bf16[1024,1536]{1,0:T(8,128)(2,1)} %bitcast.19, bf16[192,1024]{1,0:T(8,128)(2,1)} %get-tuple-element.37.refs_2_.dq, ...), custom_call_target="tpu_custom_call" | custom-call | flops 1000 | bytes 1000 | tf_op jit(solution)/shard_map/weight_grads/pallas_call | solution.py:277
  104.3 3.1 %collective-permute-done.6 = bf16[4,2,96,768]{3,2,1,0:T(8,128)(2,1)S(1)} collective-permute-done((bf16[4,2,96,768]{3,2,1,0:T(8,128)(2,1)}, bf16[4,2,96,768]{3,2,1,0:T(8,128)(2,1)S(1)}, u32[]{:S(2)}, u32[]{:S(2)}) %collective-permute-start.6) | collective-permute-done | bytes 1179680 | tf_op jit(solution)/shard_map/ppermute | solution.py:424
  107.3 3.2 %add_convert_fusion = bf16[4,2,96,768]{3,2,1,0:T(8,128)(2,1)} fusion(f32[4,2,96,768]{3,2,1,0:T(8,128)} %get-tuple-element.45, bf16[4,2,96,768]{3,2,1,0:T(8,128)(2,1)S(1)} %collective-permute-done.6), kind=kLoop, calls=%fused_computation | loop fusion | flops 1769472 | bytes 4718592 | tf_op jit(solution)/shard_map/convert_element_type | solution.py:425
  110.5 33.2 %all-gather.9.cloned.1.call-done.near = bf16[768,1024]{1,0:T(8,128)(2,1)} async-done(((bf16[192,1024]{1,0:T(8,128)(2,1)}), bf16[768,1024]{1,0:T(8,128)(2,1)}) %all-gather.9.cloned.1.call-update) | async-done | bytes 1572880 | tf_op jit(solution)/shard_map/all_gather | solution.py:373
  144.4 1.0 copy-done
  145.4 4.8 %finish.1 = bf16[8,128,1536]{2,1,0:T(8,128)(2,1)} custom-call(s32[1]{0:T(128)} %bitcast.9.place, bf16[1024,1536]{1,0:T(8,128)(2,1)} %bitcast.14, bf16[1024,1536]{1,0:T(8,128)(2,1)} %bitcast.20, f32[1536]{0:T(1024)} %gain.3, bf16[8,128,1536]{2,1,0:T(8,128)(2,1)} %copy-done), custom_call_target="tpu_custom_call" | custom-call | flops 10000000 | bytes 5000000 | tf_op jit(solution)/shard_map/finish/pallas_call | solution.py:344
  150.2 5.7 %all-to-all-start.1 = ((bf16[8,128,1536]{2,1,0:T(8,128)(2,1)}), bf16[8,128,1536]{2,1,0:T(8,128)(2,1)S(1)}, u32[]{:S(2)}, u32[]{:S(2)}) async-start(bf16[8,128,1536]{2,1,0:T(8,128)(2,1)} %finish.1), calls=%async_computation.1 | async-start | bytes 6291456 | tf_op jit(solution)/shard_map/all_to_all | solution.py:368
  155.9 11.8 %reduce-scatter.3.cloned.1.call-done = bf16[1,2,96,768]{3,2,1,0:T(8,128)(2,1)} async-done(((bf16[4,2,96,768]{3,2,1,0:T(8,128)(2,1)}), bf16[1,2,96,768]{3,2,1,0:T(8,128)(2,1)}) %reduce-scatter.3.cloned.1.call-update) | async-done | bytes 294928 | tf_op jit(solution)/shard_map/reduce_scatter | solution.py:427
  167.7 38.3 %all-gather.11.cloned.1.call-done.far = bf16[768,1024]{1,0:T(8,128)(2,1)} async-done(((bf16[192,1024]{1,0:T(8,128)(2,1)}), bf16[768,1024]{1,0:T(8,128)(2,1)}) %all-gather.11.cloned.1.call-update) | async-done | bytes 1572880 | tf_op jit(solution)/shard_map/all_gather | solution.py:373
  206.0 9.9 %output.1 = bf16[1024,1536]{1,0:T(8,128)(2,1)} custom-call(bf16[1024,1536]{1,0:T(8,128)(2,1)} %bitcast.15, bf16[768,1024]{1,0:T(8,128)(2,1)} %all-gather.9.cloned.1.call-done.near, bf16[768,1024]{1,0:T(8,128)(2,1)} %all-gather.11.cloned.1.call-done.far, bf16[768,1536]{1,0:T(8,128)(2,1)} %all-gather.5.cloned.1.call-done.near_weight, ...), custom_call_target="tpu_custom_call" | custom-call | flops 1000 | bytes 1000 | tf_op jit(solution)/shard_map/output/pallas_call | solution.py:318
  215.9 6.1 %reduce-scatter.5.cloned.1.call-done = bf16[1,96,768]{2,1,0:T(8,128)(2,1)} async-done(((bf16[2,96,768]{2,1,0:T(8,128)(2,1)}), bf16[1,96,768]{2,1,0:T(8,128)(2,1)}) %reduce-scatter.5.cloned.1.call-update) | async-done | bytes 147472 | tf_op jit(solution)/shard_map/reduce_scatter | solution.py:428
  222.0 2.0 reshape.47
  223.9 1.7 copy.13
  (36 shorter events, 3.1 us)
Async XLA Ops:
  7.2 68.7 %all-gather.5.cloned.1.call-start = ((), (), s32[]{:S(2)}) async-start(), calls=%async_computation.4 | async-start | bytes 2949120 | tf_op jit(solution)/shard_map/all_gather | solution.py:373
  7.9 72.1 %all-gather.7.cloned.1.call-start = ((), (), s32[]{:S(2)}) async-start(), calls=%async_computation.5 | async-start | bytes 2949120 | tf_op jit(solution)/shard_map/all_gather | solution.py:373
  7.9 16.9 %collective-permute-start = (bf16[192,1536]{1,0:T(8,128)(2,1)}, bf16[192,1536]{1,0:T(8,128)(2,1)S(1)}, u32[]{:S(2)}, u32[]{:S(2)}) collective-permute-start(bf16[192,1536]{1,0:T(8,128)(2,1)} %out_w.1), channel_id=1, source_target_pairs={{0,1},{1,0},{2,3},{3,2},{4,5},{5,4},{6,7},{7,6},{8,9},{9,8},{10,11... | collective-permute-start | bytes 1769480 | tf_op jit(solution)/shard_map/ppermute | solution.py:364
  8.4 23.2 %copy-start.5 = (s32[2,2048]{1,0:T(2,128)S(1)}, s32[2,2048]{1,0:T(2,128)}, u32[]{:S(2)}) copy-start(s32[2,2048]{1,0:T(2,128)} %param.15) | copy-start | bytes 49156
  8.4 23.2 %copy-start.6 = (s32[2]{0:T(128)S(1)}, s32[2]{0:T(128)}, u32[]{:S(2)}) copy-start(s32[2]{0:T(128)} %lengths.1) | copy-start | bytes 28
  24.8 0.8 copy-start.3
  25.7 12.1 %collective-permute-start.1 = (bf16[384,512]{1,0:T(8,128)(2,1)}, bf16[384,512]{1,0:T(8,128)(2,1)S(1)}, u32[]{:S(2)}, u32[]{:S(2)}) collective-permute-start(bf16[384,512]{1,0:T(8,128)(2,1)} %get-tuple-element.33), channel_id=1, source_target_pairs={{0,8},{8,16},{16,24},{1,9},{9,17},{17,25},{2,10},{10,18},{18,26},{... | collective-permute-start | bytes 1179656 | tf_op jit(solution)/shard_map/ppermute | solution.py:405
  29.1 11.8 %collective-permute-start.2 = (bf16[384,512]{1,0:T(8,128)(2,1)}, bf16[384,512]{1,0:T(8,128)(2,1)S(1)}, u32[]{:S(2)}, u32[]{:S(2)}) collective-permute-start(bf16[384,512]{1,0:T(8,128)(2,1)} %get-tuple-element.34), channel_id=1, source_target_pairs={{8,0},{16,8},{24,16},{9,1},{17,9},{25,17},{10,2},{18,10},{26,18},{... | collective-permute-start | bytes 1179656 | tf_op jit(solution)/shard_map/ppermute | solution.py:406
  37.8 3.1 %copy-start.7 = (bf16[384,512]{1,0:T(8,128)(2,1)}, bf16[384,512]{1,0:T(8,128)(2,1)S(1)}, u32[]{:S(2)}) copy-start(bf16[384,512]{1,0:T(8,128)(2,1)S(1)} %collective-permute-done.1.before) | copy-start | bytes 1179652
  40.9 0.7 copy-start.8
  59.9 11.0 %collective-permute-start.3 = (bf16[384,512]{1,0:T(8,128)(2,1)}, bf16[384,512]{1,0:T(8,128)(2,1)S(1)}, u32[]{:S(2)}, u32[]{:S(2)}) collective-permute-start(bf16[384,512]{1,0:T(8,128)(2,1)} %get-tuple-element.39), channel_id=1, source_target_pairs={{0,8},{8,16},{16,24},{1,9},{9,17},{17,25},{2,10},{10,18},{18,26},{... | collective-permute-start | bytes 1179656 | tf_op jit(solution)/shard_map/ppermute | solution.py:411
  63.0 10.7 %collective-permute-start.4 = (bf16[384,512]{1,0:T(8,128)(2,1)}, bf16[384,512]{1,0:T(8,128)(2,1)S(1)}, u32[]{:S(2)}, u32[]{:S(2)}) collective-permute-start(bf16[384,512]{1,0:T(8,128)(2,1)} %get-tuple-element.40), channel_id=1, source_target_pairs={{8,0},{16,8},{24,16},{9,1},{17,9},{25,17},{10,2},{18,10},{26,18},{... | collective-permute-start | bytes 1179656 | tf_op jit(solution)/shard_map/ppermute | solution.py:410
  65.7 10.1 %collective-permute-start.5 = (bf16[192,1024]{1,0:T(8,128)(2,1)}, bf16[192,1024]{1,0:T(8,128)(2,1)S(1)}, u32[]{:S(2)}, u32[]{:S(2)}) collective-permute-start(bf16[192,1024]{1,0:T(8,128)(2,1)} %get-tuple-element.41.refs_6_), channel_id=1, source_target_pairs={{0,1},{1,0},{2,3},{3,2},{4,5},{5,4},{6,7},{7,6},{8,9},{9,8},{10,11... | collective-permute-start | bytes 1179656 | tf_op jit(solution)/shard_map/ppermute | solution.py:364
  70.9 9.1 %copy-start.1 = (bf16[384,512]{1,0:T(8,128)(2,1)}, bf16[384,512]{1,0:T(8,128)(2,1)S(1)}, u32[]{:S(2)}) copy-start(bf16[384,512]{1,0:T(8,128)(2,1)S(1)} %collective-permute-done.3.refs_4_.left) | copy-start | bytes 1179652
  73.7 6.3 %copy-start.2 = (bf16[384,512]{1,0:T(8,128)(2,1)}, bf16[384,512]{1,0:T(8,128)(2,1)S(1)}, u32[]{:S(2)}) copy-start(bf16[384,512]{1,0:T(8,128)(2,1)S(1)} %collective-permute-done.4.refs_5_.right) | copy-start | bytes 1179652
  75.9 12.1 %copy-start.4 = (bf16[192,1024]{1,0:T(8,128)(2,1)}, bf16[192,1024]{1,0:T(8,128)(2,1)S(1)}, u32[]{:S(2)}) copy-start(bf16[192,1024]{1,0:T(8,128)(2,1)S(1)} %collective-permute-done.5) | copy-start | bytes 1179652
  88.0 55.8 %all-to-all-start = ((bf16[8,128,1536]{2,1,0:T(8,128)(2,1)}), bf16[8,128,1536]{2,1,0:T(8,128)(2,1)S(1)}, u32[]{:S(2)}, u32[]{:S(2)}) async-start(bf16[8,128,1536]{2,1,0:T(8,128)(2,1)} %bitcast.17), calls=%async_computation | async-start | bytes 6291456 | tf_op jit(solution)/shard_map/all_to_all | solution.py:368
  94.0 49.7 %all-gather.9.cloned.1.call-start = ((), (), s32[]{:S(2)}) async-start(), calls=%async_computation.6 | async-start | bytes 1966080 | tf_op jit(solution)/shard_map/all_gather | solution.py:373
  94.7 73.0 %reduce-scatter.3.cloned.1.call-start = ((), (), s32[]{:S(2)}) async-start(), calls=%async_computation.8 | async-start | bytes 1474560 | tf_op jit(solution)/shard_map/reduce_scatter | solution.py:427
  104.3 3.1 %collective-permute-start.6 = (bf16[4,2,96,768]{3,2,1,0:T(8,128)(2,1)}, bf16[4,2,96,768]{3,2,1,0:T(8,128)(2,1)S(1)}, u32[]{:S(2)}, u32[]{:S(2)}) collective-permute-start(bf16[4,2,96,768]{3,2,1,0:T(8,128)(2,1)} %get-tuple-element.46), channel_id=1, source_target_pairs={{0,32},{32,0},{64,96},{96,64},{1,33},{33,1},{65,97},{97,65},{2,34}... | collective-permute-start | bytes 3538952 | tf_op jit(solution)/shard_map/ppermute | solution.py:424
  143.7 1.7 copy-start
  143.8 62.3 %all-gather.11.cloned.1.call-start = ((), (), s32[]{:S(2)}) async-start(), calls=%async_computation.7 | async-start | bytes 1966080 | tf_op jit(solution)/shard_map/all_gather | solution.py:373
  150.2 65.7 %all-to-all-start.1 = ((bf16[8,128,1536]{2,1,0:T(8,128)(2,1)}), bf16[8,128,1536]{2,1,0:T(8,128)(2,1)S(1)}, u32[]{:S(2)}, u32[]{:S(2)}) async-start(bf16[8,128,1536]{2,1,0:T(8,128)(2,1)} %finish.1), calls=%async_computation.1 | async-start | bytes 6291456 | tf_op jit(solution)/shard_map/all_to_all | solution.py:368
  155.9 66.1 %reduce-scatter.5.cloned.1.call-start = ((), (), s32[]{:S(2)}) async-start(), calls=%async_computation.9 | async-start | bytes 442368 | tf_op jit(solution)/shard_map/reduce_scatter | solution.py:428
Sparse Core Ops, SparseCore 0:
  9.7 35.4 all-gather.4
  46.8 33.1 all-gather.6
  96.5 47.2 all-gather.8
  146.0 21.6 reduce-scatter.2
  169.8 36.2 all-gather.10
  208.2 13.7 reduce-scatter.4

commit v5 on v4

--- a/solution.py
+++ b/solution.py
@@ -151,57 +151,58 @@
     dafter[...] = acc[:, CTX + frames :].astype(BF16)
 
 
-def attention(q, kv, before, after, g, seg_keys, seg_rows, live):
+def attention(rec, q, kv, before, after, g, seg_keys, seg_rows, live):
     width, rows = q.shape
     recs, span, _ = seg_keys.shape
     frames = rows // recs
-    by_rec = lambda n, m: pl.BlockSpec((n, m), lambda r: (0, r))
+    by_rec = lambda n, m: pl.BlockSpec((n, m), lambda i: (0, rec))
+    whole = lambda n, m: pl.BlockSpec((n, m), lambda i: (0, 0))
     return pl.pallas_call(
         attention_body,
-        grid=(recs,),
+        grid=(1,),
         in_specs=[
             by_rec(width, frames),
             by_rec(2 * width, frames),
             by_rec(2 * width, CTX),
             by_rec(2 * width, CTX),
             by_rec(width, frames),
-            pl.BlockSpec((1, span, 1), lambda r: (r, 0, 0)),
-            pl.BlockSpec((1, 1, frames), lambda r: (r, 0, 0)),
+            pl.BlockSpec((1, span, 1), lambda i: (rec, 0, 0)),
+            pl.BlockSpec((1, 1, frames), lambda i: (rec, 0, 0)),
             by_rec(1, frames),
         ],
         out_specs=[
-            by_rec(width, frames),
-            by_rec(width, frames),
-            by_rec(2 * width, frames),
-            by_rec(2 * width, CTX),
-            by_rec(2 * width, CTX),
+            whole(width, frames),
+            whole(width, frames),
+            whole(2 * width, frames),
+            whole(2 * width, CTX),
+            whole(2 * width, CTX),
         ],
         out_shape=[
-            jax.ShapeDtypeStruct((width, rows), BF16),
-            jax.ShapeDtypeStruct((width, rows), BF16),
-            jax.ShapeDtypeStruct((2 * width, rows), F32),
-            jax.ShapeDtypeStruct((2 * width, recs * CTX), BF16),
-            jax.ShapeDtypeStruct((2 * width, recs * CTX), BF16),
+            jax.ShapeDtypeStruct((width, frames), BF16),
+            jax.ShapeDtypeStruct((width, frames), BF16),
+            jax.ShapeDtypeStruct((2 * width, frames), F32),
+            jax.ShapeDtypeStruct((2 * width, CTX), BF16),
+            jax.ShapeDtypeStruct((2 * width, CTX), BF16),
         ],
         scratch_shapes=[pltpu.VMEM((2 * width, span), F32), pltpu.VMEM((3 * CTX, CTX), F32)],
         compiler_params=params(),
-        cost_estimate=pl.CostEstimate(flops=2400000000, bytes_accessed=8000000, transcendentals=0),
+        cost_estimate=pl.CostEstimate(flops=1000, bytes_accessed=1000, transcendentals=0),
         name="attention",
     )(q, kv, before, after, g, seg_keys, seg_rows, live)
 
 
+def kv_grads(own, left, right):
+    beside = jnp.concatenate([left[...], right[...]], axis=1).astype(F32)
+    return (own[...] + beside).astype(BF16)
+
+
 def back_body(dq, own, left, right, weight, out, flipped):
     width = dq.shape[0]
 
     @pl.when(pl.program_id(0) == 0)
     def _():
-        beside = []
-        for rec in range(own.shape[1] // (2 * CTX)):
-            cols = slice(rec * CTX, (rec + 1) * CTX)
-            beside += [left[:, cols], right[:, cols]]
-        beside = jnp.concatenate(beside, axis=1).astype(F32)
         flipped[:, :width] = dq[...].T
-        flipped[:, width:] = (own[...] + beside).astype(BF16).T
+        flipped[:, width:] = kv_grads(own, left, right).T
 
     out[...] = dot_nn(flipped[...], weight[...]).astype(BF16)
 
@@ -209,7 +210,7 @@
 def back_rows(dq, own, left, right, weight):
     width, rows = dq.shape
     model = weight.shape[1]
-    tile = 256
+    tile = 512
     full = lambda n, m: pl.BlockSpec((n, m), lambda i: (0, 0))
     by_col = lambda n: pl.BlockSpec((n, tile), lambda i: (0, i))
     return pl.pallas_call(
@@ -226,73 +227,73 @@
         out_shape=jax.ShapeDtypeStruct((rows, model), BF16),
         scratch_shapes=[pltpu.VMEM((rows, 3 * width), BF16)],
         compiler_params=params(),
-        cost_estimate=pl.CostEstimate(flops=1800000000, bytes_accessed=8000000, transcendentals=0),
+        cost_estimate=pl.CostEstimate(flops=900000000, bytes_accessed=4000000, transcendentals=0),
         name="back",
     )(dq, own, left, right, weight)
 
 
-def weight_grads_body(normed, cot, dq, own, left, right, mixed, sent, kept, gkv):
-    width = dq.shape[0]
+def weight_grads_body(core, normed, cot, *rest):
+    pieces, (sent, kept, kv, query, mixed) = rest[:-5], rest[-5:]
+    width, frames = pieces[0].shape
+    del core
 
     @pl.when(pl.program_id(0) == 0)
     def _():
-        beside = []
-        for rec in range(own.shape[1] // (2 * CTX)):
-            cols = slice(rec * CTX, (rec + 1) * CTX)
-            beside += [left[:, cols], right[:, cols]]
-        gkv[...] = (own[...] + jnp.concatenate(beside, axis=1).astype(F32)).astype(BF16)
+        for rec in range(2):
+            dq, own, left, right, out = pieces[5 * rec : 5 * rec + 5]
+            cols = slice(rec * frames, (rec + 1) * frames)
+            kv[:, cols] = kv_grads(own, left, right)
+            query[:, cols] = dq[...]
+            mixed[:, cols] = out[...]
 
     turned = normed[...].T
     sums = [
-        dot_nt(turned, dq[...]),
-        dot_nt(turned, gkv[...]),
+        dot_nt(turned, query[...]),
+        dot_nt(turned, kv[...]),
         dot_nt(cot[...].T, mixed[...]),
     ]
     offsets = (0, width, 3 * width)
 
+    def write(target):
+        for part, offset in zip(sums, offsets):
+            shape = (target.shape[0], target.shape[2], part.shape[1])
+            cols = slice(offset, offset + part.shape[1])
+            target[:, 0, :, cols] = part.reshape(shape).astype(target.dtype)
+
     @pl.when(pl.program_id(0) < 2)
     def _():
-        for part, offset in zip(sums, offsets):
-            shape = (sent.shape[0], sent.shape[2], part.shape[1])
-            sent[:, 0, :, offset : offset + part.shape[1]] = part.astype(BF16).reshape(shape)
+        write(sent)
 
     @pl.when(pl.program_id(0) >= 2)
     def _():
-        for part, offset in zip(sums, offsets):
-            shape = (kept.shape[0], kept.shape[2], part.shape[1])
-            kept[:, 0, :, offset : offset + part.shape[1]] = part.reshape(shape)
-
-
-def weight_grads(core, normed, cotangent, dq, own, left, right, mixed):
+        write(kept)
+
+
+def weight_grads(core, normed, cotangent, pieces):
     rows, model = normed.shape
-    width = dq.shape[0]
+    width = pieces[0].shape[0]
     block = model // 4
 
     def by_step(i, c):
         return (0, (i % 2) * 2 + jnp.where(i < 2, 1 - c[0], c[0]))
 
-    full = lambda n: pl.BlockSpec((n, rows), lambda i, c: (0, 0))
-    half = pl.BlockSpec((2 * width, rows // 2), lambda i, c: (0, 0))
     part = (4, 1, block // 4, 4 * width)
     return pl.pallas_call(
-        lambda c, *refs: weight_grads_body(*refs),
+        weight_grads_body,
         grid_spec=pltpu.PrefetchScalarGridSpec(
             num_scalar_prefetch=1,
             grid=(4,),
-            in_specs=[
-                pl.BlockSpec((rows, block), by_step),
-                pl.BlockSpec((rows, block), by_step),
-                full(width),
-                full(2 * width),
-                half,
-                half,
-                full(width),
-            ],
+            in_specs=[pl.BlockSpec((rows, block), by_step)] * 2
+            + [pl.BlockSpec(piece.shape, lambda i, c: (0, 0)) for piece in pieces],
             out_specs=[
                 pl.BlockSpec(part, lambda i, c: (0, jnp.minimum(i, 1), 0, 0)),
                 pl.BlockSpec(part, lambda i, c: (0, jnp.maximum(i, 2) - 2, 0, 0)),
             ],
-            scratch_shapes=[pltpu.VMEM((2 * width, rows), BF16)],
+            scratch_shapes=[
+                pltpu.VMEM((2 * width, rows), BF16),
+                pltpu.VMEM((width, rows), BF16),
+                pltpu.VMEM((width, rows), BF16),
+            ],
         ),
         out_shape=[
             jax.ShapeDtypeStruct((4, 2, block // 4, 4 * width), BF16),
@@ -301,30 +302,37 @@
         compiler_params=params(),
         cost_estimate=pl.CostEstimate(flops=1000, bytes_accessed=1000, transcendentals=0),
         name="weight_grads",
-    )(core, normed, cotangent, dq, own, left, right, mixed)
-
-
-def output_body(tok, near, far, near_weight, far_weight, out):
-    total = dot_nn(near[...].T, near_weight[...]) + dot_nn(far[...].T, far_weight[...])
+    )(core, normed, cotangent, *pieces)
+
+
+def output_body(tok, near, far, weight, out, stacked):
+    side = lax.axis_index("chan") & 1
+    width = weight.shape[0] // 8
+    for z in range(4):
+        rows = slice(z * width, (z + 1) * width)
+        for offset, source in ((side, near), (1 - side, far)):
+            place = pl.multiple_of((2 * z + offset) * width, width)
+            stacked[pl.ds(place, width), :] = source[rows, :]
+    total = dot_nn(stacked[...].T, weight[...])
     out[...] = (tok[...].astype(F32) + total).astype(BF16)
 
 
-def output_rows(tokens, near, far, near_weight, far_weight):
+def output_rows(tokens, near, far, weight):
     rows, model = tokens.shape
     depth = near.shape[0]
     by_row = pl.BlockSpec((CTX, model), lambda i: (i, 0))
     by_col = pl.BlockSpec((depth, CTX), lambda i: (0, i))
-    full = pl.BlockSpec((depth, model), lambda i: (0, 0))
     return pl.pallas_call(
         output_body,
         grid=(rows // CTX,),
-        in_specs=[by_row, by_col, by_col, full, full],
+        in_specs=[by_row, by_col, by_col, pl.BlockSpec((2 * depth, model), lambda i: (0, 0))],
         out_specs=by_row,
         out_shape=jax.ShapeDtypeStruct((rows, model), BF16),
+        scratch_shapes=[pltpu.VMEM((2 * depth, CTX), BF16)],
         compiler_params=params(),
         cost_estimate=pl.CostEstimate(flops=1000, bytes_accessed=1000, transcendentals=0),
         name="output",
-    )(tokens, near, far, near_weight, far_weight)
+    )(tokens, near, far, weight)
 
 
 def finish_body(place, tok, cot, gain, parts, out):
@@ -368,6 +376,29 @@
     return lax.all_to_all(array, "chan", 0, 0, tiled=True)
 
 
+def pick(array, index, axis):
+    return lax.dynamic_index_in_dim(array, index, axis, keepdims=False)
+
+
+def frame_sums(sent, kept):
+    frame = lax.axis_index("frames")
+    got = lax.ppermute(sent, "batch", [(0, 1), (1, 0), (2, 3), (3, 2)])
+    pair = kept + got.astype(F32)
+    sums = pick(pair, frame, 0)
+    for shift in (1, 3, 2):
+        sent = pick(pair, (frame + shift) & 3, 0).astype(BF16)
+        got = lax.ppermute(sent, "frames", [(i, (i + shift) % 4) for i in range(4)])
+        sums = sums + got.astype(F32)
+    return sums
+
+
+def row_sums(sums):
+    row = lax.axis_index("batch") >> 1
+    sent = pick(sums, 1 - row, 0).astype(BF16)
+    got = lax.ppermute(sent, "batch", [(0, 2), (1, 3), (2, 0), (3, 1)])
+    return pick(sums, row, 0) + got.astype(F32)
+
+
 def over_z(array):
     groups = [[0, 2, 4, 6], [1, 3, 5, 7]]
     return lax.all_gather(array, "chan", axis_index_groups=groups, tiled=True)
@@ -382,8 +413,8 @@
     scalar = lambda value: value.reshape(1).astype(jnp.int32)
 
     weight = qkv_weight.transpose(1, 2, 0).reshape(3 * width, model)
-    near_out = over_z(out_weight)
-    peer_out = to_peer(out_weight, (0, 1))
+    tie = lax.optimization_barrier
+    full_out = lax.all_gather(out_weight, "chan", tiled=True)
 
     flat_tokens = tokens.reshape(rows, model)
     flat_cot = cotangent.reshape(rows, model)
@@ -399,40 +430,47 @@
     size = lax.axis_size("frames")
     up = [(i, i + 1) for i in range(size - 1)]
     down = [(i + 1, i) for i in range(size - 1)]
-    tie = lax.optimization_barrier
-    kv_first, kv_last, peer_out = tie((kv_first, kv_last, peer_out))
-    far_out = over_z(peer_out)
     before = lax.ppermute(kv_last, "frames", up)
     after = lax.ppermute(kv_first, "frames", down)
-    mixed, dq, dkv, dbefore, dafter = attention(
-        q, kv, before, after, g, seg_keys, seg_rows, live
-    )
-    from_right = lax.ppermute(dbefore, "frames", down)
-    from_left = lax.ppermute(dafter, "frames", up)
+
+    results = []
+    for rec in range(recs):
+        mixed, dq, dkv, dbefore, dafter = attention(
+            rec, q, kv, before, after, g, seg_keys, seg_rows, live
+        )
+        right = lax.ppermute(dbefore, "frames", down)
+        left = lax.ppermute(dafter, "frames", up)
+        results.append([dq, dkv, left, right, mixed])
+
+    mixed = jnp.concatenate([result[4] for result in results], axis=1)
     near_mixed = over_z(mixed)
     peer_mixed = to_peer(mixed, (0, 1))
-    from_left, from_right, peer_mixed, near_out, far_out = tie(
-        (from_left, from_right, peer_mixed, near_out, far_out)
-    )
+    first = results[0]
+    first[0], peer_mixed, _ = tie((first[0], peer_mixed, results[1][0]))
     far_mixed = over_z(peer_mixed)
 
-    back = back_rows(dq, dkv, from_left, from_right, weight)
-    parts = to_all(back.reshape(lax.axis_size("chan"), -1, model))
+    count = lax.axis_size("chan")
+    backs = [
+        back_rows(*result[:4], weight).reshape(count, -1, model) for result in results
+    ]
+    parts = [to_all(back) for back in backs]
+    parts[0], full_out = tie((parts[0], full_out))
+    results[1][0], _ = tie((results[1][0], backs[0]))
 
     core = scalar(lax.axis_index("batch") & 1)
-    sent, kept = weight_grads(core, normed, flat_cot, dq, dkv, from_left, from_right, mixed)
-    pair = lax.ppermute(sent, "batch", [(0, 1), (1, 0), (2, 3), (3, 2)])
-    pair = (kept + pair.astype(F32)).astype(BF16)
-    pair, near_mixed, parts = tie((pair, near_mixed, parts))
-    sums = lax.psum_scatter(pair, "frames", scatter_dimension=0)
-    sums = lax.psum_scatter(
-        sums, "batch", scatter_dimension=0, axis_index_groups=[[0, 2], [1, 3]]
-    )
-    grad_proj = sums.astype(F32).reshape(-1, 4, width)
-
-    pieces = finish(scalar(me), flat_tokens, flat_cot, norm_gain, parts)
-    grad_tokens = to_all(pieces)
-    output = output_rows(flat_tokens, near_mixed, far_mixed, near_out, far_out)
+    sent, kept = weight_grads(core, normed, flat_cot, results[0] + results[1])
+    sums = frame_sums(sent, kept)
+    sums, parts[1] = tie((sums, parts[1]))
+    grad_proj = row_sums(sums).reshape(-1, 4, width)
+
+    grad_tokens = []
+    for rec in range(recs):
+        pieces = finish(
+            scalar(rec * count + me), flat_tokens, flat_cot, norm_gain, parts[rec]
+        )
+        grad_tokens.append(to_all(pieces).reshape(frames, model))
+    grad_tokens = jnp.stack(grad_tokens)
+    output = output_rows(flat_tokens, near_mixed, far_mixed, full_out)
     shape = (recs, frames, model)
     return (output.reshape(shape), grad_tokens.reshape(shape), grad_proj)
 

time: 234 us -> 231 us (0.987)
  waiting for transfers between devices: 121 us -> 79.5 us
  starting transfers between devices: 24.6 us -> 52.5 us
  Pallas kernels: 60.9 us -> 67.5 us
  other arithmetic: 3.29 us -> 7.37 us
    all_gather x4 -> x2, waiting for transfers between devices: 75.6 us -> 0.01 us  [over_z(): return lax.all_gather(array, 'chan', axis_index_groups=groups, tiled=True)]
    ppermute x3 -> x9, waiting for transfers between devices: 10.6 us -> 31.4 us  [the longest x1 17.8 us: row_sums(): got = lax.ppermute(sent, 'batch', [(0, 2), (1, 3), (2, 0), (3, 1)])]
    all_to_all x2 -> x4, waiting for transfers between devices: 0.01 us -> 20.2 us  [to_all(): return lax.all_to_all(array, 'chan', 0, 0, tiled=True)]
    all_to_all x2 -> x4, starting transfers between devices: 11.7 us -> 29.9 us  [to_all(): return lax.all_to_all(array, 'chan', 0, 0, tiled=True)]
    reduce_scatter x2 -> x0, waiting for transfers between devices: 17.8 us -> none  [the longest x1 11.8 us: shards(): sums = lax.psum_scatter(pair, 'frames', scatter_dimension=0)]
    ppermute x3 -> x9, starting transfers between devices: 5.86 us -> 16.6 us  [the longest x2 6.21 us: shards(): left = lax.ppermute(dafter, 'frames', up)]
    ppermute x2 -> x1, waiting for transfers between devices: 7.98 us -> 18.3 us  [to_peer(): return lax.ppermute(array, 'chan', pairs)]
    add x0 -> x3, other arithmetic: none -> 5.35 us  [the longest x1 2.26 us: frame_sums(): pair = kept + got.astype(F32)]
  transfers between devices with their start and end apart: 15 -> 19, of which waited for: 12 -> 8; matrix products, arithmetic and copies ran while one was open for 2% -> 5% of each run, Pallas kernels for 23% -> 29%
where the time goes in v5:
time: 231 us; the launch traced here: 230 us
  waiting for transfers between devices  79.5 us (34%)
  Pallas kernels  67.5 us (29%)
  starting transfers between devices  52.5 us (23%)
  between operations  14 us (6%)
  local copies, waits for them, and re-layouts  8.8 us (4%)
  other arithmetic  7.37 us (3%)
    all_to_all x4, starting transfers between devices, to_all(): return lax.all_to_all(array, 'chan', 0, 0, tiled=True)  29.9 us
    pallas_call x2, Pallas kernels, attention(): pl.pallas_call(attention_body, grid=(1,), in_specs=[by_rec(width, frames)...  20.4 us
    all_to_all x4, waiting for transfers between devices, to_all(): return lax.all_to_all(array, 'chan', 0, 0, tiled=True)  20.2 us
    ppermute x1, waiting for transfers between devices, to_peer(): return lax.ppermute(array, 'chan', pairs)  18.3 us
    ppermute x1, waiting for transfers between devices, row_sums(): got = lax.ppermute(sent, 'batch', [(0, 2), (1, 3), (2, 0), (3, 1)])  17.8 us
    ppermute x3, waiting for transfers between devices, frame_sums(): got = lax.ppermute(sent, 'frames', [(i, (i + shift) % 4) for i in range(4)])  13.6 us
    pallas_call x1, Pallas kernels, project(): pl.pallas_call(project_body, grid=(rows // CTX,), in_specs=[pl.BlockSpec(...  10.6 us
    pallas_call x2, Pallas kernels, back_rows(): pl.pallas_call(back_body, grid=(model // tile,), in_specs=[full(width, ro...  10.3 us
  transfers between devices with their start and end apart: 19, of which 8 were waited for; matrix products, arithmetic and copies ran while one was open for 5% of the time, Pallas kernels for 29%

profile of v5, /device:TPU:18, one launch (start us, length us, event | category | flops | bytes accessed | tf_op | source)
XLA Modules:
  0.0 229.8 jit_solution(9500896209941181541)
XLA Ops:
  7.9 10.6 %project.1 = (bf16[1024,1536]{1,0:T(8,128)(2,1)}, bf16[192,1024]{1,0:T(8,128)(2,1)}, bf16[384,1024]{1,0:T(8,128)(2,1)}, bf16[192,1024]{1,0:T(8,128)(2,1)}, bf16[...) custom-call(s32[2]{0:T(128)} %lengths.1, bf16[1024,1536]{1,0:T(8,128)(2,1)} %bitcast.31, ...), custom_call_target="tpu_custom_call" | custom-call | flops 2400000000 | bytes 15000000 | tf_op jit(solution)/shard_map/project/pallas_call | solution.py:75
  18.6 3.4 %collective-permute-start = (bf16[384,512]{1,0:T(8,128)(2,1)}, bf16[384,512]{1,0:T(8,128)(2,1)S(1)}, u32[]{:S(2)}, u32[]{:S(2)}) collective-permute-start(bf16[384,512]{1,0:T(8,128)(2,1)} %get-tuple-element.31), channel_id=1, source_target_pairs={{0,8},{8,16},{16,24},{1,9},{9,17},{17,25},{2,10},{10,18},{18,26},{... | collective-permute-start | bytes 1179656 | tf_op jit(solution)/shard_map/ppermute | solution.py:433
  22.0 2.5 %collective-permute-start.1 = (bf16[384,512]{1,0:T(8,128)(2,1)}, bf16[384,512]{1,0:T(8,128)(2,1)S(1)}, u32[]{:S(2)}, u32[]{:S(2)}) collective-permute-start(bf16[384,512]{1,0:T(8,128)(2,1)} %get-tuple-element.32), channel_id=1, source_target_pairs={{8,0},{16,8},{24,16},{9,1},{17,9},{25,17},{10,2},{18,10},{26,18},{... | collective-permute-start | bytes 1179656 | tf_op jit(solution)/shard_map/ppermute | solution.py:434
  24.6 1.3 copy.11.seg_keys
  26.5 5.0 %collective-permute-done.before = bf16[384,512]{1,0:T(8,128)(2,1)S(1)} collective-permute-done((bf16[384,512]{1,0:T(8,128)(2,1)}, bf16[384,512]{1,0:T(8,128)(2,1)S(1)}, u32[]{:S(2)}, u32[]{:S(2)}) %collective-permute-start) | collective-permute-done | bytes 393248 | tf_op jit(solution)/shard_map/ppermute | solution.py:433
  31.5 3.1 %collective-permute-done.1.after = bf16[384,512]{1,0:T(8,128)(2,1)S(1)} collective-permute-done((bf16[384,512]{1,0:T(8,128)(2,1)}, bf16[384,512]{1,0:T(8,128)(2,1)S(1)}, u32[]{:S(2)}, u32[]{:S(2)}) %collective-permute-start.1) | collective-permute-done | bytes 393248 | tf_op jit(solution)/shard_map/ppermute | solution.py:434
  35.4 10.3 %attention.3 = (bf16[192,512]{1,0:T(8,128)(2,1)}, bf16[192,512]{1,0:T(8,128)(2,1)}, f32[384,512]{1,0:T(8,128)}, bf16[384,256]{1,0:T(8,128)(2,1)}, bf16[384,256]{1,0:T(8,128)(2,1)}) custom-call(bf16[192,1024]{1,0:T(8,128)(2,1)} %get-tuple-element.29.q, bf16[384,1024]{1,0:T(8,128)(2,1)} %get-tuple-element.30.kv, bf16[384,512]{1,0:T(8,128)(2,1)} %copy-done.3, ...), custom_call_target="tpu_custom_call" | custom-call | flops 1000 | bytes 1000 | tf_op jit(solution)/shard_map/attention/pallas_call | solution.py:160
  45.7 3.1 %collective-permute-start.5 = (bf16[384,256]{1,0:T(8,128)(2,1)}, bf16[384,256]{1,0:T(8,128)(2,1)S(1)}, u32[]{:S(2)}, u32[]{:S(2)}) collective-permute-start(bf16[384,256]{1,0:T(8,128)(2,1)} %get-tuple-element.49), channel_id=1, source_target_pairs={{0,8},{8,16},{16,24},{1,9},{9,17},{17,25},{2,10},{10,18},{18,26},{... | collective-permute-start | bytes 589832 | tf_op jit(solution)/shard_map/ppermute | solution.py:442
  48.8 2.9 %collective-permute-start.6 = (bf16[384,256]{1,0:T(8,128)(2,1)}, bf16[384,256]{1,0:T(8,128)(2,1)S(1)}, u32[]{:S(2)}, u32[]{:S(2)}) collective-permute-start(bf16[384,256]{1,0:T(8,128)(2,1)} %get-tuple-element.50), channel_id=1, source_target_pairs={{8,0},{16,8},{24,16},{9,1},{17,9},{25,17},{10,2},{18,10},{26,18},{... | collective-permute-start | bytes 589832 | tf_op jit(solution)/shard_map/ppermute | solution.py:441
  51.7 10.2 %attention.2 = (bf16[192,512]{1,0:T(8,128)(2,1)}, bf16[192,512]{1,0:T(8,128)(2,1)}, f32[384,512]{1,0:T(8,128)}, bf16[384,256]{1,0:T(8,128)(2,1)}, bf16[384,256]{1,0:T(8,128)(2,1)}) custom-call(bf16[192,1024]{1,0:T(8,128)(2,1)} %get-tuple-element.29.q, bf16[384,1024]{1,0:T(8,128)(2,1)} %get-tuple-element.30.kv, bf16[384,512]{1,0:T(8,128)(2,1)} %copy-done.3, ...), custom_call_target="tpu_custom_call" | custom-call | flops 1000 | bytes 1000 | tf_op jit(solution)/shard_map/attention/pallas_call | solution.py:160
  63.6 5.2 %back.3 = bf16[512,1536]{1,0:T(8,128)(2,1)} custom-call(bf16[192,512]{1,0:T(8,128)(2,1)} %get-tuple-element.47.rest_5_.dq, f32[384,512]{1,0:T(8,128)} %get-tuple-element.48.rest_6_.own, bf16[384,256]{1,0:T(8,128)(2,1)} %copy-done.6, bf16[384,256]{1,0:T(8,128)(2,1)} %copy-done.7, bf16[576,1536]{1,0:T(8,128)(2,1)} %bitcast.40), custom_call_target="tpu_custom_call" | custom-call | flops 900000000 | bytes 4000000 | tf_op jit(solution)/shard_map/back/pallas_call | solution.py:216
  68.8 8.4 %all-to-all-start.2 = ((bf16[8,64,1536]{2,1,0:T(8,128)(2,1)}), bf16[8,64,1536]{2,1,0:T(8,128)(2,1)S(1)}, u32[]{:S(2)}, u32[]{:S(2)}) async-start(bf16[8,64,1536]{2,1,0:T(8,128)(2,1)} %bitcast.43), calls=%async_computation.2 | async-start | bytes 3145728 | tf_op jit(solution)/shard_map/all_to_all | solution.py:376
  77.4 3.1 %collective-permute-start.3 = (bf16[384,256]{1,0:T(8,128)(2,1)S(1)}, bf16[384,256]{1,0:T(8,128)(2,1)S(1)}, u32[]{:S(2)}, u32[]{:S(2)}) collective-permute-start(bf16[384,256]{1,0:T(8,128)(2,1)S(1)} %copy-done.15), channel_id=1, source_target_pairs={{0,8},{8,16},{16,24},{1,9},{9,17},{17,25},{2,10},{10,18},{18,26},{... | collective-permute-start | bytes 589832 | tf_op jit(solution)/shard_map/ppermute | solution.py:442
  80.5 2.7 %collective-permute-start.4 = (bf16[384,256]{1,0:T(8,128)(2,1)S(1)}, bf16[384,256]{1,0:T(8,128)(2,1)S(1)}, u32[]{:S(2)}, u32[]{:S(2)}) collective-permute-start(bf16[384,256]{1,0:T(8,128)(2,1)S(1)} %copy-done.14), channel_id=1, source_target_pairs={{8,0},{16,8},{24,16},{9,1},{17,9},{25,17},{10,2},{18,10},{26,18},{... | collective-permute-start | bytes 589832 | tf_op jit(solution)/shard_map/ppermute | solution.py:441
  83.2 18.3 %collective-permute-done.2 = bf16[192,1024]{1,0:T(8,128)(2,1)S(1)} collective-permute-done((bf16[192,1024]{1,0:T(8,128)(2,1)S(1)}, bf16[192,1024]{1,0:T(8,128)(2,1)S(1)}, u32[]{:S(2)}, u32[]{:S(2)}) %collective-permute-start.2) | collective-permute-done | bytes 393248 | tf_op jit(solution)/shard_map/ppermute | solution.py:372
  102.3 5.1 %back.2 = bf16[512,1536]{1,0:T(8,128)(2,1)} custom-call(bf16[192,512]{1,0:T(8,128)(2,1)} %get-tuple-element.40.dq.rest_0_, f32[384,512]{1,0:T(8,128)} %get-tuple-element.41.own.rest_1_, bf16[384,256]{1,0:T(8,128)(2,1)} %copy-done.8, bf16[384,256]{1,0:T(8,128)(2,1)} %copy-done.9, bf16[576,1536]{1,0:T(8,128)(2,1)} %bitcast.41), custom_call_target="tpu_custom_call" | custom-call | flops 900000000 | bytes 4000000 | tf_op jit(solution)/shard_map/back/pallas_call | solution.py:216
  107.4 9.4 %weight_grads.1 = (bf16[4,2,96,768]{3,2,1,0:T(8,128)(2,1)}, f32[4,2,96,768]{3,2,1,0:T(8,128)}) custom-call(s32[1]{0:T(128)} %bitcast.11.core, bf16[1024,1536]{1,0:T(8,128)(2,1)} %get-tuple-element.46.normed, bf16[1024,1536]{1,0:T(8,128)(2,1)} %bitcast.36, bf16[192,512]{1,0:T(8,128)(2,1)} %get-tuple-element.40.dq.rest_0_, ...), custom_call_target="tpu_custom_call" | custom-call | flops 1000 | bytes 1000 | tf_op jit(solution)/shard_map/weight_grads/pallas_call | solution.py:281
  117.0 7.5 %all-to-all-start = ((bf16[8,64,1536]{2,1,0:T(8,128)(2,1)}), bf16[8,64,1536]{2,1,0:T(8,128)(2,1)S(1)}, u32[]{:S(2)}, u32[]{:S(2)}) async-start(bf16[8,64,1536]{2,1,0:T(8,128)(2,1)} %bitcast.6), calls=%async_computation | async-start | bytes 3145728 | tf_op jit(solution)/shard_map/all_to_all | solution.py:376
  124.5 2.3 convert_add_fusion
  129.6 2.1 collective-permute-start.9
  131.7 8.4 %collective-permute-done.10 = bf16[2,96,768]{2,1,0:T(8,128)(2,1)S(1)} collective-permute-done((bf16[2,96,768]{2,1,0:T(8,128)(2,1)}, bf16[2,96,768]{2,1,0:T(8,128)(2,1)S(1)}, u32[]{:S(2)}, u32[]{:S(2)}) %collective-permute-start.10) | collective-permute-done | bytes 294944 | tf_op jit(solution)/shard_map/ppermute | solution.py:390
  140.1 5.0 %collective-permute-done.8 = bf16[2,96,768]{2,1,0:T(8,128)(2,1)S(1)} collective-permute-done((bf16[2,96,768]{2,1,0:T(8,128)(2,1)}, bf16[2,96,768]{2,1,0:T(8,128)(2,1)S(1)}, u32[]{:S(2)}, u32[]{:S(2)}) %collective-permute-start.8) | collective-permute-done | bytes 294944 | tf_op jit(solution)/shard_map/ppermute | solution.py:390
  145.3 2.0 fusion.1
  147.3 3.4 %finish.3 = bf16[8,64,1536]{2,1,0:T(8,128)(2,1)} custom-call(s32[1]{0:T(128)} %bitcast.10.place, bf16[1024,1536]{1,0:T(8,128)(2,1)} %bitcast.32, bf16[1024,1536]{1,0:T(8,128)(2,1)} %bitcast.37, f32[1536]{0:T(1024)} %gain.5, bf16[8,64,1536]{2,1,0:T(8,128)(2,1)} %copy-done), custom_call_target="tpu_custom_call" | custom-call | flops 10000000 | bytes 5000000 | tf_op jit(solution)/shard_map/finish/pallas_call | solution.py:352
  150.7 8.3 %all-to-all-start.3 = ((bf16[8,64,1536]{2,1,0:T(8,128)(2,1)}), bf16[8,64,1536]{2,1,0:T(8,128)(2,1)S(1)}, u32[]{:S(2)}, u32[]{:S(2)}) async-start(bf16[8,64,1536]{2,1,0:T(8,128)(2,1)} %finish.3), calls=%async_computation.3 | async-start | bytes 3145728 | tf_op jit(solution)/shard_map/all_to_all | solution.py:376
  159.7 3.4 %finish.2 = bf16[8,64,1536]{2,1,0:T(8,128)(2,1)} custom-call(s32[1]{0:T(128)} %bitcast.8.place, bf16[1024,1536]{1,0:T(8,128)(2,1)} %bitcast.33, bf16[1024,1536]{1,0:T(8,128)(2,1)} %bitcast.38, f32[1536]{0:T(1024)} %gain.5, bf16[8,64,1536]{2,1,0:T(8,128)(2,1)} %copy-done.1), custom_call_target="tpu_custom_call" | custom-call | flops 10000000 | bytes 5000000 | tf_op jit(solution)/shard_map/finish/pallas_call | solution.py:352
  163.1 20.2 %all-to-all-done.3 = bf16[8,64,1536]{2,1,0:T(8,128)(2,1)S(1)} async-done(((bf16[8,64,1536]{2,1,0:T(8,128)(2,1)}), bf16[8,64,1536]{2,1,0:T(8,128)(2,1)S(1)}, u32[]{:S(2)}, u32[]{:S(2)}) %all-to-all-start.3) | async-done | bytes 1572896 | tf_op jit(solution)/shard_map/all_to_all | solution.py:376
  183.4 5.6 %all-to-all-start.1 = ((bf16[8,64,1536]{2,1,0:T(8,128)(2,1)}), bf16[8,64,1536]{2,1,0:T(8,128)(2,1)S(1)}, u32[]{:S(2)}, u32[]{:S(2)}) async-start(bf16[8,64,1536]{2,1,0:T(8,128)(2,1)} %finish.2), calls=%async_computation.1 | async-start | bytes 3145728 | tf_op jit(solution)/shard_map/all_to_all | solution.py:376
  190.0 1.4 collective-permute-start.11
  191.4 17.8 %collective-permute-done.11 = bf16[96,768]{1,0:T(8,128)(2,1)} collective-permute-done((bf16[96,768]{1,0:T(8,128)(2,1)S(1)}, bf16[96,768]{1,0:T(8,128)(2,1)}, u32[]{:S(2)}, u32[]{:S(2)}) %collective-permute-start.11) | collective-permute-done | bytes 147488 | tf_op jit(solution)/shard_map/ppermute | solution.py:398
  211.3 10.0 %output.1 = bf16[1024,1536]{1,0:T(8,128)(2,1)} custom-call(bf16[1024,1536]{1,0:T(8,128)(2,1)} %bitcast.34, bf16[768,1024]{1,0:T(8,128)(2,1)} %all-gather.4.cloned.1.call-done.near, bf16[768,1024]{1,0:T(8,128)(2,1)} %all-gather.6.cloned.1.call-done.far, bf16[1536,1536]{1,0:T(8,128)(2,1)} %all-gather.8.cloned.1.call-done.weight), custom_call_target="tpu_custom_call" | custom-call | flops 1000 | bytes 1000 | tf_op jit(solution)/shard_map/output/pallas_call | solution.py:325
  221.3 1.9 pad_maximum_fusion
  (64 shorter events, 11.7 us)
Async XLA Ops:
  7.2 152.5 %all-gather.8.cloned.1.call-start = ((), (), s32[]{:S(2)}) async-start(), calls=%async_computation.6 | async-start | bytes 5308416 | tf_op jit(solution)/shard_map/all_gather | solution.py:417
  7.9 16.6 %copy-start.12 = (s32[2,2048]{1,0:T(2,128)S(1)}, s32[2,2048]{1,0:T(2,128)}, u32[]{:S(2)}) copy-start(s32[2,2048]{1,0:T(2,128)} %param.15) | copy-start | bytes 49156
  7.9 16.6 %copy-start.13 = (s32[2]{0:T(128)S(1)}, s32[2]{0:T(128)}, u32[]{:S(2)}) copy-start(s32[2]{0:T(128)} %lengths.1) | copy-start | bytes 28
  18.6 13.0 %collective-permute-start = (bf16[384,512]{1,0:T(8,128)(2,1)}, bf16[384,512]{1,0:T(8,128)(2,1)S(1)}, u32[]{:S(2)}, u32[]{:S(2)}) collective-permute-start(bf16[384,512]{1,0:T(8,128)(2,1)} %get-tuple-element.31), channel_id=1, source_target_pairs={{0,8},{8,16},{16,24},{1,9},{9,17},{17,25},{2,10},{10,18},{18,26},{... | collective-permute-start | bytes 1179656 | tf_op jit(solution)/shard_map/ppermute | solution.py:433
  22.0 12.7 %collective-permute-start.1 = (bf16[384,512]{1,0:T(8,128)(2,1)}, bf16[384,512]{1,0:T(8,128)(2,1)S(1)}, u32[]{:S(2)}, u32[]{:S(2)}) collective-permute-start(bf16[384,512]{1,0:T(8,128)(2,1)} %get-tuple-element.32), channel_id=1, source_target_pairs={{8,0},{16,8},{24,16},{9,1},{17,9},{25,17},{10,2},{18,10},{26,18},{... | collective-permute-start | bytes 1179656 | tf_op jit(solution)/shard_map/ppermute | solution.py:434
  31.5 3.1 %copy-start.3 = (bf16[384,512]{1,0:T(8,128)(2,1)}, bf16[384,512]{1,0:T(8,128)(2,1)S(1)}, u32[]{:S(2)}) copy-start(bf16[384,512]{1,0:T(8,128)(2,1)S(1)} %collective-permute-done.before) | copy-start | bytes 1179652
  34.7 0.8 copy-start.4
  45.7 17.2 %collective-permute-start.5 = (bf16[384,256]{1,0:T(8,128)(2,1)}, bf16[384,256]{1,0:T(8,128)(2,1)S(1)}, u32[]{:S(2)}, u32[]{:S(2)}) collective-permute-start(bf16[384,256]{1,0:T(8,128)(2,1)} %get-tuple-element.49), channel_id=1, source_target_pairs={{0,8},{8,16},{16,24},{1,9},{9,17},{17,25},{2,10},{10,18},{18,26},{... | collective-permute-start | bytes 589832 | tf_op jit(solution)/shard_map/ppermute | solution.py:442
  48.8 14.1 %collective-permute-start.6 = (bf16[384,256]{1,0:T(8,128)(2,1)}, bf16[384,256]{1,0:T(8,128)(2,1)S(1)}, u32[]{:S(2)}, u32[]{:S(2)}) collective-permute-start(bf16[384,256]{1,0:T(8,128)(2,1)} %get-tuple-element.50), channel_id=1, source_target_pairs={{8,0},{16,8},{24,16},{9,1},{17,9},{25,17},{10,2},{18,10},{26,18},{... | collective-permute-start | bytes 589832 | tf_op jit(solution)/shard_map/ppermute | solution.py:441
  68.8 8.4 %copy-start.10 = (bf16[192,512]{1,0:T(8,128)(2,1)S(1)}, bf16[192,512]{1,0:T(8,128)(2,1)}, u32[]{:S(2)}) copy-start(bf16[192,512]{1,0:T(8,128)(2,1)} %get-tuple-element.36.rest_9_) | copy-start | bytes 589828
  68.8 8.6 %copy-start.15 = (bf16[384,256]{1,0:T(8,128)(2,1)S(1)}, bf16[384,256]{1,0:T(8,128)(2,1)}, u32[]{:S(2)}) copy-start(bf16[384,256]{1,0:T(8,128)(2,1)} %get-tuple-element.42) | copy-start | bytes 589828
  68.8 11.7 %copy-start.14 = (bf16[384,256]{1,0:T(8,128)(2,1)S(1)}, bf16[384,256]{1,0:T(8,128)(2,1)}, u32[]{:S(2)}) copy-start(bf16[384,256]{1,0:T(8,128)(2,1)} %get-tuple-element.43) | copy-start | bytes 589828
  68.8 48.2 %all-to-all-start.2 = ((bf16[8,64,1536]{2,1,0:T(8,128)(2,1)}), bf16[8,64,1536]{2,1,0:T(8,128)(2,1)S(1)}, u32[]{:S(2)}, u32[]{:S(2)}) async-start(bf16[8,64,1536]{2,1,0:T(8,128)(2,1)} %bitcast.43), calls=%async_computation.2 | async-start | bytes 3145728 | tf_op jit(solution)/shard_map/all_to_all | solution.py:376
  77.2 134.1 %all-gather.4.cloned.1.call-start = ((), (), s32[]{:S(2)}) async-start(), calls=%async_computation.4 | async-start | bytes 1966080 | tf_op jit(solution)/shard_map/all_gather | solution.py:404
  77.2 30.2 %copy-start.5 = (bf16[192,1024]{1,0:T(8,128)(2,1)}, bf16[192,1024]{1,0:T(8,128)(2,1)S(1)}, u32[]{:S(2)}) copy-start(bf16[192,1024]{1,0:T(8,128)(2,1)S(1)} %constant_dynamic-update-slice_fusion) | copy-start | bytes 1179652
  77.2 24.3 %collective-permute-start.2 = (bf16[192,1024]{1,0:T(8,128)(2,1)S(1)}, bf16[192,1024]{1,0:T(8,128)(2,1)S(1)}, u32[]{:S(2)}, u32[]{:S(2)}) collective-permute-start(bf16[192,1024]{1,0:T(8,128)(2,1)S(1)} %constant_dynamic-update-slice_fusion), channel_id=1, source_target_pairs={{0,1},{1,0},{2,3},{3,2},{4,5},{5,4},{6,7},{7,6},{8,9},{9,8},{10,11... | collective-permute-start | bytes 1179656 | tf_op jit(solution)/shard_map/ppermute | solution.py:372
  77.4 24.1 %collective-permute-start.3 = (bf16[384,256]{1,0:T(8,128)(2,1)S(1)}, bf16[384,256]{1,0:T(8,128)(2,1)S(1)}, u32[]{:S(2)}, u32[]{:S(2)}) collective-permute-start(bf16[384,256]{1,0:T(8,128)(2,1)S(1)} %copy-done.15), channel_id=1, source_target_pairs={{0,8},{8,16},{16,24},{1,9},{9,17},{17,25},{2,10},{10,18},{18,26},{... | collective-permute-start | bytes 589832 | tf_op jit(solution)/shard_map/ppermute | solution.py:442
  80.5 21.0 %collective-permute-start.4 = (bf16[384,256]{1,0:T(8,128)(2,1)S(1)}, bf16[384,256]{1,0:T(8,128)(2,1)S(1)}, u32[]{:S(2)}, u32[]{:S(2)}) collective-permute-start(bf16[384,256]{1,0:T(8,128)(2,1)S(1)} %copy-done.14), channel_id=1, source_target_pairs={{8,0},{16,8},{24,16},{9,1},{17,9},{25,17},{10,2},{18,10},{26,18},{... | collective-permute-start | bytes 589832 | tf_op jit(solution)/shard_map/ppermute | solution.py:441
  101.5 15.3 %copy-start.11 = (bf16[192,1024]{1,0:T(8,128)(2,1)}, bf16[192,1024]{1,0:T(8,128)(2,1)S(1)}, u32[]{:S(2)}) copy-start(bf16[192,1024]{1,0:T(8,128)(2,1)S(1)} %collective-permute-done.2) | copy-start | bytes 1179652
  101.5 0.8 copy-start.9
  116.8 7.7 %collective-permute-start.7 = (bf16[4,2,96,768]{3,2,1,0:T(8,128)(2,1)}, bf16[4,2,96,768]{3,2,1,0:T(8,128)(2,1)}, u32[]{:S(2)}, u32[]{:S(2)}) collective-permute-start(bf16[4,2,96,768]{3,2,1,0:T(8,128)(2,1)} %get-tuple-element.52), channel_id=1, source_target_pairs={{0,32},{32,0},{64,96},{96,64},{1,33},{33,1},{65,97},{97,65},{2,34}... | collective-permute-start | bytes 3538952 | tf_op jit(solution)/shard_map/ppermute | solution.py:385
  117.0 9.8 %copy-start = (bf16[8,64,1536]{2,1,0:T(8,128)(2,1)}, bf16[8,64,1536]{2,1,0:T(8,128)(2,1)S(1)}, u32[]{:S(2)}) copy-start(bf16[8,64,1536]{2,1,0:T(8,128)(2,1)S(1)} %all-to-all-done.2.parts) | copy-start | bytes 4718596
  117.0 33.7 %all-to-all-start = ((bf16[8,64,1536]{2,1,0:T(8,128)(2,1)}), bf16[8,64,1536]{2,1,0:T(8,128)(2,1)S(1)}, u32[]{:S(2)}, u32[]{:S(2)}) async-start(bf16[8,64,1536]{2,1,0:T(8,128)(2,1)} %bitcast.6), calls=%async_computation | async-start | bytes 3145728 | tf_op jit(solution)/shard_map/all_to_all | solution.py:376
  126.8 1.6 copy-start.2
  128.4 11.6 %collective-permute-start.10 = (bf16[2,96,768]{2,1,0:T(8,128)(2,1)}, bf16[2,96,768]{2,1,0:T(8,128)(2,1)S(1)}, u32[]{:S(2)}, u32[]{:S(2)}) collective-permute-start(bf16[2,96,768]{2,1,0:T(8,128)(2,1)} %get-tuple-element.56), channel_id=1, source_target_pairs={{0,16},{8,24},{16,0},{24,8},{1,17},{9,25},{17,1},{25,9},{2,18},{10... | collective-permute-start | bytes 884744 | tf_op jit(solution)/shard_map/ppermute | solution.py:390
  129.3 15.8 %collective-permute-start.8 = (bf16[2,96,768]{2,1,0:T(8,128)(2,1)}, bf16[2,96,768]{2,1,0:T(8,128)(2,1)S(1)}, u32[]{:S(2)}, u32[]{:S(2)}) collective-permute-start(bf16[2,96,768]{2,1,0:T(8,128)(2,1)} %get-tuple-element.55), channel_id=1, source_target_pairs={{0,8},{8,16},{16,24},{24,0},{1,9},{9,17},{17,25},{25,1},{2,10},{10... | collective-permute-start | bytes 884744 | tf_op jit(solution)/shard_map/ppermute | solution.py:390
  129.6 15.7 %collective-permute-start.9 = (bf16[2,96,768]{2,1,0:T(8,128)(2,1)S(1)}, bf16[2,96,768]{2,1,0:T(8,128)(2,1)S(1)}, u32[]{:S(2)}, u32[]{:S(2)}) collective-permute-start(bf16[2,96,768]{2,1,0:T(8,128)(2,1)S(1)} %get-tuple-element.57), channel_id=1, source_target_pairs={{0,24},{8,0},{16,8},{24,16},{1,25},{9,1},{17,9},{25,17},{2,26},{10... | collective-permute-start | bytes 884744 | tf_op jit(solution)/shard_map/ppermute | solution.py:390
  150.7 9.0 %copy-start.1 = (bf16[8,64,1536]{2,1,0:T(8,128)(2,1)}, bf16[8,64,1536]{2,1,0:T(8,128)(2,1)S(1)}, u32[]{:S(2)}) copy-start(bf16[8,64,1536]{2,1,0:T(8,128)(2,1)S(1)} %all-to-all-done.parts) | copy-start | bytes 4718596
  150.7 32.7 %all-to-all-start.3 = ((bf16[8,64,1536]{2,1,0:T(8,128)(2,1)}), bf16[8,64,1536]{2,1,0:T(8,128)(2,1)S(1)}, u32[]{:S(2)}, u32[]{:S(2)}) async-start(bf16[8,64,1536]{2,1,0:T(8,128)(2,1)} %finish.3), calls=%async_computation.3 | async-start | bytes 3145728 | tf_op jit(solution)/shard_map/all_to_all | solution.py:376
  159.0 52.4 %all-gather.6.cloned.1.call-start = ((), (), s32[]{:S(2)}) async-start(), calls=%async_computation.5 | async-start | bytes 1966080 | tf_op jit(solution)/shard_map/all_gather | solution.py:404
  183.4 37.9 %all-to-all-start.1 = ((bf16[8,64,1536]{2,1,0:T(8,128)(2,1)}), bf16[8,64,1536]{2,1,0:T(8,128)(2,1)S(1)}, u32[]{:S(2)}, u32[]{:S(2)}) async-start(bf16[8,64,1536]{2,1,0:T(8,128)(2,1)} %finish.2), calls=%async_computation.1 | async-start | bytes 3145728 | tf_op jit(solution)/shard_map/all_to_all | solution.py:376
  190.0 19.2 %collective-permute-start.11 = (bf16[96,768]{1,0:T(8,128)(2,1)S(1)}, bf16[96,768]{1,0:T(8,128)(2,1)}, u32[]{:S(2)}, u32[]{:S(2)}) collective-permute-start(bf16[96,768]{1,0:T(8,128)(2,1)S(1)} %fusion.5), channel_id=1, source_target_pairs={{0,64},{32,96},{64,0},{96,32},{1,65},{33,97},{65,1},{97,33},{2,66}... | collective-permute-start | bytes 442376 | tf_op jit(solution)/shard_map/ppermute | solution.py:398
  (3 other events, 2.1 us)
Sparse Core Ops, SparseCore 0:
  10.3 89.5 all-gather.7
  117.1 40.9 all-gather.3
  161.4 37.1 all-gather.5

commit v6 on v5

--- a/solution.py
+++ b/solution.py
@@ -10,6 +10,8 @@
 EPS = 1e-05
 NEG = -1e30
 VMEM_LIMIT = 60 * 1024 * 1024
+
+SHIFTS = ((1, 0), (3, 0), (0, 1), (1, 1), (3, 1), (2, 0), (2, 1))
 
 F32 = jnp.float32
 BF16 = jnp.bfloat16
@@ -300,68 +302,107 @@
             jax.ShapeDtypeStruct((4, 2, block // 4, 4 * width), F32),
         ],
         compiler_params=params(),
-        cost_estimate=pl.CostEstimate(flops=1000, bytes_accessed=1000, transcendentals=0),
+        cost_estimate=pl.CostEstimate(flops=10000000000, bytes_accessed=12000000, transcendentals=0),
         name="weight_grads",
     )(core, normed, cotangent, *pieces)
 
 
-def output_body(tok, near, far, weight, out, stacked):
-    side = lax.axis_index("chan") & 1
-    width = weight.shape[0] // 8
-    for z in range(4):
-        rows = slice(z * width, (z + 1) * width)
-        for offset, source in ((side, near), (1 - side, far)):
-            place = pl.multiple_of((2 * z + offset) * width, width)
-            stacked[pl.ds(place, width), :] = source[rows, :]
-    total = dot_nn(stacked[...].T, weight[...])
+def output_body(tok, first, second, own_weight, other_weight, out, own, other):
+    core = lax.axis_index("batch") & 1
+    half = own_weight.shape[0] // 8
+    rec = pl.program_id(0) // 2
+
+    def fill(source):
+        for chan in range(8):
+            rows = slice(chan * half, (chan + 1) * half)
+            for offset, target in ((core, own), (1 - core, other)):
+                place = pl.multiple_of((2 * chan + offset) * half, half)
+                target[rows, :] = source[pl.ds(place, half), :]
+
+    pl.when(rec == 0)(lambda: fill(first))
+    pl.when(rec == 1)(lambda: fill(second))
+    total = dot_nn(own[...].T, own_weight[...]) + dot_nn(other[...].T, other_weight[...])
     out[...] = (tok[...].astype(F32) + total).astype(BF16)
 
 
-def output_rows(tokens, near, far, weight):
+def output_rows(tokens, mixed, own_weight, other_weight):
     rows, model = tokens.shape
-    depth = near.shape[0]
+    depth = own_weight.shape[0]
     by_row = pl.BlockSpec((CTX, model), lambda i: (i, 0))
-    by_col = pl.BlockSpec((depth, CTX), lambda i: (0, i))
+    by_col = pl.BlockSpec((2 * depth, CTX), lambda i: (0, i % 2))
+    full = pl.BlockSpec((depth, model), lambda i: (0, 0))
     return pl.pallas_call(
         output_body,
         grid=(rows // CTX,),
-        in_specs=[by_row, by_col, by_col, pl.BlockSpec((2 * depth, model), lambda i: (0, 0))],
+        in_specs=[by_row, by_col, by_col, full, full],
         out_specs=by_row,
         out_shape=jax.ShapeDtypeStruct((rows, model), BF16),
-        scratch_shapes=[pltpu.VMEM((2 * depth, CTX), BF16)],
-        compiler_params=params(),
-        cost_estimate=pl.CostEstimate(flops=1000, bytes_accessed=1000, transcendentals=0),
+        scratch_shapes=[pltpu.VMEM((depth, CTX), BF16)] * 2,
+        compiler_params=params(),
+        cost_estimate=pl.CostEstimate(flops=10000000000, bytes_accessed=12000000, transcendentals=0),
         name="output",
-    )(tokens, near, far, weight)
-
-
-def finish_body(place, tok, cot, gain, parts, out):
-    back = jnp.sum(parts[...].astype(F32), axis=0)
-    scaled, inverse = norm_stats(tok[...])
-    weighted = back * gain[...][None, :]
-    first = jnp.mean(weighted, axis=-1, keepdims=True)
-    second = jnp.mean(weighted * scaled, axis=-1, keepdims=True)
-    grad = inverse * (weighted - first - scaled * second) + cot[...].astype(F32)
-    out[...] = jnp.broadcast_to(grad.astype(BF16)[None], out.shape)
+    )(tokens, *mixed, own_weight, other_weight)
+
+
+def finish_body(place, gain, *refs):
+    out = refs[-1]
+    chunk = refs[0].shape[0]
+    for rec in range(2):
+        tok, cot, parts = refs[3 * rec : 3 * rec + 3]
+        back = jnp.sum(parts[...].astype(F32), axis=0)
+        scaled, inverse = norm_stats(tok[...])
+        weighted = back * gain[...][None, :]
+        first = jnp.mean(weighted, axis=-1, keepdims=True)
+        second = jnp.mean(weighted * scaled, axis=-1, keepdims=True)
+        grad = inverse * (weighted - first - scaled * second) + cot[...].astype(F32)
+        out[rec * chunk : (rec + 1) * chunk, :] = grad.astype(BF16)
 
 
 def finish(place, tokens, cotangent, gain, parts):
-    count, chunk, model = parts.shape
-    here = pl.BlockSpec((chunk, model), lambda i, p: (p[0], 0))
+    count, chunk, model = parts[0].shape
+    at = lambda rec: pl.BlockSpec((chunk, model), lambda i, p: (rec * count + p[0], 0))
     whole = pl.BlockSpec((count, chunk, model), lambda i, p: (0, 0, 0))
     return pl.pallas_call(
         finish_body,
         grid_spec=pltpu.PrefetchScalarGridSpec(
             num_scalar_prefetch=1,
             grid=(1,),
-            in_specs=[here, here, pl.BlockSpec((model,), lambda i, p: (0,)), whole],
-            out_specs=whole,
+            in_specs=[pl.BlockSpec((model,), lambda i, p: (0,))]
+            + [at(0), at(0), whole, at(1), at(1), whole],
+            out_specs=pl.BlockSpec((2 * chunk, model), lambda i, p: (0, 0)),
         ),
-        out_shape=jax.ShapeDtypeStruct((count, chunk, model), BF16),
+        out_shape=jax.ShapeDtypeStruct((2 * chunk, model), BF16),
         compiler_params=params(),
         cost_estimate=pl.CostEstimate(flops=10000000, bytes_accessed=5000000, transcendentals=0),
         name="finish",
-    )(place, tokens, cotangent, gain, parts)
+    )(place, gain, tokens, cotangent, parts[0], tokens, cotangent, parts[1])
+
+
+def assemble_body(places, *refs):
+    pieces, out = refs[:-1], refs[-1]
+    chunk = pieces[0].shape[0] // 2
+    half = out.shape[0] // 2
+    for index, piece in enumerate(pieces):
+        for rec in range(2):
+            place = pl.multiple_of(rec * half + places[index] * chunk, chunk)
+            out[pl.ds(place, chunk), :] = piece[rec * chunk : (rec + 1) * chunk, :]
+
+
+def assemble(places, pieces):
+    chunk, model = pieces[0].shape
+    count = len(pieces)
+    tile = 512
+    by_col = lambda n: pl.BlockSpec((n, tile), lambda i: (0, i))
+    return pl.pallas_call(
+        assemble_body,
+        grid=(model // tile,),
+        in_specs=[pl.BlockSpec(memory_space=pltpu.SMEM)] + [by_col(chunk)] * count,
+        out_specs=by_col(count * chunk),
+        out_shape=jax.ShapeDtypeStruct((count * chunk, model), BF16),
+        compiler_params=params(),
+        cost_estimate=pl.CostEstimate(flops=0, bytes_accessed=6000000, transcendentals=0),
+        name="assemble",
+    )(places, *pieces)
 
 
 def to_peer(array, shift):
@@ -372,6 +413,11 @@
     return lax.ppermute(array, "chan", pairs)
 
 
+def peer_index(me, shift, sign):
+    dz, dy = shift
+    return (((me >> 1) + sign * dz) & 3) * 2 + ((me & 1) ^ dy)
+
+
 def to_all(array):
     return lax.all_to_all(array, "chan", 0, 0, tiled=True)
 
@@ -380,10 +426,12 @@
     return lax.dynamic_index_in_dim(array, index, axis, keepdims=False)
 
 
-def frame_sums(sent, kept):
+def core_swap(array):
+    return lax.ppermute(array, "batch", [(0, 1), (1, 0), (2, 3), (3, 2)])
+
+
+def frame_sums(pair):
     frame = lax.axis_index("frames")
-    got = lax.ppermute(sent, "batch", [(0, 1), (1, 0), (2, 3), (3, 2)])
-    pair = kept + got.astype(F32)
     sums = pick(pair, frame, 0)
     for shift in (1, 3, 2):
         sent = pick(pair, (frame + shift) & 3, 0).astype(BF16)
@@ -397,11 +445,6 @@
     sent = pick(sums, 1 - row, 0).astype(BF16)
     got = lax.ppermute(sent, "batch", [(0, 2), (1, 3), (2, 0), (3, 1)])
     return pick(sums, row, 0) + got.astype(F32)
-
-
-def over_z(array):
-    groups = [[0, 2, 4, 6], [1, 3, 5, 7]]
-    return lax.all_gather(array, "chan", axis_index_groups=groups, tiled=True)
 
 
 def shards(tokens, cotangent, norm_gain, norm_bias, qkv_weight, out_weight, lengths, segments):
@@ -414,7 +457,9 @@
 
     weight = qkv_weight.transpose(1, 2, 0).reshape(3 * width, model)
     tie = lax.optimization_barrier
-    full_out = lax.all_gather(out_weight, "chan", tiled=True)
+    core = lax.axis_index("batch") & 1
+    half_out = lax.dynamic_slice_in_dim(out_weight, core * (width // 2), width // 2, 0)
+    own_out = lax.all_gather(half_out, "chan", tiled=True)
 
     flat_tokens = tokens.reshape(rows, model)
     flat_cot = cotangent.reshape(rows, model)
@@ -442,35 +487,31 @@
         left = lax.ppermute(dafter, "frames", up)
         results.append([dq, dkv, left, right, mixed])
 
-    mixed = jnp.concatenate([result[4] for result in results], axis=1)
-    near_mixed = over_z(mixed)
-    peer_mixed = to_peer(mixed, (0, 1))
-    first = results[0]
-    first[0], peer_mixed, _ = tie((first[0], peer_mixed, results[1][0]))
-    far_mixed = over_z(peer_mixed)
-
+    first, second = results
     count = lax.axis_size("chan")
-    backs = [
-        back_rows(*result[:4], weight).reshape(count, -1, model) for result in results
-    ]
-    parts = [to_all(back) for back in backs]
-    parts[0], full_out = tie((parts[0], full_out))
-    results[1][0], _ = tie((results[1][0], backs[0]))
-
-    core = scalar(lax.axis_index("batch") & 1)
-    sent, kept = weight_grads(core, normed, flat_cot, results[0] + results[1])
-    sums = frame_sums(sent, kept)
-    sums, parts[1] = tie((sums, parts[1]))
+    mixed = [lax.all_gather(result[4], "chan", tiled=True) for result in results]
+    own_out, first[0] = tie((own_out, first[0]))
+    other_out = core_swap(own_out)
+    second[0], _ = tie((second[0], first[0]))
+
+    split = lambda back: back.reshape(count, -1, model)
+    second_back = split(back_rows(*second[:4], weight))
+    first[0], second_back = tie((first[0], second_back))
+    first_back = split(back_rows(*first[:4], weight))
+    parts = [to_all(first_back), to_all(second_back)]
+
+    first[0], first_back, mixed[1], parts[1] = tie((first[0], first_back, mixed[1], parts[1]))
+    sent, kept = weight_grads(scalar(core), normed, flat_cot, first + second)
+    sums = frame_sums(kept + core_swap(sent).astype(F32))
+    sums, parts[0], mixed[0], other_out = tie((sums, parts[0], mixed[0], other_out))
     grad_proj = row_sums(sums).reshape(-1, 4, width)
 
-    grad_tokens = []
-    for rec in range(recs):
-        pieces = finish(
-            scalar(rec * count + me), flat_tokens, flat_cot, norm_gain, parts[rec]
-        )
-        grad_tokens.append(to_all(pieces).reshape(frames, model))
-    grad_tokens = jnp.stack(grad_tokens)
-    output = output_rows(flat_tokens, near_mixed, far_mixed, full_out)
+    piece = finish(scalar(me), flat_tokens, flat_cot, norm_gain, parts)
+    places = jnp.stack([me] + [peer_index(me, shift, -1) for shift in SHIFTS]).astype(jnp.int32)
+    output = output_rows(flat_tokens, mixed, own_out, other_out)
+    pieces = [to_peer(piece, shift) for shift in SHIFTS]
+    pieces[0], output = tie((pieces[0], output))
+    grad_tokens = assemble(places, [piece] + pieces)
     shape = (recs, frames, model)
     return (output.reshape(shape), grad_tokens.reshape(shape), grad_proj)
 

time: 231 us -> 249 us (1.078)
  waiting for transfers between devices: 79.5 us -> 96.9 us
  other arithmetic: 7.37 us -> 3.24 us
  Pallas kernels: 67.5 us -> 70.3 us
    all_gather x3, waiting for transfers between devices: 0.02 us -> 56.1 us  [the longest x2 52.8 us: shards(): lax.all_gather(result[4], 'chan', tiled=True)]
    all_to_all x4 -> x2, waiting for transfers between devices: 20.2 us -> 0.01 us  [to_all(): return lax.all_to_all(array, 'chan', 0, 0, tiled=True)]
    ppermute x1, waiting for transfers between devices: 17.8 us -> 0.66 us  [row_sums(): got = lax.ppermute(sent, 'batch', [(0, 2), (1, 3), (2, 0), (3, 1)])]
    all_to_all x4 -> x2, starting transfers between devices: 29.9 us -> 13.3 us  [to_all(): return lax.all_to_all(array, 'chan', 0, 0, tiled=True)]
    ppermute x1 -> x7, starting transfers between devices: 0.13 us -> 14.7 us  [to_peer(): return lax.ppermute(array, 'chan', pairs)]
    pallas_call x0 -> x1, Pallas kernels: none -> 4.47 us  [assemble(): pl.pallas_call(assemble_body, grid=(model // tile,), in_specs=[pl.BlockSp...]
    ppermute x1 -> x7, waiting for transfers between devices: 18.3 us -> 14 us  [to_peer(): return lax.ppermute(array, 'chan', pairs)]
    ppermute x2, waiting for transfers between devices: 0.01 us -> 3.11 us  [shards(): right = lax.ppermute(dbefore, 'frames', down)]
  transfers between devices with their start and end apart: 19 -> 24, of which waited for: 8 -> 13; matrix products, arithmetic and copies ran while one was open for 5% -> 3% of each run, Pallas kernels for 29% -> 25%
where the time goes in v6:
time: 249 us; the launch traced here: 247 us
  waiting for transfers between devices  96.9 us (39%)
  Pallas kernels  70.3 us (28%)
  starting transfers between devices  52.4 us (21%)
  between operations  14 us (6%)
  local copies, waits for them, and re-layouts  10.2 us (4%)
  other arithmetic  3.24 us (1%)
    all_gather x2, waiting for transfers between devices, shards(): lax.all_gather(result[4], 'chan', tiled=True)  52.8 us
    pallas_call x2, Pallas kernels, attention(): pl.pallas_call(attention_body, grid=(1,), in_specs=[by_rec(width, frames)...  20.5 us
    ppermute x7, starting transfers between devices, to_peer(): return lax.ppermute(array, 'chan', pairs)  14.7 us
    ppermute x7, waiting for transfers between devices, to_peer(): return lax.ppermute(array, 'chan', pairs)  14 us
    all_to_all x2, starting transfers between devices, to_all(): return lax.all_to_all(array, 'chan', 0, 0, tiled=True)  13.3 us
    ppermute x3, waiting for transfers between devices, frame_sums(): got = lax.ppermute(sent, 'frames', [(i, (i + shift) % 4) for i in range(4)])  12.9 us
    pallas_call x1, Pallas kernels, project(): pl.pallas_call(project_body, grid=(rows // CTX,), in_specs=[pl.BlockSpec(...  10.7 us
    pallas_call x1, Pallas kernels, output_rows(): pl.pallas_call(output_body, grid=(rows // CTX,), in_specs=[by_row, by_col...  10.6 us
  transfers between devices with their start and end apart: 24, of which 13 were waited for; matrix products, arithmetic and copies ran while one was open for 3% of the time, Pallas kernels for 25%

profile of v6, /device:TPU:18, one launch (start us, length us, event | category | flops | bytes accessed | tf_op | source)
XLA Modules:
  0.0 247.0 jit_solution(17338617587662763865)
XLA Ops:
  9.0 10.7 %project.1 = (bf16[1024,1536]{1,0:T(8,128)(2,1)}, bf16[192,1024]{1,0:T(8,128)(2,1)}, bf16[384,1024]{1,0:T(8,128)(2,1)}, bf16[192,1024]{1,0:T(8,128)(2,1)}, bf16[...) custom-call(s32[2]{0:T(128)} %lengths.1, bf16[1024,1536]{1,0:T(8,128)(2,1)} %bitcast.40, ...), custom_call_target="tpu_custom_call" | custom-call | flops 2400000000 | bytes 15000000 | tf_op jit(solution)/shard_map/project/pallas_call | solution.py:77
  19.7 3.4 %collective-permute-start = (bf16[384,512]{1,0:T(8,128)(2,1)}, bf16[384,512]{1,0:T(8,128)(2,1)S(1)}, u32[]{:S(2)}, u32[]{:S(2)}) collective-permute-start(bf16[384,512]{1,0:T(8,128)(2,1)} %get-tuple-element.39), channel_id=1, source_target_pairs={{0,8},{8,16},{16,24},{1,9},{9,17},{17,25},{2,10},{10,18},{18,26},{... | collective-permute-start | bytes 1179656 | tf_op jit(solution)/shard_map/ppermute | solution.py:478
  23.1 2.5 collective-permute-start.1
  27.6 5.0 %collective-permute-done.before = bf16[384,512]{1,0:T(8,128)(2,1)S(1)} collective-permute-done((bf16[384,512]{1,0:T(8,128)(2,1)}, bf16[384,512]{1,0:T(8,128)(2,1)S(1)}, u32[]{:S(2)}, u32[]{:S(2)}) %collective-permute-start) | collective-permute-done | bytes 393248 | tf_op jit(solution)/shard_map/ppermute | solution.py:478
  32.6 3.1 %collective-permute-done.1.after = bf16[384,512]{1,0:T(8,128)(2,1)S(1)} collective-permute-done((bf16[384,512]{1,0:T(8,128)(2,1)}, bf16[384,512]{1,0:T(8,128)(2,1)S(1)}, u32[]{:S(2)}, u32[]{:S(2)}) %collective-permute-start.1) | collective-permute-done | bytes 393248 | tf_op jit(solution)/shard_map/ppermute | solution.py:479
  36.6 10.2 %attention.3 = (bf16[192,512]{1,0:T(8,128)(2,1)}, bf16[192,512]{1,0:T(8,128)(2,1)}, f32[384,512]{1,0:T(8,128)}, bf16[384,256]{1,0:T(8,128)(2,1)}, bf16[384,256]{1,0:T(8,128)(2,1)}) custom-call(bf16[192,1024]{1,0:T(8,128)(2,1)} %get-tuple-element.37.q, bf16[384,1024]{1,0:T(8,128)(2,1)} %get-tuple-element.38.kv, bf16[384,512]{1,0:T(8,128)(2,1)} %copy-done.3, ...), custom_call_target="tpu_custom_call" | custom-call | flops 1000 | bytes 1000 | tf_op jit(solution)/shard_map/attention/pallas_call | solution.py:162
  46.8 3.1 %collective-permute-start.2 = (bf16[384,256]{1,0:T(8,128)(2,1)}, bf16[384,256]{1,0:T(8,128)(2,1)S(1)}, u32[]{:S(2)}, u32[]{:S(2)}) collective-permute-start(bf16[384,256]{1,0:T(8,128)(2,1)} %get-tuple-element.48), channel_id=1, source_target_pairs={{0,8},{8,16},{16,24},{1,9},{9,17},{17,25},{2,10},{10,18},{18,26},{... | collective-permute-start | bytes 589832 | tf_op jit(solution)/shard_map/ppermute | solution.py:487
  49.9 2.9 %collective-permute-start.3 = (bf16[384,256]{1,0:T(8,128)(2,1)}, bf16[384,256]{1,0:T(8,128)(2,1)S(1)}, u32[]{:S(2)}, u32[]{:S(2)}) collective-permute-start(bf16[384,256]{1,0:T(8,128)(2,1)} %get-tuple-element.49), channel_id=1, source_target_pairs={{8,0},{16,8},{24,16},{9,1},{17,9},{25,17},{10,2},{18,10},{26,18},{... | collective-permute-start | bytes 589832 | tf_op jit(solution)/shard_map/ppermute | solution.py:486
  52.9 10.2 %attention.2 = (bf16[192,512]{1,0:T(8,128)(2,1)}, bf16[192,512]{1,0:T(8,128)(2,1)}, f32[384,512]{1,0:T(8,128)}, bf16[384,256]{1,0:T(8,128)(2,1)}, bf16[384,256]{1,0:T(8,128)(2,1)}) custom-call(bf16[192,1024]{1,0:T(8,128)(2,1)} %get-tuple-element.37.q, bf16[384,1024]{1,0:T(8,128)(2,1)} %get-tuple-element.38.kv, bf16[384,512]{1,0:T(8,128)(2,1)} %copy-done.3, ...), custom_call_target="tpu_custom_call" | custom-call | flops 1000 | bytes 1000 | tf_op jit(solution)/shard_map/attention/pallas_call | solution.py:162
  63.1 3.4 %all-gather.4.cloned.1.call-done.own_weight = bf16[768,1536]{1,0:T(8,128)(2,1)} async-done(((bf16[96,1536]{1,0:T(8,128)(2,1)}), bf16[768,1536]{1,0:T(8,128)(2,1)}) %all-gather.4.cloned.1.call-update) | async-done | bytes 2359312 | tf_op jit(solution)/shard_map/all_gather | solution.py:462
  67.2 5.1 %back.2 = bf16[512,1536]{1,0:T(8,128)(2,1)} custom-call(bf16[192,512]{1,0:T(8,128)(2,1)} %get-tuple-element.46.dq.rest_5_, f32[384,512]{1,0:T(8,128)} %get-tuple-element.47.own.rest_6_, bf16[384,256]{1,0:T(8,128)(2,1)} %copy-done.11, bf16[384,256]{1,0:T(8,128)(2,1)} %copy-done.12, bf16[576,1536]{1,0:T(8,128)(2,1)} %bitcast.45), custom_call_target="tpu_custom_call" | custom-call | flops 900000000 | bytes 4000000 | tf_op jit(solution)/shard_map/back/pallas_call | solution.py:218
  72.3 6.6 %all-to-all-start = ((bf16[8,64,1536]{2,1,0:T(8,128)(2,1)}), bf16[8,64,1536]{2,1,0:T(8,128)(2,1)S(1)}, u32[]{:S(2)}, u32[]{:S(2)}) async-start(bf16[8,64,1536]{2,1,0:T(8,128)(2,1)} %bitcast.47), calls=%async_computation | async-start | bytes 3145728 | tf_op jit(solution)/shard_map/all_to_all | solution.py:422
  78.9 3.4 %collective-permute-start.4 = (bf16[384,256]{1,0:T(8,128)(2,1)S(1)}, bf16[384,256]{1,0:T(8,128)(2,1)S(1)}, u32[]{:S(2)}, u32[]{:S(2)}) collective-permute-start(bf16[384,256]{1,0:T(8,128)(2,1)S(1)} %copy-done.18), channel_id=1, source_target_pairs={{0,8},{8,16},{16,24},{1,9},{9,17},{17,25},{2,10},{10,18},{18,26},{... | collective-permute-start | bytes 589832 | tf_op jit(solution)/shard_map/ppermute | solution.py:487
  82.3 2.5 %collective-permute-start.5 = (bf16[384,256]{1,0:T(8,128)(2,1)S(1)}, bf16[384,256]{1,0:T(8,128)(2,1)S(1)}, u32[]{:S(2)}, u32[]{:S(2)}) collective-permute-start(bf16[384,256]{1,0:T(8,128)(2,1)S(1)} %copy-done.17), channel_id=1, source_target_pairs={{8,0},{16,8},{24,16},{9,1},{17,9},{25,17},{10,2},{18,10},{26,18},{... | collective-permute-start | bytes 589832 | tf_op jit(solution)/shard_map/ppermute | solution.py:486
  86.8 3.1 %collective-permute-done.5.right.rest_3_ = bf16[384,256]{1,0:T(8,128)(2,1)S(1)} collective-permute-done((bf16[384,256]{1,0:T(8,128)(2,1)S(1)}, bf16[384,256]{1,0:T(8,128)(2,1)S(1)}, u32[]{:S(2)}, u32[]{:S(2)}) %collective-permute-start.5) | collective-permute-done | bytes 196640 | tf_op jit(solution)/shard_map/ppermute | solution.py:486
  90.5 5.1 %back.3 = bf16[512,1536]{1,0:T(8,128)(2,1)} custom-call(bf16[192,512]{1,0:T(8,128)(2,1)} %get-tuple-element.56.dq.rest_0_, f32[384,512]{1,0:T(8,128)} %get-tuple-element.51.own.rest_1_, bf16[384,256]{1,0:T(8,128)(2,1)} %copy-done.13, bf16[384,256]{1,0:T(8,128)(2,1)} %copy-done.14, bf16[576,1536]{1,0:T(8,128)(2,1)} %bitcast.46), custom_call_target="tpu_custom_call" | custom-call | flops 900000000 | bytes 4000000 | tf_op jit(solution)/shard_map/back/pallas_call | solution.py:218
  95.7 30.0 %all-gather.6.cloned.1.call-done.second = bf16[1536,512]{1,0:T(8,128)(2,1)} async-done(((bf16[192,512]{1,0:T(8,128)(2,1)}), bf16[1536,512]{1,0:T(8,128)(2,1)}) %all-gather.6.cloned.1.call-update) | async-done | bytes 1572880 | tf_op jit(solution)/shard_map/all_gather | solution.py:492
  125.7 9.9 %weight_grads.1 = (bf16[4,2,96,768]{3,2,1,0:T(8,128)(2,1)}, f32[4,2,96,768]{3,2,1,0:T(8,128)}) custom-call(s32[1]{0:T(128)} %bitcast.3.core, bf16[1024,1536]{1,0:T(8,128)(2,1)} %get-tuple-element.36.normed, bf16[1024,1536]{1,0:T(8,128)(2,1)} %bitcast.37, bf16[192,512]{1,0:T(8,128)(2,1)} %get-tuple-element.56.dq.rest_0_, ...), custom_call_target="tpu_custom_call" | custom-call | flops 10000000000 | bytes 12000000 | tf_op jit(solution)/shard_map/weight_grads/pallas_call | solution.py:283
  135.7 6.7 %all-to-all-start.1 = ((bf16[8,64,1536]{2,1,0:T(8,128)(2,1)}), bf16[8,64,1536]{2,1,0:T(8,128)(2,1)S(1)}, u32[]{:S(2)}, u32[]{:S(2)}) async-start(bf16[8,64,1536]{2,1,0:T(8,128)(2,1)} %bitcast.9), calls=%async_computation.1 | async-start | bytes 3145728 | tf_op jit(solution)/shard_map/all_to_all | solution.py:422
  147.9 2.1 collective-permute-start.9
  150.0 5.8 %collective-permute-done.7 = bf16[2,96,768]{2,1,0:T(8,128)(2,1)S(1)} collective-permute-done((bf16[2,96,768]{2,1,0:T(8,128)(2,1)S(1)}, bf16[2,96,768]{2,1,0:T(8,128)(2,1)S(1)}, u32[]{:S(2)}, u32[]{:S(2)}) %collective-permute-start.7) | collective-permute-done | bytes 294944 | tf_op jit(solution)/shard_map/ppermute | solution.py:438
  156.7 6.3 %collective-permute-done.9 = bf16[2,96,768]{2,1,0:T(8,128)(2,1)S(1)} collective-permute-done((bf16[2,96,768]{2,1,0:T(8,128)(2,1)S(1)}, bf16[2,96,768]{2,1,0:T(8,128)(2,1)S(1)}, u32[]{:S(2)}, u32[]{:S(2)}) %collective-permute-start.9) | collective-permute-done | bytes 294944 | tf_op jit(solution)/shard_map/ppermute | solution.py:438
  164.1 22.8 %all-gather.8.cloned.1.call-done.first = bf16[1536,512]{1,0:T(8,128)(2,1)} async-done(((bf16[192,512]{1,0:T(8,128)(2,1)}), bf16[1536,512]{1,0:T(8,128)(2,1)}) %all-gather.8.cloned.1.call-update) | async-done | bytes 1572880 | tf_op jit(solution)/shard_map/all_gather | solution.py:492
  188.1 3.9 %finish.1.refs_0_ = bf16[128,1536]{1,0:T(8,128)(2,1)} custom-call(s32[1]{0:T(128)} %bitcast.place, f32[1536]{0:T(1024)} %gain.3, bf16[1024,1536]{1,0:T(8,128)(2,1)} %bitcast.41, bf16[1024,1536]{1,0:T(8,128)(2,1)} %bitcast.38, bf16[8,64,1536]{2,1,0:T(8,128)(2,1)} %copy-done.1, bf16[1024,1536]{1,0:T(8,128)(2,1)} %bitcast.42, bf16[1024,1536]{1,0:T(8,128)(2,1)} %bitcast.39, ...), custom_call_target="tpu_custom_call" | custom-call | flops 10000000 | bytes 5000000 | tf_op jit(solution)/shard_map/finish/pallas_call | solution.py:365
  193.2 2.0 collective-permute-start.12
  195.2 2.2 collective-permute-start.18
  201.6 4.1 %collective-permute-start.15 = (bf16[128,1536]{1,0:T(8,128)(2,1)}, bf16[128,1536]{1,0:T(8,128)(2,1)S(1)}, u32[]{:S(2)}, u32[]{:S(2)}) collective-permute-start(bf16[128,1536]{1,0:T(8,128)(2,1)} %finish.1.refs_0_), channel_id=1, source_target_pairs={{0,7},{1,6},{2,1},{3,0},{4,3},{5,2},{6,5},{7,4},{8,15},{9,14},{10,... | collective-permute-start | bytes 1179656 | tf_op jit(solution)/shard_map/ppermute | solution.py:413
  206.6 3.6 %collective-permute-start.17 = (bf16[128,1536]{1,0:T(8,128)(2,1)}, bf16[128,1536]{1,0:T(8,128)(2,1)}, u32[]{:S(2)}, u32[]{:S(2)}) collective-permute-start(bf16[128,1536]{1,0:T(8,128)(2,1)} %finish.1.refs_0_), channel_id=1, source_target_pairs={{0,5},{1,4},{2,7},{3,6},{4,1},{5,0},{6,3},{7,2},{8,13},{9,12},{10,... | collective-permute-start | bytes 1179656 | tf_op jit(solution)/shard_map/ppermute | solution.py:413
  210.2 10.6 %output.1 = bf16[1024,1536]{1,0:T(8,128)(2,1)} custom-call(bf16[1024,1536]{1,0:T(8,128)(2,1)} %bitcast.43, bf16[1536,512]{1,0:T(8,128)(2,1)} %all-gather.8.cloned.1.call-done.first, bf16[1536,512]{1,0:T(8,128)(2,1)} %all-gather.6.cloned.1.call-done.second, bf16[768,1536]{1,0:T(8,128)(2,1)} %all-gather.4.cloned.1.call-done.own_weight, ...), custom_call_target="tpu_custom_call" | custom-call | flops 10000000000 | bytes 12000000 | tf_op jit(solution)/shard_map/output/pallas_call | solution.py:334
  221.9 7.8 %collective-permute-done.15.refs_5_ = bf16[128,1536]{1,0:T(8,128)(2,1)S(1)} collective-permute-done((bf16[128,1536]{1,0:T(8,128)(2,1)}, bf16[128,1536]{1,0:T(8,128)(2,1)S(1)}, u32[]{:S(2)}, u32[]{:S(2)}) %collective-permute-start.15) | collective-permute-done | bytes 393248 | tf_op jit(solution)/shard_map/ppermute | solution.py:413
  229.7 6.2 %collective-permute-done.17.refs_7_ = bf16[128,1536]{1,0:T(8,128)(2,1)} collective-permute-done((bf16[128,1536]{1,0:T(8,128)(2,1)}, bf16[128,1536]{1,0:T(8,128)(2,1)}, u32[]{:S(2)}, u32[]{:S(2)}) %collective-permute-start.17) | collective-permute-done | bytes 393248 | tf_op jit(solution)/shard_map/ppermute | solution.py:413
  236.0 4.5 %assemble.1 = bf16[1024,1536]{1,0:T(8,128)(2,1)} custom-call(s32[8]{0:T(128)} %stack.32.places, bf16[128,1536]{1,0:T(8,128)(2,1)} %finish.1.refs_0_, bf16[128,1536]{1,0:T(8,128)(2,1)} %copy-done.5, bf16[128,1536]{1,0:T(8,128)(2,1)} %copy-done.6, bf16[128,1536]{1,0:T(8,128)(2,1)} %copy-done.7, bf16[128,1536]{1,0:T(8,128)(2,1)} %copy-done.8, ...), custom_call_target="tpu_custom_call" | custom-call | bytes 6000000 | tf_op jit(solution)/shard_map/assemble/pallas_call | solution.py:396
  (79 shorter events, 24.3 us)
Async XLA Ops:
  7.2 59.3 %all-gather.4.cloned.1.call-start = ((), (), s32[]{:S(2)}) async-start(), calls=%async_computation.2 | async-start | bytes 2654208 | tf_op jit(solution)/shard_map/all_gather | solution.py:462
  9.0 116.7 %all-gather.6.cloned.1.call-start = ((), (), s32[]{:S(2)}) async-start(), calls=%async_computation.3 | async-start | bytes 1769472 | tf_op jit(solution)/shard_map/all_gather | solution.py:492
  9.0 16.6 %copy-start.15 = (s32[2,2048]{1,0:T(2,128)S(1)}, s32[2,2048]{1,0:T(2,128)}, u32[]{:S(2)}) copy-start(s32[2,2048]{1,0:T(2,128)} %param.15) | copy-start | bytes 49156
  9.0 16.6 %copy-start.16 = (s32[2]{0:T(128)S(1)}, s32[2]{0:T(128)}, u32[]{:S(2)}) copy-start(s32[2]{0:T(128)} %lengths.1) | copy-start | bytes 28
  19.7 13.0 %collective-permute-start = (bf16[384,512]{1,0:T(8,128)(2,1)}, bf16[384,512]{1,0:T(8,128)(2,1)S(1)}, u32[]{:S(2)}, u32[]{:S(2)}) collective-permute-start(bf16[384,512]{1,0:T(8,128)(2,1)} %get-tuple-element.39), channel_id=1, source_target_pairs={{0,8},{8,16},{16,24},{1,9},{9,17},{17,25},{2,10},{10,18},{18,26},{... | collective-permute-start | bytes 1179656 | tf_op jit(solution)/shard_map/ppermute | solution.py:478
  23.1 12.7 %collective-permute-start.1 = (bf16[384,512]{1,0:T(8,128)(2,1)}, bf16[384,512]{1,0:T(8,128)(2,1)S(1)}, u32[]{:S(2)}, u32[]{:S(2)}) collective-permute-start(bf16[384,512]{1,0:T(8,128)(2,1)} %get-tuple-element.40), channel_id=1, source_target_pairs={{8,0},{16,8},{24,16},{9,1},{17,9},{25,17},{10,2},{18,10},{26,18},{... | collective-permute-start | bytes 1179656 | tf_op jit(solution)/shard_map/ppermute | solution.py:479
  46.8 19.6 %collective-permute-start.2 = (bf16[384,256]{1,0:T(8,128)(2,1)}, bf16[384,256]{1,0:T(8,128)(2,1)S(1)}, u32[]{:S(2)}, u32[]{:S(2)}) collective-permute-start(bf16[384,256]{1,0:T(8,128)(2,1)} %get-tuple-element.48), channel_id=1, source_target_pairs={{0,8},{8,16},{16,24},{1,9},{9,17},{17,25},{2,10},{10,18},{18,26},{... | collective-permute-start | bytes 589832 | tf_op jit(solution)/shard_map/ppermute | solution.py:487
  49.9 16.5 %collective-permute-start.3 = (bf16[384,256]{1,0:T(8,128)(2,1)}, bf16[384,256]{1,0:T(8,128)(2,1)S(1)}, u32[]{:S(2)}, u32[]{:S(2)}) collective-permute-start(bf16[384,256]{1,0:T(8,128)(2,1)} %get-tuple-element.49), channel_id=1, source_target_pairs={{8,0},{16,8},{24,16},{9,1},{17,9},{25,17},{10,2},{18,10},{26,18},{... | collective-permute-start | bytes 589832 | tf_op jit(solution)/shard_map/ppermute | solution.py:486
  72.3 10.0 %copy-start.17 = (bf16[384,256]{1,0:T(8,128)(2,1)S(1)}, bf16[384,256]{1,0:T(8,128)(2,1)}, u32[]{:S(2)}) copy-start(bf16[384,256]{1,0:T(8,128)(2,1)} %get-tuple-element.53) | copy-start | bytes 589828
  72.3 53.4 %all-to-all-start = ((bf16[8,64,1536]{2,1,0:T(8,128)(2,1)}), bf16[8,64,1536]{2,1,0:T(8,128)(2,1)S(1)}, u32[]{:S(2)}, u32[]{:S(2)}) async-start(bf16[8,64,1536]{2,1,0:T(8,128)(2,1)} %bitcast.47), calls=%async_computation | async-start | bytes 3145728 | tf_op jit(solution)/shard_map/all_to_all | solution.py:422
  78.9 108.0 %all-gather.8.cloned.1.call-start = ((), (), s32[]{:S(2)}) async-start(), calls=%async_computation.4 | async-start | bytes 1769472 | tf_op jit(solution)/shard_map/all_gather | solution.py:492
  78.9 7.9 %collective-permute-start.4 = (bf16[384,256]{1,0:T(8,128)(2,1)S(1)}, bf16[384,256]{1,0:T(8,128)(2,1)S(1)}, u32[]{:S(2)}, u32[]{:S(2)}) collective-permute-start(bf16[384,256]{1,0:T(8,128)(2,1)S(1)} %copy-done.18), channel_id=1, source_target_pairs={{0,8},{8,16},{16,24},{1,9},{9,17},{17,25},{2,10},{10,18},{18,26},{... | collective-permute-start | bytes 589832 | tf_op jit(solution)/shard_map/ppermute | solution.py:487
  82.3 7.6 %collective-permute-start.5 = (bf16[384,256]{1,0:T(8,128)(2,1)S(1)}, bf16[384,256]{1,0:T(8,128)(2,1)S(1)}, u32[]{:S(2)}, u32[]{:S(2)}) collective-permute-start(bf16[384,256]{1,0:T(8,128)(2,1)S(1)} %copy-done.17), channel_id=1, source_target_pairs={{8,0},{16,8},{24,16},{9,1},{17,9},{25,17},{10,2},{18,10},{26,18},{... | collective-permute-start | bytes 589832 | tf_op jit(solution)/shard_map/ppermute | solution.py:486
  84.8 102.1 %collective-permute-start.10 = (bf16[768,1536]{1,0:T(8,128)(2,1)}, bf16[768,1536]{1,0:T(8,128)(2,1)}, u32[]{:S(2)}, u32[]{:S(2)}) collective-permute-start(bf16[768,1536]{1,0:T(8,128)(2,1)} %all-gather.4.cloned.1.call-done.own_weight), channel_id=1, source_target_pairs={{0,32},{32,0},{64,96},{96,64},{1,33},{33,1},{65,97},{97,65},{2,34}... | collective-permute-start | bytes 7077896 | tf_op jit(solution)/shard_map/ppermute | solution.py:430
  125.7 9.9 %copy-start = (bf16[8,64,1536]{2,1,0:T(8,128)(2,1)}, bf16[8,64,1536]{2,1,0:T(8,128)(2,1)S(1)}, u32[]{:S(2)}) copy-start(bf16[8,64,1536]{2,1,0:T(8,128)(2,1)S(1)} %all-to-all-done.refs_5_) | copy-start | bytes 4718596
  135.6 6.8 %collective-permute-start.6 = (bf16[4,2,96,768]{3,2,1,0:T(8,128)(2,1)}, bf16[4,2,96,768]{3,2,1,0:T(8,128)(2,1)S(1)}, u32[]{:S(2)}, u32[]{:S(2)}) collective-permute-start(bf16[4,2,96,768]{3,2,1,0:T(8,128)(2,1)} %get-tuple-element.59), channel_id=1, source_target_pairs={{0,32},{32,0},{64,96},{96,64},{1,33},{33,1},{65,97},{97,65},{2,34}... | collective-permute-start | bytes 3538952 | tf_op jit(solution)/shard_map/ppermute | solution.py:430
  135.7 51.2 %all-to-all-start.1 = ((bf16[8,64,1536]{2,1,0:T(8,128)(2,1)}), bf16[8,64,1536]{2,1,0:T(8,128)(2,1)S(1)}, u32[]{:S(2)}, u32[]{:S(2)}) async-start(bf16[8,64,1536]{2,1,0:T(8,128)(2,1)} %bitcast.9), calls=%async_computation.1 | async-start | bytes 3145728 | tf_op jit(solution)/shard_map/all_to_all | solution.py:422
  145.8 9.9 %collective-permute-start.7 = (bf16[2,96,768]{2,1,0:T(8,128)(2,1)S(1)}, bf16[2,96,768]{2,1,0:T(8,128)(2,1)S(1)}, u32[]{:S(2)}, u32[]{:S(2)}) collective-permute-start(bf16[2,96,768]{2,1,0:T(8,128)(2,1)S(1)} %get-tuple-element.69), channel_id=1, source_target_pairs={{0,8},{8,16},{16,24},{24,0},{1,9},{9,17},{17,25},{25,1},{2,10},{10... | collective-permute-start | bytes 884744 | tf_op jit(solution)/shard_map/ppermute | solution.py:438
  147.4 9.3 %collective-permute-start.8 = (bf16[2,96,768]{2,1,0:T(8,128)(2,1)S(1)}, bf16[2,96,768]{2,1,0:T(8,128)(2,1)S(1)}, u32[]{:S(2)}, u32[]{:S(2)}) collective-permute-start(bf16[2,96,768]{2,1,0:T(8,128)(2,1)S(1)} %get-tuple-element.71), channel_id=1, source_target_pairs={{0,24},{8,0},{16,8},{24,16},{1,25},{9,1},{17,9},{25,17},{2,26},{10... | collective-permute-start | bytes 884744 | tf_op jit(solution)/shard_map/ppermute | solution.py:438
  147.9 15.0 %collective-permute-start.9 = (bf16[2,96,768]{2,1,0:T(8,128)(2,1)S(1)}, bf16[2,96,768]{2,1,0:T(8,128)(2,1)S(1)}, u32[]{:S(2)}, u32[]{:S(2)}) collective-permute-start(bf16[2,96,768]{2,1,0:T(8,128)(2,1)S(1)} %get-tuple-element.70), channel_id=1, source_target_pairs={{0,16},{8,24},{16,0},{24,8},{1,17},{9,25},{17,1},{25,9},{2,18},{10... | collective-permute-start | bytes 884744 | tf_op jit(solution)/shard_map/ppermute | solution.py:438
  192.0 13.8 %collective-permute-start.11 = (bf16[128,1536]{1,0:T(8,128)(2,1)}, bf16[128,1536]{1,0:T(8,128)(2,1)S(1)}, u32[]{:S(2)}, u32[]{:S(2)}) collective-permute-start(bf16[128,1536]{1,0:T(8,128)(2,1)} %finish.1.refs_0_), channel_id=1, source_target_pairs={{0,2},{1,3},{2,4},{3,5},{4,6},{5,7},{6,0},{7,1},{8,10},{9,11},{10,... | collective-permute-start | bytes 1179656 | tf_op jit(solution)/shard_map/ppermute | solution.py:413
  193.2 13.4 %collective-permute-start.12 = (bf16[128,1536]{1,0:T(8,128)(2,1)}, bf16[128,1536]{1,0:T(8,128)(2,1)S(1)}, u32[]{:S(2)}, u32[]{:S(2)}) collective-permute-start(bf16[128,1536]{1,0:T(8,128)(2,1)} %finish.1.refs_0_), channel_id=1, source_target_pairs={{0,6},{1,7},{2,0},{3,1},{4,2},{5,3},{6,4},{7,5},{8,14},{9,15},{10,... | collective-permute-start | bytes 1179656 | tf_op jit(solution)/shard_map/ppermute | solution.py:413
  195.2 6.4 %collective-permute-start.18 = (bf16[96,768]{1,0:T(8,128)(2,1)S(1)}, bf16[96,768]{1,0:T(8,128)(2,1)S(1)}, u32[]{:S(2)}, u32[]{:S(2)}) collective-permute-start(bf16[96,768]{1,0:T(8,128)(2,1)S(1)} %fusion.5), channel_id=1, source_target_pairs={{0,64},{32,96},{64,0},{96,32},{1,65},{33,97},{65,1},{97,33},{2,66}... | collective-permute-start | bytes 442376 | tf_op jit(solution)/shard_map/ppermute | solution.py:446
  198.0 23.9 %collective-permute-start.13 = (bf16[128,1536]{1,0:T(8,128)(2,1)}, bf16[128,1536]{1,0:T(8,128)(2,1)S(1)}, u32[]{:S(2)}, u32[]{:S(2)}) collective-permute-start(bf16[128,1536]{1,0:T(8,128)(2,1)} %finish.1.refs_0_), channel_id=1, source_target_pairs={{0,1},{1,0},{2,3},{3,2},{4,5},{5,4},{6,7},{7,6},{8,9},{9,8},{10,11... | collective-permute-start | bytes 1179656 | tf_op jit(solution)/shard_map/ppermute | solution.py:413
  199.6 22.4 %collective-permute-start.14 = (bf16[128,1536]{1,0:T(8,128)(2,1)}, bf16[128,1536]{1,0:T(8,128)(2,1)S(1)}, u32[]{:S(2)}, u32[]{:S(2)}) collective-permute-start(bf16[128,1536]{1,0:T(8,128)(2,1)} %finish.1.refs_0_), channel_id=1, source_target_pairs={{0,3},{1,2},{2,5},{3,4},{4,7},{5,6},{6,1},{7,0},{8,11},{9,10},{10,... | collective-permute-start | bytes 1179656 | tf_op jit(solution)/shard_map/ppermute | solution.py:413
  201.6 28.1 %collective-permute-start.15 = (bf16[128,1536]{1,0:T(8,128)(2,1)}, bf16[128,1536]{1,0:T(8,128)(2,1)S(1)}, u32[]{:S(2)}, u32[]{:S(2)}) collective-permute-start(bf16[128,1536]{1,0:T(8,128)(2,1)} %finish.1.refs_0_), channel_id=1, source_target_pairs={{0,7},{1,6},{2,1},{3,0},{4,3},{5,2},{6,5},{7,4},{8,15},{9,14},{10,... | collective-permute-start | bytes 1179656 | tf_op jit(solution)/shard_map/ppermute | solution.py:413
  205.7 15.1 %copy-start.5 = (bf16[128,1536]{1,0:T(8,128)(2,1)}, bf16[128,1536]{1,0:T(8,128)(2,1)S(1)}, u32[]{:S(2)}) copy-start(bf16[128,1536]{1,0:T(8,128)(2,1)S(1)} %collective-permute-done.11.refs_1_) | copy-start | bytes 1179652
  205.7 24.0 %collective-permute-start.16 = (bf16[128,1536]{1,0:T(8,128)(2,1)}, bf16[128,1536]{1,0:T(8,128)(2,1)S(1)}, u32[]{:S(2)}, u32[]{:S(2)}) collective-permute-start(bf16[128,1536]{1,0:T(8,128)(2,1)} %finish.1.refs_0_), channel_id=1, source_target_pairs={{0,4},{1,5},{2,6},{3,7},{4,0},{5,1},{6,2},{7,3},{8,12},{9,13},{10,... | collective-permute-start | bytes 1179656 | tf_op jit(solution)/shard_map/ppermute | solution.py:413
  206.6 14.2 %copy-start.6 = (bf16[128,1536]{1,0:T(8,128)(2,1)}, bf16[128,1536]{1,0:T(8,128)(2,1)S(1)}, u32[]{:S(2)}) copy-start(bf16[128,1536]{1,0:T(8,128)(2,1)S(1)} %collective-permute-done.12.refs_2_) | copy-start | bytes 1179652
  206.6 29.3 %collective-permute-start.17 = (bf16[128,1536]{1,0:T(8,128)(2,1)}, bf16[128,1536]{1,0:T(8,128)(2,1)}, u32[]{:S(2)}, u32[]{:S(2)}) collective-permute-start(bf16[128,1536]{1,0:T(8,128)(2,1)} %finish.1.refs_0_), channel_id=1, source_target_pairs={{0,5},{1,4},{2,7},{3,6},{4,1},{5,0},{6,3},{7,2},{8,13},{9,12},{10,... | collective-permute-start | bytes 1179656 | tf_op jit(solution)/shard_map/ppermute | solution.py:413
  221.9 14.0 %copy-start.7 = (bf16[128,1536]{1,0:T(8,128)(2,1)}, bf16[128,1536]{1,0:T(8,128)(2,1)S(1)}, u32[]{:S(2)}) copy-start(bf16[128,1536]{1,0:T(8,128)(2,1)S(1)} %collective-permute-done.13.refs_3_) | copy-start | bytes 1179652
  221.9 14.0 %copy-start.8 = (bf16[128,1536]{1,0:T(8,128)(2,1)}, bf16[128,1536]{1,0:T(8,128)(2,1)S(1)}, u32[]{:S(2)}) copy-start(bf16[128,1536]{1,0:T(8,128)(2,1)S(1)} %collective-permute-done.14.refs_4_) | copy-start | bytes 1179652
  (11 other events, 30.8 us)
Sparse Core Ops, SparseCore 0:
  10.3 56.0 all-gather.3
  68.7 56.8 all-gather.5
  128.0 58.9 all-gather.7

commit v7 on v6

--- a/solution.py
+++ b/solution.py
@@ -9,7 +9,6 @@
 CTX = 256
 EPS = 1e-05
 NEG = -1e30
-VMEM_LIMIT = 60 * 1024 * 1024
 
 SHIFTS = ((1, 0), (3, 0), (0, 1), (1, 1), (3, 1), (2, 0), (2, 1))
 
@@ -17,8 +16,8 @@
 BF16 = jnp.bfloat16
 
 
-def params():
-    return pltpu.CompilerParams(vmem_limit_bytes=VMEM_LIMIT)
+def params(mebibytes=60):
+    return pltpu.CompilerParams(vmem_limit_bytes=mebibytes * 1024 * 1024)
 
 
 def dot_nn(a, b):
@@ -140,7 +139,8 @@
             weights = jnp.exp(scores - jnp.max(scores, axis=0, keepdims=True))
             weights = weights * (1.0 / jnp.sum(weights, axis=0, keepdims=True))
             rounded = weights.astype(BF16)
-            mixed[d, cols] = (dot_nn(v_t, rounded) * live[:, cols]).astype(BF16)
+            out = (dot_nn(v_t, rounded) * live[:, cols]).astype(BF16)
+            mixed[:, d, cols] = jnp.broadcast_to(out[None], (mixed.shape[0],) + out.shape)
             grad_w = dot_tn(v_t, g_t)
             total = jnp.sum(weights * grad_w, axis=0, keepdims=True)
             grad_s = (weights * (grad_w - total)).astype(BF16)
@@ -173,14 +173,14 @@
             by_rec(1, frames),
         ],
         out_specs=[
-            whole(width, frames),
+            pl.BlockSpec((8, width, frames), lambda i: (0, 0, 0)),
             whole(width, frames),
             whole(2 * width, frames),
             whole(2 * width, CTX),
             whole(2 * width, CTX),
         ],
         out_shape=[
-            jax.ShapeDtypeStruct((width, frames), BF16),
+            jax.ShapeDtypeStruct((8, width, frames), BF16),
             jax.ShapeDtypeStruct((width, frames), BF16),
             jax.ShapeDtypeStruct((2 * width, frames), F32),
             jax.ShapeDtypeStruct((2 * width, CTX), BF16),
@@ -246,7 +246,7 @@
             cols = slice(rec * frames, (rec + 1) * frames)
             kv[:, cols] = kv_grads(own, left, right)
             query[:, cols] = dq[...]
-            mixed[:, cols] = out[...]
+            mixed[:, cols] = out[0]
 
     turned = normed[...].T
     sums = [
@@ -279,6 +279,11 @@
     def by_step(i, c):
         return (0, (i % 2) * 2 + jnp.where(i < 2, 1 - c[0], c[0]))
 
+    def first_block(piece):
+        if piece.ndim == 2:
+            return pl.BlockSpec(piece.shape, lambda i, c: (0, 0))
+        return pl.BlockSpec((1,) + piece.shape[1:], lambda i, c: (0, 0, 0))
+
     part = (4, 1, block // 4, 4 * width)
     return pl.pallas_call(
         weight_grads_body,
@@ -286,7 +291,7 @@
             num_scalar_prefetch=1,
             grid=(4,),
             in_specs=[pl.BlockSpec((rows, block), by_step)] * 2
-            + [pl.BlockSpec(piece.shape, lambda i, c: (0, 0)) for piece in pieces],
+            + [first_block(piece) for piece in pieces],
             out_specs=[
                 pl.BlockSpec(part, lambda i, c: (0, jnp.minimum(i, 1), 0, 0)),
                 pl.BlockSpec(part, lambda i, c: (0, jnp.maximum(i, 2) - 2, 0, 0)),
@@ -338,7 +343,7 @@
         out_specs=by_row,
         out_shape=jax.ShapeDtypeStruct((rows, model), BF16),
         scratch_shapes=[pltpu.VMEM((depth, CTX), BF16)] * 2,
-        compiler_params=params(),
+        compiler_params=params(28),
         cost_estimate=pl.CostEstimate(flops=10000000000, bytes_accessed=12000000, transcendentals=0),
         name="output",
     )(tokens, *mixed, own_weight, other_weight)
@@ -399,7 +404,7 @@
         in_specs=[pl.BlockSpec(memory_space=pltpu.SMEM)] + [by_col(chunk)] * count,
         out_specs=by_col(count * chunk),
         out_shape=jax.ShapeDtypeStruct((count * chunk, model), BF16),
-        compiler_params=params(),
+        compiler_params=params(16),
         cost_estimate=pl.CostEstimate(flops=0, bytes_accessed=6000000, transcendentals=0),
         name="assemble",
     )(places, *pieces)
@@ -489,21 +494,21 @@
 
     first, second = results
     count = lax.axis_size("chan")
-    mixed = [lax.all_gather(result[4], "chan", tiled=True) for result in results]
-    own_out, first[0] = tie((own_out, first[0]))
-    other_out = core_swap(own_out)
+    mixed = [to_all(result[4]).reshape(count * width, frames) for result in results]
     second[0], _ = tie((second[0], first[0]))
 
     split = lambda back: back.reshape(count, -1, model)
+    second[0], mixed[0], mixed[1] = tie((second[0], mixed[0], mixed[1]))
     second_back = split(back_rows(*second[:4], weight))
-    first[0], second_back = tie((first[0], second_back))
+    first[0], second_back, own_out = tie((first[0], second_back, own_out))
     first_back = split(back_rows(*first[:4], weight))
     parts = [to_all(first_back), to_all(second_back)]
 
-    first[0], first_back, mixed[1], parts[1] = tie((first[0], first_back, mixed[1], parts[1]))
+    first[0], first_back, parts[1] = tie((first[0], first_back, parts[1]))
+    other_out = core_swap(own_out)
     sent, kept = weight_grads(scalar(core), normed, flat_cot, first + second)
     sums = frame_sums(kept + core_swap(sent).astype(F32))
-    sums, parts[0], mixed[0], other_out = tie((sums, parts[0], mixed[0], other_out))
+    sums, parts[0] = tie((sums, parts[0]))
     grad_proj = row_sums(sums).reshape(-1, 4, width)
 
     piece = finish(scalar(me), flat_tokens, flat_cot, norm_gain, parts)

time: 249 us -> 241 us (0.968)
  waiting for transfers between devices: 96.9 us -> 67.5 us
  starting transfers between devices: 52.4 us -> 65 us
  local copies, waits for them, and re-layouts: 10.2 us -> 15.9 us
    all_gather x2 -> x0, waiting for transfers between devices: 52.8 us -> none  [shards(): lax.all_gather(result[4], 'chan', tiled=True)]
    all_to_all x2 -> x4, waiting for transfers between devices: 0.01 us -> 29.2 us  [to_all(): return lax.all_to_all(array, 'chan', 0, 0, tiled=True)]
    all_to_all x2 -> x4, starting transfers between devices: 13.3 us -> 27.5 us  [to_all(): return lax.all_to_all(array, 'chan', 0, 0, tiled=True)]
    unnamed x38 -> x44, local copies, waits for them, and re-layouts: 4.78 us -> 9.36 us
    ppermute x7, waiting for transfers between devices: 14 us -> 9.81 us  [to_peer(): return lax.ppermute(array, 'chan', pairs)]
    all_gather x1, waiting for transfers between devices: 3.35 us -> 0.02 us  [shards(): own_out = lax.all_gather(half_out, 'chan', tiled=True)]
  transfers between devices with their start and end apart: 24 -> 24, of which waited for: 13 -> 13; matrix products, arithmetic and copies ran while one was open for 3% -> 4% of each run, Pallas kernels for 25% -> 23%
where the time goes in v7:
time: 241 us; the launch traced here: 237 us
  Pallas kernels  69.1 us (29%)
  waiting for transfers between devices  67.5 us (28%)
  starting transfers between devices  65 us (27%)
  local copies, waits for them, and re-layouts  15.9 us (7%)
  between operations  14.3 us (6%)
  other arithmetic  5.03 us (2%)
    all_to_all x4, waiting for transfers between devices, to_all(): return lax.all_to_all(array, 'chan', 0, 0, tiled=True)  29.2 us
    all_to_all x4, starting transfers between devices, to_all(): return lax.all_to_all(array, 'chan', 0, 0, tiled=True)  27.5 us
    pallas_call x2, Pallas kernels, attention(): pl.pallas_call(attention_body, grid=(1,), in_specs=[by_rec(width, frames)...  20.4 us
    ppermute x7, starting transfers between devices, to_peer(): return lax.ppermute(array, 'chan', pairs)  14 us
    ppermute x3, waiting for transfers between devices, frame_sums(): got = lax.ppermute(sent, 'frames', [(i, (i + shift) % 4) for i in range(4)])  12.7 us
    pallas_call x1, Pallas kernels, project(): pl.pallas_call(project_body, grid=(rows // CTX,), in_specs=[pl.BlockSpec(...  10.6 us
    pallas_call x2, Pallas kernels, back_rows(): pl.pallas_call(back_body, grid=(model // tile,), in_specs=[full(width, ro...  10.2 us
    pallas_call x1, Pallas kernels, weight_grads(): pl.pallas_call(weight_grads_body, grid_spec=pltpu.PrefetchScalarGridSpec(...  9.92 us
  transfers between devices with their start and end apart: 24, of which 13 were waited for; matrix products, arithmetic and copies ran while one was open for 4% of the time, Pallas kernels for 23%

profile of v7, /device:TPU:18, one launch (start us, length us, event | category | flops | bytes accessed | tf_op | source)
XLA Modules:
  0.0 236.8 jit_solution(14956827358976026022)
XLA Ops:
  9.0 10.6 %project.1 = (bf16[1024,1536]{1,0:T(8,128)(2,1)}, bf16[192,1024]{1,0:T(8,128)(2,1)}, bf16[384,1024]{1,0:T(8,128)(2,1)}, bf16[192,1024]{1,0:T(8,128)(2,1)}, bf16[...) custom-call(s32[2]{0:T(128)} %lengths.1, bf16[1024,1536]{1,0:T(8,128)(2,1)} %bitcast.38, ...), custom_call_target="tpu_custom_call" | custom-call | flops 2400000000 | bytes 15000000 | tf_op jit(solution)/shard_map/project/pallas_call | solution.py:76
  19.6 3.4 %collective-permute-start = (bf16[384,512]{1,0:T(8,128)(2,1)}, bf16[384,512]{1,0:T(8,128)(2,1)S(1)}, u32[]{:S(2)}, u32[]{:S(2)}) collective-permute-start(bf16[384,512]{1,0:T(8,128)(2,1)} %get-tuple-element.38), channel_id=1, source_target_pairs={{0,8},{8,16},{16,24},{1,9},{9,17},{17,25},{2,10},{10,18},{18,26},{... | collective-permute-start | bytes 1179656 | tf_op jit(solution)/shard_map/ppermute | solution.py:483
  23.0 2.5 %collective-permute-start.1 = (bf16[384,512]{1,0:T(8,128)(2,1)}, bf16[384,512]{1,0:T(8,128)(2,1)S(1)}, u32[]{:S(2)}, u32[]{:S(2)}) collective-permute-start(bf16[384,512]{1,0:T(8,128)(2,1)} %get-tuple-element.39), channel_id=1, source_target_pairs={{8,0},{16,8},{24,16},{9,1},{17,9},{25,17},{10,2},{18,10},{26,18},{... | collective-permute-start | bytes 1179656 | tf_op jit(solution)/shard_map/ppermute | solution.py:484
  27.6 5.0 %collective-permute-done.before = bf16[384,512]{1,0:T(8,128)(2,1)S(1)} collective-permute-done((bf16[384,512]{1,0:T(8,128)(2,1)}, bf16[384,512]{1,0:T(8,128)(2,1)S(1)}, u32[]{:S(2)}, u32[]{:S(2)}) %collective-permute-start) | collective-permute-done | bytes 393248 | tf_op jit(solution)/shard_map/ppermute | solution.py:483
  32.6 3.1 %collective-permute-done.1.after = bf16[384,512]{1,0:T(8,128)(2,1)S(1)} collective-permute-done((bf16[384,512]{1,0:T(8,128)(2,1)}, bf16[384,512]{1,0:T(8,128)(2,1)S(1)}, u32[]{:S(2)}, u32[]{:S(2)}) %collective-permute-start.1) | collective-permute-done | bytes 393248 | tf_op jit(solution)/shard_map/ppermute | solution.py:484
  36.5 10.2 %attention.3 = (bf16[8,192,512]{2,1,0:T(8,128)(2,1)}, bf16[192,512]{1,0:T(8,128)(2,1)}, f32[384,512]{1,0:T(8,128)}, bf16[384,256]{1,0:T(8,128)(2,1)}, bf16[384,256]{1,0:T(8,128)(2,1)}) custom-call(bf16[192,1024]{1,0:T(8,128)(2,1)} %get-tuple-element.36.q, bf16[384,1024]{1,0:T(8,128)(2,1)} %get-tuple-element.37.kv, bf16[384,512]{1,0:T(8,128)(2,1)} %copy-done.12, ...), custom_call_target="tpu_custom_call" | custom-call | flops 1000 | bytes 1000 | tf_op jit(solution)/shard_map/attention/pallas_call | solution.py:162
  46.7 8.3 %all-to-all-start.1 = ((bf16[8,192,512]{2,1,0:T(8,128)(2,1)}), bf16[8,192,512]{2,1,0:T(8,128)(2,1)S(1)}, u32[]{:S(2)}, u32[]{:S(2)}) async-start(bf16[8,192,512]{2,1,0:T(8,128)(2,1)} %get-tuple-element.46.rest_9_), calls=%async_computation.1 | async-start | bytes 3145728 | tf_op jit(solution)/shard_map/all_to_all | solution.py:427
  55.0 10.2 %attention.2 = (bf16[8,192,512]{2,1,0:T(8,128)(2,1)}, bf16[192,512]{1,0:T(8,128)(2,1)}, f32[384,512]{1,0:T(8,128)}, bf16[384,256]{1,0:T(8,128)(2,1)}, bf16[384,256]{1,0:T(8,128)(2,1)}) custom-call(bf16[192,1024]{1,0:T(8,128)(2,1)} %get-tuple-element.36.q, bf16[384,1024]{1,0:T(8,128)(2,1)} %get-tuple-element.37.kv, bf16[384,512]{1,0:T(8,128)(2,1)} %copy-done.12, ...), custom_call_target="tpu_custom_call" | custom-call | flops 1000 | bytes 1000 | tf_op jit(solution)/shard_map/attention/pallas_call | solution.py:162
  65.2 12.5 %all-to-all-done.1 = bf16[8,192,512]{2,1,0:T(8,128)(2,1)S(1)} async-done(((bf16[8,192,512]{2,1,0:T(8,128)(2,1)}), bf16[8,192,512]{2,1,0:T(8,128)(2,1)S(1)}, u32[]{:S(2)}, u32[]{:S(2)}) %all-to-all-start.1) | async-done | bytes 1572896 | tf_op jit(solution)/shard_map/all_to_all | solution.py:427
  77.7 6.7 %all-to-all-start = ((bf16[8,192,512]{2,1,0:T(8,128)(2,1)}), bf16[8,192,512]{2,1,0:T(8,128)(2,1)S(1)}, u32[]{:S(2)}, u32[]{:S(2)}) async-start(bf16[8,192,512]{2,1,0:T(8,128)(2,1)} %get-tuple-element.45.rest_4_), calls=%async_computation | async-start | bytes 3145728 | tf_op jit(solution)/shard_map/all_to_all | solution.py:427
  84.4 3.4 %collective-permute-start.2 = (bf16[384,256]{1,0:T(8,128)(2,1)}, bf16[384,256]{1,0:T(8,128)(2,1)S(1)}, u32[]{:S(2)}, u32[]{:S(2)}) collective-permute-start(bf16[384,256]{1,0:T(8,128)(2,1)} %get-tuple-element.49), channel_id=1, source_target_pairs={{0,8},{8,16},{16,24},{1,9},{9,17},{17,25},{2,10},{10,18},{18,26},{... | collective-permute-start | bytes 589832 | tf_op jit(solution)/shard_map/ppermute | solution.py:492
  87.8 2.5 %collective-permute-start.3 = (bf16[384,256]{1,0:T(8,128)(2,1)}, bf16[384,256]{1,0:T(8,128)(2,1)S(1)}, u32[]{:S(2)}, u32[]{:S(2)}) collective-permute-start(bf16[384,256]{1,0:T(8,128)(2,1)} %get-tuple-element.50), channel_id=1, source_target_pairs={{8,0},{16,8},{24,16},{9,1},{17,9},{25,17},{10,2},{18,10},{26,18},{... | collective-permute-start | bytes 589832 | tf_op jit(solution)/shard_map/ppermute | solution.py:491
  90.3 14.0 %all-to-all-done = bf16[8,192,512]{2,1,0:T(8,128)(2,1)S(1)} async-done(((bf16[8,192,512]{2,1,0:T(8,128)(2,1)}), bf16[8,192,512]{2,1,0:T(8,128)(2,1)S(1)}, u32[]{:S(2)}, u32[]{:S(2)}) %all-to-all-start) | async-done | bytes 1572896 | tf_op jit(solution)/shard_map/all_to_all | solution.py:427
  105.0 5.1 %back.2 = bf16[512,1536]{1,0:T(8,128)(2,1)} custom-call(bf16[192,512]{1,0:T(8,128)(2,1)} %get-tuple-element.47.dq.rest_5_, f32[384,512]{1,0:T(8,128)} %get-tuple-element.48.own.rest_6_, bf16[384,256]{1,0:T(8,128)(2,1)} %copy-done.14, bf16[384,256]{1,0:T(8,128)(2,1)} %copy-done.15, bf16[576,1536]{1,0:T(8,128)(2,1)} %bitcast.49), custom_call_target="tpu_custom_call" | custom-call | flops 900000000 | bytes 4000000 | tf_op jit(solution)/shard_map/back/pallas_call | solution.py:218
  110.2 6.4 %all-to-all-start.2 = ((bf16[8,64,1536]{2,1,0:T(8,128)(2,1)}), bf16[8,64,1536]{2,1,0:T(8,128)(2,1)S(1)}, u32[]{:S(2)}, u32[]{:S(2)}) async-start(bf16[8,64,1536]{2,1,0:T(8,128)(2,1)} %bitcast.51), calls=%async_computation.2 | async-start | bytes 3145728 | tf_op jit(solution)/shard_map/all_to_all | solution.py:427
  116.5 3.4 %collective-permute-start.4 = (bf16[384,256]{1,0:T(8,128)(2,1)S(1)}, bf16[384,256]{1,0:T(8,128)(2,1)S(1)}, u32[]{:S(2)}, u32[]{:S(2)}) collective-permute-start(bf16[384,256]{1,0:T(8,128)(2,1)S(1)} %copy-done.21), channel_id=1, source_target_pairs={{0,8},{8,16},{16,24},{1,9},{9,17},{17,25},{2,10},{10,18},{18,26},{... | collective-permute-start | bytes 589832 | tf_op jit(solution)/shard_map/ppermute | solution.py:492
  119.9 2.5 %collective-permute-start.5 = (bf16[384,256]{1,0:T(8,128)(2,1)S(1)}, bf16[384,256]{1,0:T(8,128)(2,1)S(1)}, u32[]{:S(2)}, u32[]{:S(2)}) collective-permute-start(bf16[384,256]{1,0:T(8,128)(2,1)S(1)} %copy-done.20), channel_id=1, source_target_pairs={{8,0},{16,8},{24,16},{9,1},{17,9},{25,17},{10,2},{18,10},{26,18},{... | collective-permute-start | bytes 589832 | tf_op jit(solution)/shard_map/ppermute | solution.py:491
  124.1 3.4 %collective-permute-done.5.right.rest_3_ = bf16[384,256]{1,0:T(8,128)(2,1)S(1)} collective-permute-done((bf16[384,256]{1,0:T(8,128)(2,1)S(1)}, bf16[384,256]{1,0:T(8,128)(2,1)S(1)}, u32[]{:S(2)}, u32[]{:S(2)}) %collective-permute-start.5) | collective-permute-done | bytes 196640 | tf_op jit(solution)/shard_map/ppermute | solution.py:491
  128.2 5.1 %back.3 = bf16[512,1536]{1,0:T(8,128)(2,1)} custom-call(bf16[192,512]{1,0:T(8,128)(2,1)} %get-tuple-element.56.dq.rest_0_, f32[384,512]{1,0:T(8,128)} %get-tuple-element.52.own.rest_1_, bf16[384,256]{1,0:T(8,128)(2,1)} %copy-done.16, bf16[384,256]{1,0:T(8,128)(2,1)} %copy-done.17, bf16[576,1536]{1,0:T(8,128)(2,1)} %bitcast.50), custom_call_target="tpu_custom_call" | custom-call | flops 900000000 | bytes 4000000 | tf_op jit(solution)/shard_map/back/pallas_call | solution.py:218
  133.3 2.7 %all-to-all-done.2.refs_5_ = bf16[8,64,1536]{2,1,0:T(8,128)(2,1)S(1)} async-done(((bf16[8,64,1536]{2,1,0:T(8,128)(2,1)}), bf16[8,64,1536]{2,1,0:T(8,128)(2,1)S(1)}, u32[]{:S(2)}, u32[]{:S(2)}) %all-to-all-start.2) | async-done | bytes 1572896 | tf_op jit(solution)/shard_map/all_to_all | solution.py:427
  136.0 9.9 %weight_grads.1 = (bf16[4,2,96,768]{3,2,1,0:T(8,128)(2,1)}, f32[4,2,96,768]{3,2,1,0:T(8,128)}) custom-call(s32[1]{0:T(128)} %bitcast.3.core, bf16[1024,1536]{1,0:T(8,128)(2,1)} %get-tuple-element.35.normed, bf16[1024,1536]{1,0:T(8,128)(2,1)} %bitcast.45, bf16[192,512]{1,0:T(8,128)(2,1)} %get-tuple-element.56.dq.rest_0_, ...), custom_call_target="tpu_custom_call" | custom-call | flops 10000000000 | bytes 12000000 | tf_op jit(solution)/shard_map/weight_grads/pallas_call | solution.py:288
  146.6 6.2 %all-to-all-start.3 = ((bf16[8,64,1536]{2,1,0:T(8,128)(2,1)}), bf16[8,64,1536]{2,1,0:T(8,128)(2,1)S(1)}, u32[]{:S(2)}, u32[]{:S(2)}) async-start(bf16[8,64,1536]{2,1,0:T(8,128)(2,1)} %bitcast.11), calls=%async_computation.3 | async-start | bytes 3145728 | tf_op jit(solution)/shard_map/all_to_all | solution.py:427
  160.3 5.8 %collective-permute-done.7 = bf16[2,96,768]{2,1,0:T(8,128)(2,1)S(1)} collective-permute-done((bf16[2,96,768]{2,1,0:T(8,128)(2,1)S(1)}, bf16[2,96,768]{2,1,0:T(8,128)(2,1)S(1)}, u32[]{:S(2)}, u32[]{:S(2)}) %collective-permute-start.7) | collective-permute-done | bytes 294944 | tf_op jit(solution)/shard_map/ppermute | solution.py:443
  167.0 6.0 %collective-permute-done.9 = bf16[2,96,768]{2,1,0:T(8,128)(2,1)S(1)} collective-permute-done((bf16[2,96,768]{2,1,0:T(8,128)(2,1)S(1)}, bf16[2,96,768]{2,1,0:T(8,128)(2,1)S(1)}, u32[]{:S(2)}, u32[]{:S(2)}) %collective-permute-start.9) | collective-permute-done | bytes 294944 | tf_op jit(solution)/shard_map/ppermute | solution.py:443
  176.3 4.0 %finish.1.refs_0_ = bf16[128,1536]{1,0:T(8,128)(2,1)} custom-call(s32[1]{0:T(128)} %bitcast.place, f32[1536]{0:T(1024)} %gain.3, bf16[1024,1536]{1,0:T(8,128)(2,1)} %bitcast.39, bf16[1024,1536]{1,0:T(8,128)(2,1)} %bitcast.46, bf16[8,64,1536]{2,1,0:T(8,128)(2,1)} %copy-done.9, bf16[1024,1536]{1,0:T(8,128)(2,1)} %bitcast.40, bf16[1024,1536]{1,0:T(8,128)(2,1)} %bitcast.47, ...), custom_call_target="tpu_custom_call" | custom-call | flops 10000000 | bytes 5000000 | tf_op jit(solution)/shard_map/finish/pallas_call | solution.py:370
  186.9 2.8 %collective-permute-start.14 = (bf16[128,1536]{1,0:T(8,128)(2,1)}, bf16[128,1536]{1,0:T(8,128)(2,1)}, u32[]{:S(2)}, u32[]{:S(2)}) collective-permute-start(bf16[128,1536]{1,0:T(8,128)(2,1)} %finish.1.refs_0_), channel_id=1, source_target_pairs={{0,3},{1,2},{2,5},{3,4},{4,7},{5,6},{6,1},{7,0},{8,11},{9,10},{10,... | collective-permute-start | bytes 1179656 | tf_op jit(solution)/shard_map/ppermute | solution.py:418
  189.7 2.5 %collective-permute-done.18 = bf16[96,768]{1,0:T(8,128)(2,1)} collective-permute-done((bf16[96,768]{1,0:T(8,128)(2,1)}, bf16[96,768]{1,0:T(8,128)(2,1)}, u32[]{:S(2)}, u32[]{:S(2)}) %collective-permute-start.18) | collective-permute-done | bytes 147488 | tf_op jit(solution)/shard_map/ppermute | solution.py:451
  195.3 5.2 %collective-permute-start.17 = (bf16[128,1536]{1,0:T(8,128)(2,1)}, bf16[128,1536]{1,0:T(8,128)(2,1)}, u32[]{:S(2)}, u32[]{:S(2)}) collective-permute-start(bf16[128,1536]{1,0:T(8,128)(2,1)} %finish.1.refs_0_), channel_id=1, source_target_pairs={{0,5},{1,4},{2,7},{3,6},{4,1},{5,0},{6,3},{7,2},{8,13},{9,12},{10,... | collective-permute-start | bytes 1179656 | tf_op jit(solution)/shard_map/ppermute | solution.py:418
  203.3 9.7 %output.1 = bf16[1024,1536]{1,0:T(8,128)(2,1)} custom-call(bf16[1024,1536]{1,0:T(8,128)(2,1)S(1)} %bitcast.41, bf16[1536,512]{1,0:T(8,128)(2,1)S(1)} %bitcast.43, bf16[1536,512]{1,0:T(8,128)(2,1)S(1)} %bitcast.42, bf16[768,1536]{1,0:T(8,128)(2,1)} %all-gather.2.cloned.1.call-done.own_weight, bf16[768,1536]{1,0:T(8,128)(2,1)} %collective-permute-done.11.other_weight), custom_call_target="tpu_custom_call" | custom-call | flops 10000000000 | bytes 12000000 | tf_op jit(solution)/shard_map/output/pallas_call | solution.py:339
  215.0 3.3 %collective-permute-done.15.refs_5_ = bf16[128,1536]{1,0:T(8,128)(2,1)} collective-permute-done((bf16[128,1536]{1,0:T(8,128)(2,1)}, bf16[128,1536]{1,0:T(8,128)(2,1)}, u32[]{:S(2)}, u32[]{:S(2)}) %collective-permute-start.15) | collective-permute-done | bytes 393248 | tf_op jit(solution)/shard_map/ppermute | solution.py:418
  218.3 6.5 %collective-permute-done.17.refs_7_ = bf16[128,1536]{1,0:T(8,128)(2,1)} collective-permute-done((bf16[128,1536]{1,0:T(8,128)(2,1)}, bf16[128,1536]{1,0:T(8,128)(2,1)}, u32[]{:S(2)}, u32[]{:S(2)}) %collective-permute-start.17) | collective-permute-done | bytes 393248 | tf_op jit(solution)/shard_map/ppermute | solution.py:418
  225.8 4.2 %assemble.1 = bf16[1024,1536]{1,0:T(8,128)(2,1)} custom-call(s32[8]{0:T(128)S(1)} %stack.32.places, bf16[128,1536]{1,0:T(8,128)(2,1)S(1)} %copy-done.5, bf16[128,1536]{1,0:T(8,128)(2,1)S(1)} %copy-done.7, bf16[128,1536]{1,0:T(8,128)(2,1)} %collective-permute-done.12.refs_2_, bf16[128,1536]{1,0:T(8,128)(2,1)} %collective-permute-done.13.refs_3_, ...), custom_call_target="tpu_custom_call" | custom-call | bytes 6000000 | tf_op jit(solution)/shard_map/assemble/pallas_call | solution.py:401
  (83 shorter events, 35.5 us)
Async XLA Ops:
  7.2 103.0 %all-gather.2.cloned.1.call-start = ((), (), s32[]{:S(2)}) async-start(), calls=%async_computation.4 | async-start | bytes 2654208 | tf_op jit(solution)/shard_map/all_gather | solution.py:467
  9.0 16.6 %copy-start.18 = (s32[2,2048]{1,0:T(2,128)S(1)}, s32[2,2048]{1,0:T(2,128)}, u32[]{:S(2)}) copy-start(s32[2,2048]{1,0:T(2,128)} %param.15) | copy-start | bytes 49156
  9.0 16.6 %copy-start.19 = (s32[2]{0:T(128)S(1)}, s32[2]{0:T(128)}, u32[]{:S(2)}) copy-start(s32[2]{0:T(128)} %lengths.1) | copy-start | bytes 28
  19.6 13.0 %collective-permute-start = (bf16[384,512]{1,0:T(8,128)(2,1)}, bf16[384,512]{1,0:T(8,128)(2,1)S(1)}, u32[]{:S(2)}, u32[]{:S(2)}) collective-permute-start(bf16[384,512]{1,0:T(8,128)(2,1)} %get-tuple-element.38), channel_id=1, source_target_pairs={{0,8},{8,16},{16,24},{1,9},{9,17},{17,25},{2,10},{10,18},{18,26},{... | collective-permute-start | bytes 1179656 | tf_op jit(solution)/shard_map/ppermute | solution.py:483
  23.0 12.7 %collective-permute-start.1 = (bf16[384,512]{1,0:T(8,128)(2,1)}, bf16[384,512]{1,0:T(8,128)(2,1)S(1)}, u32[]{:S(2)}, u32[]{:S(2)}) collective-permute-start(bf16[384,512]{1,0:T(8,128)(2,1)} %get-tuple-element.39), channel_id=1, source_target_pairs={{8,0},{16,8},{24,16},{9,1},{17,9},{25,17},{10,2},{18,10},{26,18},{... | collective-permute-start | bytes 1179656 | tf_op jit(solution)/shard_map/ppermute | solution.py:484
  46.7 31.0 %all-to-all-start.1 = ((bf16[8,192,512]{2,1,0:T(8,128)(2,1)}), bf16[8,192,512]{2,1,0:T(8,128)(2,1)S(1)}, u32[]{:S(2)}, u32[]{:S(2)}) async-start(bf16[8,192,512]{2,1,0:T(8,128)(2,1)} %get-tuple-element.46.rest_9_), calls=%async_computation.1 | async-start | bytes 3145728 | tf_op jit(solution)/shard_map/all_to_all | solution.py:427
  77.7 32.4 %copy-start.1 = (bf16[8,192,512]{2,1,0:T(8,128)(2,1)}, bf16[8,192,512]{2,1,0:T(8,128)(2,1)S(1)}, u32[]{:S(2)}) copy-start(bf16[8,192,512]{2,1,0:T(8,128)(2,1)S(1)} %all-to-all-done.1) | copy-start | bytes 4718596
  77.7 26.6 %all-to-all-start = ((bf16[8,192,512]{2,1,0:T(8,128)(2,1)}), bf16[8,192,512]{2,1,0:T(8,128)(2,1)S(1)}, u32[]{:S(2)}, u32[]{:S(2)}) async-start(bf16[8,192,512]{2,1,0:T(8,128)(2,1)} %get-tuple-element.45.rest_4_), calls=%async_computation | async-start | bytes 3145728 | tf_op jit(solution)/shard_map/all_to_all | solution.py:427
  84.4 19.8 %collective-permute-start.2 = (bf16[384,256]{1,0:T(8,128)(2,1)}, bf16[384,256]{1,0:T(8,128)(2,1)S(1)}, u32[]{:S(2)}, u32[]{:S(2)}) collective-permute-start(bf16[384,256]{1,0:T(8,128)(2,1)} %get-tuple-element.49), channel_id=1, source_target_pairs={{0,8},{8,16},{16,24},{1,9},{9,17},{17,25},{2,10},{10,18},{18,26},{... | collective-permute-start | bytes 589832 | tf_op jit(solution)/shard_map/ppermute | solution.py:492
  87.8 16.5 %collective-permute-start.3 = (bf16[384,256]{1,0:T(8,128)(2,1)}, bf16[384,256]{1,0:T(8,128)(2,1)S(1)}, u32[]{:S(2)}, u32[]{:S(2)}) collective-permute-start(bf16[384,256]{1,0:T(8,128)(2,1)} %get-tuple-element.50), channel_id=1, source_target_pairs={{8,0},{16,8},{24,16},{9,1},{17,9},{25,17},{10,2},{18,10},{26,18},{... | collective-permute-start | bytes 589832 | tf_op jit(solution)/shard_map/ppermute | solution.py:491
  110.1 9.8 %copy-start.20 = (bf16[384,256]{1,0:T(8,128)(2,1)S(1)}, bf16[384,256]{1,0:T(8,128)(2,1)}, u32[]{:S(2)}) copy-start(bf16[384,256]{1,0:T(8,128)(2,1)} %get-tuple-element.54) | copy-start | bytes 589828
  110.2 25.9 %all-to-all-start.2 = ((bf16[8,64,1536]{2,1,0:T(8,128)(2,1)}), bf16[8,64,1536]{2,1,0:T(8,128)(2,1)S(1)}, u32[]{:S(2)}, u32[]{:S(2)}) async-start(bf16[8,64,1536]{2,1,0:T(8,128)(2,1)} %bitcast.51), calls=%async_computation.2 | async-start | bytes 3145728 | tf_op jit(solution)/shard_map/all_to_all | solution.py:427
  116.5 7.6 %collective-permute-start.4 = (bf16[384,256]{1,0:T(8,128)(2,1)S(1)}, bf16[384,256]{1,0:T(8,128)(2,1)S(1)}, u32[]{:S(2)}, u32[]{:S(2)}) collective-permute-start(bf16[384,256]{1,0:T(8,128)(2,1)S(1)} %copy-done.21), channel_id=1, source_target_pairs={{0,8},{8,16},{16,24},{1,9},{9,17},{17,25},{2,10},{10,18},{18,26},{... | collective-permute-start | bytes 589832 | tf_op jit(solution)/shard_map/ppermute | solution.py:492
  119.9 7.6 %collective-permute-start.5 = (bf16[384,256]{1,0:T(8,128)(2,1)S(1)}, bf16[384,256]{1,0:T(8,128)(2,1)S(1)}, u32[]{:S(2)}, u32[]{:S(2)}) collective-permute-start(bf16[384,256]{1,0:T(8,128)(2,1)S(1)} %copy-done.20), channel_id=1, source_target_pairs={{8,0},{16,8},{24,16},{9,1},{17,9},{25,17},{10,2},{18,10},{26,18},{... | collective-permute-start | bytes 589832 | tf_op jit(solution)/shard_map/ppermute | solution.py:491
  136.0 9.9 %copy-start.8 = (bf16[8,64,1536]{2,1,0:T(8,128)(2,1)}, bf16[8,64,1536]{2,1,0:T(8,128)(2,1)S(1)}, u32[]{:S(2)}) copy-start(bf16[8,64,1536]{2,1,0:T(8,128)(2,1)S(1)} %all-to-all-done.2.refs_5_) | copy-start | bytes 4718596
  146.0 6.7 %collective-permute-start.6 = (bf16[4,2,96,768]{3,2,1,0:T(8,128)(2,1)}, bf16[4,2,96,768]{3,2,1,0:T(8,128)(2,1)S(1)}, u32[]{:S(2)}, u32[]{:S(2)}) collective-permute-start(bf16[4,2,96,768]{3,2,1,0:T(8,128)(2,1)} %get-tuple-element.58), channel_id=1, source_target_pairs={{0,32},{32,0},{64,96},{96,64},{1,33},{33,1},{65,97},{97,65},{2,34}... | collective-permute-start | bytes 3538952 | tf_op jit(solution)/shard_map/ppermute | solution.py:435
  146.1 40.9 %collective-permute-start.11 = (bf16[768,1536]{1,0:T(8,128)(2,1)}, bf16[768,1536]{1,0:T(8,128)(2,1)}, u32[]{:S(2)}, u32[]{:S(2)}) collective-permute-start(bf16[768,1536]{1,0:T(8,128)(2,1)} %all-gather.2.cloned.1.call-done.own_weight), channel_id=1, source_target_pairs={{0,32},{32,0},{64,96},{96,64},{1,33},{33,1},{65,97},{97,65},{2,34}... | collective-permute-start | bytes 7077896 | tf_op jit(solution)/shard_map/ppermute | solution.py:435
  146.6 28.6 %all-to-all-start.3 = ((bf16[8,64,1536]{2,1,0:T(8,128)(2,1)}), bf16[8,64,1536]{2,1,0:T(8,128)(2,1)S(1)}, u32[]{:S(2)}, u32[]{:S(2)}) async-start(bf16[8,64,1536]{2,1,0:T(8,128)(2,1)} %bitcast.11), calls=%async_computation.3 | async-start | bytes 3145728 | tf_op jit(solution)/shard_map/all_to_all | solution.py:427
  156.2 10.0 %collective-permute-start.7 = (bf16[2,96,768]{2,1,0:T(8,128)(2,1)S(1)}, bf16[2,96,768]{2,1,0:T(8,128)(2,1)S(1)}, u32[]{:S(2)}, u32[]{:S(2)}) collective-permute-start(bf16[2,96,768]{2,1,0:T(8,128)(2,1)S(1)} %get-tuple-element.67), channel_id=1, source_target_pairs={{0,8},{8,16},{16,24},{24,0},{1,9},{9,17},{17,25},{25,1},{2,10},{10... | collective-permute-start | bytes 884744 | tf_op jit(solution)/shard_map/ppermute | solution.py:443
  157.7 9.3 %collective-permute-start.8 = (bf16[2,96,768]{2,1,0:T(8,128)(2,1)S(1)}, bf16[2,96,768]{2,1,0:T(8,128)(2,1)S(1)}, u32[]{:S(2)}, u32[]{:S(2)}) collective-permute-start(bf16[2,96,768]{2,1,0:T(8,128)(2,1)S(1)} %get-tuple-element.69), channel_id=1, source_target_pairs={{0,24},{8,0},{16,8},{24,16},{1,25},{9,1},{17,9},{25,17},{2,26},{10... | collective-permute-start | bytes 884744 | tf_op jit(solution)/shard_map/ppermute | solution.py:443
  158.3 14.8 %collective-permute-start.9 = (bf16[2,96,768]{2,1,0:T(8,128)(2,1)S(1)}, bf16[2,96,768]{2,1,0:T(8,128)(2,1)S(1)}, u32[]{:S(2)}, u32[]{:S(2)}) collective-permute-start(bf16[2,96,768]{2,1,0:T(8,128)(2,1)S(1)} %get-tuple-element.68), channel_id=1, source_target_pairs={{0,16},{8,24},{16,0},{24,8},{1,17},{9,25},{17,1},{25,9},{2,18},{10... | collective-permute-start | bytes 884744 | tf_op jit(solution)/shard_map/ppermute | solution.py:443
  176.3 24.2 %copy-start = (bf16[2,512,1536]{2,1,0:T(8,128)(2,1)S(1)}, bf16[2,512,1536]{2,1,0:T(8,128)(2,1)}, u32[]{:S(2)}) copy-start(bf16[2,512,1536]{2,1,0:T(8,128)(2,1)} %param.8) | copy-start | bytes 9437188
  180.3 13.4 %collective-permute-start.10 = (bf16[128,1536]{1,0:T(8,128)(2,1)}, bf16[128,1536]{1,0:T(8,128)(2,1)S(1)}, u32[]{:S(2)}, u32[]{:S(2)}) collective-permute-start(bf16[128,1536]{1,0:T(8,128)(2,1)} %finish.1.refs_0_), channel_id=1, source_target_pairs={{0,2},{1,3},{2,4},{3,5},{4,6},{5,7},{6,0},{7,1},{8,10},{9,11},{10,... | collective-permute-start | bytes 1179656 | tf_op jit(solution)/shard_map/ppermute | solution.py:418
  181.8 13.5 %collective-permute-start.12 = (bf16[128,1536]{1,0:T(8,128)(2,1)}, bf16[128,1536]{1,0:T(8,128)(2,1)}, u32[]{:S(2)}, u32[]{:S(2)}) collective-permute-start(bf16[128,1536]{1,0:T(8,128)(2,1)} %finish.1.refs_0_), channel_id=1, source_target_pairs={{0,6},{1,7},{2,0},{3,1},{4,2},{5,3},{6,4},{7,5},{8,14},{9,15},{10,... | collective-permute-start | bytes 1179656 | tf_op jit(solution)/shard_map/ppermute | solution.py:418
  185.2 7.0 %collective-permute-start.18 = (bf16[96,768]{1,0:T(8,128)(2,1)}, bf16[96,768]{1,0:T(8,128)(2,1)}, u32[]{:S(2)}, u32[]{:S(2)}) collective-permute-start(bf16[96,768]{1,0:T(8,128)(2,1)} %fusion.5), channel_id=1, source_target_pairs={{0,64},{32,96},{64,0},{96,32},{1,65},{33,97},{65,1},{97,33},{2,66}... | collective-permute-start | bytes 442376 | tf_op jit(solution)/shard_map/ppermute | solution.py:451
  186.5 28.5 %collective-permute-start.13 = (bf16[128,1536]{1,0:T(8,128)(2,1)}, bf16[128,1536]{1,0:T(8,128)(2,1)}, u32[]{:S(2)}, u32[]{:S(2)}) collective-permute-start(bf16[128,1536]{1,0:T(8,128)(2,1)} %finish.1.refs_0_), channel_id=1, source_target_pairs={{0,1},{1,0},{2,3},{3,2},{4,5},{5,4},{6,7},{7,6},{8,9},{9,8},{10,11... | collective-permute-start | bytes 1179656 | tf_op jit(solution)/shard_map/ppermute | solution.py:418
  186.9 28.0 %collective-permute-start.14 = (bf16[128,1536]{1,0:T(8,128)(2,1)}, bf16[128,1536]{1,0:T(8,128)(2,1)}, u32[]{:S(2)}, u32[]{:S(2)}) collective-permute-start(bf16[128,1536]{1,0:T(8,128)(2,1)} %finish.1.refs_0_), channel_id=1, source_target_pairs={{0,3},{1,2},{2,5},{3,4},{4,7},{5,6},{6,1},{7,0},{8,11},{9,10},{10,... | collective-permute-start | bytes 1179656 | tf_op jit(solution)/shard_map/ppermute | solution.py:418
  192.2 26.1 %collective-permute-start.15 = (bf16[128,1536]{1,0:T(8,128)(2,1)}, bf16[128,1536]{1,0:T(8,128)(2,1)}, u32[]{:S(2)}, u32[]{:S(2)}) collective-permute-start(bf16[128,1536]{1,0:T(8,128)(2,1)} %finish.1.refs_0_), channel_id=1, source_target_pairs={{0,7},{1,6},{2,1},{3,0},{4,3},{5,2},{6,5},{7,4},{8,15},{9,14},{10,... | collective-permute-start | bytes 1179656 | tf_op jit(solution)/shard_map/ppermute | solution.py:418
  194.5 23.8 %collective-permute-start.16 = (bf16[128,1536]{1,0:T(8,128)(2,1)}, bf16[128,1536]{1,0:T(8,128)(2,1)}, u32[]{:S(2)}, u32[]{:S(2)}) collective-permute-start(bf16[128,1536]{1,0:T(8,128)(2,1)} %finish.1.refs_0_), channel_id=1, source_target_pairs={{0,4},{1,5},{2,6},{3,7},{4,0},{5,1},{6,2},{7,3},{8,12},{9,13},{10,... | collective-permute-start | bytes 1179656 | tf_op jit(solution)/shard_map/ppermute | solution.py:418
  195.3 29.5 %collective-permute-start.17 = (bf16[128,1536]{1,0:T(8,128)(2,1)}, bf16[128,1536]{1,0:T(8,128)(2,1)}, u32[]{:S(2)}, u32[]{:S(2)}) collective-permute-start(bf16[128,1536]{1,0:T(8,128)(2,1)} %finish.1.refs_0_), channel_id=1, source_target_pairs={{0,5},{1,4},{2,7},{3,6},{4,1},{5,0},{6,3},{7,2},{8,13},{9,12},{10,... | collective-permute-start | bytes 1179656 | tf_op jit(solution)/shard_map/ppermute | solution.py:418
  203.3 9.7 %copy-start.11 = (f32[2,96,768]{2,1,0:T(8,128)S(1)}, f32[2,96,768]{2,1,0:T(8,128)}, u32[]{:S(2)}) copy-start(f32[2,96,768]{2,1,0:T(8,128)} %fusion.1) | copy-start | bytes 1769476
  203.3 21.4 %copy-start.5 = (bf16[128,1536]{1,0:T(8,128)(2,1)S(1)}, bf16[128,1536]{1,0:T(8,128)(2,1)}, u32[]{:S(2)}) copy-start(bf16[128,1536]{1,0:T(8,128)(2,1)} %finish.1.refs_0_) | copy-start | bytes 1179652
  (14 other events, 28.8 us)
Sparse Core Ops, SparseCore 0:
  10.3 68.3 all-gather.1

commit v8 on v6

--- a/solution.py
+++ b/solution.py
@@ -9,7 +9,6 @@
 CTX = 256
 EPS = 1e-05
 NEG = -1e30
-VMEM_LIMIT = 60 * 1024 * 1024
 
 SHIFTS = ((1, 0), (3, 0), (0, 1), (1, 1), (3, 1), (2, 0), (2, 1))
 
@@ -17,8 +16,8 @@
 BF16 = jnp.bfloat16
 
 
-def params():
-    return pltpu.CompilerParams(vmem_limit_bytes=VMEM_LIMIT)
+def params(mebibytes=60):
+    return pltpu.CompilerParams(vmem_limit_bytes=mebibytes * 1024 * 1024)
 
 
 def dot_nn(a, b):
@@ -307,41 +306,40 @@
     )(core, normed, cotangent, *pieces)
 
 
-def output_body(tok, first, second, own_weight, other_weight, out, own, other):
+def output_body(tok, near, far, *refs):
+    weights, (out, stacks) = refs[:4], refs[4:]
     core = lax.axis_index("batch") & 1
-    half = own_weight.shape[0] // 8
-    rec = pl.program_id(0) // 2
-
-    def fill(source):
-        for chan in range(8):
-            rows = slice(chan * half, (chan + 1) * half)
-            for offset, target in ((core, own), (1 - core, other)):
-                place = pl.multiple_of((2 * chan + offset) * half, half)
-                target[rows, :] = source[pl.ds(place, half), :]
-
-    pl.when(rec == 0)(lambda: fill(first))
-    pl.when(rec == 1)(lambda: fill(second))
-    total = dot_nn(own[...].T, own_weight[...]) + dot_nn(other[...].T, other_weight[...])
-    out[...] = (tok[...].astype(F32) + total).astype(BF16)
-
-
-def output_rows(tokens, mixed, own_weight, other_weight):
+    half = weights[0].shape[0] // 4
+    total = tok[...].astype(F32)
+    for index, weight in enumerate(weights):
+        offset = core if index < 2 else 1 - core
+        source = (near, far)[index % 2]
+        for z in range(4):
+            place = pl.multiple_of((2 * z + offset) * half, half)
+            stacks[index, z * half : (z + 1) * half, :] = source[pl.ds(place, half), :]
+        total = total + dot_nn(stacks[index].T, weight[...])
+    out[...] = total.astype(BF16)
+
+
+def output_rows(tokens, near, far, weights):
     rows, model = tokens.shape
-    depth = own_weight.shape[0]
+    depth = weights[0].shape[0]
     by_row = pl.BlockSpec((CTX, model), lambda i: (i, 0))
-    by_col = pl.BlockSpec((2 * depth, CTX), lambda i: (0, i % 2))
+    by_col = pl.BlockSpec((2 * depth, CTX), lambda i: (0, i))
     full = pl.BlockSpec((depth, model), lambda i: (0, 0))
     return pl.pallas_call(
         output_body,
         grid=(rows // CTX,),
-        in_specs=[by_row, by_col, by_col, full, full],
+        in_specs=[by_row, by_col, by_col] + [full] * 4,
         out_specs=by_row,
         out_shape=jax.ShapeDtypeStruct((rows, model), BF16),
-        scratch_shapes=[pltpu.VMEM((depth, CTX), BF16)] * 2,
-        compiler_params=params(),
-        cost_estimate=pl.CostEstimate(flops=10000000000, bytes_accessed=12000000, transcendentals=0),
+        scratch_shapes=[pltpu.VMEM((4, depth, CTX), BF16)],
+        compiler_params=params(28),
+        cost_estimate=pl.CostEstimate(
+            flops=10000000000, bytes_accessed=12000000, transcendentals=0
+        ),
         name="output",
-    )(tokens, *mixed, own_weight, other_weight)
+    )(tokens, near, far, *weights)
 
 
 def finish_body(place, gain, *refs):
@@ -399,7 +397,7 @@
         in_specs=[pl.BlockSpec(memory_space=pltpu.SMEM)] + [by_col(chunk)] * count,
         out_specs=by_col(count * chunk),
         out_shape=jax.ShapeDtypeStruct((count * chunk, model), BF16),
-        compiler_params=params(),
+        compiler_params=params(16),
         cost_estimate=pl.CostEstimate(flops=0, bytes_accessed=6000000, transcendentals=0),
         name="assemble",
     )(places, *pieces)
@@ -447,6 +445,11 @@
     return pick(sums, row, 0) + got.astype(F32)
 
 
+def over_z(array):
+    groups = [[0, 2, 4, 6], [1, 3, 5, 7]]
+    return lax.all_gather(array, "chan", axis_index_groups=groups, tiled=True)
+
+
 def shards(tokens, cotangent, norm_gain, norm_bias, qkv_weight, out_weight, lengths, segments):
     recs, frames, model = tokens.shape
     rows = recs * frames
@@ -459,7 +462,7 @@
     tie = lax.optimization_barrier
     core = lax.axis_index("batch") & 1
     half_out = lax.dynamic_slice_in_dim(out_weight, core * (width // 2), width // 2, 0)
-    own_out = lax.all_gather(half_out, "chan", tiled=True)
+    near_out = over_z(half_out)
 
     flat_tokens = tokens.reshape(rows, model)
     flat_cot = cotangent.reshape(rows, model)
@@ -477,6 +480,8 @@
     down = [(i + 1, i) for i in range(size - 1)]
     before = lax.ppermute(kv_last, "frames", up)
     after = lax.ppermute(kv_first, "frames", down)
+    before, after, near_out = tie((before, after, near_out))
+    far_out = to_peer(near_out, (0, 1))
 
     results = []
     for rec in range(recs):
@@ -489,26 +494,30 @@
 
     first, second = results
     count = lax.axis_size("chan")
-    mixed = [lax.all_gather(result[4], "chan", tiled=True) for result in results]
-    own_out, first[0] = tie((own_out, first[0]))
-    other_out = core_swap(own_out)
+    mixed = jnp.concatenate([first[4], second[4]], axis=1)
+    near_mixed = over_z(mixed)
+    peer_mixed = to_peer(mixed, (0, 1))
+    far_mixed = over_z(peer_mixed)
     second[0], _ = tie((second[0], first[0]))
 
     split = lambda back: back.reshape(count, -1, model)
     second_back = split(back_rows(*second[:4], weight))
-    first[0], second_back = tie((first[0], second_back))
+    first[0], second_back, far_out = tie((first[0], second_back, far_out))
     first_back = split(back_rows(*first[:4], weight))
     parts = [to_all(first_back), to_all(second_back)]
 
-    first[0], first_back, mixed[1], parts[1] = tie((first[0], first_back, mixed[1], parts[1]))
+    first[0], first_back, parts[1] = tie((first[0], first_back, parts[1]))
     sent, kept = weight_grads(scalar(core), normed, flat_cot, first + second)
     sums = frame_sums(kept + core_swap(sent).astype(F32))
-    sums, parts[0], mixed[0], other_out = tie((sums, parts[0], mixed[0], other_out))
+    sums, parts[0], near_mixed = tie((sums, parts[0], near_mixed))
     grad_proj = row_sums(sums).reshape(-1, 4, width)
 
     piece = finish(scalar(me), flat_tokens, flat_cot, norm_gain, parts)
     places = jnp.stack([me] + [peer_index(me, shift, -1) for shift in SHIFTS]).astype(jnp.int32)
-    output = output_rows(flat_tokens, mixed, own_out, other_out)
+    own = [near_out, far_out]
+    output = output_rows(
+        flat_tokens, near_mixed, far_mixed, own + [core_swap(array) for array in own]
+    )
     pieces = [to_peer(piece, shift) for shift in SHIFTS]
     pieces[0], output = tie((pieces[0], output))
     grad_tokens = assemble(places, [piece] + pieces)

time: 249 us -> 211 us (0.85)
  waiting for transfers between devices: 96.9 us -> 43.7 us
  starting transfers between devices: 52.4 us -> 58.5 us
  local copies, waits for them, and re-layouts: 10.2 us -> 14.9 us
    all_gather x3, waiting for transfers between devices: 56.1 us -> 0.81 us  [over_z(): return lax.all_gather(array, 'chan', axis_index_groups=groups, tiled=True)]
    ppermute x7 -> x9, waiting for transfers between devices: 14 us -> 9.91 us  [to_peer(): return lax.ppermute(array, 'chan', pairs)]
    all_to_all x2, waiting for transfers between devices: 0.01 us -> 4.01 us  [to_all(): return lax.all_to_all(array, 'chan', 0, 0, tiled=True)]
    unnamed x38 -> x45, local copies, waits for them, and re-layouts: 4.78 us -> 8.37 us
    all_to_all x2, starting transfers between devices: 13.3 us -> 16.7 us  [to_all(): return lax.all_to_all(array, 'chan', 0, 0, tiled=True)]
    ppermute x7 -> x9, starting transfers between devices: 14.7 us -> 17.7 us  [to_peer(): return lax.ppermute(array, 'chan', pairs)]
  transfers between devices with their start and end apart: 24 -> 27, of which waited for: 13 -> 13; matrix products, arithmetic and copies ran while one was open for 3% -> 5% of each run, Pallas kernels for 25% -> 32%
where the time goes in v8:
time: 211 us; the launch traced here: 207 us
  Pallas kernels  70.7 us (34%)
  starting transfers between devices  58.5 us (28%)
  waiting for transfers between devices  43.7 us (21%)
  local copies, waits for them, and re-layouts  14.9 us (7%)
  between operations  14 us (7%)
  other arithmetic  4.98 us (2%)
    pallas_call x2, Pallas kernels, attention(): pl.pallas_call(attention_body, grid=(1,), in_specs=[by_rec(width, frames)...  20.4 us
    ppermute x9, starting transfers between devices, to_peer(): return lax.ppermute(array, 'chan', pairs)  17.7 us
    all_to_all x2, starting transfers between devices, to_all(): return lax.all_to_all(array, 'chan', 0, 0, tiled=True)  16.7 us
    ppermute x3, waiting for transfers between devices, frame_sums(): got = lax.ppermute(sent, 'frames', [(i, (i + shift) % 4) for i in range(4)])  13.6 us
    pallas_call x1, Pallas kernels, output_rows(): pl.pallas_call(output_body, grid=(rows // CTX,), in_specs=[by_row, by_col...  11 us
    pallas_call x1, Pallas kernels, project(): pl.pallas_call(project_body, grid=(rows // CTX,), in_specs=[pl.BlockSpec(...  10.6 us
    pallas_call x2, Pallas kernels, back_rows(): pl.pallas_call(back_body, grid=(model // tile,), in_specs=[full(width, ro...  10.3 us
    pallas_call x1, Pallas kernels, weight_grads(): pl.pallas_call(weight_grads_body, grid_spec=pltpu.PrefetchScalarGridSpec(...  9.97 us
  transfers between devices with their start and end apart: 27, of which 13 were waited for; matrix products, arithmetic and copies ran while one was open for 5% of the time, Pallas kernels for 32%

profile of v8, /device:TPU:18, one launch (start us, length us, event | category | flops | bytes accessed | tf_op | source)
XLA Modules:
  0.0 206.8 jit_solution(4850534868346552534)
XLA Ops:
  9.0 10.6 %project.1 = (bf16[1024,1536]{1,0:T(8,128)(2,1)}, bf16[192,1024]{1,0:T(8,128)(2,1)}, bf16[384,1024]{1,0:T(8,128)(2,1)}, bf16[192,1024]{1,0:T(8,128)(2,1)}, bf16[...) custom-call(s32[2]{0:T(128)} %lengths.1, bf16[1024,1536]{1,0:T(8,128)(2,1)} %bitcast.36, ...), custom_call_target="tpu_custom_call" | custom-call | flops 2400000000 | bytes 15000000 | tf_op jit(solution)/shard_map/project/pallas_call | solution.py:76
  19.6 3.4 %collective-permute-start = (bf16[384,512]{1,0:T(8,128)(2,1)}, bf16[384,512]{1,0:T(8,128)(2,1)S(1)}, u32[]{:S(2)}, u32[]{:S(2)}) collective-permute-start(bf16[384,512]{1,0:T(8,128)(2,1)} %get-tuple-element.39), channel_id=1, source_target_pairs={{0,8},{8,16},{16,24},{1,9},{9,17},{17,25},{2,10},{10,18},{18,26},{... | collective-permute-start | bytes 1179656 | tf_op jit(solution)/shard_map/ppermute | solution.py:481
  23.0 2.5 %collective-permute-start.1 = (bf16[384,512]{1,0:T(8,128)(2,1)}, bf16[384,512]{1,0:T(8,128)(2,1)S(1)}, u32[]{:S(2)}, u32[]{:S(2)}) collective-permute-start(bf16[384,512]{1,0:T(8,128)(2,1)} %get-tuple-element.40), channel_id=1, source_target_pairs={{8,0},{16,8},{24,16},{9,1},{17,9},{25,17},{10,2},{18,10},{26,18},{... | collective-permute-start | bytes 1179656 | tf_op jit(solution)/shard_map/ppermute | solution.py:482
  25.5 7.1 %collective-permute-done.before = bf16[384,512]{1,0:T(8,128)(2,1)S(1)} collective-permute-done((bf16[384,512]{1,0:T(8,128)(2,1)}, bf16[384,512]{1,0:T(8,128)(2,1)S(1)}, u32[]{:S(2)}, u32[]{:S(2)}) %collective-permute-start) | collective-permute-done | bytes 393248 | tf_op jit(solution)/shard_map/ppermute | solution.py:481
  32.6 3.1 %collective-permute-done.1.after = bf16[384,512]{1,0:T(8,128)(2,1)S(1)} collective-permute-done((bf16[384,512]{1,0:T(8,128)(2,1)}, bf16[384,512]{1,0:T(8,128)(2,1)S(1)}, u32[]{:S(2)}, u32[]{:S(2)}) %collective-permute-start.1) | collective-permute-done | bytes 393248 | tf_op jit(solution)/shard_map/ppermute | solution.py:482
  39.0 10.2 %attention.3 = (bf16[192,512]{1,0:T(8,128)(2,1)}, bf16[192,512]{1,0:T(8,128)(2,1)}, f32[384,512]{1,0:T(8,128)}, bf16[384,256]{1,0:T(8,128)(2,1)}, bf16[384,256]{1,0:T(8,128)(2,1)}) custom-call(bf16[192,1024]{1,0:T(8,128)(2,1)} %get-tuple-element.37.q, bf16[384,1024]{1,0:T(8,128)(2,1)} %get-tuple-element.38.kv, bf16[384,512]{1,0:T(8,128)(2,1)} %copy-done.8, ...), custom_call_target="tpu_custom_call" | custom-call | flops 1000 | bytes 1000 | tf_op jit(solution)/shard_map/attention/pallas_call | solution.py:161
  49.2 3.4 %collective-permute-start.2 = (bf16[384,256]{1,0:T(8,128)(2,1)}, bf16[384,256]{1,0:T(8,128)(2,1)S(1)}, u32[]{:S(2)}, u32[]{:S(2)}) collective-permute-start(bf16[384,256]{1,0:T(8,128)(2,1)} %get-tuple-element.49), channel_id=1, source_target_pairs={{0,8},{8,16},{16,24},{1,9},{9,17},{17,25},{2,10},{10,18},{18,26},{... | collective-permute-start | bytes 589832 | tf_op jit(solution)/shard_map/ppermute | solution.py:492
  52.6 2.7 %collective-permute-start.3 = (bf16[384,256]{1,0:T(8,128)(2,1)}, bf16[384,256]{1,0:T(8,128)(2,1)S(1)}, u32[]{:S(2)}, u32[]{:S(2)}) collective-permute-start(bf16[384,256]{1,0:T(8,128)(2,1)} %get-tuple-element.50), channel_id=1, source_target_pairs={{8,0},{16,8},{24,16},{9,1},{17,9},{25,17},{10,2},{18,10},{26,18},{... | collective-permute-start | bytes 589832 | tf_op jit(solution)/shard_map/ppermute | solution.py:491
  55.3 10.2 %attention.2 = (bf16[192,512]{1,0:T(8,128)(2,1)}, bf16[192,512]{1,0:T(8,128)(2,1)}, f32[384,512]{1,0:T(8,128)}, bf16[384,256]{1,0:T(8,128)(2,1)}, bf16[384,256]{1,0:T(8,128)(2,1)}) custom-call(bf16[192,1024]{1,0:T(8,128)(2,1)} %get-tuple-element.37.q, bf16[384,1024]{1,0:T(8,128)(2,1)} %get-tuple-element.38.kv, bf16[384,512]{1,0:T(8,128)(2,1)} %copy-done.8, ...), custom_call_target="tpu_custom_call" | custom-call | flops 1000 | bytes 1000 | tf_op jit(solution)/shard_map/attention/pallas_call | solution.py:161
  66.3 5.1 %back.2 = bf16[512,1536]{1,0:T(8,128)(2,1)} custom-call(bf16[192,512]{1,0:T(8,128)(2,1)} %get-tuple-element.47.dq.rest_5_, f32[384,512]{1,0:T(8,128)} %get-tuple-element.48.own.rest_6_, bf16[384,256]{1,0:T(8,128)(2,1)} %copy-done.12, bf16[384,256]{1,0:T(8,128)(2,1)} %copy-done.13, bf16[576,1536]{1,0:T(8,128)(2,1)} %bitcast.45), custom_call_target="tpu_custom_call" | custom-call | flops 900000000 | bytes 4000000 | tf_op jit(solution)/shard_map/back/pallas_call | solution.py:217
  71.4 7.7 %all-to-all-start = ((bf16[8,64,1536]{2,1,0:T(8,128)(2,1)}), bf16[8,64,1536]{2,1,0:T(8,128)(2,1)S(1)}, u32[]{:S(2)}, u32[]{:S(2)}) async-start(bf16[8,64,1536]{2,1,0:T(8,128)(2,1)} %bitcast.47), calls=%async_computation | async-start | bytes 3145728 | tf_op jit(solution)/shard_map/all_to_all | solution.py:420
  80.0 3.1 %collective-permute-start.5 = (bf16[384,256]{1,0:T(8,128)(2,1)S(1)}, bf16[384,256]{1,0:T(8,128)(2,1)S(1)}, u32[]{:S(2)}, u32[]{:S(2)}) collective-permute-start(bf16[384,256]{1,0:T(8,128)(2,1)S(1)} %copy-done.21), channel_id=1, source_target_pairs={{0,8},{8,16},{16,24},{1,9},{9,17},{17,25},{2,10},{10,18},{18,26},{... | collective-permute-start | bytes 589832 | tf_op jit(solution)/shard_map/ppermute | solution.py:492
  83.1 2.8 %collective-permute-start.6 = (bf16[384,256]{1,0:T(8,128)(2,1)S(1)}, bf16[384,256]{1,0:T(8,128)(2,1)S(1)}, u32[]{:S(2)}, u32[]{:S(2)}) collective-permute-start(bf16[384,256]{1,0:T(8,128)(2,1)S(1)} %copy-done.20), channel_id=1, source_target_pairs={{8,0},{16,8},{24,16},{9,1},{17,9},{25,17},{10,2},{18,10},{26,18},{... | collective-permute-start | bytes 589832 | tf_op jit(solution)/shard_map/ppermute | solution.py:491
  87.5 3.1 %collective-permute-done.6.right.rest_3_ = bf16[384,256]{1,0:T(8,128)(2,1)S(1)} collective-permute-done((bf16[384,256]{1,0:T(8,128)(2,1)S(1)}, bf16[384,256]{1,0:T(8,128)(2,1)S(1)}, u32[]{:S(2)}, u32[]{:S(2)}) %collective-permute-start.6) | collective-permute-done | bytes 196640 | tf_op jit(solution)/shard_map/ppermute | solution.py:491
  91.3 5.2 %back.3 = bf16[512,1536]{1,0:T(8,128)(2,1)} custom-call(bf16[192,512]{1,0:T(8,128)(2,1)} %get-tuple-element.57.dq.rest_0_, f32[384,512]{1,0:T(8,128)} %get-tuple-element.53.own.rest_1_, bf16[384,256]{1,0:T(8,128)(2,1)} %copy-done.14, bf16[384,256]{1,0:T(8,128)(2,1)} %copy-done.15, bf16[576,1536]{1,0:T(8,128)(2,1)} %bitcast.46), custom_call_target="tpu_custom_call" | custom-call | flops 900000000 | bytes 4000000 | tf_op jit(solution)/shard_map/back/pallas_call | solution.py:217
  97.8 10.0 %weight_grads.1 = (bf16[4,2,96,768]{3,2,1,0:T(8,128)(2,1)}, f32[4,2,96,768]{3,2,1,0:T(8,128)}) custom-call(s32[1]{0:T(128)} %bitcast.3.core, bf16[1024,1536]{1,0:T(8,128)(2,1)} %get-tuple-element.36.normed, bf16[1024,1536]{1,0:T(8,128)(2,1)} %bitcast.41, bf16[192,512]{1,0:T(8,128)(2,1)} %get-tuple-element.57.dq.rest_0_, ...), custom_call_target="tpu_custom_call" | custom-call | flops 10000000000 | bytes 12000000 | tf_op jit(solution)/shard_map/weight_grads/pallas_call | solution.py:282
  108.7 9.1 %all-to-all-start.1 = ((bf16[8,64,1536]{2,1,0:T(8,128)(2,1)}), bf16[8,64,1536]{2,1,0:T(8,128)(2,1)S(1)}, u32[]{:S(2)}, u32[]{:S(2)}) async-start(bf16[8,64,1536]{2,1,0:T(8,128)(2,1)} %bitcast.9), calls=%async_computation.1 | async-start | bytes 3145728 | tf_op jit(solution)/shard_map/all_to_all | solution.py:420
  118.3 1.9 convert_add_fusion
  123.3 1.8 collective-permute-start.9
  125.2 8.1 %collective-permute-done.10 = bf16[2,96,768]{2,1,0:T(8,128)(2,1)S(1)} collective-permute-done((bf16[2,96,768]{2,1,0:T(8,128)(2,1)S(1)}, bf16[2,96,768]{2,1,0:T(8,128)(2,1)S(1)}, u32[]{:S(2)}, u32[]{:S(2)}) %collective-permute-start.10) | collective-permute-done | bytes 294944 | tf_op jit(solution)/shard_map/ppermute | solution.py:436
  133.2 5.3 %collective-permute-done.8 = bf16[2,96,768]{2,1,0:T(8,128)(2,1)S(1)} collective-permute-done((bf16[2,96,768]{2,1,0:T(8,128)(2,1)S(1)}, bf16[2,96,768]{2,1,0:T(8,128)(2,1)S(1)}, u32[]{:S(2)}, u32[]{:S(2)}) %collective-permute-start.8) | collective-permute-done | bytes 294944 | tf_op jit(solution)/shard_map/ppermute | solution.py:436
  138.8 2.0 fusion.1
  140.8 2.7 %all-to-all-done.1.refs_2_ = bf16[8,64,1536]{2,1,0:T(8,128)(2,1)S(1)} async-done(((bf16[8,64,1536]{2,1,0:T(8,128)(2,1)}), bf16[8,64,1536]{2,1,0:T(8,128)(2,1)S(1)}, u32[]{:S(2)}, u32[]{:S(2)}) %all-to-all-start.1) | async-done | bytes 1572896 | tf_op jit(solution)/shard_map/all_to_all | solution.py:420
  144.7 4.1 %finish.1.refs_0_ = bf16[128,1536]{1,0:T(8,128)(2,1)} custom-call(s32[1]{0:T(128)} %bitcast.place, f32[1536]{0:T(1024)} %gain.3, bf16[1024,1536]{1,0:T(8,128)(2,1)} %bitcast.37, bf16[1024,1536]{1,0:T(8,128)(2,1)} %bitcast.42, bf16[8,64,1536]{2,1,0:T(8,128)(2,1)} %copy-done.5, bf16[1024,1536]{1,0:T(8,128)(2,1)} %bitcast.38, bf16[1024,1536]{1,0:T(8,128)(2,1)} %bitcast.43, ...), custom_call_target="tpu_custom_call" | custom-call | flops 10000000 | bytes 5000000 | tf_op jit(solution)/shard_map/finish/pallas_call | solution.py:363
  148.7 3.9 %collective-permute-start.11 = (bf16[128,1536]{1,0:T(8,128)(2,1)}, bf16[128,1536]{1,0:T(8,128)(2,1)}, u32[]{:S(2)}, u32[]{:S(2)}) collective-permute-start(bf16[128,1536]{1,0:T(8,128)(2,1)} %finish.1.refs_0_), channel_id=1, source_target_pairs={{0,2},{1,3},{2,4},{3,5},{4,6},{5,7},{6,0},{7,1},{8,10},{9,11},{10,... | collective-permute-start | bytes 1179656 | tf_op jit(solution)/shard_map/ppermute | solution.py:411
  155.0 2.2 %collective-permute-start.21 = (bf16[96,768]{1,0:T(8,128)(2,1)}, bf16[96,768]{1,0:T(8,128)(2,1)}, u32[]{:S(2)}, u32[]{:S(2)}) collective-permute-start(bf16[96,768]{1,0:T(8,128)(2,1)} %fusion.5), channel_id=1, source_target_pairs={{0,64},{32,96},{64,0},{96,32},{1,65},{33,97},{65,1},{97,33},{2,66}... | collective-permute-start | bytes 442376 | tf_op jit(solution)/shard_map/ppermute | solution.py:444
  157.4 4.4 %collective-permute-start.17 = (bf16[128,1536]{1,0:T(8,128)(2,1)}, bf16[128,1536]{1,0:T(8,128)(2,1)}, u32[]{:S(2)}, u32[]{:S(2)}) collective-permute-start(bf16[128,1536]{1,0:T(8,128)(2,1)} %finish.1.refs_0_), channel_id=1, source_target_pairs={{0,3},{1,2},{2,5},{3,4},{4,7},{5,6},{6,1},{7,0},{8,11},{9,10},{10,... | collective-permute-start | bytes 1179656 | tf_op jit(solution)/shard_map/ppermute | solution.py:411
  164.3 5.9 %collective-permute-start.20 = (bf16[128,1536]{1,0:T(8,128)(2,1)}, bf16[128,1536]{1,0:T(8,128)(2,1)}, u32[]{:S(2)}, u32[]{:S(2)}) collective-permute-start(bf16[128,1536]{1,0:T(8,128)(2,1)} %finish.1.refs_0_), channel_id=1, source_target_pairs={{0,5},{1,4},{2,7},{3,6},{4,1},{5,0},{6,3},{7,2},{8,13},{9,12},{10,... | collective-permute-start | bytes 1179656 | tf_op jit(solution)/shard_map/ppermute | solution.py:411
  173.0 11.0 %output.1 = bf16[1024,1536]{1,0:T(8,128)(2,1)} custom-call(bf16[1024,1536]{1,0:T(8,128)(2,1)S(1)} %bitcast.39, bf16[768,1024]{1,0:T(8,128)(2,1)S(1)} %copy-done.2, bf16[768,1024]{1,0:T(8,128)(2,1)S(1)} %copy-done.3, bf16[384,1536]{1,0:T(8,128)(2,1)} %all-gather.4.cloned.1.call-done.refs_0_, bf16[384,1536]{1,0:T(8,128)(2,1)} %collective-permute-done.4.refs_1_, ...), custom_call_target="tpu_custom_call" | custom-call | flops 10000000000 | bytes 12000000 | tf_op jit(solution)/shard_map/output/pallas_call | solution.py:330
  186.0 3.3 %collective-permute-done.18.refs_5_ = bf16[128,1536]{1,0:T(8,128)(2,1)} collective-permute-done((bf16[128,1536]{1,0:T(8,128)(2,1)}, bf16[128,1536]{1,0:T(8,128)(2,1)}, u32[]{:S(2)}, u32[]{:S(2)}) %collective-permute-start.18) | collective-permute-done | bytes 393248 | tf_op jit(solution)/shard_map/ppermute | solution.py:411
  189.3 6.6 %collective-permute-done.20.refs_7_ = bf16[128,1536]{1,0:T(8,128)(2,1)} collective-permute-done((bf16[128,1536]{1,0:T(8,128)(2,1)}, bf16[128,1536]{1,0:T(8,128)(2,1)}, u32[]{:S(2)}, u32[]{:S(2)}) %collective-permute-start.20) | collective-permute-done | bytes 393248 | tf_op jit(solution)/shard_map/ppermute | solution.py:411
  195.9 4.3 %assemble.1 = bf16[1024,1536]{1,0:T(8,128)(2,1)} custom-call(s32[8]{0:T(128)S(1)} %stack.32.places, bf16[128,1536]{1,0:T(8,128)(2,1)S(1)} %copy-done.1, bf16[128,1536]{1,0:T(8,128)(2,1)} %collective-permute-done.11.refs_1_, bf16[128,1536]{1,0:T(8,128)(2,1)} %collective-permute-done.15.refs_2_, bf16[128,1536]{1,0:T(8,128)(2,1)} %collective-permute-done.16.refs_3_, ...), custom_call_target="tpu_custom_call" | custom-call | bytes 6000000 | tf_op jit(solution)/shard_map/assemble/pallas_call | solution.py:394
  (93 shorter events, 26.0 us)
Async XLA Ops:
  7.2 29.3 %all-gather.4.cloned.1.call-start = ((), (), s32[]{:S(2)}) async-start(), calls=%async_computation.2 | async-start | bytes 1474560 | tf_op jit(solution)/shard_map/all_gather | solution.py:450
  8.9 28.1 %copy-start.18 = (s32[2,2048]{1,0:T(2,128)S(1)}, s32[2,2048]{1,0:T(2,128)}, u32[]{:S(2)}) copy-start(s32[2,2048]{1,0:T(2,128)} %param.15) | copy-start | bytes 49156
  8.9 28.1 %copy-start.19 = (s32[2]{0:T(128)S(1)}, s32[2]{0:T(128)}, u32[]{:S(2)}) copy-start(s32[2]{0:T(128)} %lengths.1) | copy-start | bytes 28
  19.6 13.0 %collective-permute-start = (bf16[384,512]{1,0:T(8,128)(2,1)}, bf16[384,512]{1,0:T(8,128)(2,1)S(1)}, u32[]{:S(2)}, u32[]{:S(2)}) collective-permute-start(bf16[384,512]{1,0:T(8,128)(2,1)} %get-tuple-element.39), channel_id=1, source_target_pairs={{0,8},{8,16},{16,24},{1,9},{9,17},{17,25},{2,10},{10,18},{18,26},{... | collective-permute-start | bytes 1179656 | tf_op jit(solution)/shard_map/ppermute | solution.py:481
  23.0 12.7 %collective-permute-start.1 = (bf16[384,512]{1,0:T(8,128)(2,1)}, bf16[384,512]{1,0:T(8,128)(2,1)S(1)}, u32[]{:S(2)}, u32[]{:S(2)}) collective-permute-start(bf16[384,512]{1,0:T(8,128)(2,1)} %get-tuple-element.40), channel_id=1, source_target_pairs={{8,0},{16,8},{24,16},{9,1},{17,9},{25,17},{10,2},{18,10},{26,18},{... | collective-permute-start | bytes 1179656 | tf_op jit(solution)/shard_map/ppermute | solution.py:482
  36.5 34.9 %collective-permute-start.4 = (bf16[384,1536]{1,0:T(8,128)(2,1)}, bf16[384,1536]{1,0:T(8,128)(2,1)}, u32[]{:S(2)}, u32[]{:S(2)}) collective-permute-start(bf16[384,1536]{1,0:T(8,128)(2,1)} %all-gather.4.cloned.1.call-done.refs_0_), channel_id=1, source_target_pairs={{0,1},{1,0},{2,3},{3,2},{4,5},{5,4},{6,7},{7,6},{8,9},{9,8},{10,11... | collective-permute-start | bytes 3538952 | tf_op jit(solution)/shard_map/ppermute | solution.py:411
  49.2 16.3 %collective-permute-start.2 = (bf16[384,256]{1,0:T(8,128)(2,1)}, bf16[384,256]{1,0:T(8,128)(2,1)S(1)}, u32[]{:S(2)}, u32[]{:S(2)}) collective-permute-start(bf16[384,256]{1,0:T(8,128)(2,1)} %get-tuple-element.49), channel_id=1, source_target_pairs={{0,8},{8,16},{16,24},{1,9},{9,17},{17,25},{2,10},{10,18},{18,26},{... | collective-permute-start | bytes 589832 | tf_op jit(solution)/shard_map/ppermute | solution.py:492
  52.6 12.9 %collective-permute-start.3 = (bf16[384,256]{1,0:T(8,128)(2,1)}, bf16[384,256]{1,0:T(8,128)(2,1)S(1)}, u32[]{:S(2)}, u32[]{:S(2)}) collective-permute-start(bf16[384,256]{1,0:T(8,128)(2,1)} %get-tuple-element.50), channel_id=1, source_target_pairs={{8,0},{16,8},{24,16},{9,1},{17,9},{25,17},{10,2},{18,10},{26,18},{... | collective-permute-start | bytes 589832 | tf_op jit(solution)/shard_map/ppermute | solution.py:491
  71.4 11.7 %copy-start.20 = (bf16[384,256]{1,0:T(8,128)(2,1)S(1)}, bf16[384,256]{1,0:T(8,128)(2,1)}, u32[]{:S(2)}) copy-start(bf16[384,256]{1,0:T(8,128)(2,1)} %get-tuple-element.55) | copy-start | bytes 589828
  71.4 26.4 %all-to-all-start = ((bf16[8,64,1536]{2,1,0:T(8,128)(2,1)}), bf16[8,64,1536]{2,1,0:T(8,128)(2,1)S(1)}, u32[]{:S(2)}, u32[]{:S(2)}) async-start(bf16[8,64,1536]{2,1,0:T(8,128)(2,1)} %bitcast.47), calls=%async_computation | async-start | bytes 3145728 | tf_op jit(solution)/shard_map/all_to_all | solution.py:420
  79.1 61.7 %all-gather.6.cloned.1.call-start = ((), (), s32[]{:S(2)}) async-start(), calls=%async_computation.3 | async-start | bytes 1966080 | tf_op jit(solution)/shard_map/all_gather | solution.py:450
  79.9 90.3 %all-gather.8.cloned.1.call-start = ((), (), s32[]{:S(2)}) async-start(), calls=%async_computation.4 | async-start | bytes 1966080 | tf_op jit(solution)/shard_map/all_gather | solution.py:450
  80.0 7.6 %collective-permute-start.5 = (bf16[384,256]{1,0:T(8,128)(2,1)S(1)}, bf16[384,256]{1,0:T(8,128)(2,1)S(1)}, u32[]{:S(2)}, u32[]{:S(2)}) collective-permute-start(bf16[384,256]{1,0:T(8,128)(2,1)S(1)} %copy-done.21), channel_id=1, source_target_pairs={{0,8},{8,16},{16,24},{1,9},{9,17},{17,25},{2,10},{10,18},{18,26},{... | collective-permute-start | bytes 589832 | tf_op jit(solution)/shard_map/ppermute | solution.py:492
  83.1 7.6 %collective-permute-start.6 = (bf16[384,256]{1,0:T(8,128)(2,1)S(1)}, bf16[384,256]{1,0:T(8,128)(2,1)S(1)}, u32[]{:S(2)}, u32[]{:S(2)}) collective-permute-start(bf16[384,256]{1,0:T(8,128)(2,1)S(1)} %copy-done.20), channel_id=1, source_target_pairs={{8,0},{16,8},{24,16},{9,1},{17,9},{25,17},{10,2},{18,10},{26,18},{... | collective-permute-start | bytes 589832 | tf_op jit(solution)/shard_map/ppermute | solution.py:491
  85.8 22.0 %collective-permute-start.12 = (bf16[192,1024]{1,0:T(8,128)(2,1)}, bf16[192,1024]{1,0:T(8,128)(2,1)S(1)}, u32[]{:S(2)}, u32[]{:S(2)}) collective-permute-start(bf16[192,1024]{1,0:T(8,128)(2,1)} %copy-done.10), channel_id=1, source_target_pairs={{0,1},{1,0},{2,3},{3,2},{4,5},{5,4},{6,7},{7,6},{8,9},{9,8},{10,11... | collective-permute-start | bytes 1179656 | tf_op jit(solution)/shard_map/ppermute | solution.py:411
  107.8 10.5 %collective-permute-start.7 = (bf16[4,2,96,768]{3,2,1,0:T(8,128)(2,1)}, bf16[4,2,96,768]{3,2,1,0:T(8,128)(2,1)S(1)}, u32[]{:S(2)}, u32[]{:S(2)}) collective-permute-start(bf16[4,2,96,768]{3,2,1,0:T(8,128)(2,1)} %get-tuple-element.61), channel_id=1, source_target_pairs={{0,32},{32,0},{64,96},{96,64},{1,33},{33,1},{65,97},{97,65},{2,34}... | collective-permute-start | bytes 3538952 | tf_op jit(solution)/shard_map/ppermute | solution.py:428
  108.7 34.8 %all-to-all-start.1 = ((bf16[8,64,1536]{2,1,0:T(8,128)(2,1)}), bf16[8,64,1536]{2,1,0:T(8,128)(2,1)S(1)}, u32[]{:S(2)}, u32[]{:S(2)}) async-start(bf16[8,64,1536]{2,1,0:T(8,128)(2,1)} %bitcast.9), calls=%async_computation.1 | async-start | bytes 3145728 | tf_op jit(solution)/shard_map/all_to_all | solution.py:420
  117.8 39.5 %collective-permute-start.13 = (bf16[384,1536]{1,0:T(8,128)(2,1)}, bf16[384,1536]{1,0:T(8,128)(2,1)}, u32[]{:S(2)}, u32[]{:S(2)}) collective-permute-start(bf16[384,1536]{1,0:T(8,128)(2,1)} %all-gather.4.cloned.1.call-done.refs_0_), channel_id=1, source_target_pairs={{0,32},{32,0},{64,96},{96,64},{1,33},{33,1},{65,97},{97,65},{2,34}... | collective-permute-start | bytes 3538952 | tf_op jit(solution)/shard_map/ppermute | solution.py:428
  118.0 39.4 %collective-permute-start.14 = (bf16[384,1536]{1,0:T(8,128)(2,1)}, bf16[384,1536]{1,0:T(8,128)(2,1)}, u32[]{:S(2)}, u32[]{:S(2)}) collective-permute-start(bf16[384,1536]{1,0:T(8,128)(2,1)} %collective-permute-done.4.refs_1_), channel_id=1, source_target_pairs={{0,32},{32,0},{64,96},{96,64},{1,33},{33,1},{65,97},{97,65},{2,34}... | collective-permute-start | bytes 3538952 | tf_op jit(solution)/shard_map/ppermute | solution.py:428
  121.7 11.5 %collective-permute-start.10 = (bf16[2,96,768]{2,1,0:T(8,128)(2,1)S(1)}, bf16[2,96,768]{2,1,0:T(8,128)(2,1)S(1)}, u32[]{:S(2)}, u32[]{:S(2)}) collective-permute-start(bf16[2,96,768]{2,1,0:T(8,128)(2,1)S(1)} %get-tuple-element.70), channel_id=1, source_target_pairs={{0,16},{8,24},{16,0},{24,8},{1,17},{9,25},{17,1},{25,9},{2,18},{10... | collective-permute-start | bytes 884744 | tf_op jit(solution)/shard_map/ppermute | solution.py:436
  123.1 15.4 %collective-permute-start.8 = (bf16[2,96,768]{2,1,0:T(8,128)(2,1)S(1)}, bf16[2,96,768]{2,1,0:T(8,128)(2,1)S(1)}, u32[]{:S(2)}, u32[]{:S(2)}) collective-permute-start(bf16[2,96,768]{2,1,0:T(8,128)(2,1)S(1)} %get-tuple-element.69), channel_id=1, source_target_pairs={{0,8},{8,16},{16,24},{24,0},{1,9},{9,17},{17,25},{25,1},{2,10},{10... | collective-permute-start | bytes 884744 | tf_op jit(solution)/shard_map/ppermute | solution.py:436
  123.3 15.5 %collective-permute-start.9 = (bf16[2,96,768]{2,1,0:T(8,128)(2,1)S(1)}, bf16[2,96,768]{2,1,0:T(8,128)(2,1)S(1)}, u32[]{:S(2)}, u32[]{:S(2)}) collective-permute-start(bf16[2,96,768]{2,1,0:T(8,128)(2,1)S(1)} %get-tuple-element.71), channel_id=1, source_target_pairs={{0,24},{8,0},{16,8},{24,16},{1,25},{9,1},{17,9},{25,17},{2,26},{10... | collective-permute-start | bytes 884744 | tf_op jit(solution)/shard_map/ppermute | solution.py:436
  144.7 25.5 %copy-start = (bf16[2,512,1536]{2,1,0:T(8,128)(2,1)S(1)}, bf16[2,512,1536]{2,1,0:T(8,128)(2,1)}, u32[]{:S(2)}) copy-start(bf16[2,512,1536]{2,1,0:T(8,128)(2,1)} %param.8) | copy-start | bytes 9437188
  148.7 14.4 %collective-permute-start.11 = (bf16[128,1536]{1,0:T(8,128)(2,1)}, bf16[128,1536]{1,0:T(8,128)(2,1)}, u32[]{:S(2)}, u32[]{:S(2)}) collective-permute-start(bf16[128,1536]{1,0:T(8,128)(2,1)} %finish.1.refs_0_), channel_id=1, source_target_pairs={{0,2},{1,3},{2,4},{3,5},{4,6},{5,7},{6,0},{7,1},{8,10},{9,11},{10,... | collective-permute-start | bytes 1179656 | tf_op jit(solution)/shard_map/ppermute | solution.py:411
  152.6 11.6 %collective-permute-start.15 = (bf16[128,1536]{1,0:T(8,128)(2,1)}, bf16[128,1536]{1,0:T(8,128)(2,1)}, u32[]{:S(2)}, u32[]{:S(2)}) collective-permute-start(bf16[128,1536]{1,0:T(8,128)(2,1)} %finish.1.refs_0_), channel_id=1, source_target_pairs={{0,6},{1,7},{2,0},{3,1},{4,2},{5,3},{6,4},{7,5},{8,14},{9,15},{10,... | collective-permute-start | bytes 1179656 | tf_op jit(solution)/shard_map/ppermute | solution.py:411
  155.0 7.2 %collective-permute-start.21 = (bf16[96,768]{1,0:T(8,128)(2,1)}, bf16[96,768]{1,0:T(8,128)(2,1)}, u32[]{:S(2)}, u32[]{:S(2)}) collective-permute-start(bf16[96,768]{1,0:T(8,128)(2,1)} %fusion.5), channel_id=1, source_target_pairs={{0,64},{32,96},{64,0},{96,32},{1,65},{33,97},{65,1},{97,33},{2,66}... | collective-permute-start | bytes 442376 | tf_op jit(solution)/shard_map/ppermute | solution.py:444
  157.3 38.6 %copy-start.1 = (bf16[128,1536]{1,0:T(8,128)(2,1)S(1)}, bf16[128,1536]{1,0:T(8,128)(2,1)}, u32[]{:S(2)}) copy-start(bf16[128,1536]{1,0:T(8,128)(2,1)} %finish.1.refs_0_) | copy-start | bytes 1179652
  157.3 28.7 %collective-permute-start.16 = (bf16[128,1536]{1,0:T(8,128)(2,1)}, bf16[128,1536]{1,0:T(8,128)(2,1)}, u32[]{:S(2)}, u32[]{:S(2)}) collective-permute-start(bf16[128,1536]{1,0:T(8,128)(2,1)} %finish.1.refs_0_), channel_id=1, source_target_pairs={{0,1},{1,0},{2,3},{3,2},{4,5},{5,4},{6,7},{7,6},{8,9},{9,8},{10,11... | collective-permute-start | bytes 1179656 | tf_op jit(solution)/shard_map/ppermute | solution.py:411
  157.4 28.6 %collective-permute-start.17 = (bf16[128,1536]{1,0:T(8,128)(2,1)}, bf16[128,1536]{1,0:T(8,128)(2,1)}, u32[]{:S(2)}, u32[]{:S(2)}) collective-permute-start(bf16[128,1536]{1,0:T(8,128)(2,1)} %finish.1.refs_0_), channel_id=1, source_target_pairs={{0,3},{1,2},{2,5},{3,4},{4,7},{5,6},{6,1},{7,0},{8,11},{9,10},{10,... | collective-permute-start | bytes 1179656 | tf_op jit(solution)/shard_map/ppermute | solution.py:411
  162.2 27.1 %collective-permute-start.18 = (bf16[128,1536]{1,0:T(8,128)(2,1)}, bf16[128,1536]{1,0:T(8,128)(2,1)}, u32[]{:S(2)}, u32[]{:S(2)}) collective-permute-start(bf16[128,1536]{1,0:T(8,128)(2,1)} %finish.1.refs_0_), channel_id=1, source_target_pairs={{0,7},{1,6},{2,1},{3,0},{4,3},{5,2},{6,5},{7,4},{8,15},{9,14},{10,... | collective-permute-start | bytes 1179656 | tf_op jit(solution)/shard_map/ppermute | solution.py:411
  163.1 26.2 %collective-permute-start.19 = (bf16[128,1536]{1,0:T(8,128)(2,1)}, bf16[128,1536]{1,0:T(8,128)(2,1)}, u32[]{:S(2)}, u32[]{:S(2)}) collective-permute-start(bf16[128,1536]{1,0:T(8,128)(2,1)} %finish.1.refs_0_), channel_id=1, source_target_pairs={{0,4},{1,5},{2,6},{3,7},{4,0},{5,1},{6,2},{7,3},{8,12},{9,13},{10,... | collective-permute-start | bytes 1179656 | tf_op jit(solution)/shard_map/ppermute | solution.py:411
  164.3 31.6 %collective-permute-start.20 = (bf16[128,1536]{1,0:T(8,128)(2,1)}, bf16[128,1536]{1,0:T(8,128)(2,1)}, u32[]{:S(2)}, u32[]{:S(2)}) collective-permute-start(bf16[128,1536]{1,0:T(8,128)(2,1)} %finish.1.refs_0_), channel_id=1, source_target_pairs={{0,5},{1,4},{2,7},{3,6},{4,1},{5,0},{6,3},{7,2},{8,13},{9,12},{10,... | collective-permute-start | bytes 1179656 | tf_op jit(solution)/shard_map/ppermute | solution.py:411
  (17 other events, 66.9 us)
Sparse Core Ops, SparseCore 0:
  9.7 26.7 all-gather.3
  82.1 28.0 all-gather.5
  111.9 39.6 all-gather.7

commit v9 on v8

--- a/solution.py
+++ b/solution.py
@@ -10,7 +10,7 @@
 EPS = 1e-05
 NEG = -1e30
 
-SHIFTS = ((1, 0), (3, 0), (0, 1), (1, 1), (3, 1), (2, 0), (2, 1))
+SHIFTS = ((2, 1), (2, 0), (3, 1), (1, 1), (0, 1), (3, 0), (1, 0))
 
 F32 = jnp.float32
 BF16 = jnp.bfloat16
@@ -234,7 +234,7 @@
 
 
 def weight_grads_body(core, normed, cot, *rest):
-    pieces, (sent, kept, kv, query, mixed) = rest[:-5], rest[-5:]
+    pieces, (sent, kept, grads, mixed) = rest[:-4], rest[-4:]
     width, frames = pieces[0].shape
     del core
 
@@ -242,21 +242,15 @@
     def _():
         for rec in range(2):
             dq, own, left, right, out = pieces[5 * rec : 5 * rec + 5]
-            cols = slice(rec * frames, (rec + 1) * frames)
-            kv[:, cols] = kv_grads(own, left, right)
-            query[:, cols] = dq[...]
-            mixed[:, cols] = out[...]
-
-    turned = normed[...].T
-    sums = [
-        dot_nt(turned, query[...]),
-        dot_nt(turned, kv[...]),
-        dot_nt(cot[...].T, mixed[...]),
-    ]
-    offsets = (0, width, 3 * width)
+            rows = slice(rec * frames, (rec + 1) * frames)
+            stacked = jnp.concatenate([dq[...], kv_grads(own, left, right)], axis=0)
+            grads[rows, :] = stacked.T
+            mixed[rows, :] = out[...].T
+
+    sums = [dot_nn(normed[...].T, grads[...]), dot_nn(cot[...].T, mixed[...])]
 
     def write(target):
-        for part, offset in zip(sums, offsets):
+        for part, offset in zip(sums, (0, 3 * width)):
             shape = (target.shape[0], target.shape[2], part.shape[1])
             cols = slice(offset, offset + part.shape[1])
             target[:, 0, :, cols] = part.reshape(shape).astype(target.dtype)
@@ -291,14 +285,13 @@
                 pl.BlockSpec(part, lambda i, c: (0, jnp.maximum(i, 2) - 2, 0, 0)),
             ],
             scratch_shapes=[
-                pltpu.VMEM((2 * width, rows), BF16),
-                pltpu.VMEM((width, rows), BF16),
-                pltpu.VMEM((width, rows), BF16),
+                pltpu.VMEM((rows, 3 * width), BF16),
+                pltpu.VMEM((rows, width), BF16),
             ],
         ),
         out_shape=[
             jax.ShapeDtypeStruct((4, 2, block // 4, 4 * width), BF16),
-            jax.ShapeDtypeStruct((4, 2, block // 4, 4 * width), F32),
+            jax.ShapeDtypeStruct((4, 2, block // 4, 4 * width), BF16),
         ],
         compiler_params=params(),
         cost_estimate=pl.CostEstimate(flops=10000000000, bytes_accessed=12000000, transcendentals=0),
@@ -480,36 +473,41 @@
     down = [(i + 1, i) for i in range(size - 1)]
     before = lax.ppermute(kv_last, "frames", up)
     after = lax.ppermute(kv_first, "frames", down)
-    before, after, near_out = tie((before, after, near_out))
-    far_out = to_peer(near_out, (0, 1))
-
-    results = []
-    for rec in range(recs):
+    half_out, kv_first = tie((half_out, kv_first))
+    peer_out = to_peer(half_out, (0, 1))
+    before, after, peer_out = tie((before, after, peer_out))
+    far_out = over_z(peer_out)
+
+    results = [None] * recs
+    for rec in reversed(range(recs)):
         mixed, dq, dkv, dbefore, dafter = attention(
             rec, q, kv, before, after, g, seg_keys, seg_rows, live
         )
         right = lax.ppermute(dbefore, "frames", down)
         left = lax.ppermute(dafter, "frames", up)
-        results.append([dq, dkv, left, right, mixed])
+        mixed, q = tie((mixed, q))
+        results[rec] = [dq, dkv, left, right, mixed]
 
     first, second = results
     count = lax.axis_size("chan")
-    mixed = jnp.concatenate([first[4], second[4]], axis=1)
+    second[0], _ = tie((second[0], first[0]))
+
+    split = lambda back: back.reshape(count, -1, model)
+    second_back = split(back_rows(*second[:4], weight))
+    mixed, second_back = tie((jnp.concatenate([first[4], second[4]], axis=1), second_back))
     near_mixed = over_z(mixed)
     peer_mixed = to_peer(mixed, (0, 1))
+    first[0], second_back, far_out, near_out = tie((first[0], second_back, far_out, near_out))
+    sent, kept = weight_grads(scalar(core), normed, flat_cot, first + second)
+    second_parts = to_all(second_back)
+    first[0], sent, second_parts = tie((first[0], sent, second_parts))
+    first_back = split(back_rows(*first[:4], weight))
+    first_back, peer_mixed = tie((first_back, peer_mixed))
     far_mixed = over_z(peer_mixed)
-    second[0], _ = tie((second[0], first[0]))
-
-    split = lambda back: back.reshape(count, -1, model)
-    second_back = split(back_rows(*second[:4], weight))
-    first[0], second_back, far_out = tie((first[0], second_back, far_out))
-    first_back = split(back_rows(*first[:4], weight))
-    parts = [to_all(first_back), to_all(second_back)]
-
-    first[0], first_back, parts[1] = tie((first[0], first_back, parts[1]))
-    sent, kept = weight_grads(scalar(core), normed, flat_cot, first + second)
-    sums = frame_sums(kept + core_swap(sent).astype(F32))
-    sums, parts[0], near_mixed = tie((sums, parts[0], near_mixed))
+    parts = [to_all(first_back), second_parts]
+
+    sums = frame_sums(kept.astype(F32) + core_swap(sent).astype(F32))
+    sums, parts[0] = tie((sums, parts[0]))
     grad_proj = row_sums(sums).reshape(-1, 4, width)
 
     piece = finish(scalar(me), flat_tokens, flat_cot, norm_gain, parts)

time: 211 us -> 212 us (level)
  the two profiles are of different devices: /device:TPU:18 before, /device:TPU:14 now
where the time goes in v9:
time: 212 us; the launch traced here: 211 us
  Pallas kernels  70.3 us (33%)
  starting transfers between devices  68.1 us (32%)
  waiting for transfers between devices  35.2 us (17%)
  local copies, waits for them, and re-layouts  15.8 us (7%)
  between operations  14.1 us (7%)
  other arithmetic  7.13 us (3%)
    ppermute x9, starting transfers between devices, to_peer(): return lax.ppermute(array, 'chan', pairs)  30.6 us
    pallas_call x2, Pallas kernels, attention(): pl.pallas_call(attention_body, grid=(1,), in_specs=[by_rec(width, frames)...  20.5 us
    all_to_all x2, starting transfers between devices, to_all(): return lax.all_to_all(array, 'chan', 0, 0, tiled=True)  13.3 us
    ppermute x3, waiting for transfers between devices, frame_sums(): got = lax.ppermute(sent, 'frames', [(i, (i + shift) % 4) for i in range(4)])  12.2 us
    pallas_call x1, Pallas kernels, output_rows(): pl.pallas_call(output_body, grid=(rows // CTX,), in_specs=[by_row, by_col...  10.9 us
    pallas_call x2, Pallas kernels, back_rows(): pl.pallas_call(back_body, grid=(model // tile,), in_specs=[full(width, ro...  10.7 us
    pallas_call x1, Pallas kernels, project(): pl.pallas_call(project_body, grid=(rows // CTX,), in_specs=[pl.BlockSpec(...  10.7 us
    ppermute x2, starting transfers between devices, shards(): right = lax.ppermute(dbefore, 'frames', down)  9.3 us
  transfers between devices with their start and end apart: 28, of which 7 were waited for; matrix products, arithmetic and copies ran while one was open for 6% of the time, Pallas kernels for 31%

profile of v9, /device:TPU:14, one launch (start us, length us, event | category | flops | bytes accessed | tf_op | source)
XLA Modules:
  0.0 210.7 jit_solution(3457227291298181759)
XLA Ops:
  9.0 10.7 %project.1 = (bf16[1024,1536]{1,0:T(8,128)(2,1)}, bf16[192,1024]{1,0:T(8,128)(2,1)}, bf16[384,1024]{1,0:T(8,128)(2,1)}, bf16[192,1024]{1,0:T(8,128)(2,1)}, bf16[...) custom-call(s32[2]{0:T(128)} %lengths.1, bf16[1024,1536]{1,0:T(8,128)(2,1)} %bitcast.36, ...), custom_call_target="tpu_custom_call" | custom-call | flops 2400000000 | bytes 15000000 | tf_op jit(solution)/shard_map/project/pallas_call | solution.py:76
  21.0 4.6 %collective-permute-start.1 = (bf16[384,512]{1,0:T(8,128)(2,1)}, bf16[384,512]{1,0:T(8,128)(2,1)S(1)}, u32[]{:S(2)}, u32[]{:S(2)}) collective-permute-start(bf16[384,512]{1,0:T(8,128)(2,1)} %get-tuple-element.49), channel_id=1, source_target_pairs={{8,0},{16,8},{24,16},{9,1},{17,9},{25,17},{10,2},{18,10},{26,18},{... | collective-permute-start | bytes 1179656 | tf_op jit(solution)/shard_map/ppermute | solution.py:475
  25.6 2.4 %collective-permute-start.2 = (bf16[96,1536]{1,0:T(8,128)(2,1)S(1)}, bf16[96,1536]{1,0:T(8,128)(2,1)S(1)}, u32[]{:S(2)}, u32[]{:S(2)}) collective-permute-start(bf16[96,1536]{1,0:T(8,128)(2,1)S(1)} %copy-done.10), channel_id=1, source_target_pairs={{0,1},{1,0},{2,3},{3,2},{4,5},{5,4},{6,7},{7,6},{8,9},{9,8},{10,11... | collective-permute-start | bytes 884744 | tf_op jit(solution)/shard_map/ppermute | solution.py:404
  27.9 7.4 %collective-permute-done.2 = bf16[96,1536]{1,0:T(8,128)(2,1)S(1)} collective-permute-done((bf16[96,1536]{1,0:T(8,128)(2,1)S(1)}, bf16[96,1536]{1,0:T(8,128)(2,1)S(1)}, u32[]{:S(2)}, u32[]{:S(2)}) %collective-permute-start.2) | collective-permute-done | bytes 294944 | tf_op jit(solution)/shard_map/ppermute | solution.py:404
  38.2 10.2 %attention.2 = (bf16[192,512]{1,0:T(8,128)(2,1)}, bf16[192,512]{1,0:T(8,128)(2,1)}, f32[384,512]{1,0:T(8,128)}, bf16[384,256]{1,0:T(8,128)(2,1)}, bf16[384,256]{1,0:T(8,128)(2,1)}) custom-call(bf16[192,1024]{1,0:T(8,128)(2,1)} %get-tuple-element.56.q, bf16[384,1024]{1,0:T(8,128)(2,1)} %get-tuple-element.47.kv, bf16[384,512]{1,0:T(8,128)(2,1)} %copy-done.8, ...), custom_call_target="tpu_custom_call" | custom-call | flops 1000 | bytes 1000 | tf_op jit(solution)/shard_map/attention/pallas_call | solution.py:161
  49.7 4.7 %collective-permute-start.4 = (bf16[384,256]{1,0:T(8,128)(2,1)}, bf16[384,256]{1,0:T(8,128)(2,1)S(1)}, u32[]{:S(2)}, u32[]{:S(2)}) collective-permute-start(bf16[384,256]{1,0:T(8,128)(2,1)} %get-tuple-element.65), channel_id=1, source_target_pairs={{8,0},{16,8},{24,16},{9,1},{17,9},{25,17},{10,2},{18,10},{26,18},{... | collective-permute-start | bytes 589832 | tf_op jit(solution)/shard_map/ppermute | solution.py:486
  54.5 10.3 %attention.3 = (bf16[192,512]{1,0:T(8,128)(2,1)}, bf16[192,512]{1,0:T(8,128)(2,1)}, f32[384,512]{1,0:T(8,128)}, bf16[384,256]{1,0:T(8,128)(2,1)}, bf16[384,256]{1,0:T(8,128)(2,1)}) custom-call(bf16[192,1024]{1,0:T(8,128)(2,1)} %get-tuple-element.56.q, bf16[384,1024]{1,0:T(8,128)(2,1)} %get-tuple-element.47.kv, bf16[384,512]{1,0:T(8,128)(2,1)} %copy-done.8, ...), custom_call_target="tpu_custom_call" | custom-call | flops 1000 | bytes 1000 | tf_op jit(solution)/shard_map/attention/pallas_call | solution.py:161
  67.3 5.1 %back.2 = bf16[512,1536]{1,0:T(8,128)(2,1)} custom-call(bf16[192,512]{1,0:T(8,128)(2,1)} %get-tuple-element.62.dq.rest_5_, f32[384,512]{1,0:T(8,128)} %get-tuple-element.63.own.rest_6_, bf16[384,256]{1,0:T(8,128)(2,1)} %copy-done.14, bf16[384,256]{1,0:T(8,128)(2,1)} %copy-done.15, bf16[576,1536]{1,0:T(8,128)(2,1)} %bitcast.45), custom_call_target="tpu_custom_call" | custom-call | flops 900000000 | bytes 4000000 | tf_op jit(solution)/shard_map/back/pallas_call | solution.py:217
  72.5 7.2 %all-to-all-start = ((bf16[8,64,1536]{2,1,0:T(8,128)(2,1)}), bf16[8,64,1536]{2,1,0:T(8,128)(2,1)S(1)}, u32[]{:S(2)}, u32[]{:S(2)}) async-start(bf16[8,64,1536]{2,1,0:T(8,128)(2,1)} %bitcast.48), calls=%async_computation | async-start | bytes 3145728 | tf_op jit(solution)/shard_map/all_to_all | solution.py:413
  81.0 4.6 %collective-permute-start.6 = (bf16[384,256]{1,0:T(8,128)(2,1)S(1)}, bf16[384,256]{1,0:T(8,128)(2,1)S(1)}, u32[]{:S(2)}, u32[]{:S(2)}) collective-permute-start(bf16[384,256]{1,0:T(8,128)(2,1)S(1)} %copy-done.21), channel_id=1, source_target_pairs={{8,0},{16,8},{24,16},{9,1},{17,9},{25,17},{10,2},{18,10},{26,18},{... | collective-permute-start | bytes 589832 | tf_op jit(solution)/shard_map/ppermute | solution.py:486
  85.6 3.6 %collective-permute-start.11 = (bf16[192,1024]{1,0:T(8,128)(2,1)S(1)}, bf16[192,1024]{1,0:T(8,128)(2,1)S(1)}, u32[]{:S(2)}, u32[]{:S(2)}) collective-permute-start(bf16[192,1024]{1,0:T(8,128)(2,1)S(1)} %copy-done.7), channel_id=1, source_target_pairs={{0,1},{1,0},{2,3},{3,2},{4,5},{5,4},{6,7},{7,6},{8,9},{9,8},{10,11... | collective-permute-start | bytes 1179656 | tf_op jit(solution)/shard_map/ppermute | solution.py:404
  89.9 9.0 %weight_grads.1 = (bf16[4,2,96,768]{3,2,1,0:T(8,128)(2,1)}, bf16[4,2,96,768]{3,2,1,0:T(8,128)(2,1)}) custom-call(s32[1]{0:T(128)} %bitcast.3.core, bf16[1024,1536]{1,0:T(8,128)(2,1)} %get-tuple-element.45.normed, bf16[1024,1536]{1,0:T(8,128)(2,1)} %bitcast.41, bf16[192,512]{1,0:T(8,128)(2,1)} %get-tuple-element.76.rest_0_.dq, ...), custom_call_target="tpu_custom_call" | custom-call | flops 10000000000 | bytes 12000000 | tf_op jit(solution)/shard_map/weight_grads/pallas_call | solution.py:276
  98.9 5.8 %all-to-all-done.refs_5_ = bf16[8,64,1536]{2,1,0:T(8,128)(2,1)S(1)} async-done(((bf16[8,64,1536]{2,1,0:T(8,128)(2,1)}), bf16[8,64,1536]{2,1,0:T(8,128)(2,1)S(1)}, u32[]{:S(2)}, u32[]{:S(2)}) %all-to-all-start) | async-done | bytes 1572896 | tf_op jit(solution)/shard_map/all_to_all | solution.py:413
  104.7 5.7 %back.3 = bf16[512,1536]{1,0:T(8,128)(2,1)} custom-call(bf16[192,512]{1,0:T(8,128)(2,1)} %get-tuple-element.76.rest_0_.dq, f32[384,512]{1,0:T(8,128)} %get-tuple-element.69.rest_1_.own, bf16[384,256]{1,0:T(8,128)(2,1)} %copy-done.16, bf16[384,256]{1,0:T(8,128)(2,1)} %copy-done.17, bf16[576,1536]{1,0:T(8,128)(2,1)} %bitcast.46), custom_call_target="tpu_custom_call" | custom-call | flops 900000000 | bytes 4000000 | tf_op jit(solution)/shard_map/back/pallas_call | solution.py:217
  111.2 6.1 %all-to-all-start.1 = ((bf16[8,64,1536]{2,1,0:T(8,128)(2,1)}), bf16[8,64,1536]{2,1,0:T(8,128)(2,1)S(1)}, u32[]{:S(2)}, u32[]{:S(2)}) async-start(bf16[8,64,1536]{2,1,0:T(8,128)(2,1)} %bitcast.47), calls=%async_computation.1 | async-start | bytes 3145728 | tf_op jit(solution)/shard_map/all_to_all | solution.py:413
  122.3 3.2 %collective-permute-start.8 = (bf16[2,96,768]{2,1,0:T(8,128)(2,1)S(1)}, bf16[2,96,768]{2,1,0:T(8,128)(2,1)S(1)}, u32[]{:S(2)}, u32[]{:S(2)}) collective-permute-start(bf16[2,96,768]{2,1,0:T(8,128)(2,1)S(1)} %get-tuple-element.87), channel_id=1, source_target_pairs={{0,8},{8,16},{16,24},{24,0},{1,9},{9,17},{17,25},{25,1},{2,10},{10... | collective-permute-start | bytes 884744 | tf_op jit(solution)/shard_map/ppermute | solution.py:429
  125.5 6.8 %collective-permute-done.10 = bf16[2,96,768]{2,1,0:T(8,128)(2,1)S(1)} collective-permute-done((bf16[2,96,768]{2,1,0:T(8,128)(2,1)S(1)}, bf16[2,96,768]{2,1,0:T(8,128)(2,1)S(1)}, u32[]{:S(2)}, u32[]{:S(2)}) %collective-permute-start.10) | collective-permute-done | bytes 294944 | tf_op jit(solution)/shard_map/ppermute | solution.py:429
  132.3 5.4 %collective-permute-done.9 = bf16[2,96,768]{2,1,0:T(8,128)(2,1)S(1)} collective-permute-done((bf16[2,96,768]{2,1,0:T(8,128)(2,1)S(1)}, bf16[2,96,768]{2,1,0:T(8,128)(2,1)S(1)}, u32[]{:S(2)}, u32[]{:S(2)}) %collective-permute-start.9) | collective-permute-done | bytes 294944 | tf_op jit(solution)/shard_map/ppermute | solution.py:429
  137.7 2.0 fusion.1
  139.7 2.5 %all-to-all-done.1.refs_2_ = bf16[8,64,1536]{2,1,0:T(8,128)(2,1)S(1)} async-done(((bf16[8,64,1536]{2,1,0:T(8,128)(2,1)}), bf16[8,64,1536]{2,1,0:T(8,128)(2,1)S(1)}, u32[]{:S(2)}, u32[]{:S(2)}) %all-to-all-start.1) | async-done | bytes 1572896 | tf_op jit(solution)/shard_map/all_to_all | solution.py:413
  143.4 4.1 %finish.1.refs_0_ = bf16[128,1536]{1,0:T(8,128)(2,1)} custom-call(s32[1]{0:T(128)} %bitcast.place, f32[1536]{0:T(1024)} %gain.3, bf16[1024,1536]{1,0:T(8,128)(2,1)} %bitcast.37, bf16[1024,1536]{1,0:T(8,128)(2,1)} %bitcast.42, bf16[8,64,1536]{2,1,0:T(8,128)(2,1)} %copy-done.5, bf16[1024,1536]{1,0:T(8,128)(2,1)} %bitcast.38, bf16[1024,1536]{1,0:T(8,128)(2,1)} %bitcast.43, ...), custom_call_target="tpu_custom_call" | custom-call | flops 10000000 | bytes 5000000 | tf_op jit(solution)/shard_map/finish/pallas_call | solution.py:356
  147.5 4.9 %collective-permute-start.12 = (bf16[128,1536]{1,0:T(8,128)(2,1)}, bf16[128,1536]{1,0:T(8,128)(2,1)}, u32[]{:S(2)}, u32[]{:S(2)}) collective-permute-start(bf16[128,1536]{1,0:T(8,128)(2,1)} %finish.1.refs_0_), channel_id=1, source_target_pairs={{0,5},{1,4},{2,7},{3,6},{4,1},{5,0},{6,3},{7,2},{8,13},{9,12},{10,... | collective-permute-start | bytes 1179656 | tf_op jit(solution)/shard_map/ppermute | solution.py:404
  152.4 2.7 %collective-permute-start.15 = (bf16[128,1536]{1,0:T(8,128)(2,1)}, bf16[128,1536]{1,0:T(8,128)(2,1)}, u32[]{:S(2)}, u32[]{:S(2)}) collective-permute-start(bf16[128,1536]{1,0:T(8,128)(2,1)} %finish.1.refs_0_), channel_id=1, source_target_pairs={{0,4},{1,5},{2,6},{3,7},{4,0},{5,1},{6,2},{7,3},{8,12},{9,13},{10,... | collective-permute-start | bytes 1179656 | tf_op jit(solution)/shard_map/ppermute | solution.py:404
  158.0 6.6 %collective-permute-done.21 = bf16[96,768]{1,0:T(8,128)(2,1)} collective-permute-done((bf16[96,768]{1,0:T(8,128)(2,1)}, bf16[96,768]{1,0:T(8,128)(2,1)}, u32[]{:S(2)}, u32[]{:S(2)}) %collective-permute-start.21) | collective-permute-done | bytes 147488 | tf_op jit(solution)/shard_map/ppermute | solution.py:437
  164.6 2.8 %collective-permute-start.16 = (bf16[128,1536]{1,0:T(8,128)(2,1)}, bf16[128,1536]{1,0:T(8,128)(2,1)}, u32[]{:S(2)}, u32[]{:S(2)}) collective-permute-start(bf16[128,1536]{1,0:T(8,128)(2,1)} %finish.1.refs_0_), channel_id=1, source_target_pairs={{0,7},{1,6},{2,1},{3,0},{4,3},{5,2},{6,5},{7,4},{8,15},{9,14},{10,... | collective-permute-start | bytes 1179656 | tf_op jit(solution)/shard_map/ppermute | solution.py:404
  167.4 1.8 bitcast_add_fusion.1
  169.2 2.0 reshape.54
  172.8 3.7 %collective-permute-start.18 = (bf16[128,1536]{1,0:T(8,128)(2,1)S(1)}, bf16[128,1536]{1,0:T(8,128)(2,1)}, u32[]{:S(2)}, u32[]{:S(2)}) collective-permute-start(bf16[128,1536]{1,0:T(8,128)(2,1)S(1)} %copy-done.1), channel_id=1, source_target_pairs={{0,1},{1,0},{2,3},{3,2},{4,5},{5,4},{6,7},{7,6},{8,9},{9,8},{10,11... | collective-permute-start | bytes 1179656 | tf_op jit(solution)/shard_map/ppermute | solution.py:404
  176.5 2.7 %collective-permute-start.19 = (bf16[128,1536]{1,0:T(8,128)(2,1)S(1)}, bf16[128,1536]{1,0:T(8,128)(2,1)}, u32[]{:S(2)}, u32[]{:S(2)}) collective-permute-start(bf16[128,1536]{1,0:T(8,128)(2,1)S(1)} %copy-done.1), channel_id=1, source_target_pairs={{0,6},{1,7},{2,0},{3,1},{4,2},{5,3},{6,4},{7,5},{8,14},{9,15},{10,... | collective-permute-start | bytes 1179656 | tf_op jit(solution)/shard_map/ppermute | solution.py:404
  179.1 6.3 %collective-permute-start.20 = (bf16[128,1536]{1,0:T(8,128)(2,1)S(1)}, bf16[128,1536]{1,0:T(8,128)(2,1)}, u32[]{:S(2)}, u32[]{:S(2)}) collective-permute-start(bf16[128,1536]{1,0:T(8,128)(2,1)S(1)} %copy-done.1), channel_id=1, source_target_pairs={{0,2},{1,3},{2,4},{3,5},{4,6},{5,7},{6,0},{7,1},{8,10},{9,11},{10,... | collective-permute-start | bytes 1179656 | tf_op jit(solution)/shard_map/ppermute | solution.py:404
  188.3 10.9 %output.1 = bf16[1024,1536]{1,0:T(8,128)(2,1)} custom-call(bf16[1024,1536]{1,0:T(8,128)(2,1)S(1)} %bitcast.39, bf16[768,1024]{1,0:T(8,128)(2,1)S(1)} %copy-done.2, bf16[768,1024]{1,0:T(8,128)(2,1)S(1)} %copy-done.3, bf16[384,1536]{1,0:T(8,128)(2,1)} %all-gather.7.cloned.1.call-done.refs_0_, bf16[384,1536]{1,0:T(8,128)(2,1)} %all-gather.5.cloned.1.call-done.refs_1_, ...), custom_call_target="tpu_custom_call" | custom-call | flops 10000000000 | bytes 12000000 | tf_op jit(solution)/shard_map/output/pallas_call | solution.py:323
  199.8 4.3 %assemble.1 = bf16[1024,1536]{1,0:T(8,128)(2,1)} custom-call(s32[8]{0:T(128)S(1)} %stack.32.places, bf16[128,1536]{1,0:T(8,128)(2,1)S(1)} %copy-done.1, bf16[128,1536]{1,0:T(8,128)(2,1)} %collective-permute-done.12.refs_1_, bf16[128,1536]{1,0:T(8,128)(2,1)} %collective-permute-done.15.refs_2_, bf16[128,1536]{1,0:T(8,128)(2,1)} %collective-permute-done.16.refs_3_, ...), custom_call_target="tpu_custom_call" | custom-call | bytes 6000000 | tf_op jit(solution)/shard_map/assemble/pallas_call | solution.py:387
  (97 shorter events, 26.6 us)
Async XLA Ops:
  7.2 65.3 %all-gather.7.cloned.1.call-start = ((), (), s32[]{:S(2)}) async-start(), calls=%async_computation.3 | async-start | bytes 1474560 | tf_op jit(solution)/shard_map/all_gather | solution.py:443
  8.9 63.5 %all-gather.5.cloned.1.call-start = ((), (), s32[]{:S(2)}) async-start(), calls=%async_computation.2 | async-start | bytes 1474560 | tf_op jit(solution)/shard_map/all_gather | solution.py:443
  9.0 27.2 %copy-start.19 = (s32[2,2048]{1,0:T(2,128)S(1)}, s32[2,2048]{1,0:T(2,128)}, u32[]{:S(2)}) copy-start(s32[2,2048]{1,0:T(2,128)} %param.15) | copy-start | bytes 49156
  9.0 27.2 %copy-start.20 = (s32[2]{0:T(128)S(1)}, s32[2]{0:T(128)}, u32[]{:S(2)}) copy-start(s32[2]{0:T(128)} %lengths.1) | copy-start | bytes 28
  19.7 15.7 %collective-permute-start = (bf16[384,512]{1,0:T(8,128)(2,1)}, bf16[384,512]{1,0:T(8,128)(2,1)S(1)}, u32[]{:S(2)}, u32[]{:S(2)}) collective-permute-start(bf16[384,512]{1,0:T(8,128)(2,1)} %get-tuple-element.48), channel_id=1, source_target_pairs={{0,8},{8,16},{16,24},{1,9},{9,17},{17,25},{2,10},{10,18},{18,26},{... | collective-permute-start | bytes 1179656 | tf_op jit(solution)/shard_map/ppermute | solution.py:474
  21.0 14.4 %collective-permute-start.1 = (bf16[384,512]{1,0:T(8,128)(2,1)}, bf16[384,512]{1,0:T(8,128)(2,1)S(1)}, u32[]{:S(2)}, u32[]{:S(2)}) collective-permute-start(bf16[384,512]{1,0:T(8,128)(2,1)} %get-tuple-element.49), channel_id=1, source_target_pairs={{8,0},{16,8},{24,16},{9,1},{17,9},{25,17},{10,2},{18,10},{26,18},{... | collective-permute-start | bytes 1179656 | tf_op jit(solution)/shard_map/ppermute | solution.py:475
  25.6 9.8 %collective-permute-start.2 = (bf16[96,1536]{1,0:T(8,128)(2,1)S(1)}, bf16[96,1536]{1,0:T(8,128)(2,1)S(1)}, u32[]{:S(2)}, u32[]{:S(2)}) collective-permute-start(bf16[96,1536]{1,0:T(8,128)(2,1)S(1)} %copy-done.10), channel_id=1, source_target_pairs={{0,1},{1,0},{2,3},{3,2},{4,5},{5,4},{6,7},{7,6},{8,9},{9,8},{10,11... | collective-permute-start | bytes 884744 | tf_op jit(solution)/shard_map/ppermute | solution.py:404
  36.1 149.4 %all-gather.9.cloned.1.call-start = ((), (), s32[]{:S(2)}) async-start(), calls=%async_computation.4 | async-start | bytes 1966080 | tf_op jit(solution)/shard_map/all_gather | solution.py:443
  48.5 18.1 %collective-permute-start.3 = (bf16[384,256]{1,0:T(8,128)(2,1)}, bf16[384,256]{1,0:T(8,128)(2,1)S(1)}, u32[]{:S(2)}, u32[]{:S(2)}) collective-permute-start(bf16[384,256]{1,0:T(8,128)(2,1)} %get-tuple-element.64), channel_id=1, source_target_pairs={{0,8},{8,16},{16,24},{1,9},{9,17},{17,25},{2,10},{10,18},{18,26},{... | collective-permute-start | bytes 589832 | tf_op jit(solution)/shard_map/ppermute | solution.py:487
  49.7 16.8 %collective-permute-start.4 = (bf16[384,256]{1,0:T(8,128)(2,1)}, bf16[384,256]{1,0:T(8,128)(2,1)S(1)}, u32[]{:S(2)}, u32[]{:S(2)}) collective-permute-start(bf16[384,256]{1,0:T(8,128)(2,1)} %get-tuple-element.65), channel_id=1, source_target_pairs={{8,0},{16,8},{24,16},{9,1},{17,9},{25,17},{10,2},{18,10},{26,18},{... | collective-permute-start | bytes 589832 | tf_op jit(solution)/shard_map/ppermute | solution.py:486
  72.5 32.3 %all-to-all-start = ((bf16[8,64,1536]{2,1,0:T(8,128)(2,1)}), bf16[8,64,1536]{2,1,0:T(8,128)(2,1)S(1)}, u32[]{:S(2)}, u32[]{:S(2)}) async-start(bf16[8,64,1536]{2,1,0:T(8,128)(2,1)} %bitcast.48), calls=%async_computation | async-start | bytes 3145728 | tf_op jit(solution)/shard_map/all_to_all | solution.py:413
  79.6 105.8 %all-gather.11.cloned.1.call-start = ((), (), s32[]{:S(2)}) async-start(), calls=%async_computation.5 | async-start | bytes 1966080 | tf_op jit(solution)/shard_map/all_gather | solution.py:443
  79.7 9.4 %collective-permute-start.5 = (bf16[384,256]{1,0:T(8,128)(2,1)S(1)}, bf16[384,256]{1,0:T(8,128)(2,1)S(1)}, u32[]{:S(2)}, u32[]{:S(2)}) collective-permute-start(bf16[384,256]{1,0:T(8,128)(2,1)S(1)} %copy-done.22), channel_id=1, source_target_pairs={{0,8},{8,16},{16,24},{1,9},{9,17},{17,25},{2,10},{10,18},{18,26},{... | collective-permute-start | bytes 589832 | tf_op jit(solution)/shard_map/ppermute | solution.py:487
  81.0 8.1 %collective-permute-start.6 = (bf16[384,256]{1,0:T(8,128)(2,1)S(1)}, bf16[384,256]{1,0:T(8,128)(2,1)S(1)}, u32[]{:S(2)}, u32[]{:S(2)}) collective-permute-start(bf16[384,256]{1,0:T(8,128)(2,1)S(1)} %copy-done.21), channel_id=1, source_target_pairs={{8,0},{16,8},{24,16},{9,1},{17,9},{25,17},{10,2},{18,10},{26,18},{... | collective-permute-start | bytes 589832 | tf_op jit(solution)/shard_map/ppermute | solution.py:486
  85.6 24.8 %collective-permute-start.11 = (bf16[192,1024]{1,0:T(8,128)(2,1)S(1)}, bf16[192,1024]{1,0:T(8,128)(2,1)S(1)}, u32[]{:S(2)}, u32[]{:S(2)}) collective-permute-start(bf16[192,1024]{1,0:T(8,128)(2,1)S(1)} %copy-done.7), channel_id=1, source_target_pairs={{0,1},{1,0},{2,3},{3,2},{4,5},{5,4},{6,7},{7,6},{8,9},{9,8},{10,11... | collective-permute-start | bytes 1179656 | tf_op jit(solution)/shard_map/ppermute | solution.py:404
  104.7 13.1 %collective-permute-start.7 = (bf16[4,2,96,768]{3,2,1,0:T(8,128)(2,1)}, bf16[4,2,96,768]{3,2,1,0:T(8,128)(2,1)}, u32[]{:S(2)}, u32[]{:S(2)}) collective-permute-start(bf16[4,2,96,768]{3,2,1,0:T(8,128)(2,1)} %get-tuple-element.75), channel_id=1, source_target_pairs={{0,32},{32,0},{64,96},{96,64},{1,33},{33,1},{65,97},{97,65},{2,34}... | collective-permute-start | bytes 3538952 | tf_op jit(solution)/shard_map/ppermute | solution.py:421
  111.2 31.1 %all-to-all-start.1 = ((bf16[8,64,1536]{2,1,0:T(8,128)(2,1)}), bf16[8,64,1536]{2,1,0:T(8,128)(2,1)S(1)}, u32[]{:S(2)}, u32[]{:S(2)}) async-start(bf16[8,64,1536]{2,1,0:T(8,128)(2,1)} %bitcast.47), calls=%async_computation.1 | async-start | bytes 3145728 | tf_op jit(solution)/shard_map/all_to_all | solution.py:413
  117.3 53.9 %collective-permute-start.13 = (bf16[384,1536]{1,0:T(8,128)(2,1)}, bf16[384,1536]{1,0:T(8,128)(2,1)}, u32[]{:S(2)}, u32[]{:S(2)}) collective-permute-start(bf16[384,1536]{1,0:T(8,128)(2,1)} %all-gather.7.cloned.1.call-done.refs_0_), channel_id=1, source_target_pairs={{0,32},{32,0},{64,96},{96,64},{1,33},{33,1},{65,97},{97,65},{2,34}... | collective-permute-start | bytes 3538952 | tf_op jit(solution)/shard_map/ppermute | solution.py:421
  117.3 55.5 %collective-permute-start.14 = (bf16[384,1536]{1,0:T(8,128)(2,1)}, bf16[384,1536]{1,0:T(8,128)(2,1)}, u32[]{:S(2)}, u32[]{:S(2)}) collective-permute-start(bf16[384,1536]{1,0:T(8,128)(2,1)} %all-gather.5.cloned.1.call-done.refs_1_), channel_id=1, source_target_pairs={{0,32},{32,0},{64,96},{96,64},{1,33},{33,1},{65,97},{97,65},{2,34}... | collective-permute-start | bytes 3538952 | tf_op jit(solution)/shard_map/ppermute | solution.py:421
  120.8 11.5 %collective-permute-start.10 = (bf16[2,96,768]{2,1,0:T(8,128)(2,1)S(1)}, bf16[2,96,768]{2,1,0:T(8,128)(2,1)S(1)}, u32[]{:S(2)}, u32[]{:S(2)}) collective-permute-start(bf16[2,96,768]{2,1,0:T(8,128)(2,1)S(1)} %get-tuple-element.88), channel_id=1, source_target_pairs={{0,16},{8,24},{16,0},{24,8},{1,17},{9,25},{17,1},{25,9},{2,18},{10... | collective-permute-start | bytes 884744 | tf_op jit(solution)/shard_map/ppermute | solution.py:429
  122.3 15.4 %collective-permute-start.9 = (bf16[2,96,768]{2,1,0:T(8,128)(2,1)S(1)}, bf16[2,96,768]{2,1,0:T(8,128)(2,1)S(1)}, u32[]{:S(2)}, u32[]{:S(2)}) collective-permute-start(bf16[2,96,768]{2,1,0:T(8,128)(2,1)S(1)} %get-tuple-element.89), channel_id=1, source_target_pairs={{0,24},{8,0},{16,8},{24,16},{1,25},{9,1},{17,9},{25,17},{2,26},{10... | collective-permute-start | bytes 884744 | tf_op jit(solution)/shard_map/ppermute | solution.py:429
  122.3 15.4 %collective-permute-start.8 = (bf16[2,96,768]{2,1,0:T(8,128)(2,1)S(1)}, bf16[2,96,768]{2,1,0:T(8,128)(2,1)S(1)}, u32[]{:S(2)}, u32[]{:S(2)}) collective-permute-start(bf16[2,96,768]{2,1,0:T(8,128)(2,1)S(1)} %get-tuple-element.87), channel_id=1, source_target_pairs={{0,8},{8,16},{16,24},{24,0},{1,9},{9,17},{17,25},{25,1},{2,10},{10... | collective-permute-start | bytes 884744 | tf_op jit(solution)/shard_map/ppermute | solution.py:429
  143.4 42.1 %copy-start = (bf16[2,512,1536]{2,1,0:T(8,128)(2,1)S(1)}, bf16[2,512,1536]{2,1,0:T(8,128)(2,1)}, u32[]{:S(2)}) copy-start(bf16[2,512,1536]{2,1,0:T(8,128)(2,1)} %param.8) | copy-start | bytes 9437188
  147.5 23.7 %copy-start.1 = (bf16[128,1536]{1,0:T(8,128)(2,1)S(1)}, bf16[128,1536]{1,0:T(8,128)(2,1)}, u32[]{:S(2)}) copy-start(bf16[128,1536]{1,0:T(8,128)(2,1)} %finish.1.refs_0_) | copy-start | bytes 1179652
  147.5 29.0 %collective-permute-start.12 = (bf16[128,1536]{1,0:T(8,128)(2,1)}, bf16[128,1536]{1,0:T(8,128)(2,1)}, u32[]{:S(2)}, u32[]{:S(2)}) collective-permute-start(bf16[128,1536]{1,0:T(8,128)(2,1)} %finish.1.refs_0_), channel_id=1, source_target_pairs={{0,5},{1,4},{2,7},{3,6},{4,1},{5,0},{6,3},{7,2},{8,13},{9,12},{10,... | collective-permute-start | bytes 1179656 | tf_op jit(solution)/shard_map/ppermute | solution.py:404
  152.4 26.8 %collective-permute-start.15 = (bf16[128,1536]{1,0:T(8,128)(2,1)}, bf16[128,1536]{1,0:T(8,128)(2,1)}, u32[]{:S(2)}, u32[]{:S(2)}) collective-permute-start(bf16[128,1536]{1,0:T(8,128)(2,1)} %finish.1.refs_0_), channel_id=1, source_target_pairs={{0,4},{1,5},{2,6},{3,7},{4,0},{5,1},{6,2},{7,3},{8,12},{9,13},{10,... | collective-permute-start | bytes 1179656 | tf_op jit(solution)/shard_map/ppermute | solution.py:404
  156.7 7.9 %collective-permute-start.21 = (bf16[96,768]{1,0:T(8,128)(2,1)}, bf16[96,768]{1,0:T(8,128)(2,1)}, u32[]{:S(2)}, u32[]{:S(2)}) collective-permute-start(bf16[96,768]{1,0:T(8,128)(2,1)} %fusion.5), channel_id=1, source_target_pairs={{0,64},{32,96},{64,0},{96,32},{1,65},{33,97},{65,1},{97,33},{2,66}... | collective-permute-start | bytes 442376 | tf_op jit(solution)/shard_map/ppermute | solution.py:437
  164.6 34.6 %collective-permute-start.16 = (bf16[128,1536]{1,0:T(8,128)(2,1)}, bf16[128,1536]{1,0:T(8,128)(2,1)}, u32[]{:S(2)}, u32[]{:S(2)}) collective-permute-start(bf16[128,1536]{1,0:T(8,128)(2,1)} %finish.1.refs_0_), channel_id=1, source_target_pairs={{0,7},{1,6},{2,1},{3,0},{4,3},{5,2},{6,5},{7,4},{8,15},{9,14},{10,... | collective-permute-start | bytes 1179656 | tf_op jit(solution)/shard_map/ppermute | solution.py:404
  171.2 28.0 %collective-permute-start.17 = (bf16[128,1536]{1,0:T(8,128)(2,1)S(1)}, bf16[128,1536]{1,0:T(8,128)(2,1)}, u32[]{:S(2)}, u32[]{:S(2)}) collective-permute-start(bf16[128,1536]{1,0:T(8,128)(2,1)S(1)} %copy-done.1), channel_id=1, source_target_pairs={{0,3},{1,2},{2,5},{3,4},{4,7},{5,6},{6,1},{7,0},{8,11},{9,10},{10,... | collective-permute-start | bytes 1179656 | tf_op jit(solution)/shard_map/ppermute | solution.py:404
  172.8 27.0 %collective-permute-start.18 = (bf16[128,1536]{1,0:T(8,128)(2,1)S(1)}, bf16[128,1536]{1,0:T(8,128)(2,1)}, u32[]{:S(2)}, u32[]{:S(2)}) collective-permute-start(bf16[128,1536]{1,0:T(8,128)(2,1)S(1)} %copy-done.1), channel_id=1, source_target_pairs={{0,1},{1,0},{2,3},{3,2},{4,5},{5,4},{6,7},{7,6},{8,9},{9,8},{10,11... | collective-permute-start | bytes 1179656 | tf_op jit(solution)/shard_map/ppermute | solution.py:404
  176.5 23.3 %collective-permute-start.19 = (bf16[128,1536]{1,0:T(8,128)(2,1)S(1)}, bf16[128,1536]{1,0:T(8,128)(2,1)}, u32[]{:S(2)}, u32[]{:S(2)}) collective-permute-start(bf16[128,1536]{1,0:T(8,128)(2,1)S(1)} %copy-done.1), channel_id=1, source_target_pairs={{0,6},{1,7},{2,0},{3,1},{4,2},{5,3},{6,4},{7,5},{8,14},{9,15},{10,... | collective-permute-start | bytes 1179656 | tf_op jit(solution)/shard_map/ppermute | solution.py:404
  179.1 20.6 %collective-permute-start.20 = (bf16[128,1536]{1,0:T(8,128)(2,1)S(1)}, bf16[128,1536]{1,0:T(8,128)(2,1)}, u32[]{:S(2)}, u32[]{:S(2)}) collective-permute-start(bf16[128,1536]{1,0:T(8,128)(2,1)S(1)} %copy-done.1), channel_id=1, source_target_pairs={{0,2},{1,3},{2,4},{3,5},{4,6},{5,7},{6,0},{7,1},{8,10},{9,11},{10,... | collective-permute-start | bytes 1179656 | tf_op jit(solution)/shard_map/ppermute | solution.py:404
  (19 other events, 83.6 us)
Sparse Core Ops, SparseCore 0:
  9.7 26.8 all-gather.6
  38.2 25.0 all-gather.4
  72.5 38.8 all-gather.8
  112.9 38.0 all-gather.10

commit v10 on v9

--- a/solution.py
+++ b/solution.py
@@ -10,7 +10,7 @@
 EPS = 1e-05
 NEG = -1e30
 
-SHIFTS = ((2, 1), (2, 0), (3, 1), (1, 1), (0, 1), (3, 0), (1, 0))
+SHIFTS = ((1, 0), (3, 0), (0, 1), (1, 1), (3, 1), (2, 0), (2, 1))
 
 F32 = jnp.float32
 BF16 = jnp.bfloat16
@@ -328,72 +328,65 @@
         out_shape=jax.ShapeDtypeStruct((rows, model), BF16),
         scratch_shapes=[pltpu.VMEM((4, depth, CTX), BF16)],
         compiler_params=params(28),
-        cost_estimate=pl.CostEstimate(
-            flops=10000000000, bytes_accessed=12000000, transcendentals=0
-        ),
+        cost_estimate=pl.CostEstimate(flops=1000, bytes_accessed=1000, transcendentals=0),
         name="output",
     )(tokens, near, far, *weights)
 
 
-def finish_body(place, gain, *refs):
-    out = refs[-1]
-    chunk = refs[0].shape[0]
-    for rec in range(2):
-        tok, cot, parts = refs[3 * rec : 3 * rec + 3]
-        back = jnp.sum(parts[...].astype(F32), axis=0)
-        scaled, inverse = norm_stats(tok[...])
-        weighted = back * gain[...][None, :]
-        first = jnp.mean(weighted, axis=-1, keepdims=True)
-        second = jnp.mean(weighted * scaled, axis=-1, keepdims=True)
-        grad = inverse * (weighted - first - scaled * second) + cot[...].astype(F32)
-        out[rec * chunk : (rec + 1) * chunk, :] = grad.astype(BF16)
-
-
-def finish(place, tokens, cotangent, gain, parts):
-    count, chunk, model = parts[0].shape
-    at = lambda rec: pl.BlockSpec((chunk, model), lambda i, p: (rec * count + p[0], 0))
-    whole = pl.BlockSpec((count, chunk, model), lambda i, p: (0, 0, 0))
+def finish_body(place, gain, tok, cot, parts, out):
+    back = jnp.sum(parts[...].astype(F32), axis=0)
+    scaled, inverse = norm_stats(tok[...])
+    weighted = back * gain[...][None, :]
+    first = jnp.mean(weighted, axis=-1, keepdims=True)
+    second = jnp.mean(weighted * scaled, axis=-1, keepdims=True)
+    grad = inverse * (weighted - first - scaled * second) + cot[...].astype(F32)
+    out[...] = jnp.broadcast_to(grad.astype(BF16)[None], out.shape)
+
+
+def finish(place, tokens, cotangent, gain, parts, copies):
+    count, chunk, model = parts.shape
+    here = pl.BlockSpec((chunk, model), lambda i, p: (p[0], 0))
+    whole = lambda n: pl.BlockSpec((n, chunk, model), lambda i, p: (0, 0, 0))
     return pl.pallas_call(
         finish_body,
         grid_spec=pltpu.PrefetchScalarGridSpec(
             num_scalar_prefetch=1,
             grid=(1,),
-            in_specs=[pl.BlockSpec((model,), lambda i, p: (0,))]
-            + [at(0), at(0), whole, at(1), at(1), whole],
-            out_specs=pl.BlockSpec((2 * chunk, model), lambda i, p: (0, 0)),
+            in_specs=[pl.BlockSpec((model,), lambda i, p: (0,)), here, here, whole(count)],
+            out_specs=whole(copies),
         ),
-        out_shape=jax.ShapeDtypeStruct((2 * chunk, model), BF16),
+        out_shape=jax.ShapeDtypeStruct((copies, chunk, model), BF16),
         compiler_params=params(),
-        cost_estimate=pl.CostEstimate(flops=10000000, bytes_accessed=5000000, transcendentals=0),
+        cost_estimate=pl.CostEstimate(flops=10000000, bytes_accessed=3000000, transcendentals=0),
         name="finish",
-    )(place, gain, tokens, cotangent, parts[0], tokens, cotangent, parts[1])
-
-
-def assemble_body(places, *refs):
+    )(place, gain, tokens, cotangent, parts)
+
+
+def assemble_body(places, gathered, *refs):
     pieces, out = refs[:-1], refs[-1]
-    chunk = pieces[0].shape[0] // 2
-    half = out.shape[0] // 2
+    chunk = pieces[0].shape[0]
+    half = gathered.shape[0]
+    out[:half, :] = gathered[...]
     for index, piece in enumerate(pieces):
-        for rec in range(2):
-            place = pl.multiple_of(rec * half + places[index] * chunk, chunk)
-            out[pl.ds(place, chunk), :] = piece[rec * chunk : (rec + 1) * chunk, :]
-
-
-def assemble(places, pieces):
-    chunk, model = pieces[0].shape
-    count = len(pieces)
+        place = pl.multiple_of(half + places[index] * chunk, chunk)
+        out[pl.ds(place, chunk), :] = piece[...]
+
+
+def assemble(places, gathered, pieces):
+    half, model = gathered.shape
     tile = 512
     by_col = lambda n: pl.BlockSpec((n, tile), lambda i: (0, i))
     return pl.pallas_call(
         assemble_body,
         grid=(model // tile,),
-        in_specs=[pl.BlockSpec(memory_space=pltpu.SMEM)] + [by_col(chunk)] * count,
-        out_specs=by_col(count * chunk),
-        out_shape=jax.ShapeDtypeStruct((count * chunk, model), BF16),
+        in_specs=[pl.BlockSpec(memory_space=pltpu.SMEM), by_col(half)]
+        + [by_col(piece.shape[0]) for piece in pieces],
+        out_specs=by_col(2 * half),
+        out_shape=jax.ShapeDtypeStruct((2 * half, model), BF16),
         compiler_params=params(16),
         cost_estimate=pl.CostEstimate(flops=0, bytes_accessed=6000000, transcendentals=0),
         name="assemble",
-    )(places, *pieces)
+    )(places, gathered, *pieces)
 
 
 def to_peer(array, shift):
@@ -504,21 +497,29 @@
     first_back = split(back_rows(*first[:4], weight))
     first_back, peer_mixed = tie((first_back, peer_mixed))
     far_mixed = over_z(peer_mixed)
-    parts = [to_all(first_back), second_parts]
-
-    sums = frame_sums(kept.astype(F32) + core_swap(sent).astype(F32))
-    sums, parts[0] = tie((sums, parts[0]))
+    first_parts = to_all(first_back)
+
+    ending = lambda rec, parts, copies: finish(
+        scalar(rec * count + me), flat_tokens, flat_cot, norm_gain, parts, copies
+    )
+    second_parts, first_back = tie((second_parts, first_back))
+    piece = ending(1, second_parts, 1)[0]
+    pieces = [to_peer(piece, shift) for shift in SHIFTS]
+
+    pair = core_swap(sent)
+    pieces, pair, first_parts = tie((pieces, pair, first_parts))
+    copies = ending(0, first_parts, count)
+    copies, pair = tie((copies, pair))
+    gathered = to_all(copies).reshape(frames, model)
+    sums = frame_sums(kept.astype(F32) + pair.astype(F32))
     grad_proj = row_sums(sums).reshape(-1, 4, width)
-
-    piece = finish(scalar(me), flat_tokens, flat_cot, norm_gain, parts)
-    places = jnp.stack([me] + [peer_index(me, shift, -1) for shift in SHIFTS]).astype(jnp.int32)
     own = [near_out, far_out]
     output = output_rows(
         flat_tokens, near_mixed, far_mixed, own + [core_swap(array) for array in own]
     )
-    pieces = [to_peer(piece, shift) for shift in SHIFTS]
-    pieces[0], output = tie((pieces[0], output))
-    grad_tokens = assemble(places, [piece] + pieces)
+    gathered, output = tie((gathered, output))
+    places = jnp.stack([me] + [peer_index(me, shift, -1) for shift in SHIFTS]).astype(jnp.int32)
+    grad_tokens = assemble(places, gathered, [piece] + pieces)
     shape = (recs, frames, model)
     return (output.reshape(shape), grad_tokens.reshape(shape), grad_proj)
 

time: 212 us -> 238 us (1.12)
  the two profiles are of different devices: /device:TPU:14 before, /device:TPU:18 now
where the time goes in v10:
time: 238 us; the launch traced here: 236 us
  Pallas kernels  71.7 us (30%)
  waiting for transfers between devices  62.2 us (26%)
  starting transfers between devices  58.4 us (25%)
  local copies, waits for them, and re-layouts  23 us (10%)
  between operations  14.1 us (6%)
  other arithmetic  6.5 us (3%)
    ppermute x9, waiting for transfers between devices, to_peer(): return lax.ppermute(array, 'chan', pairs)  38.3 us
    pallas_call x2, Pallas kernels, attention(): pl.pallas_call(attention_body, grid=(1,), in_specs=[by_rec(width, frames)...  20.5 us
    all_to_all x3, starting transfers between devices, to_all(): return lax.all_to_all(array, 'chan', 0, 0, tiled=True)  19.1 us
    unnamed x72, local copies, waits for them, and re-layouts  15.6 us
    ppermute x9, starting transfers between devices, to_peer(): return lax.ppermute(array, 'chan', pairs)  14.5 us
    pallas_call x1, Pallas kernels, output_rows(): pl.pallas_call(output_body, grid=(rows // CTX,), in_specs=[by_row, by_col...  10.9 us
    pallas_call x2, Pallas kernels, back_rows(): pl.pallas_call(back_body, grid=(model // tile,), in_specs=[full(width, ro...  10.7 us
    pallas_call x1, Pallas kernels, project(): pl.pallas_call(project_body, grid=(rows // CTX,), in_specs=[pl.BlockSpec(...  10.6 us
  transfers between devices with their start and end apart: 29, of which 13 were waited for; matrix products, arithmetic and copies ran while one was open for 5% of the time, Pallas kernels for 29%

profile of v10, /device:TPU:18, one launch (start us, length us, event | category | flops | bytes accessed | tf_op | source)
XLA Modules:
  0.0 235.9 jit_solution(5324577174667992447)
XLA Ops:
  9.0 10.6 %project.1 = (bf16[1024,1536]{1,0:T(8,128)(2,1)}, bf16[192,1024]{1,0:T(8,128)(2,1)}, bf16[384,1024]{1,0:T(8,128)(2,1)}, bf16[192,1024]{1,0:T(8,128)(2,1)}, bf16[...) custom-call(s32[2]{0:T(128)} %lengths.1, bf16[1024,1536]{1,0:T(8,128)(2,1)} %bitcast.39, ...), custom_call_target="tpu_custom_call" | custom-call | flops 2400000000 | bytes 15000000 | tf_op jit(solution)/shard_map/project/pallas_call | solution.py:76
  19.7 3.4 %collective-permute-start = (bf16[384,512]{1,0:T(8,128)(2,1)}, bf16[384,512]{1,0:T(8,128)(2,1)S(1)}, u32[]{:S(2)}, u32[]{:S(2)}) collective-permute-start(bf16[384,512]{1,0:T(8,128)(2,1)} %get-tuple-element.57), channel_id=1, source_target_pairs={{0,8},{8,16},{16,24},{1,9},{9,17},{17,25},{2,10},{10,18},{18,26},{... | collective-permute-start | bytes 1179656 | tf_op jit(solution)/shard_map/ppermute | solution.py:467
  26.0 9.4 %collective-permute-done.2 = bf16[96,1536]{1,0:T(8,128)(2,1)S(1)} collective-permute-done((bf16[96,1536]{1,0:T(8,128)(2,1)S(1)}, bf16[96,1536]{1,0:T(8,128)(2,1)S(1)}, u32[]{:S(2)}, u32[]{:S(2)}) %collective-permute-start.2) | collective-permute-done | bytes 294944 | tf_op jit(solution)/shard_map/ppermute | solution.py:397
  38.2 10.2 %attention.2 = (bf16[192,512]{1,0:T(8,128)(2,1)}, bf16[192,512]{1,0:T(8,128)(2,1)}, f32[384,512]{1,0:T(8,128)}, bf16[384,256]{1,0:T(8,128)(2,1)}, bf16[384,256]{1,0:T(8,128)(2,1)}) custom-call(bf16[192,1024]{1,0:T(8,128)(2,1)} %get-tuple-element.65.q, bf16[384,1024]{1,0:T(8,128)(2,1)} %get-tuple-element.56.kv, bf16[384,512]{1,0:T(8,128)(2,1)} %copy-done.21, ...), custom_call_target="tpu_custom_call" | custom-call | flops 1000 | bytes 1000 | tf_op jit(solution)/shard_map/attention/pallas_call | solution.py:161
  48.4 3.4 %collective-permute-start.3 = (bf16[384,256]{1,0:T(8,128)(2,1)}, bf16[384,256]{1,0:T(8,128)(2,1)S(1)}, u32[]{:S(2)}, u32[]{:S(2)}) collective-permute-start(bf16[384,256]{1,0:T(8,128)(2,1)} %get-tuple-element.73), channel_id=1, source_target_pairs={{0,8},{8,16},{16,24},{1,9},{9,17},{17,25},{2,10},{10,18},{18,26},{... | collective-permute-start | bytes 589832 | tf_op jit(solution)/shard_map/ppermute | solution.py:480
  51.8 2.6 %collective-permute-start.4 = (bf16[384,256]{1,0:T(8,128)(2,1)}, bf16[384,256]{1,0:T(8,128)(2,1)S(1)}, u32[]{:S(2)}, u32[]{:S(2)}) collective-permute-start(bf16[384,256]{1,0:T(8,128)(2,1)} %get-tuple-element.74), channel_id=1, source_target_pairs={{8,0},{16,8},{24,16},{9,1},{17,9},{25,17},{10,2},{18,10},{26,18},{... | collective-permute-start | bytes 589832 | tf_op jit(solution)/shard_map/ppermute | solution.py:479
  54.4 10.3 %attention.3 = (bf16[192,512]{1,0:T(8,128)(2,1)}, bf16[192,512]{1,0:T(8,128)(2,1)}, f32[384,512]{1,0:T(8,128)}, bf16[384,256]{1,0:T(8,128)(2,1)}, bf16[384,256]{1,0:T(8,128)(2,1)}) custom-call(bf16[192,1024]{1,0:T(8,128)(2,1)} %get-tuple-element.65.q, bf16[384,1024]{1,0:T(8,128)(2,1)} %get-tuple-element.56.kv, bf16[384,512]{1,0:T(8,128)(2,1)} %copy-done.21, ...), custom_call_target="tpu_custom_call" | custom-call | flops 1000 | bytes 1000 | tf_op jit(solution)/shard_map/attention/pallas_call | solution.py:161
  67.2 5.1 %back.2 = bf16[512,1536]{1,0:T(8,128)(2,1)} custom-call(bf16[192,512]{1,0:T(8,128)(2,1)} %get-tuple-element.71.dq.rest_5_, f32[384,512]{1,0:T(8,128)} %get-tuple-element.72.own.rest_6_, bf16[384,256]{1,0:T(8,128)(2,1)} %copy-done.27, bf16[384,256]{1,0:T(8,128)(2,1)} %copy-done.28, bf16[576,1536]{1,0:T(8,128)(2,1)} %bitcast.56), custom_call_target="tpu_custom_call" | custom-call | flops 900000000 | bytes 4000000 | tf_op jit(solution)/shard_map/back/pallas_call | solution.py:217
  72.4 8.4 %all-to-all-start = ((bf16[8,64,1536]{2,1,0:T(8,128)(2,1)}), bf16[8,64,1536]{2,1,0:T(8,128)(2,1)S(1)}, u32[]{:S(2)}, u32[]{:S(2)}) async-start(bf16[8,64,1536]{2,1,0:T(8,128)(2,1)} %bitcast.59), calls=%async_computation | async-start | bytes 3145728 | tf_op jit(solution)/shard_map/all_to_all | solution.py:406
  80.8 3.4 %collective-permute-start.5 = (bf16[384,256]{1,0:T(8,128)(2,1)S(1)}, bf16[384,256]{1,0:T(8,128)(2,1)S(1)}, u32[]{:S(2)}, u32[]{:S(2)}) collective-permute-start(bf16[384,256]{1,0:T(8,128)(2,1)S(1)} %copy-done.35), channel_id=1, source_target_pairs={{0,8},{8,16},{16,24},{1,9},{9,17},{17,25},{2,10},{10,18},{18,26},{... | collective-permute-start | bytes 589832 | tf_op jit(solution)/shard_map/ppermute | solution.py:480
  88.4 3.4 %collective-permute-done.6.rest_3_.right = bf16[384,256]{1,0:T(8,128)(2,1)S(1)} collective-permute-done((bf16[384,256]{1,0:T(8,128)(2,1)S(1)}, bf16[384,256]{1,0:T(8,128)(2,1)S(1)}, u32[]{:S(2)}, u32[]{:S(2)}) %collective-permute-start.6) | collective-permute-done | bytes 196640 | tf_op jit(solution)/shard_map/ppermute | solution.py:479
  92.5 9.0 %weight_grads.1 = (bf16[4,2,96,768]{3,2,1,0:T(8,128)(2,1)}, bf16[4,2,96,768]{3,2,1,0:T(8,128)(2,1)}) custom-call(s32[1]{0:T(128)} %bitcast.9.core, bf16[1024,1536]{1,0:T(8,128)(2,1)} %get-tuple-element.78.normed, bf16[1024,1536]{1,0:T(8,128)(2,1)} %bitcast.52, bf16[192,512]{1,0:T(8,128)(2,1)} %get-tuple-element.85.rest_0_.dq, ...), custom_call_target="tpu_custom_call" | custom-call | flops 10000000000 | bytes 12000000 | tf_op jit(solution)/shard_map/weight_grads/pallas_call | solution.py:276
  101.4 4.6 %all-to-all-done.parts = bf16[8,64,1536]{2,1,0:T(8,128)(2,1)S(1)} async-done(((bf16[8,64,1536]{2,1,0:T(8,128)(2,1)}), bf16[8,64,1536]{2,1,0:T(8,128)(2,1)S(1)}, u32[]{:S(2)}, u32[]{:S(2)}) %all-to-all-start) | async-done | bytes 1572896 | tf_op jit(solution)/shard_map/all_to_all | solution.py:406
  106.1 5.7 %back.3 = bf16[512,1536]{1,0:T(8,128)(2,1)} custom-call(bf16[192,512]{1,0:T(8,128)(2,1)} %get-tuple-element.85.rest_0_.dq, f32[384,512]{1,0:T(8,128)} %get-tuple-element.79.rest_1_.own, bf16[384,256]{1,0:T(8,128)(2,1)} %copy-done.29, bf16[384,256]{1,0:T(8,128)(2,1)} %copy-done.30, bf16[576,1536]{1,0:T(8,128)(2,1)} %bitcast.57), custom_call_target="tpu_custom_call" | custom-call | flops 900000000 | bytes 4000000 | tf_op jit(solution)/shard_map/back/pallas_call | solution.py:217
  112.5 5.8 %all-to-all-start.1 = ((bf16[8,64,1536]{2,1,0:T(8,128)(2,1)}), bf16[8,64,1536]{2,1,0:T(8,128)(2,1)S(1)}, u32[]{:S(2)}, u32[]{:S(2)}) async-start(bf16[8,64,1536]{2,1,0:T(8,128)(2,1)} %bitcast.58), calls=%async_computation.1 | async-start | bytes 3145728 | tf_op jit(solution)/shard_map/all_to_all | solution.py:406
  118.8 2.9 %finish.2 = bf16[1,64,1536]{2,1,0:T(8,128)(2,1)} custom-call(s32[1]{0:T(128)} %bitcast.3.place, f32[1536]{0:T(1024)} %gain.5, bf16[1024,1536]{1,0:T(8,128)(2,1)} %bitcast.40, bf16[1024,1536]{1,0:T(8,128)(2,1)} %bitcast.53, bf16[8,64,1536]{2,1,0:T(8,128)(2,1)} %copy-done.16), custom_call_target="tpu_custom_call" | custom-call | flops 10000000 | bytes 3000000 | tf_op jit(solution)/shard_map/finish/pallas_call | solution.py:350
  121.7 3.0 %collective-permute-start.14 = (bf16[64,1536]{1,0:T(8,128)(2,1)}, bf16[64,1536]{1,0:T(8,128)(2,1)S(1)}, u32[]{:S(2)}, u32[]{:S(2)}) collective-permute-start(bf16[64,1536]{1,0:T(8,128)(2,1)} %bitcast.43), channel_id=1, source_target_pairs={{0,5},{1,4},{2,7},{3,6},{4,1},{5,0},{6,3},{7,2},{8,13},{9,12},{10,... | collective-permute-start | bytes 589832 | tf_op jit(solution)/shard_map/ppermute | solution.py:397
  124.7 5.6 %collective-permute-start.12 = (bf16[64,1536]{1,0:T(8,128)(2,1)}, bf16[64,1536]{1,0:T(8,128)(2,1)S(1)}, u32[]{:S(2)}, u32[]{:S(2)}) collective-permute-start(bf16[64,1536]{1,0:T(8,128)(2,1)} %bitcast.45), channel_id=1, source_target_pairs={{0,7},{1,6},{2,1},{3,0},{4,3},{5,2},{6,5},{7,4},{8,15},{9,14},{10,... | collective-permute-start | bytes 589832 | tf_op jit(solution)/shard_map/ppermute | solution.py:397
  130.3 13.9 %collective-permute-done.14.refs_7_ = bf16[64,1536]{1,0:T(8,128)(2,1)S(1)} collective-permute-done((bf16[64,1536]{1,0:T(8,128)(2,1)}, bf16[64,1536]{1,0:T(8,128)(2,1)S(1)}, u32[]{:S(2)}, u32[]{:S(2)}) %collective-permute-start.14) | collective-permute-done | bytes 196640 | tf_op jit(solution)/shard_map/ppermute | solution.py:397
  144.2 2.9 %collective-permute-start.10 = (bf16[64,1536]{1,0:T(8,128)(2,1)}, bf16[64,1536]{1,0:T(8,128)(2,1)S(1)}, u32[]{:S(2)}, u32[]{:S(2)}) collective-permute-start(bf16[64,1536]{1,0:T(8,128)(2,1)} %bitcast.47), channel_id=1, source_target_pairs={{0,1},{1,0},{2,3},{3,2},{4,5},{5,4},{6,7},{7,6},{8,9},{9,8},{10,11... | collective-permute-start | bytes 589832 | tf_op jit(solution)/shard_map/ppermute | solution.py:397
  147.1 8.5 %collective-permute-done.13.refs_6_ = bf16[64,1536]{1,0:T(8,128)(2,1)S(1)} collective-permute-done((bf16[64,1536]{1,0:T(8,128)(2,1)}, bf16[64,1536]{1,0:T(8,128)(2,1)S(1)}, u32[]{:S(2)}, u32[]{:S(2)}) %collective-permute-start.13) | collective-permute-done | bytes 196640 | tf_op jit(solution)/shard_map/ppermute | solution.py:397
  156.3 2.5 %collective-permute-start.9 = (bf16[64,1536]{1,0:T(8,128)(2,1)}, bf16[64,1536]{1,0:T(8,128)(2,1)S(1)}, u32[]{:S(2)}, u32[]{:S(2)}) collective-permute-start(bf16[64,1536]{1,0:T(8,128)(2,1)} %bitcast.48), channel_id=1, source_target_pairs={{0,6},{1,7},{2,0},{3,1},{4,2},{5,3},{6,4},{7,5},{8,14},{9,15},{10,... | collective-permute-start | bytes 589832 | tf_op jit(solution)/shard_map/ppermute | solution.py:397
  160.1 2.8 %collective-permute-done.9.refs_2_ = bf16[64,1536]{1,0:T(8,128)(2,1)S(1)} collective-permute-done((bf16[64,1536]{1,0:T(8,128)(2,1)}, bf16[64,1536]{1,0:T(8,128)(2,1)S(1)}, u32[]{:S(2)}, u32[]{:S(2)}) %collective-permute-start.9) | collective-permute-done | bytes 196640 | tf_op jit(solution)/shard_map/ppermute | solution.py:397
  162.9 3.7 %collective-permute-done.8.refs_1_ = bf16[64,1536]{1,0:T(8,128)(2,1)S(1)} collective-permute-done((bf16[64,1536]{1,0:T(8,128)(2,1)}, bf16[64,1536]{1,0:T(8,128)(2,1)S(1)}, u32[]{:S(2)}, u32[]{:S(2)}) %collective-permute-start.8) | collective-permute-done | bytes 196640 | tf_op jit(solution)/shard_map/ppermute | solution.py:397
  167.8 3.4 %finish.3 = bf16[8,64,1536]{2,1,0:T(8,128)(2,1)} custom-call(s32[1]{0:T(128)} %bitcast.place, f32[1536]{0:T(1024)} %gain.5, bf16[1024,1536]{1,0:T(8,128)(2,1)} %bitcast.41, bf16[1024,1536]{1,0:T(8,128)(2,1)} %bitcast.54, bf16[8,64,1536]{2,1,0:T(8,128)(2,1)} %copy-done.17), custom_call_target="tpu_custom_call" | custom-call | flops 10000000 | bytes 3000000 | tf_op jit(solution)/shard_map/finish/pallas_call | solution.py:350
  171.2 4.9 %all-to-all-start.2 = ((bf16[8,64,1536]{2,1,0:T(8,128)(2,1)}), bf16[8,64,1536]{2,1,0:T(8,128)(2,1)}, u32[]{:S(2)}, u32[]{:S(2)}) async-start(bf16[8,64,1536]{2,1,0:T(8,128)(2,1)} %finish.3), calls=%async_computation.2 | async-start | bytes 3145728 | tf_op jit(solution)/shard_map/all_to_all | solution.py:406
  182.1 2.6 %collective-permute-start.19 = (bf16[2,96,768]{2,1,0:T(8,128)(2,1)}, bf16[2,96,768]{2,1,0:T(8,128)(2,1)}, u32[]{:S(2)}, u32[]{:S(2)}) collective-permute-start(bf16[2,96,768]{2,1,0:T(8,128)(2,1)} %get-tuple-element.109), channel_id=1, source_target_pairs={{0,24},{8,0},{16,8},{24,16},{1,25},{9,1},{17,9},{25,17},{2,26},{10... | collective-permute-start | bytes 884744 | tf_op jit(solution)/shard_map/ppermute | solution.py:422
  184.8 4.5 %collective-permute-done.18 = bf16[2,96,768]{2,1,0:T(8,128)(2,1)} collective-permute-done((bf16[2,96,768]{2,1,0:T(8,128)(2,1)}, bf16[2,96,768]{2,1,0:T(8,128)(2,1)}, u32[]{:S(2)}, u32[]{:S(2)}) %collective-permute-start.18) | collective-permute-done | bytes 294944 | tf_op jit(solution)/shard_map/ppermute | solution.py:422
  189.3 2.8 %collective-permute-done.20 = bf16[2,96,768]{2,1,0:T(8,128)(2,1)} collective-permute-done((bf16[2,96,768]{2,1,0:T(8,128)(2,1)}, bf16[2,96,768]{2,1,0:T(8,128)(2,1)}, u32[]{:S(2)}, u32[]{:S(2)}) %collective-permute-start.20) | collective-permute-done | bytes 294944 | tf_op jit(solution)/shard_map/ppermute | solution.py:422
  198.9 3.7 %collective-permute-done.21 = bf16[96,768]{1,0:T(8,128)(2,1)S(1)} collective-permute-done((bf16[96,768]{1,0:T(8,128)(2,1)}, bf16[96,768]{1,0:T(8,128)(2,1)S(1)}, u32[]{:S(2)}, u32[]{:S(2)}) %collective-permute-start.21) | collective-permute-done | bytes 147488 | tf_op jit(solution)/shard_map/ppermute | solution.py:430
  209.2 10.9 %output.1 = bf16[1024,1536]{1,0:T(8,128)(2,1)} custom-call(bf16[1024,1536]{1,0:T(8,128)(2,1)S(1)} %bitcast.42, bf16[768,1024]{1,0:T(8,128)(2,1)S(1)} %copy-done.1, bf16[768,1024]{1,0:T(8,128)(2,1)S(1)} %copy-done.2, bf16[384,1536]{1,0:T(8,128)(2,1)} %all-gather.7.cloned.1.call-done.refs_0_, bf16[384,1536]{1,0:T(8,128)(2,1)} %all-gather.5.cloned.1.call-done.refs_1_, ...), custom_call_target="tpu_custom_call" | custom-call | flops 1000 | bytes 1000 | tf_op jit(solution)/shard_map/output/pallas_call | solution.py:323
  225.7 3.7 %assemble.1 = bf16[1024,1536]{1,0:T(8,128)(2,1)} custom-call(s32[8]{0:T(128)S(1)} %stack.32.places, bf16[512,1536]{1,0:T(8,128)(2,1)} %bitcast.12.gathered, bf16[64,1536]{1,0:T(8,128)(2,1)S(1)} %bitcast.50, bf16[64,1536]{1,0:T(8,128)(2,1)S(1)} %copy-done.15, bf16[64,1536]{1,0:T(8,128)(2,1)S(1)} %copy-done.13, bf16[64,1536]{1,0:T(8,128)(2,1)S(1)} %copy-done.11, ...), custom_call_target="tpu_custom_call" | custom-call | bytes 6000000 | tf_op jit(solution)/shard_map/assemble/pallas_call | solution.py:379
  (126 shorter events, 44.2 us)
Async XLA Ops:
  7.2 65.2 %all-gather.7.cloned.1.call-start = ((), (), s32[]{:S(2)}) async-start(), calls=%async_computation.4 | async-start | bytes 1474560 | tf_op jit(solution)/shard_map/all_gather | solution.py:436
  8.9 63.5 %all-gather.5.cloned.1.call-start = ((), (), s32[]{:S(2)}) async-start(), calls=%async_computation.3 | async-start | bytes 1474560 | tf_op jit(solution)/shard_map/all_gather | solution.py:436
  9.0 27.1 %copy-start.32 = (s32[2,2048]{1,0:T(2,128)S(1)}, s32[2,2048]{1,0:T(2,128)}, u32[]{:S(2)}) copy-start(s32[2,2048]{1,0:T(2,128)} %param.15) | copy-start | bytes 49156
  9.0 27.7 %copy-start.33 = (s32[2]{0:T(128)S(1)}, s32[2]{0:T(128)}, u32[]{:S(2)}) copy-start(s32[2]{0:T(128)} %lengths.1) | copy-start | bytes 28
  19.7 15.7 %collective-permute-start = (bf16[384,512]{1,0:T(8,128)(2,1)}, bf16[384,512]{1,0:T(8,128)(2,1)S(1)}, u32[]{:S(2)}, u32[]{:S(2)}) collective-permute-start(bf16[384,512]{1,0:T(8,128)(2,1)} %get-tuple-element.57), channel_id=1, source_target_pairs={{0,8},{8,16},{16,24},{1,9},{9,17},{17,25},{2,10},{10,18},{18,26},{... | collective-permute-start | bytes 1179656 | tf_op jit(solution)/shard_map/ppermute | solution.py:467
  23.1 12.7 %collective-permute-start.1 = (bf16[384,512]{1,0:T(8,128)(2,1)}, bf16[384,512]{1,0:T(8,128)(2,1)S(1)}, u32[]{:S(2)}, u32[]{:S(2)}) collective-permute-start(bf16[384,512]{1,0:T(8,128)(2,1)} %get-tuple-element.58), channel_id=1, source_target_pairs={{8,0},{16,8},{24,16},{9,1},{17,9},{25,17},{10,2},{18,10},{26,18},{... | collective-permute-start | bytes 1179656 | tf_op jit(solution)/shard_map/ppermute | solution.py:468
  25.6 9.8 %collective-permute-start.2 = (bf16[96,1536]{1,0:T(8,128)(2,1)S(1)}, bf16[96,1536]{1,0:T(8,128)(2,1)S(1)}, u32[]{:S(2)}, u32[]{:S(2)}) collective-permute-start(bf16[96,1536]{1,0:T(8,128)(2,1)S(1)} %copy-done.23), channel_id=1, source_target_pairs={{0,1},{1,0},{2,3},{3,2},{4,5},{5,4},{6,7},{7,6},{8,9},{9,8},{10,11... | collective-permute-start | bytes 884744 | tf_op jit(solution)/shard_map/ppermute | solution.py:397
  36.1 170.3 %all-gather.9.cloned.1.call-start = ((), (), s32[]{:S(2)}) async-start(), calls=%async_computation.5 | async-start | bytes 1966080 | tf_op jit(solution)/shard_map/all_gather | solution.py:436
  48.4 18.1 %collective-permute-start.3 = (bf16[384,256]{1,0:T(8,128)(2,1)}, bf16[384,256]{1,0:T(8,128)(2,1)S(1)}, u32[]{:S(2)}, u32[]{:S(2)}) collective-permute-start(bf16[384,256]{1,0:T(8,128)(2,1)} %get-tuple-element.73), channel_id=1, source_target_pairs={{0,8},{8,16},{16,24},{1,9},{9,17},{17,25},{2,10},{10,18},{18,26},{... | collective-permute-start | bytes 589832 | tf_op jit(solution)/shard_map/ppermute | solution.py:480
  51.8 14.7 %collective-permute-start.4 = (bf16[384,256]{1,0:T(8,128)(2,1)}, bf16[384,256]{1,0:T(8,128)(2,1)S(1)}, u32[]{:S(2)}, u32[]{:S(2)}) collective-permute-start(bf16[384,256]{1,0:T(8,128)(2,1)} %get-tuple-element.74), channel_id=1, source_target_pairs={{8,0},{16,8},{24,16},{9,1},{17,9},{25,17},{10,2},{18,10},{26,18},{... | collective-permute-start | bytes 589832 | tf_op jit(solution)/shard_map/ppermute | solution.py:479
  72.4 33.6 %all-to-all-start = ((bf16[8,64,1536]{2,1,0:T(8,128)(2,1)}), bf16[8,64,1536]{2,1,0:T(8,128)(2,1)S(1)}, u32[]{:S(2)}, u32[]{:S(2)}) async-start(bf16[8,64,1536]{2,1,0:T(8,128)(2,1)} %bitcast.59), calls=%async_computation | async-start | bytes 3145728 | tf_op jit(solution)/shard_map/all_to_all | solution.py:406
  80.8 7.6 %collective-permute-start.5 = (bf16[384,256]{1,0:T(8,128)(2,1)S(1)}, bf16[384,256]{1,0:T(8,128)(2,1)S(1)}, u32[]{:S(2)}, u32[]{:S(2)}) collective-permute-start(bf16[384,256]{1,0:T(8,128)(2,1)S(1)} %copy-done.35), channel_id=1, source_target_pairs={{0,8},{8,16},{16,24},{1,9},{9,17},{17,25},{2,10},{10,18},{18,26},{... | collective-permute-start | bytes 589832 | tf_op jit(solution)/shard_map/ppermute | solution.py:480
  84.2 7.6 %collective-permute-start.6 = (bf16[384,256]{1,0:T(8,128)(2,1)S(1)}, bf16[384,256]{1,0:T(8,128)(2,1)S(1)}, u32[]{:S(2)}, u32[]{:S(2)}) collective-permute-start(bf16[384,256]{1,0:T(8,128)(2,1)S(1)} %copy-done.34), channel_id=1, source_target_pairs={{8,0},{16,8},{24,16},{9,1},{17,9},{25,17},{10,2},{18,10},{26,18},{... | collective-permute-start | bytes 589832 | tf_op jit(solution)/shard_map/ppermute | solution.py:479
  86.7 25.0 %collective-permute-start.7 = (bf16[192,1024]{1,0:T(8,128)(2,1)S(1)}, bf16[192,1024]{1,0:T(8,128)(2,1)S(1)}, u32[]{:S(2)}, u32[]{:S(2)}) collective-permute-start(bf16[192,1024]{1,0:T(8,128)(2,1)S(1)} %copy-done.20), channel_id=1, source_target_pairs={{0,1},{1,0},{2,3},{3,2},{4,5},{5,4},{6,7},{7,6},{8,9},{9,8},{10,11... | collective-permute-start | bytes 1179656 | tf_op jit(solution)/shard_map/ppermute | solution.py:397
  112.5 54.1 %all-to-all-start.1 = ((bf16[8,64,1536]{2,1,0:T(8,128)(2,1)}), bf16[8,64,1536]{2,1,0:T(8,128)(2,1)S(1)}, u32[]{:S(2)}, u32[]{:S(2)}) async-start(bf16[8,64,1536]{2,1,0:T(8,128)(2,1)} %bitcast.58), calls=%async_computation.1 | async-start | bytes 3145728 | tf_op jit(solution)/shard_map/all_to_all | solution.py:406
  118.2 88.1 %all-gather.11.cloned.1.call-start = ((), (), s32[]{:S(2)}) async-start(), calls=%async_computation.6 | async-start | bytes 1966080 | tf_op jit(solution)/shard_map/all_gather | solution.py:436
  118.2 48.3 %collective-permute-start.15 = (bf16[4,2,96,768]{3,2,1,0:T(8,128)(2,1)}, bf16[4,2,96,768]{3,2,1,0:T(8,128)(2,1)}, u32[]{:S(2)}, u32[]{:S(2)}) collective-permute-start(bf16[4,2,96,768]{3,2,1,0:T(8,128)(2,1)} %get-tuple-element.89), channel_id=1, source_target_pairs={{0,32},{32,0},{64,96},{96,64},{1,33},{33,1},{65,97},{97,65},{2,34}... | collective-permute-start | bytes 3538952 | tf_op jit(solution)/shard_map/ppermute | solution.py:414
  121.7 22.6 %collective-permute-start.14 = (bf16[64,1536]{1,0:T(8,128)(2,1)}, bf16[64,1536]{1,0:T(8,128)(2,1)S(1)}, u32[]{:S(2)}, u32[]{:S(2)}) collective-permute-start(bf16[64,1536]{1,0:T(8,128)(2,1)} %bitcast.43), channel_id=1, source_target_pairs={{0,5},{1,4},{2,7},{3,6},{4,1},{5,0},{6,3},{7,2},{8,13},{9,12},{10,... | collective-permute-start | bytes 589832 | tf_op jit(solution)/shard_map/ppermute | solution.py:397
  124.6 31.0 %collective-permute-start.13 = (bf16[64,1536]{1,0:T(8,128)(2,1)}, bf16[64,1536]{1,0:T(8,128)(2,1)S(1)}, u32[]{:S(2)}, u32[]{:S(2)}) collective-permute-start(bf16[64,1536]{1,0:T(8,128)(2,1)} %bitcast.44), channel_id=1, source_target_pairs={{0,4},{1,5},{2,6},{3,7},{4,0},{5,1},{6,2},{7,3},{8,12},{9,13},{10,... | collective-permute-start | bytes 589832 | tf_op jit(solution)/shard_map/ppermute | solution.py:397
  124.7 34.2 %collective-permute-start.12 = (bf16[64,1536]{1,0:T(8,128)(2,1)}, bf16[64,1536]{1,0:T(8,128)(2,1)S(1)}, u32[]{:S(2)}, u32[]{:S(2)}) collective-permute-start(bf16[64,1536]{1,0:T(8,128)(2,1)} %bitcast.45), channel_id=1, source_target_pairs={{0,7},{1,6},{2,1},{3,0},{4,3},{5,2},{6,5},{7,4},{8,15},{9,14},{10,... | collective-permute-start | bytes 589832 | tf_op jit(solution)/shard_map/ppermute | solution.py:397
  130.3 29.2 %collective-permute-start.11 = (bf16[64,1536]{1,0:T(8,128)(2,1)}, bf16[64,1536]{1,0:T(8,128)(2,1)S(1)}, u32[]{:S(2)}, u32[]{:S(2)}) collective-permute-start(bf16[64,1536]{1,0:T(8,128)(2,1)} %bitcast.46), channel_id=1, source_target_pairs={{0,3},{1,2},{2,5},{3,4},{4,7},{5,6},{6,1},{7,0},{8,11},{9,10},{10,... | collective-permute-start | bytes 589832 | tf_op jit(solution)/shard_map/ppermute | solution.py:397
  144.2 15.4 %collective-permute-start.10 = (bf16[64,1536]{1,0:T(8,128)(2,1)}, bf16[64,1536]{1,0:T(8,128)(2,1)S(1)}, u32[]{:S(2)}, u32[]{:S(2)}) collective-permute-start(bf16[64,1536]{1,0:T(8,128)(2,1)} %bitcast.47), channel_id=1, source_target_pairs={{0,1},{1,0},{2,3},{3,2},{4,5},{5,4},{6,7},{7,6},{8,9},{9,8},{10,11... | collective-permute-start | bytes 589832 | tf_op jit(solution)/shard_map/ppermute | solution.py:397
  156.3 6.6 %collective-permute-start.9 = (bf16[64,1536]{1,0:T(8,128)(2,1)}, bf16[64,1536]{1,0:T(8,128)(2,1)S(1)}, u32[]{:S(2)}, u32[]{:S(2)}) collective-permute-start(bf16[64,1536]{1,0:T(8,128)(2,1)} %bitcast.48), channel_id=1, source_target_pairs={{0,6},{1,7},{2,0},{3,1},{4,2},{5,3},{6,4},{7,5},{8,14},{9,15},{10,... | collective-permute-start | bytes 589832 | tf_op jit(solution)/shard_map/ppermute | solution.py:397
  159.5 7.1 %collective-permute-start.8 = (bf16[64,1536]{1,0:T(8,128)(2,1)}, bf16[64,1536]{1,0:T(8,128)(2,1)S(1)}, u32[]{:S(2)}, u32[]{:S(2)}) collective-permute-start(bf16[64,1536]{1,0:T(8,128)(2,1)} %bitcast.49), channel_id=1, source_target_pairs={{0,2},{1,3},{2,4},{3,5},{4,6},{5,7},{6,0},{7,1},{8,10},{9,11},{10,... | collective-permute-start | bytes 589832 | tf_op jit(solution)/shard_map/ppermute | solution.py:397
  159.5 46.9 %collective-permute-start.16 = (bf16[384,1536]{1,0:T(8,128)(2,1)}, bf16[384,1536]{1,0:T(8,128)(2,1)}, u32[]{:S(2)}, u32[]{:S(2)}) collective-permute-start(bf16[384,1536]{1,0:T(8,128)(2,1)} %all-gather.7.cloned.1.call-done.refs_0_), channel_id=1, source_target_pairs={{0,32},{32,0},{64,96},{96,64},{1,33},{33,1},{65,97},{97,65},{2,34}... | collective-permute-start | bytes 3538952 | tf_op jit(solution)/shard_map/ppermute | solution.py:414
  159.6 46.8 %collective-permute-start.17 = (bf16[384,1536]{1,0:T(8,128)(2,1)}, bf16[384,1536]{1,0:T(8,128)(2,1)}, u32[]{:S(2)}, u32[]{:S(2)}) collective-permute-start(bf16[384,1536]{1,0:T(8,128)(2,1)} %all-gather.5.cloned.1.call-done.refs_1_), channel_id=1, source_target_pairs={{0,32},{32,0},{64,96},{96,64},{1,33},{33,1},{65,97},{97,65},{2,34}... | collective-permute-start | bytes 3538952 | tf_op jit(solution)/shard_map/ppermute | solution.py:414
  171.2 49.0 %all-to-all-start.2 = ((bf16[8,64,1536]{2,1,0:T(8,128)(2,1)}), bf16[8,64,1536]{2,1,0:T(8,128)(2,1)}, u32[]{:S(2)}, u32[]{:S(2)}) async-start(bf16[8,64,1536]{2,1,0:T(8,128)(2,1)} %finish.3), calls=%async_computation.2 | async-start | bytes 3145728 | tf_op jit(solution)/shard_map/all_to_all | solution.py:406
  180.0 9.3 %collective-permute-start.18 = (bf16[2,96,768]{2,1,0:T(8,128)(2,1)}, bf16[2,96,768]{2,1,0:T(8,128)(2,1)}, u32[]{:S(2)}, u32[]{:S(2)}) collective-permute-start(bf16[2,96,768]{2,1,0:T(8,128)(2,1)} %get-tuple-element.107), channel_id=1, source_target_pairs={{0,8},{8,16},{16,24},{24,0},{1,9},{9,17},{17,25},{25,1},{2,10},{10... | collective-permute-start | bytes 884744 | tf_op jit(solution)/shard_map/ppermute | solution.py:422
  181.5 10.7 %collective-permute-start.20 = (bf16[2,96,768]{2,1,0:T(8,128)(2,1)}, bf16[2,96,768]{2,1,0:T(8,128)(2,1)}, u32[]{:S(2)}, u32[]{:S(2)}) collective-permute-start(bf16[2,96,768]{2,1,0:T(8,128)(2,1)} %get-tuple-element.108), channel_id=1, source_target_pairs={{0,16},{8,24},{16,0},{24,8},{1,17},{9,25},{17,1},{25,9},{2,18},{10... | collective-permute-start | bytes 884744 | tf_op jit(solution)/shard_map/ppermute | solution.py:422
  182.1 12.2 %collective-permute-start.19 = (bf16[2,96,768]{2,1,0:T(8,128)(2,1)}, bf16[2,96,768]{2,1,0:T(8,128)(2,1)}, u32[]{:S(2)}, u32[]{:S(2)}) collective-permute-start(bf16[2,96,768]{2,1,0:T(8,128)(2,1)} %get-tuple-element.109), channel_id=1, source_target_pairs={{0,24},{8,0},{16,8},{24,16},{1,25},{9,1},{17,9},{25,17},{2,26},{10... | collective-permute-start | bytes 884744 | tf_op jit(solution)/shard_map/ppermute | solution.py:422
  184.8 21.6 %copy-start = (bf16[2,512,1536]{2,1,0:T(8,128)(2,1)S(1)}, bf16[2,512,1536]{2,1,0:T(8,128)(2,1)}, u32[]{:S(2)}) copy-start(bf16[2,512,1536]{2,1,0:T(8,128)(2,1)} %param.8) | copy-start | bytes 9437188
  197.3 5.4 %collective-permute-start.21 = (bf16[96,768]{1,0:T(8,128)(2,1)}, bf16[96,768]{1,0:T(8,128)(2,1)S(1)}, u32[]{:S(2)}, u32[]{:S(2)}) collective-permute-start(bf16[96,768]{1,0:T(8,128)(2,1)} %fusion.5), channel_id=1, source_target_pairs={{0,64},{32,96},{64,0},{96,32},{1,65},{33,97},{65,1},{97,33},{2,66}... | collective-permute-start | bytes 442376 | tf_op jit(solution)/shard_map/ppermute | solution.py:430
  (33 other events, 149.4 us)
Sparse Core Ops, SparseCore 0:
  9.7 26.7 all-gather.6
  38.2 25.0 all-gather.4
  72.5 39.3 all-gather.8
  120.4 42.1 all-gather.10

commit v11 on v9

--- a/solution.py
+++ b/solution.py
@@ -109,9 +109,10 @@
     )(lengths, tokens, cotangent, gain, bias, weight, out_w)
 
 
-def attention_body(
-    q, kv, before, after, g, seg_keys, seg_rows, live, mixed, dq, dkv, dbefore, dafter, acc, mask
-):
+def attention_body(q, kv, before, after, g, seg_keys, seg_rows, live, *refs):
+    mixed, dq, dkv, dbefore, dafter, acc, mask = refs[-7:]
+    if len(refs) > 7:
+        mixed[:, q.shape[1] :] = refs[0][...]
     width = q.shape[0]
     span = 3 * CTX
     kv_all = jnp.concatenate([before[...], kv[...], after[...]], axis=1)
@@ -152,7 +153,7 @@
     dafter[...] = acc[:, CTX + frames :].astype(BF16)
 
 
-def attention(rec, q, kv, before, after, g, seg_keys, seg_rows, live):
+def attention(rec, q, kv, before, after, g, seg_keys, seg_rows, live, *later):
     width, rows = q.shape
     recs, span, _ = seg_keys.shape
     frames = rows // recs
@@ -170,16 +171,17 @@
             pl.BlockSpec((1, span, 1), lambda i: (rec, 0, 0)),
             pl.BlockSpec((1, 1, frames), lambda i: (rec, 0, 0)),
             by_rec(1, frames),
-        ],
+        ]
+        + [whole(width, frames)] * len(later),
         out_specs=[
-            whole(width, frames),
+            whole(width, frames * (1 + len(later))),
             whole(width, frames),
             whole(2 * width, frames),
             whole(2 * width, CTX),
             whole(2 * width, CTX),
         ],
         out_shape=[
-            jax.ShapeDtypeStruct((width, frames), BF16),
+            jax.ShapeDtypeStruct((width, frames * (1 + len(later))), BF16),
             jax.ShapeDtypeStruct((width, frames), BF16),
             jax.ShapeDtypeStruct((2 * width, frames), F32),
             jax.ShapeDtypeStruct((2 * width, CTX), BF16),
@@ -189,7 +191,7 @@
         compiler_params=params(),
         cost_estimate=pl.CostEstimate(flops=1000, bytes_accessed=1000, transcendentals=0),
         name="attention",
-    )(q, kv, before, after, g, seg_keys, seg_rows, live)
+    )(q, kv, before, after, g, seg_keys, seg_rows, live, *later)
 
 
 def kv_grads(own, left, right):
@@ -241,11 +243,11 @@
     @pl.when(pl.program_id(0) == 0)
     def _():
         for rec in range(2):
-            dq, own, left, right, out = pieces[5 * rec : 5 * rec + 5]
+            dq, own, left, right = pieces[4 * rec : 4 * rec + 4]
             rows = slice(rec * frames, (rec + 1) * frames)
             stacked = jnp.concatenate([dq[...], kv_grads(own, left, right)], axis=0)
             grads[rows, :] = stacked.T
-            mixed[rows, :] = out[...].T
+            mixed[rows, :] = pieces[-1][:, rows].T
 
     sums = [dot_nn(normed[...].T, grads[...]), dot_nn(cot[...].T, mixed[...])]
 
@@ -299,74 +301,70 @@
     )(core, normed, cotangent, *pieces)
 
 
-def output_body(tok, near, far, *refs):
-    weights, (out, stacks) = refs[:4], refs[4:]
-    core = lax.axis_index("batch") & 1
-    half = weights[0].shape[0] // 4
-    total = tok[...].astype(F32)
-    for index, weight in enumerate(weights):
-        offset = core if index < 2 else 1 - core
-        source = (near, far)[index % 2]
-        for z in range(4):
-            place = pl.multiple_of((2 * z + offset) * half, half)
-            stacks[index, z * half : (z + 1) * half, :] = source[pl.ds(place, half), :]
-        total = total + dot_nn(stacks[index].T, weight[...])
-    out[...] = total.astype(BF16)
-
-
-def output_rows(tokens, near, far, weights):
+def output_body(tok, near, far, near_weight, far_weight, out):
+    total = dot_nn(near[...].T, near_weight[...]) + dot_nn(far[...].T, far_weight[...])
+    out[...] = (tok[...].astype(F32) + total).astype(BF16)
+
+
+def output_rows(tokens, near, far, near_weight, far_weight):
     rows, model = tokens.shape
-    depth = weights[0].shape[0]
-    by_row = pl.BlockSpec((CTX, model), lambda i: (i, 0))
-    by_col = pl.BlockSpec((2 * depth, CTX), lambda i: (0, i))
+    depth = near.shape[0]
+    block = 2 * CTX
+    by_row = pl.BlockSpec((block, model), lambda i: (i, 0))
+    by_col = pl.BlockSpec((depth, block), lambda i: (0, i))
     full = pl.BlockSpec((depth, model), lambda i: (0, 0))
     return pl.pallas_call(
         output_body,
-        grid=(rows // CTX,),
-        in_specs=[by_row, by_col, by_col] + [full] * 4,
+        grid=(rows // block,),
+        in_specs=[by_row, by_col, by_col, full, full],
         out_specs=by_row,
         out_shape=jax.ShapeDtypeStruct((rows, model), BF16),
-        scratch_shapes=[pltpu.VMEM((4, depth, CTX), BF16)],
-        compiler_params=params(28),
+        compiler_params=params(),
         cost_estimate=pl.CostEstimate(
             flops=10000000000, bytes_accessed=12000000, transcendentals=0
         ),
         name="output",
-    )(tokens, near, far, *weights)
-
-
-def finish_body(place, gain, *refs):
+    )(tokens, near, far, near_weight, far_weight)
+
+
+def finish_body(place, gain, tok, cot, parts, *refs):
     out = refs[-1]
-    chunk = refs[0].shape[0]
-    for rec in range(2):
-        tok, cot, parts = refs[3 * rec : 3 * rec + 3]
-        back = jnp.sum(parts[...].astype(F32), axis=0)
-        scaled, inverse = norm_stats(tok[...])
-        weighted = back * gain[...][None, :]
-        first = jnp.mean(weighted, axis=-1, keepdims=True)
-        second = jnp.mean(weighted * scaled, axis=-1, keepdims=True)
-        grad = inverse * (weighted - first - scaled * second) + cot[...].astype(F32)
-        out[rec * chunk : (rec + 1) * chunk, :] = grad.astype(BF16)
-
-
-def finish(place, tokens, cotangent, gain, parts):
-    count, chunk, model = parts[0].shape
-    at = lambda rec: pl.BlockSpec((chunk, model), lambda i, p: (rec * count + p[0], 0))
-    whole = pl.BlockSpec((count, chunk, model), lambda i, p: (0, 0, 0))
+    chunk = tok.shape[0]
+    back = jnp.sum(parts[...].astype(F32), axis=0)
+    scaled, inverse = norm_stats(tok[...])
+    weighted = back * gain[...][None, :]
+    first = jnp.mean(weighted, axis=-1, keepdims=True)
+    second = jnp.mean(weighted * scaled, axis=-1, keepdims=True)
+    grad = inverse * (weighted - first - scaled * second) + cot[...].astype(F32)
+    out[:chunk, :] = grad.astype(BF16)
+    if len(refs) > 1:
+        out[chunk:, :] = refs[0][...]
+
+
+def finish(place, tokens, cotangent, gain, parts, *later):
+    count, chunk, model = parts.shape
+    here = pl.BlockSpec((chunk, model), lambda i, p: (p[0], 0))
+    whole = lambda n: pl.BlockSpec((n, model), lambda i, p: (0, 0))
+    rows = chunk * (1 + len(later))
     return pl.pallas_call(
         finish_body,
         grid_spec=pltpu.PrefetchScalarGridSpec(
             num_scalar_prefetch=1,
             grid=(1,),
-            in_specs=[pl.BlockSpec((model,), lambda i, p: (0,))]
-            + [at(0), at(0), whole, at(1), at(1), whole],
-            out_specs=pl.BlockSpec((2 * chunk, model), lambda i, p: (0, 0)),
+            in_specs=[
+                pl.BlockSpec((model,), lambda i, p: (0,)),
+                here,
+                here,
+                pl.BlockSpec((count, chunk, model), lambda i, p: (0, 0, 0)),
+            ]
+            + [whole(chunk)] * len(later),
+            out_specs=whole(rows),
         ),
-        out_shape=jax.ShapeDtypeStruct((2 * chunk, model), BF16),
+        out_shape=jax.ShapeDtypeStruct((rows, model), BF16),
         compiler_params=params(),
-        cost_estimate=pl.CostEstimate(flops=10000000, bytes_accessed=5000000, transcendentals=0),
+        cost_estimate=pl.CostEstimate(flops=10000000, bytes_accessed=3000000, transcendentals=0),
         name="finish",
-    )(place, gain, tokens, cotangent, parts[0], tokens, cotangent, parts[1])
+    )(place, gain, tokens, cotangent, parts, *later)
 
 
 def assemble_body(places, *refs):
@@ -435,7 +433,7 @@
     row = lax.axis_index("batch") >> 1
     sent = pick(sums, 1 - row, 0).astype(BF16)
     got = lax.ppermute(sent, "batch", [(0, 2), (1, 3), (2, 0), (3, 1)])
-    return pick(sums, row, 0) + got.astype(F32)
+    return pick(sums, row, 0), got
 
 
 def over_z(array):
@@ -454,8 +452,7 @@
     weight = qkv_weight.transpose(1, 2, 0).reshape(3 * width, model)
     tie = lax.optimization_barrier
     core = lax.axis_index("batch") & 1
-    half_out = lax.dynamic_slice_in_dim(out_weight, core * (width // 2), width // 2, 0)
-    near_out = over_z(half_out)
+    near_out = over_z(out_weight)
 
     flat_tokens = tokens.reshape(rows, model)
     flat_cot = cotangent.reshape(rows, model)
@@ -473,20 +470,20 @@
     down = [(i + 1, i) for i in range(size - 1)]
     before = lax.ppermute(kv_last, "frames", up)
     after = lax.ppermute(kv_first, "frames", down)
-    half_out, kv_first = tie((half_out, kv_first))
-    peer_out = to_peer(half_out, (0, 1))
+    late_out, _ = tie((out_weight, kv_first))
+    peer_out = to_peer(late_out, (0, 1))
     before, after, peer_out = tie((before, after, peer_out))
     far_out = over_z(peer_out)
 
-    results = [None] * recs
+    results, mixed = [None] * recs, []
     for rec in reversed(range(recs)):
-        mixed, dq, dkv, dbefore, dafter = attention(
-            rec, q, kv, before, after, g, seg_keys, seg_rows, live
+        out, dq, dkv, dbefore, dafter = attention(
+            rec, q, kv, before, after, g, seg_keys, seg_rows, live, *mixed
         )
         right = lax.ppermute(dbefore, "frames", down)
         left = lax.ppermute(dafter, "frames", up)
-        mixed, q = tie((mixed, q))
-        results[rec] = [dq, dkv, left, right, mixed]
+        mixed = [out]
+        results[rec] = [dq, dkv, left, right]
 
     first, second = results
     count = lax.axis_size("chan")
@@ -494,31 +491,34 @@
 
     split = lambda back: back.reshape(count, -1, model)
     second_back = split(back_rows(*second[:4], weight))
-    mixed, second_back = tie((jnp.concatenate([first[4], second[4]], axis=1), second_back))
+    mixed, second_back = tie((mixed[0], second_back))
     near_mixed = over_z(mixed)
     peer_mixed = to_peer(mixed, (0, 1))
-    first[0], second_back, far_out, near_out = tie((first[0], second_back, far_out, near_out))
-    sent, kept = weight_grads(scalar(core), normed, flat_cot, first + second)
+    first[0], second_back, near_out = tie((first[0], second_back, near_out))
+    sent, kept = weight_grads(scalar(core), normed, flat_cot, first + second + [mixed])
     second_parts = to_all(second_back)
-    first[0], sent, second_parts = tie((first[0], sent, second_parts))
+    first[0], sent, second_parts, far_out = tie((first[0], sent, second_parts, far_out))
     first_back = split(back_rows(*first[:4], weight))
     first_back, peer_mixed = tie((first_back, peer_mixed))
     far_mixed = over_z(peer_mixed)
-    parts = [to_all(first_back), second_parts]
-
+    first_parts = to_all(first_back)
+
+    ending = lambda rec, *refs: finish(
+        scalar(rec * count + me), flat_tokens, flat_cot, norm_gain, *refs
+    )
+    second_parts, first_back = tie((second_parts, first_back))
+    piece = ending(1, second_parts)
     sums = frame_sums(kept.astype(F32) + core_swap(sent).astype(F32))
-    sums, parts[0] = tie((sums, parts[0]))
-    grad_proj = row_sums(sums).reshape(-1, 4, width)
-
-    piece = finish(scalar(me), flat_tokens, flat_cot, norm_gain, parts)
+    sums, first_parts = tie((sums, first_parts))
+    piece = ending(0, first_parts, piece)
+    pieces = [to_peer(piece, shift) for shift in SHIFTS]
+    output = output_rows(flat_tokens, near_mixed, far_mixed, near_out, far_out)
+    pieces[0], output = tie((pieces[0], output))
     places = jnp.stack([me] + [peer_index(me, shift, -1) for shift in SHIFTS]).astype(jnp.int32)
-    own = [near_out, far_out]
-    output = output_rows(
-        flat_tokens, near_mixed, far_mixed, own + [core_swap(array) for array in own]
-    )
-    pieces = [to_peer(piece, shift) for shift in SHIFTS]
-    pieces[0], output = tie((pieces[0], output))
     grad_tokens = assemble(places, [piece] + pieces)
+    sums, output = tie((sums, output))
+    own_sums, got_sums = row_sums(sums)
+    grad_proj = (own_sums + got_sums.astype(F32)).reshape(-1, 4, width)
     shape = (recs, frames, model)
     return (output.reshape(shape), grad_tokens.reshape(shape), grad_proj)
 

time: 212 us -> 203 us (0.958)
  the two profiles are of different devices: /device:TPU:14 before, /device:TPU:18 now
where the time goes in v11:
time: 203 us; the launch traced here: 201 us
  Pallas kernels  70.1 us (35%)
  starting transfers between devices  59.6 us (29%)
  waiting for transfers between devices  44.2 us (22%)
  between operations  14 us (7%)
  local copies, waits for them, and re-layouts  9.74 us (5%)
  other arithmetic  3.7 us (2%)
    ppermute x9, starting transfers between devices, to_peer(): return lax.ppermute(array, 'chan', pairs)  22.6 us
    pallas_call x2, Pallas kernels, attention(): pl.pallas_call(attention_body, grid=(1,), in_specs=[by_rec(width, frames)...  20.8 us
    all_to_all x2, starting transfers between devices, to_all(): return lax.all_to_all(array, 'chan', 0, 0, tiled=True)  13.7 us
    ppermute x9, waiting for transfers between devices, to_peer(): return lax.ppermute(array, 'chan', pairs)  12.3 us
    pallas_call x2, Pallas kernels, back_rows(): pl.pallas_call(back_body, grid=(model // tile,), in_specs=[full(width, ro...  10.8 us
    pallas_call x1, Pallas kernels, project(): pl.pallas_call(project_body, grid=(rows // CTX,), in_specs=[pl.BlockSpec(...  10.7 us
    pallas_call x1, Pallas kernels, output_rows(): pl.pallas_call(output_body, grid=(rows // block,), in_specs=[by_row, by_c...  10 us
    pallas_call x1, Pallas kernels, weight_grads(): pl.pallas_call(weight_grads_body, grid_spec=pltpu.PrefetchScalarGridSpec(...  9.13 us
  transfers between devices with their start and end apart: 26, of which 12 were waited for; matrix products, arithmetic and copies ran while one was open for 3% of the time, Pallas kernels for 35%

profile of v11, /device:TPU:18, one launch (start us, length us, event | category | flops | bytes accessed | tf_op | source)
XLA Modules:
  0.0 201.4 jit_solution(5010723878817931667)
XLA Ops:
  8.0 10.7 %project.1 = (bf16[1024,1536]{1,0:T(8,128)(2,1)}, bf16[192,1024]{1,0:T(8,128)(2,1)}, bf16[384,1024]{1,0:T(8,128)(2,1)}, bf16[192,1024]{1,0:T(8,128)(2,1)}, bf16[...) custom-call(s32[2]{0:T(128)} %lengths.1, bf16[1024,1536]{1,0:T(8,128)(2,1)} %bitcast.41, ...), custom_call_target="tpu_custom_call" | custom-call | flops 2400000000 | bytes 15000000 | tf_op jit(solution)/shard_map/project/pallas_call | solution.py:76
  19.1 3.4 %collective-permute-start = (bf16[384,512]{1,0:T(8,128)(2,1)}, bf16[384,512]{1,0:T(8,128)(2,1)S(1)}, u32[]{:S(2)}, u32[]{:S(2)}) collective-permute-start(bf16[384,512]{1,0:T(8,128)(2,1)} %get-tuple-element.48), channel_id=1, source_target_pairs={{0,8},{8,16},{16,24},{1,9},{9,17},{17,25},{2,10},{10,18},{18,26},{... | collective-permute-start | bytes 1179656 | tf_op jit(solution)/shard_map/ppermute | solution.py:471
  22.5 2.5 %collective-permute-start.1 = (bf16[384,512]{1,0:T(8,128)(2,1)}, bf16[384,512]{1,0:T(8,128)(2,1)S(1)}, u32[]{:S(2)}, u32[]{:S(2)}) collective-permute-start(bf16[384,512]{1,0:T(8,128)(2,1)} %get-tuple-element.49), channel_id=1, source_target_pairs={{8,0},{16,8},{24,16},{9,1},{17,9},{25,17},{10,2},{18,10},{26,18},{... | collective-permute-start | bytes 1179656 | tf_op jit(solution)/shard_map/ppermute | solution.py:472
  24.9 6.8 %collective-permute-done.before = bf16[384,512]{1,0:T(8,128)(2,1)S(1)} collective-permute-done((bf16[384,512]{1,0:T(8,128)(2,1)}, bf16[384,512]{1,0:T(8,128)(2,1)S(1)}, u32[]{:S(2)}, u32[]{:S(2)}) %collective-permute-start) | collective-permute-done | bytes 393248 | tf_op jit(solution)/shard_map/ppermute | solution.py:471
  31.7 3.1 %collective-permute-done.1.after = bf16[384,512]{1,0:T(8,128)(2,1)S(1)} collective-permute-done((bf16[384,512]{1,0:T(8,128)(2,1)}, bf16[384,512]{1,0:T(8,128)(2,1)S(1)}, u32[]{:S(2)}, u32[]{:S(2)}) %collective-permute-start.1) | collective-permute-done | bytes 393248 | tf_op jit(solution)/shard_map/ppermute | solution.py:472
  38.4 10.3 %attention.2 = (bf16[192,512]{1,0:T(8,128)(2,1)}, bf16[192,512]{1,0:T(8,128)(2,1)}, f32[384,512]{1,0:T(8,128)}, bf16[384,256]{1,0:T(8,128)(2,1)}, bf16[384,256]{1,0:T(8,128)(2,1)}) custom-call(bf16[192,1024]{1,0:T(8,128)(2,1)} %get-tuple-element.46.q, bf16[384,1024]{1,0:T(8,128)(2,1)} %get-tuple-element.47.kv, bf16[384,512]{1,0:T(8,128)(2,1)} %copy-done.5, ...), custom_call_target="tpu_custom_call" | custom-call | flops 1000 | bytes 1000 | tf_op jit(solution)/shard_map/attention/pallas_call | solution.py:162
  48.7 3.4 %collective-permute-start.3 = (bf16[384,256]{1,0:T(8,128)(2,1)}, bf16[384,256]{1,0:T(8,128)(2,1)S(1)}, u32[]{:S(2)}, u32[]{:S(2)}) collective-permute-start(bf16[384,256]{1,0:T(8,128)(2,1)} %get-tuple-element.61), channel_id=1, source_target_pairs={{0,8},{8,16},{16,24},{1,9},{9,17},{17,25},{2,10},{10,18},{18,26},{... | collective-permute-start | bytes 589832 | tf_op jit(solution)/shard_map/ppermute | solution.py:484
  52.1 2.6 %collective-permute-start.4 = (bf16[384,256]{1,0:T(8,128)(2,1)}, bf16[384,256]{1,0:T(8,128)(2,1)S(1)}, u32[]{:S(2)}, u32[]{:S(2)}) collective-permute-start(bf16[384,256]{1,0:T(8,128)(2,1)} %get-tuple-element.62), channel_id=1, source_target_pairs={{8,0},{16,8},{24,16},{9,1},{17,9},{25,17},{10,2},{18,10},{26,18},{... | collective-permute-start | bytes 589832 | tf_op jit(solution)/shard_map/ppermute | solution.py:483
  54.7 10.5 %attention.3 = (bf16[192,1024]{1,0:T(8,128)(2,1)}, bf16[192,512]{1,0:T(8,128)(2,1)}, f32[384,512]{1,0:T(8,128)}, bf16[384,256]{1,0:T(8,128)(2,1)}, bf16[384,256]{1,0:T(8,128)(2,1)}) custom-call(bf16[192,1024]{1,0:T(8,128)(2,1)} %get-tuple-element.46.q, bf16[384,1024]{1,0:T(8,128)(2,1)} %get-tuple-element.47.kv, bf16[384,512]{1,0:T(8,128)(2,1)} %copy-done.5, ...), custom_call_target="tpu_custom_call" | custom-call | flops 1000 | bytes 1000 | tf_op jit(solution)/shard_map/attention/pallas_call | solution.py:162
  65.9 5.1 %back.2 = bf16[512,1536]{1,0:T(8,128)(2,1)} custom-call(bf16[192,512]{1,0:T(8,128)(2,1)} %get-tuple-element.59.dq.rest_4_, f32[384,512]{1,0:T(8,128)} %get-tuple-element.60.own.rest_5_, bf16[384,256]{1,0:T(8,128)(2,1)} %copy-done.12, bf16[384,256]{1,0:T(8,128)(2,1)} %copy-done.13, bf16[576,1536]{1,0:T(8,128)(2,1)} %bitcast.46), custom_call_target="tpu_custom_call" | custom-call | flops 900000000 | bytes 4000000 | tf_op jit(solution)/shard_map/back/pallas_call | solution.py:219
  71.1 8.4 %all-to-all-start = ((bf16[8,64,1536]{2,1,0:T(8,128)(2,1)}), bf16[8,64,1536]{2,1,0:T(8,128)(2,1)S(1)}, u32[]{:S(2)}, u32[]{:S(2)}) async-start(bf16[8,64,1536]{2,1,0:T(8,128)(2,1)} %bitcast.49), calls=%async_computation | async-start | bytes 3145728 | tf_op jit(solution)/shard_map/all_to_all | solution.py:411
  79.6 3.4 %collective-permute-start.5 = (bf16[384,256]{1,0:T(8,128)(2,1)S(1)}, bf16[384,256]{1,0:T(8,128)(2,1)S(1)}, u32[]{:S(2)}, u32[]{:S(2)}) collective-permute-start(bf16[384,256]{1,0:T(8,128)(2,1)S(1)} %copy-done.19), channel_id=1, source_target_pairs={{0,8},{8,16},{16,24},{1,9},{9,17},{17,25},{2,10},{10,18},{18,26},{... | collective-permute-start | bytes 589832 | tf_op jit(solution)/shard_map/ppermute | solution.py:484
  83.0 2.5 %collective-permute-start.6 = (bf16[384,256]{1,0:T(8,128)(2,1)S(1)}, bf16[384,256]{1,0:T(8,128)(2,1)S(1)}, u32[]{:S(2)}, u32[]{:S(2)}) collective-permute-start(bf16[384,256]{1,0:T(8,128)(2,1)S(1)} %copy-done.18), channel_id=1, source_target_pairs={{8,0},{16,8},{24,16},{9,1},{17,9},{25,17},{10,2},{18,10},{26,18},{... | collective-permute-start | bytes 589832 | tf_op jit(solution)/shard_map/ppermute | solution.py:483
  87.1 3.4 %collective-permute-done.6.rest_3_.right = bf16[384,256]{1,0:T(8,128)(2,1)S(1)} collective-permute-done((bf16[384,256]{1,0:T(8,128)(2,1)S(1)}, bf16[384,256]{1,0:T(8,128)(2,1)S(1)}, u32[]{:S(2)}, u32[]{:S(2)}) %collective-permute-start.6) | collective-permute-done | bytes 196640 | tf_op jit(solution)/shard_map/ppermute | solution.py:483
  91.2 9.1 %weight_grads.1 = (bf16[4,2,96,768]{3,2,1,0:T(8,128)(2,1)}, bf16[4,2,96,768]{3,2,1,0:T(8,128)(2,1)}) custom-call(s32[1]{0:T(128)} %bitcast.core, bf16[1024,1536]{1,0:T(8,128)(2,1)} %get-tuple-element.45.normed, bf16[1024,1536]{1,0:T(8,128)(2,1)} %bitcast.38, bf16[192,512]{1,0:T(8,128)(2,1)} %get-tuple-element.74.rest_0_.dq, ...), custom_call_target="tpu_custom_call" | custom-call | flops 10000000000 | bytes 12000000 | tf_op jit(solution)/shard_map/weight_grads/pallas_call | solution.py:278
  100.3 2.0 all-to-all-done.parts
  102.3 5.7 %back.3 = bf16[512,1536]{1,0:T(8,128)(2,1)} custom-call(bf16[192,512]{1,0:T(8,128)(2,1)} %get-tuple-element.74.rest_0_.dq, f32[384,512]{1,0:T(8,128)} %get-tuple-element.65.rest_1_.own, bf16[384,256]{1,0:T(8,128)(2,1)} %copy-done.14, bf16[384,256]{1,0:T(8,128)(2,1)} %copy-done.15, bf16[576,1536]{1,0:T(8,128)(2,1)} %bitcast.47), custom_call_target="tpu_custom_call" | custom-call | flops 900000000 | bytes 4000000 | tf_op jit(solution)/shard_map/back/pallas_call | solution.py:219
  108.7 5.3 %all-to-all-start.1 = ((bf16[8,64,1536]{2,1,0:T(8,128)(2,1)}), bf16[8,64,1536]{2,1,0:T(8,128)(2,1)S(1)}, u32[]{:S(2)}, u32[]{:S(2)}) async-start(bf16[8,64,1536]{2,1,0:T(8,128)(2,1)} %bitcast.48), calls=%async_computation.1 | async-start | bytes 3145728 | tf_op jit(solution)/shard_map/all_to_all | solution.py:411
  117.1 2.2 %collective-permute-start.10 = (bf16[2,96,768]{2,1,0:T(8,128)(2,1)S(1)}, bf16[2,96,768]{2,1,0:T(8,128)(2,1)S(1)}, u32[]{:S(2)}, u32[]{:S(2)}) collective-permute-start(bf16[2,96,768]{2,1,0:T(8,128)(2,1)S(1)} %get-tuple-element.88), channel_id=1, source_target_pairs={{0,16},{8,24},{16,0},{24,8},{1,17},{9,25},{17,1},{25,9},{2,18},{10... | collective-permute-start | bytes 884744 | tf_op jit(solution)/shard_map/ppermute | solution.py:427
  121.3 3.0 %finish.2.refs_0_ = bf16[64,1536]{1,0:T(8,128)(2,1)} custom-call(s32[1]{0:T(128)} %bitcast.14.place, f32[1536]{0:T(1024)} %gain.5, bf16[1024,1536]{1,0:T(8,128)(2,1)} %bitcast.42, bf16[1024,1536]{1,0:T(8,128)(2,1)} %bitcast.39, bf16[8,64,1536]{2,1,0:T(8,128)(2,1)} %copy-done.2), custom_call_target="tpu_custom_call" | custom-call | flops 10000000 | bytes 3000000 | tf_op jit(solution)/shard_map/finish/pallas_call | solution.py:349
  124.2 4.4 %collective-permute-done.10 = bf16[2,96,768]{2,1,0:T(8,128)(2,1)S(1)} collective-permute-done((bf16[2,96,768]{2,1,0:T(8,128)(2,1)S(1)}, bf16[2,96,768]{2,1,0:T(8,128)(2,1)S(1)}, u32[]{:S(2)}, u32[]{:S(2)}) %collective-permute-start.10) | collective-permute-done | bytes 294944 | tf_op jit(solution)/shard_map/ppermute | solution.py:427
  128.6 4.7 %collective-permute-done.9 = bf16[2,96,768]{2,1,0:T(8,128)(2,1)S(1)} collective-permute-done((bf16[2,96,768]{2,1,0:T(8,128)(2,1)S(1)}, bf16[2,96,768]{2,1,0:T(8,128)(2,1)S(1)}, u32[]{:S(2)}, u32[]{:S(2)}) %collective-permute-start.9) | collective-permute-done | bytes 294944 | tf_op jit(solution)/shard_map/ppermute | solution.py:427
  133.4 2.1 %fusion.1 = f32[2,96,768]{2,1,0:T(8,128)} fusion(bf16[2,96,768]{2,1,0:T(8,128)(2,1)S(1)} %collective-permute-done.10, bf16[2,96,768]{2,1,0:T(8,128)(2,1)S(1)} %collective-permute-done.9, bf16[2,96,768]{2,1,0:T(8,128)(2,1)S(1)} %collective-permute-done.8, f32[4,2,96,768]{3,2,1,0:T(8,128)} %copy-done.3, s32[]{:T(128)S(6)} %select_n.33), kind=kLoop, calls=%fused_computation.3 | loop fusion | flops 884736 | bytes 2064388 | tf_op jit(solution)/shard_map/add | solution.py:428
  135.5 4.1 %all-to-all-done.1.parts = bf16[8,64,1536]{2,1,0:T(8,128)(2,1)S(1)} async-done(((bf16[8,64,1536]{2,1,0:T(8,128)(2,1)}), bf16[8,64,1536]{2,1,0:T(8,128)(2,1)S(1)}, u32[]{:S(2)}, u32[]{:S(2)}) %all-to-all-start.1) | async-done | bytes 1572896 | tf_op jit(solution)/shard_map/all_to_all | solution.py:411
  140.7 2.9 %finish.3.refs_0_ = bf16[128,1536]{1,0:T(8,128)(2,1)} custom-call(s32[1]{0:T(128)} %bitcast.13.place, f32[1536]{0:T(1024)} %gain.5, bf16[1024,1536]{1,0:T(8,128)(2,1)} %bitcast.43, bf16[1024,1536]{1,0:T(8,128)(2,1)} %bitcast.40, bf16[8,64,1536]{2,1,0:T(8,128)(2,1)} %copy-done.1, bf16[64,1536]{1,0:T(8,128)(2,1)} %finish.2.refs_0_), custom_call_target="tpu_custom_call" | custom-call | flops 10000000 | bytes 3000000 | tf_op jit(solution)/shard_map/finish/pallas_call | solution.py:349
  144.8 5.0 %collective-permute-start.14 = (bf16[128,1536]{1,0:T(8,128)(2,1)}, bf16[128,1536]{1,0:T(8,128)(2,1)S(1)}, u32[]{:S(2)}, u32[]{:S(2)}) collective-permute-start(bf16[128,1536]{1,0:T(8,128)(2,1)} %finish.3.refs_0_), channel_id=1, source_target_pairs={{0,7},{1,6},{2,1},{3,0},{4,3},{5,2},{6,5},{7,4},{8,15},{9,14},{10,... | collective-permute-start | bytes 1179656 | tf_op jit(solution)/shard_map/ppermute | solution.py:402
  149.8 4.8 %collective-permute-start.16 = (bf16[128,1536]{1,0:T(8,128)(2,1)}, bf16[128,1536]{1,0:T(8,128)(2,1)S(1)}, u32[]{:S(2)}, u32[]{:S(2)}) collective-permute-start(bf16[128,1536]{1,0:T(8,128)(2,1)} %finish.3.refs_0_), channel_id=1, source_target_pairs={{0,1},{1,0},{2,3},{3,2},{4,5},{5,4},{6,7},{7,6},{8,9},{9,8},{10,11... | collective-permute-start | bytes 1179656 | tf_op jit(solution)/shard_map/ppermute | solution.py:402
  154.6 6.2 %collective-permute-done.12.refs_1_ = bf16[128,1536]{1,0:T(8,128)(2,1)S(1)} collective-permute-done((bf16[128,1536]{1,0:T(8,128)(2,1)}, bf16[128,1536]{1,0:T(8,128)(2,1)S(1)}, u32[]{:S(2)}, u32[]{:S(2)}) %collective-permute-start.12) | collective-permute-done | bytes 393248 | tf_op jit(solution)/shard_map/ppermute | solution.py:402
  162.4 5.7 %collective-permute-done.13.refs_2_ = bf16[128,1536]{1,0:T(8,128)(2,1)S(1)} collective-permute-done((bf16[128,1536]{1,0:T(8,128)(2,1)}, bf16[128,1536]{1,0:T(8,128)(2,1)S(1)}, u32[]{:S(2)}, u32[]{:S(2)}) %collective-permute-start.13) | collective-permute-done | bytes 393248 | tf_op jit(solution)/shard_map/ppermute | solution.py:402
  168.1 9.5 %collective-permute-start.18 = (bf16[128,1536]{1,0:T(8,128)(2,1)}, bf16[128,1536]{1,0:T(8,128)(2,1)S(1)}, u32[]{:S(2)}, u32[]{:S(2)}) collective-permute-start(bf16[128,1536]{1,0:T(8,128)(2,1)} %finish.3.refs_0_), channel_id=1, source_target_pairs={{0,2},{1,3},{2,4},{3,5},{4,6},{5,7},{6,0},{7,1},{8,10},{9,11},{10,... | collective-permute-start | bytes 1179656 | tf_op jit(solution)/shard_map/ppermute | solution.py:402
  177.6 10.0 %output.1 = bf16[1024,1536]{1,0:T(8,128)(2,1)} custom-call(bf16[1024,1536]{1,0:T(8,128)(2,1)} %bitcast.44, bf16[768,1024]{1,0:T(8,128)(2,1)} %all-gather.9.cloned.1.call-done.near, bf16[768,1024]{1,0:T(8,128)(2,1)} %all-gather.11.cloned.1.call-done.far, bf16[768,1536]{1,0:T(8,128)(2,1)} %all-gather.5.cloned.1.call-done.near_weight, ...), custom_call_target="tpu_custom_call" | custom-call | flops 10000000000 | bytes 12000000 | tf_op jit(solution)/shard_map/output/pallas_call | solution.py:316
  189.9 2.8 %assemble.1 = bf16[1024,1536]{1,0:T(8,128)(2,1)} custom-call(s32[8]{0:T(128)S(1)} %stack.32.places, bf16[128,1536]{1,0:T(8,128)(2,1)S(1)} %copy-done, bf16[128,1536]{1,0:T(8,128)(2,1)S(1)} %collective-permute-done.12.refs_1_, bf16[128,1536]{1,0:T(8,128)(2,1)S(1)} %collective-permute-done.13.refs_2_, bf16[128,1536]{1,0:T(8,128)(2,1)S(1)} %collective-permute-done.14.refs_3_, ...), custom_call_target="tpu_custom_call" | custom-call | bytes 6000000 | tf_op jit(solution)/shard_map/assemble/pallas_call | solution.py:385
  (86 shorter events, 22.0 us)
Async XLA Ops:
  7.2 63.9 %all-gather.5.cloned.1.call-start = ((), (), s32[]{:S(2)}) async-start(), calls=%async_computation.2 | async-start | bytes 2949120 | tf_op jit(solution)/shard_map/all_gather | solution.py:441
  7.9 92.4 %all-gather.7.cloned.1.call-start = ((), (), s32[]{:S(2)}) async-start(), calls=%async_computation.3 | async-start | bytes 2949120 | tf_op jit(solution)/shard_map/all_gather | solution.py:441
  7.9 10.7 %copy-start.8 = (bf16[192,1536]{1,0:T(8,128)(2,1)S(1)}, bf16[192,1536]{1,0:T(8,128)(2,1)}, u32[]{:S(2)}) copy-start(bf16[192,1536]{1,0:T(8,128)(2,1)} %out_w.1) | copy-start | bytes 1769476
  8.0 28.4 %copy-start.16 = (s32[2,2048]{1,0:T(2,128)S(1)}, s32[2,2048]{1,0:T(2,128)}, u32[]{:S(2)}) copy-start(s32[2,2048]{1,0:T(2,128)} %param.15) | copy-start | bytes 49156
  8.0 28.4 %copy-start.17 = (s32[2]{0:T(128)S(1)}, s32[2]{0:T(128)}, u32[]{:S(2)}) copy-start(s32[2]{0:T(128)} %lengths.1) | copy-start | bytes 28
  18.7 16.7 %collective-permute-start.2 = (bf16[192,1536]{1,0:T(8,128)(2,1)S(1)}, bf16[192,1536]{1,0:T(8,128)(2,1)S(1)}, u32[]{:S(2)}, u32[]{:S(2)}) collective-permute-start(bf16[192,1536]{1,0:T(8,128)(2,1)S(1)} %copy-done.8), channel_id=1, source_target_pairs={{0,1},{1,0},{2,3},{3,2},{4,5},{5,4},{6,7},{7,6},{8,9},{9,8},{10,11... | collective-permute-start | bytes 1769480 | tf_op jit(solution)/shard_map/ppermute | solution.py:402
  19.1 12.7 %collective-permute-start = (bf16[384,512]{1,0:T(8,128)(2,1)}, bf16[384,512]{1,0:T(8,128)(2,1)S(1)}, u32[]{:S(2)}, u32[]{:S(2)}) collective-permute-start(bf16[384,512]{1,0:T(8,128)(2,1)} %get-tuple-element.48), channel_id=1, source_target_pairs={{0,8},{8,16},{16,24},{1,9},{9,17},{17,25},{2,10},{10,18},{18,26},{... | collective-permute-start | bytes 1179656 | tf_op jit(solution)/shard_map/ppermute | solution.py:471
  22.5 12.4 %collective-permute-start.1 = (bf16[384,512]{1,0:T(8,128)(2,1)}, bf16[384,512]{1,0:T(8,128)(2,1)S(1)}, u32[]{:S(2)}, u32[]{:S(2)}) collective-permute-start(bf16[384,512]{1,0:T(8,128)(2,1)} %get-tuple-element.49), channel_id=1, source_target_pairs={{8,0},{16,8},{24,16},{9,1},{17,9},{25,17},{10,2},{18,10},{26,18},{... | collective-permute-start | bytes 1179656 | tf_op jit(solution)/shard_map/ppermute | solution.py:472
  36.2 141.3 %all-gather.9.cloned.1.call-start = ((), (), s32[]{:S(2)}) async-start(), calls=%async_computation.4 | async-start | bytes 1966080 | tf_op jit(solution)/shard_map/all_gather | solution.py:441
  48.7 16.5 %collective-permute-start.3 = (bf16[384,256]{1,0:T(8,128)(2,1)}, bf16[384,256]{1,0:T(8,128)(2,1)S(1)}, u32[]{:S(2)}, u32[]{:S(2)}) collective-permute-start(bf16[384,256]{1,0:T(8,128)(2,1)} %get-tuple-element.61), channel_id=1, source_target_pairs={{0,8},{8,16},{16,24},{1,9},{9,17},{17,25},{2,10},{10,18},{18,26},{... | collective-permute-start | bytes 589832 | tf_op jit(solution)/shard_map/ppermute | solution.py:484
  52.1 13.1 %collective-permute-start.4 = (bf16[384,256]{1,0:T(8,128)(2,1)}, bf16[384,256]{1,0:T(8,128)(2,1)S(1)}, u32[]{:S(2)}, u32[]{:S(2)}) collective-permute-start(bf16[384,256]{1,0:T(8,128)(2,1)} %get-tuple-element.62), channel_id=1, source_target_pairs={{8,0},{16,8},{24,16},{9,1},{17,9},{25,17},{10,2},{18,10},{26,18},{... | collective-permute-start | bytes 589832 | tf_op jit(solution)/shard_map/ppermute | solution.py:483
  71.1 11.9 %copy-start.18 = (bf16[384,256]{1,0:T(8,128)(2,1)S(1)}, bf16[384,256]{1,0:T(8,128)(2,1)}, u32[]{:S(2)}) copy-start(bf16[384,256]{1,0:T(8,128)(2,1)} %get-tuple-element.67) | copy-start | bytes 589828
  71.1 14.4 %copy-start.10 = (bf16[192,1024]{1,0:T(8,128)(2,1)S(1)}, bf16[192,1024]{1,0:T(8,128)(2,1)}, u32[]{:S(2)}) copy-start(bf16[192,1024]{1,0:T(8,128)(2,1)} %get-tuple-element.68.rest_8_) | copy-start | bytes 1179652
  71.1 31.2 %all-to-all-start = ((bf16[8,64,1536]{2,1,0:T(8,128)(2,1)}), bf16[8,64,1536]{2,1,0:T(8,128)(2,1)S(1)}, u32[]{:S(2)}, u32[]{:S(2)}) async-start(bf16[8,64,1536]{2,1,0:T(8,128)(2,1)} %bitcast.49), calls=%async_computation | async-start | bytes 3145728 | tf_op jit(solution)/shard_map/all_to_all | solution.py:411
  79.6 98.0 %all-gather.11.cloned.1.call-start = ((), (), s32[]{:S(2)}) async-start(), calls=%async_computation.5 | async-start | bytes 1966080 | tf_op jit(solution)/shard_map/all_gather | solution.py:441
  79.6 7.6 %collective-permute-start.5 = (bf16[384,256]{1,0:T(8,128)(2,1)S(1)}, bf16[384,256]{1,0:T(8,128)(2,1)S(1)}, u32[]{:S(2)}, u32[]{:S(2)}) collective-permute-start(bf16[384,256]{1,0:T(8,128)(2,1)S(1)} %copy-done.19), channel_id=1, source_target_pairs={{0,8},{8,16},{16,24},{1,9},{9,17},{17,25},{2,10},{10,18},{18,26},{... | collective-permute-start | bytes 589832 | tf_op jit(solution)/shard_map/ppermute | solution.py:484
  83.0 7.6 %collective-permute-start.6 = (bf16[384,256]{1,0:T(8,128)(2,1)S(1)}, bf16[384,256]{1,0:T(8,128)(2,1)S(1)}, u32[]{:S(2)}, u32[]{:S(2)}) collective-permute-start(bf16[384,256]{1,0:T(8,128)(2,1)S(1)} %copy-done.18), channel_id=1, source_target_pairs={{8,0},{16,8},{24,16},{9,1},{17,9},{25,17},{10,2},{18,10},{26,18},{... | collective-permute-start | bytes 589832 | tf_op jit(solution)/shard_map/ppermute | solution.py:483
  85.5 22.5 %collective-permute-start.11 = (bf16[192,1024]{1,0:T(8,128)(2,1)S(1)}, bf16[192,1024]{1,0:T(8,128)(2,1)S(1)}, u32[]{:S(2)}, u32[]{:S(2)}) collective-permute-start(bf16[192,1024]{1,0:T(8,128)(2,1)S(1)} %copy-done.10), channel_id=1, source_target_pairs={{0,1},{1,0},{2,3},{3,2},{4,5},{5,4},{6,7},{7,6},{8,9},{9,8},{10,11... | collective-permute-start | bytes 1179656 | tf_op jit(solution)/shard_map/ppermute | solution.py:402
  102.3 11.8 %collective-permute-start.7 = (bf16[4,2,96,768]{3,2,1,0:T(8,128)(2,1)}, bf16[4,2,96,768]{3,2,1,0:T(8,128)(2,1)}, u32[]{:S(2)}, u32[]{:S(2)}) collective-permute-start(bf16[4,2,96,768]{3,2,1,0:T(8,128)(2,1)} %get-tuple-element.73), channel_id=1, source_target_pairs={{0,32},{32,0},{64,96},{96,64},{1,33},{33,1},{65,97},{97,65},{2,34}... | collective-permute-start | bytes 3538952 | tf_op jit(solution)/shard_map/ppermute | solution.py:419
  108.7 30.8 %all-to-all-start.1 = ((bf16[8,64,1536]{2,1,0:T(8,128)(2,1)}), bf16[8,64,1536]{2,1,0:T(8,128)(2,1)S(1)}, u32[]{:S(2)}, u32[]{:S(2)}) async-start(bf16[8,64,1536]{2,1,0:T(8,128)(2,1)} %bitcast.48), calls=%async_computation.1 | async-start | bytes 3145728 | tf_op jit(solution)/shard_map/all_to_all | solution.py:411
  117.1 11.6 %collective-permute-start.10 = (bf16[2,96,768]{2,1,0:T(8,128)(2,1)S(1)}, bf16[2,96,768]{2,1,0:T(8,128)(2,1)S(1)}, u32[]{:S(2)}, u32[]{:S(2)}) collective-permute-start(bf16[2,96,768]{2,1,0:T(8,128)(2,1)S(1)} %get-tuple-element.88), channel_id=1, source_target_pairs={{0,16},{8,24},{16,0},{24,8},{1,17},{9,25},{17,1},{25,9},{2,18},{10... | collective-permute-start | bytes 884744 | tf_op jit(solution)/shard_map/ppermute | solution.py:427
  119.2 14.1 %collective-permute-start.9 = (bf16[2,96,768]{2,1,0:T(8,128)(2,1)S(1)}, bf16[2,96,768]{2,1,0:T(8,128)(2,1)S(1)}, u32[]{:S(2)}, u32[]{:S(2)}) collective-permute-start(bf16[2,96,768]{2,1,0:T(8,128)(2,1)S(1)} %get-tuple-element.89), channel_id=1, source_target_pairs={{0,24},{8,0},{16,8},{24,16},{1,25},{9,1},{17,9},{25,17},{2,26},{10... | collective-permute-start | bytes 884744 | tf_op jit(solution)/shard_map/ppermute | solution.py:427
  120.6 12.8 %collective-permute-start.8 = (bf16[2,96,768]{2,1,0:T(8,128)(2,1)S(1)}, bf16[2,96,768]{2,1,0:T(8,128)(2,1)S(1)}, u32[]{:S(2)}, u32[]{:S(2)}) collective-permute-start(bf16[2,96,768]{2,1,0:T(8,128)(2,1)S(1)} %get-tuple-element.87), channel_id=1, source_target_pairs={{0,8},{8,16},{16,24},{24,0},{1,9},{9,17},{17,25},{25,1},{2,10},{10... | collective-permute-start | bytes 884744 | tf_op jit(solution)/shard_map/ppermute | solution.py:427
  143.6 17.1 %collective-permute-start.12 = (bf16[128,1536]{1,0:T(8,128)(2,1)}, bf16[128,1536]{1,0:T(8,128)(2,1)S(1)}, u32[]{:S(2)}, u32[]{:S(2)}) collective-permute-start(bf16[128,1536]{1,0:T(8,128)(2,1)} %finish.3.refs_0_), channel_id=1, source_target_pairs={{0,5},{1,4},{2,7},{3,6},{4,1},{5,0},{6,3},{7,2},{8,13},{9,12},{10,... | collective-permute-start | bytes 1179656 | tf_op jit(solution)/shard_map/ppermute | solution.py:402
  143.6 24.5 %collective-permute-start.13 = (bf16[128,1536]{1,0:T(8,128)(2,1)}, bf16[128,1536]{1,0:T(8,128)(2,1)S(1)}, u32[]{:S(2)}, u32[]{:S(2)}) collective-permute-start(bf16[128,1536]{1,0:T(8,128)(2,1)} %finish.3.refs_0_), channel_id=1, source_target_pairs={{0,4},{1,5},{2,6},{3,7},{4,0},{5,1},{6,2},{7,3},{8,12},{9,13},{10,... | collective-permute-start | bytes 1179656 | tf_op jit(solution)/shard_map/ppermute | solution.py:402
  144.8 45.1 %copy-start = (bf16[128,1536]{1,0:T(8,128)(2,1)S(1)}, bf16[128,1536]{1,0:T(8,128)(2,1)}, u32[]{:S(2)}) copy-start(bf16[128,1536]{1,0:T(8,128)(2,1)} %finish.3.refs_0_) | copy-start | bytes 1179652
  144.8 43.8 %collective-permute-start.14 = (bf16[128,1536]{1,0:T(8,128)(2,1)}, bf16[128,1536]{1,0:T(8,128)(2,1)S(1)}, u32[]{:S(2)}, u32[]{:S(2)}) collective-permute-start(bf16[128,1536]{1,0:T(8,128)(2,1)} %finish.3.refs_0_), channel_id=1, source_target_pairs={{0,7},{1,6},{2,1},{3,0},{4,3},{5,2},{6,5},{7,4},{8,15},{9,14},{10,... | collective-permute-start | bytes 1179656 | tf_op jit(solution)/shard_map/ppermute | solution.py:402
  149.8 40.1 %collective-permute-start.15 = (bf16[128,1536]{1,0:T(8,128)(2,1)}, bf16[128,1536]{1,0:T(8,128)(2,1)S(1)}, u32[]{:S(2)}, u32[]{:S(2)}) collective-permute-start(bf16[128,1536]{1,0:T(8,128)(2,1)} %finish.3.refs_0_), channel_id=1, source_target_pairs={{0,3},{1,2},{2,5},{3,4},{4,7},{5,6},{6,1},{7,0},{8,11},{9,10},{10,... | collective-permute-start | bytes 1179656 | tf_op jit(solution)/shard_map/ppermute | solution.py:402
  149.8 40.1 %collective-permute-start.16 = (bf16[128,1536]{1,0:T(8,128)(2,1)}, bf16[128,1536]{1,0:T(8,128)(2,1)S(1)}, u32[]{:S(2)}, u32[]{:S(2)}) collective-permute-start(bf16[128,1536]{1,0:T(8,128)(2,1)} %finish.3.refs_0_), channel_id=1, source_target_pairs={{0,1},{1,0},{2,3},{3,2},{4,5},{5,4},{6,7},{7,6},{8,9},{9,8},{10,11... | collective-permute-start | bytes 1179656 | tf_op jit(solution)/shard_map/ppermute | solution.py:402
  160.7 29.1 %collective-permute-start.17 = (bf16[128,1536]{1,0:T(8,128)(2,1)}, bf16[128,1536]{1,0:T(8,128)(2,1)S(1)}, u32[]{:S(2)}, u32[]{:S(2)}) collective-permute-start(bf16[128,1536]{1,0:T(8,128)(2,1)} %finish.3.refs_0_), channel_id=1, source_target_pairs={{0,6},{1,7},{2,0},{3,1},{4,2},{5,3},{6,4},{7,5},{8,14},{9,15},{10,... | collective-permute-start | bytes 1179656 | tf_op jit(solution)/shard_map/ppermute | solution.py:402
  168.1 21.8 %collective-permute-start.18 = (bf16[128,1536]{1,0:T(8,128)(2,1)}, bf16[128,1536]{1,0:T(8,128)(2,1)S(1)}, u32[]{:S(2)}, u32[]{:S(2)}) collective-permute-start(bf16[128,1536]{1,0:T(8,128)(2,1)} %finish.3.refs_0_), channel_id=1, source_target_pairs={{0,2},{1,3},{2,4},{3,5},{4,6},{5,7},{6,0},{7,1},{8,10},{9,11},{10,... | collective-permute-start | bytes 1179656 | tf_op jit(solution)/shard_map/ppermute | solution.py:402
  188.6 5.2 %collective-permute-start.19 = (bf16[96,768]{1,0:T(8,128)(2,1)S(1)}, bf16[96,768]{1,0:T(8,128)(2,1)S(1)}, u32[]{:S(2)}, u32[]{:S(2)}) collective-permute-start(bf16[96,768]{1,0:T(8,128)(2,1)S(1)} %fusion.5), channel_id=1, source_target_pairs={{0,64},{32,96},{64,0},{96,32},{1,65},{33,97},{65,1},{97,33},{2,66}... | collective-permute-start | bytes 442376 | tf_op jit(solution)/shard_map/ppermute | solution.py:435
  (14 other events, 44.0 us)
Sparse Core Ops, SparseCore 0:
  9.7 35.4 all-gather.4
  46.8 33.1 all-gather.6
  81.6 29.6 all-gather.8
  113.4 33.9 all-gather.10

commit v12 on v11

--- a/solution.py
+++ b/solution.py
@@ -49,19 +49,12 @@
     qkv = dot_nt(weight[...], rows).astype(BF16)
     q[...] = qkv[:width]
     kv[...] = qkv[width:]
-    step = pl.program_id(0)
-
-    @pl.when(step % 2 == 0)
-    def _():
-        kv_first[...] = qkv[width:]
-
-    @pl.when(step % 2 == 1)
-    def _():
-        kv_last[...] = qkv[width:]
-
-    start = lax.axis_index("frames") * (2 * CTX) + (step % 2) * CTX
-    position = start + lax.broadcasted_iota(jnp.int32, (1, CTX), 1)
-    alive = jnp.where(position < lengths[step // 2], 1.0, 0.0)
+    kv_first[...] = qkv[width:, :CTX]
+    kv_last[...] = qkv[width:, CTX:]
+    rec, frames = pl.program_id(0), tok.shape[0]
+    start = lax.axis_index("frames") * frames
+    position = start + lax.broadcasted_iota(jnp.int32, (1, frames), 1)
+    alive = jnp.where(position < lengths[rec], 1.0, 0.0)
     live[...] = alive
     g[...] = (dot_nt(out_w[...], cot[...]) * alive).astype(BF16)
 
@@ -70,12 +63,13 @@
     rows, model = tokens.shape
     width = out_w.shape[0]
     full = lambda shape: pl.BlockSpec(shape, lambda i: (0,) * len(shape))
-    by_row = pl.BlockSpec((CTX, model), lambda i: (i, 0))
-    by_col = lambda n: pl.BlockSpec((n, CTX), lambda i: (0, i))
-    by_half = pl.BlockSpec((2 * width, CTX), lambda i: (0, i // 2))
+    frames = 2 * CTX
+    by_row = pl.BlockSpec((frames, model), lambda i: (i, 0))
+    by_col = lambda n: pl.BlockSpec((n, frames), lambda i: (0, i))
+    by_half = pl.BlockSpec((2 * width, CTX), lambda i: (0, i))
     return pl.pallas_call(
         project_body,
-        grid=(rows // CTX,),
+        grid=(rows // frames,),
         in_specs=[
             pl.BlockSpec(memory_space=pltpu.SMEM),
             by_row,
@@ -119,6 +113,7 @@
     q_small = q[...] * jnp.asarray(HEAD**-0.5, BF16)
     grads = g[...]
     acc[...] = jnp.zeros_like(acc)
+    seg_column = jnp.broadcast_to(seg_keys[0], (128, acc.shape[1])).T[:, :1]
     for tile in range(2):
         cols = slice(tile * CTX, (tile + 1) * CTX)
         keys = slice(tile * CTX, tile * CTX + span)
@@ -128,7 +123,7 @@
             - lax.broadcasted_iota(jnp.int32, (span, CTX), 1)
         )
         near = jnp.abs(away) <= CTX
-        stretch = jnp.abs(seg_keys[0, keys, :] - seg_rows[0, :, cols]) <= 1
+        stretch = jnp.abs(seg_column[keys, :] - seg_rows[0, :, cols]) <= 1.0
         visible = (near & stretch) | (away == 0)
         mask[...] = jnp.where(visible, 0.0, NEG)
         for head in range(width // HEAD):
@@ -140,9 +135,10 @@
             weights = jnp.exp(scores - jnp.max(scores, axis=0, keepdims=True))
             weights = weights * (1.0 / jnp.sum(weights, axis=0, keepdims=True))
             rounded = weights.astype(BF16)
-            mixed[d, cols] = (dot_nn(v_t, rounded) * live[:, cols]).astype(BF16)
+            out = dot_nn(v_t, rounded)
+            mixed[d, cols] = (out * live[:, cols]).astype(BF16)
             grad_w = dot_tn(v_t, g_t)
-            total = jnp.sum(weights * grad_w, axis=0, keepdims=True)
+            total = jnp.sum(out * g_t.astype(F32), axis=0, keepdims=True)
             grad_s = (weights * (grad_w - total)).astype(BF16)
             dq[d, cols] = (dot_nn(k_t, grad_s) * (HEAD**-0.5)).astype(BF16)
             acc[d, keys] += dot_nt(q_t, grad_s)
@@ -155,7 +151,7 @@
 
 def attention(rec, q, kv, before, after, g, seg_keys, seg_rows, live, *later):
     width, rows = q.shape
-    recs, span, _ = seg_keys.shape
+    recs, _, span = seg_keys.shape
     frames = rows // recs
     by_rec = lambda n, m: pl.BlockSpec((n, m), lambda i: (0, rec))
     whole = lambda n, m: pl.BlockSpec((n, m), lambda i: (0, 0))
@@ -168,7 +164,7 @@
             by_rec(2 * width, CTX),
             by_rec(2 * width, CTX),
             by_rec(width, frames),
-            pl.BlockSpec((1, span, 1), lambda i: (rec, 0, 0)),
+            pl.BlockSpec((1, 1, span), lambda i: (rec, 0, 0)),
             pl.BlockSpec((1, 1, frames), lambda i: (rec, 0, 0)),
             by_rec(1, frames),
         ]
@@ -459,8 +455,9 @@
     reach = start - CTX + jnp.arange(frames + 2 * CTX, dtype=jnp.int32)
     padded = jnp.pad(segments, ((0, 0), (CTX, CTX)), constant_values=-10)
     seg_keys = lax.dynamic_slice_in_dim(padded, start, frames + 2 * CTX, 1)
-    seg_keys = jnp.where(reach[None, :] < lengths[:, None], seg_keys, -10)[:, :, None]
-    seg_rows = lax.dynamic_slice_in_dim(segments, start, frames, 1)[:, None, :]
+    seg_keys = jnp.where(reach[None, :] < lengths[:, None], seg_keys, -10)
+    seg_keys = seg_keys.astype(F32)[:, None, :]
+    seg_rows = lax.dynamic_slice_in_dim(segments, start, frames, 1).astype(F32)[:, None, :]
 
     normed, q, kv, g, kv_first, kv_last, live = project(
         lengths, flat_tokens, flat_cot, norm_gain, norm_bias, weight, out_weight

time: 203 us -> 219 us (1.079)
  waiting for transfers between devices: 44.2 us -> 69.2 us
  Pallas kernels: 70.1 us -> 65.5 us
  starting transfers between devices: 59.6 us -> 56.1 us
    all_gather x4, waiting for transfers between devices: 0.03 us -> 11.5 us  [over_z(): return lax.all_gather(array, 'chan', axis_index_groups=groups, tiled=True)]
    ppermute x9, waiting for transfers between devices: 12.3 us -> 23.6 us  [to_peer(): return lax.ppermute(array, 'chan', pairs)]
    ppermute x9, starting transfers between devices: 22.6 us -> 17.7 us  [to_peer(): return lax.ppermute(array, 'chan', pairs)]
    pallas_call x2, Pallas kernels: 20.8 us -> 18.4 us  [attention(): pl.pallas_call(attention_body, grid=(1,), in_specs=[by_rec(width, frames)...]
  transfers between devices with their start and end apart: 26 -> 26, of which waited for: 12 -> 14; matrix products, arithmetic and copies ran while one was open for 3% -> 3% of each run, Pallas kernels for 35% -> 30%
where the time goes in v12:
time: 219 us; the launch traced here: 218 us
  waiting for transfers between devices  69.2 us (32%)
  Pallas kernels  65.5 us (30%)
  starting transfers between devices  56.1 us (26%)
  between operations  14 us (6%)
  local copies, waits for them, and re-layouts  8.98 us (4%)
  other arithmetic  3.72 us (2%)
    ppermute x9, waiting for transfers between devices, to_peer(): return lax.ppermute(array, 'chan', pairs)  23.6 us
    pallas_call x2, Pallas kernels, attention(): pl.pallas_call(attention_body, grid=(1,), in_specs=[by_rec(width, frames)...  18.4 us
    ppermute x9, starting transfers between devices, to_peer(): return lax.ppermute(array, 'chan', pairs)  17.7 us
    all_to_all x2, starting transfers between devices, to_all(): return lax.all_to_all(array, 'chan', 0, 0, tiled=True)  14.2 us
    all_gather x4, waiting for transfers between devices, over_z(): return lax.all_gather(array, 'chan', axis_index_groups=groups, tiled=True)  11.5 us
    pallas_call x2, Pallas kernels, back_rows(): pl.pallas_call(back_body, grid=(model // tile,), in_specs=[full(width, ro...  10.7 us
    pallas_call x1, Pallas kernels, output_rows(): pl.pallas_call(output_body, grid=(rows // block,), in_specs=[by_row, by_c...  10 us
    ppermute x3, waiting for transfers between devices, frame_sums(): got = lax.ppermute(sent, 'frames', [(i, (i + shift) % 4) for i in range(4)])  9.41 us
  transfers between devices with their start and end apart: 26, of which 14 were waited for; matrix products, arithmetic and copies ran while one was open for 3% of the time, Pallas kernels for 30%

profile of v12, /device:TPU:18, one launch (start us, length us, event | category | flops | bytes accessed | tf_op | source)
XLA Modules:
  0.0 217.5 jit_solution(3737854583715177478)
XLA Ops:
  8.0 8.8 %project.1 = (bf16[1024,1536]{1,0:T(8,128)(2,1)}, bf16[192,1024]{1,0:T(8,128)(2,1)}, bf16[384,1024]{1,0:T(8,128)(2,1)}, bf16[192,1024]{1,0:T(8,128)(2,1)}, bf16[...) custom-call(s32[2]{0:T(128)} %lengths.1, bf16[1024,1536]{1,0:T(8,128)(2,1)} %bitcast.39, ...), custom_call_target="tpu_custom_call" | custom-call | flops 2400000000 | bytes 15000000 | tf_op jit(solution)/shard_map/project/pallas_call | solution.py:70
  17.2 3.4 %collective-permute-start = (bf16[384,512]{1,0:T(8,128)(2,1)}, bf16[384,512]{1,0:T(8,128)(2,1)S(1)}, u32[]{:S(2)}, u32[]{:S(2)}) collective-permute-start(bf16[384,512]{1,0:T(8,128)(2,1)} %get-tuple-element.48), channel_id=1, source_target_pairs={{0,8},{8,16},{16,24},{1,9},{9,17},{17,25},{2,10},{10,18},{18,26},{... | collective-permute-start | bytes 1179656 | tf_op jit(solution)/shard_map/ppermute | solution.py:468
  20.6 2.5 %collective-permute-start.1 = (bf16[384,512]{1,0:T(8,128)(2,1)}, bf16[384,512]{1,0:T(8,128)(2,1)S(1)}, u32[]{:S(2)}, u32[]{:S(2)}) collective-permute-start(bf16[384,512]{1,0:T(8,128)(2,1)} %get-tuple-element.49), channel_id=1, source_target_pairs={{8,0},{16,8},{24,16},{9,1},{17,9},{25,17},{10,2},{18,10},{26,18},{... | collective-permute-start | bytes 1179656 | tf_op jit(solution)/shard_map/ppermute | solution.py:469
  23.0 6.8 %collective-permute-done.before = bf16[384,512]{1,0:T(8,128)(2,1)S(1)} collective-permute-done((bf16[384,512]{1,0:T(8,128)(2,1)}, bf16[384,512]{1,0:T(8,128)(2,1)S(1)}, u32[]{:S(2)}, u32[]{:S(2)}) %collective-permute-start) | collective-permute-done | bytes 393248 | tf_op jit(solution)/shard_map/ppermute | solution.py:468
  29.8 3.1 %collective-permute-done.1.after = bf16[384,512]{1,0:T(8,128)(2,1)S(1)} collective-permute-done((bf16[384,512]{1,0:T(8,128)(2,1)}, bf16[384,512]{1,0:T(8,128)(2,1)S(1)}, u32[]{:S(2)}, u32[]{:S(2)}) %collective-permute-start.1) | collective-permute-done | bytes 393248 | tf_op jit(solution)/shard_map/ppermute | solution.py:469
  35.7 9.2 %attention.2 = (bf16[192,512]{1,0:T(8,128)(2,1)}, bf16[192,512]{1,0:T(8,128)(2,1)}, f32[384,512]{1,0:T(8,128)}, bf16[384,256]{1,0:T(8,128)(2,1)}, bf16[384,256]{1,0:T(8,128)(2,1)}) custom-call(bf16[192,1024]{1,0:T(8,128)(2,1)} %get-tuple-element.46.q, bf16[384,1024]{1,0:T(8,128)(2,1)} %get-tuple-element.47.kv, bf16[384,512]{1,0:T(8,128)(2,1)} %copy-done.5, ...), custom_call_target="tpu_custom_call" | custom-call | flops 1000 | bytes 1000 | tf_op jit(solution)/shard_map/attention/pallas_call | solution.py:158
  44.9 3.4 %collective-permute-start.3 = (bf16[384,256]{1,0:T(8,128)(2,1)}, bf16[384,256]{1,0:T(8,128)(2,1)S(1)}, u32[]{:S(2)}, u32[]{:S(2)}) collective-permute-start(bf16[384,256]{1,0:T(8,128)(2,1)} %get-tuple-element.61), channel_id=1, source_target_pairs={{0,8},{8,16},{16,24},{1,9},{9,17},{17,25},{2,10},{10,18},{18,26},{... | collective-permute-start | bytes 589832 | tf_op jit(solution)/shard_map/ppermute | solution.py:481
  48.3 2.6 %collective-permute-start.4 = (bf16[384,256]{1,0:T(8,128)(2,1)}, bf16[384,256]{1,0:T(8,128)(2,1)S(1)}, u32[]{:S(2)}, u32[]{:S(2)}) collective-permute-start(bf16[384,256]{1,0:T(8,128)(2,1)} %get-tuple-element.62), channel_id=1, source_target_pairs={{8,0},{16,8},{24,16},{9,1},{17,9},{25,17},{10,2},{18,10},{26,18},{... | collective-permute-start | bytes 589832 | tf_op jit(solution)/shard_map/ppermute | solution.py:480
  50.9 9.2 %attention.3 = (bf16[192,1024]{1,0:T(8,128)(2,1)}, bf16[192,512]{1,0:T(8,128)(2,1)}, f32[384,512]{1,0:T(8,128)}, bf16[384,256]{1,0:T(8,128)(2,1)}, bf16[384,256]{1,0:T(8,128)(2,1)}) custom-call(bf16[192,1024]{1,0:T(8,128)(2,1)} %get-tuple-element.46.q, bf16[384,1024]{1,0:T(8,128)(2,1)} %get-tuple-element.47.kv, bf16[384,512]{1,0:T(8,128)(2,1)} %copy-done.5, ...), custom_call_target="tpu_custom_call" | custom-call | flops 1000 | bytes 1000 | tf_op jit(solution)/shard_map/attention/pallas_call | solution.py:158
  60.9 5.1 %back.2 = bf16[512,1536]{1,0:T(8,128)(2,1)} custom-call(bf16[192,512]{1,0:T(8,128)(2,1)} %get-tuple-element.59.dq.rest_4_, f32[384,512]{1,0:T(8,128)} %get-tuple-element.60.own.rest_5_, bf16[384,256]{1,0:T(8,128)(2,1)} %copy-done.12, bf16[384,256]{1,0:T(8,128)(2,1)} %copy-done.13, bf16[576,1536]{1,0:T(8,128)(2,1)} %bitcast.44), custom_call_target="tpu_custom_call" | custom-call | flops 900000000 | bytes 4000000 | tf_op jit(solution)/shard_map/back/pallas_call | solution.py:215
  66.1 8.5 %all-to-all-start = ((bf16[8,64,1536]{2,1,0:T(8,128)(2,1)}), bf16[8,64,1536]{2,1,0:T(8,128)(2,1)S(1)}, u32[]{:S(2)}, u32[]{:S(2)}) async-start(bf16[8,64,1536]{2,1,0:T(8,128)(2,1)} %bitcast.47), calls=%async_computation | async-start | bytes 3145728 | tf_op jit(solution)/shard_map/all_to_all | solution.py:407
  74.5 3.4 %collective-permute-start.5 = (bf16[384,256]{1,0:T(8,128)(2,1)S(1)}, bf16[384,256]{1,0:T(8,128)(2,1)S(1)}, u32[]{:S(2)}, u32[]{:S(2)}) collective-permute-start(bf16[384,256]{1,0:T(8,128)(2,1)S(1)} %copy-done.19), channel_id=1, source_target_pairs={{0,8},{8,16},{16,24},{1,9},{9,17},{17,25},{2,10},{10,18},{18,26},{... | collective-permute-start | bytes 589832 | tf_op jit(solution)/shard_map/ppermute | solution.py:481
  77.9 2.5 %collective-permute-start.6 = (bf16[384,256]{1,0:T(8,128)(2,1)S(1)}, bf16[384,256]{1,0:T(8,128)(2,1)S(1)}, u32[]{:S(2)}, u32[]{:S(2)}) collective-permute-start(bf16[384,256]{1,0:T(8,128)(2,1)S(1)} %copy-done.18), channel_id=1, source_target_pairs={{8,0},{16,8},{24,16},{9,1},{17,9},{25,17},{10,2},{18,10},{26,18},{... | collective-permute-start | bytes 589832 | tf_op jit(solution)/shard_map/ppermute | solution.py:480
  82.1 3.4 %collective-permute-done.6.rest_3_.right = bf16[384,256]{1,0:T(8,128)(2,1)S(1)} collective-permute-done((bf16[384,256]{1,0:T(8,128)(2,1)S(1)}, bf16[384,256]{1,0:T(8,128)(2,1)S(1)}, u32[]{:S(2)}, u32[]{:S(2)}) %collective-permute-start.6) | collective-permute-done | bytes 196640 | tf_op jit(solution)/shard_map/ppermute | solution.py:480
  86.2 9.0 %weight_grads.1 = (bf16[4,2,96,768]{3,2,1,0:T(8,128)(2,1)}, bf16[4,2,96,768]{3,2,1,0:T(8,128)(2,1)}) custom-call(s32[1]{0:T(128)} %bitcast.core, bf16[1024,1536]{1,0:T(8,128)(2,1)} %get-tuple-element.45.normed, bf16[1024,1536]{1,0:T(8,128)(2,1)} %bitcast.36, bf16[192,512]{1,0:T(8,128)(2,1)} %get-tuple-element.74.rest_0_.dq, ...), custom_call_target="tpu_custom_call" | custom-call | flops 10000000000 | bytes 12000000 | tf_op jit(solution)/shard_map/weight_grads/pallas_call | solution.py:274
  96.6 5.7 %back.3 = bf16[512,1536]{1,0:T(8,128)(2,1)} custom-call(bf16[192,512]{1,0:T(8,128)(2,1)} %get-tuple-element.74.rest_0_.dq, f32[384,512]{1,0:T(8,128)} %get-tuple-element.65.rest_1_.own, bf16[384,256]{1,0:T(8,128)(2,1)} %copy-done.14, bf16[384,256]{1,0:T(8,128)(2,1)} %copy-done.15, bf16[576,1536]{1,0:T(8,128)(2,1)} %bitcast.45), custom_call_target="tpu_custom_call" | custom-call | flops 900000000 | bytes 4000000 | tf_op jit(solution)/shard_map/back/pallas_call | solution.py:215
  103.1 5.8 %all-to-all-start.1 = ((bf16[8,64,1536]{2,1,0:T(8,128)(2,1)}), bf16[8,64,1536]{2,1,0:T(8,128)(2,1)S(1)}, u32[]{:S(2)}, u32[]{:S(2)}) async-start(bf16[8,64,1536]{2,1,0:T(8,128)(2,1)} %bitcast.46), calls=%async_computation.1 | async-start | bytes 3145728 | tf_op jit(solution)/shard_map/all_to_all | solution.py:407
  116.1 2.9 %finish.2.refs_0_ = bf16[64,1536]{1,0:T(8,128)(2,1)} custom-call(s32[1]{0:T(128)} %bitcast.13.place, f32[1536]{0:T(1024)} %gain.5, bf16[1024,1536]{1,0:T(8,128)(2,1)} %bitcast.40, bf16[1024,1536]{1,0:T(8,128)(2,1)} %bitcast.37, bf16[8,64,1536]{2,1,0:T(8,128)(2,1)} %copy-done.2), custom_call_target="tpu_custom_call" | custom-call | flops 10000000 | bytes 3000000 | tf_op jit(solution)/shard_map/finish/pallas_call | solution.py:345
  118.9 4.5 %collective-permute-done.10 = bf16[2,96,768]{2,1,0:T(8,128)(2,1)S(1)} collective-permute-done((bf16[2,96,768]{2,1,0:T(8,128)(2,1)S(1)}, bf16[2,96,768]{2,1,0:T(8,128)(2,1)S(1)}, u32[]{:S(2)}, u32[]{:S(2)}) %collective-permute-start.10) | collective-permute-done | bytes 294944 | tf_op jit(solution)/shard_map/ppermute | solution.py:423
  123.4 4.9 %collective-permute-done.9 = bf16[2,96,768]{2,1,0:T(8,128)(2,1)S(1)} collective-permute-done((bf16[2,96,768]{2,1,0:T(8,128)(2,1)S(1)}, bf16[2,96,768]{2,1,0:T(8,128)(2,1)S(1)}, u32[]{:S(2)}, u32[]{:S(2)}) %collective-permute-start.9) | collective-permute-done | bytes 294944 | tf_op jit(solution)/shard_map/ppermute | solution.py:423
  130.4 6.7 %all-to-all-done.1.parts = bf16[8,64,1536]{2,1,0:T(8,128)(2,1)S(1)} async-done(((bf16[8,64,1536]{2,1,0:T(8,128)(2,1)}), bf16[8,64,1536]{2,1,0:T(8,128)(2,1)S(1)}, u32[]{:S(2)}, u32[]{:S(2)}) %all-to-all-start.1) | async-done | bytes 1572896 | tf_op jit(solution)/shard_map/all_to_all | solution.py:407
  138.3 2.9 %finish.3.refs_0_ = bf16[128,1536]{1,0:T(8,128)(2,1)} custom-call(s32[1]{0:T(128)} %bitcast.12.place, f32[1536]{0:T(1024)} %gain.5, bf16[1024,1536]{1,0:T(8,128)(2,1)} %bitcast.41, bf16[1024,1536]{1,0:T(8,128)(2,1)} %bitcast.38, bf16[8,64,1536]{2,1,0:T(8,128)(2,1)} %copy-done.1, bf16[64,1536]{1,0:T(8,128)(2,1)} %finish.2.refs_0_), custom_call_target="tpu_custom_call" | custom-call | flops 10000000 | bytes 3000000 | tf_op jit(solution)/shard_map/finish/pallas_call | solution.py:345
  141.9 2.7 %collective-permute-start.13 = (bf16[128,1536]{1,0:T(8,128)(2,1)}, bf16[128,1536]{1,0:T(8,128)(2,1)S(1)}, u32[]{:S(2)}, u32[]{:S(2)}) collective-permute-start(bf16[128,1536]{1,0:T(8,128)(2,1)} %finish.3.refs_0_), channel_id=1, source_target_pairs={{0,4},{1,5},{2,6},{3,7},{4,0},{5,1},{6,2},{7,3},{8,12},{9,13},{10,... | collective-permute-start | bytes 1179656 | tf_op jit(solution)/shard_map/ppermute | solution.py:398
  144.6 3.7 %collective-permute-start.14 = (bf16[128,1536]{1,0:T(8,128)(2,1)}, bf16[128,1536]{1,0:T(8,128)(2,1)S(1)}, u32[]{:S(2)}, u32[]{:S(2)}) collective-permute-start(bf16[128,1536]{1,0:T(8,128)(2,1)} %finish.3.refs_0_), channel_id=1, source_target_pairs={{0,7},{1,6},{2,1},{3,0},{4,3},{5,2},{6,5},{7,4},{8,15},{9,14},{10,... | collective-permute-start | bytes 1179656 | tf_op jit(solution)/shard_map/ppermute | solution.py:398
  149.1 3.0 %collective-permute-start.16 = (bf16[128,1536]{1,0:T(8,128)(2,1)}, bf16[128,1536]{1,0:T(8,128)(2,1)S(1)}, u32[]{:S(2)}, u32[]{:S(2)}) collective-permute-start(bf16[128,1536]{1,0:T(8,128)(2,1)} %finish.3.refs_0_), channel_id=1, source_target_pairs={{0,1},{1,0},{2,3},{3,2},{4,5},{5,4},{6,7},{7,6},{8,9},{9,8},{10,11... | collective-permute-start | bytes 1179656 | tf_op jit(solution)/shard_map/ppermute | solution.py:398
  152.1 5.2 %collective-permute-done.12.refs_1_ = bf16[128,1536]{1,0:T(8,128)(2,1)S(1)} collective-permute-done((bf16[128,1536]{1,0:T(8,128)(2,1)}, bf16[128,1536]{1,0:T(8,128)(2,1)S(1)}, u32[]{:S(2)}, u32[]{:S(2)}) %collective-permute-start.12) | collective-permute-done | bytes 393248 | tf_op jit(solution)/shard_map/ppermute | solution.py:398
  157.3 3.3 %collective-permute-start.17 = (bf16[128,1536]{1,0:T(8,128)(2,1)}, bf16[128,1536]{1,0:T(8,128)(2,1)S(1)}, u32[]{:S(2)}, u32[]{:S(2)}) collective-permute-start(bf16[128,1536]{1,0:T(8,128)(2,1)} %finish.3.refs_0_), channel_id=1, source_target_pairs={{0,6},{1,7},{2,0},{3,1},{4,2},{5,3},{6,4},{7,5},{8,14},{9,15},{10,... | collective-permute-start | bytes 1179656 | tf_op jit(solution)/shard_map/ppermute | solution.py:398
  160.6 17.9 %collective-permute-done.13.refs_2_ = bf16[128,1536]{1,0:T(8,128)(2,1)S(1)} collective-permute-done((bf16[128,1536]{1,0:T(8,128)(2,1)}, bf16[128,1536]{1,0:T(8,128)(2,1)S(1)}, u32[]{:S(2)}, u32[]{:S(2)}) %collective-permute-start.13) | collective-permute-done | bytes 393248 | tf_op jit(solution)/shard_map/ppermute | solution.py:398
  178.5 2.9 %collective-permute-start.18 = (bf16[128,1536]{1,0:T(8,128)(2,1)}, bf16[128,1536]{1,0:T(8,128)(2,1)S(1)}, u32[]{:S(2)}, u32[]{:S(2)}) collective-permute-start(bf16[128,1536]{1,0:T(8,128)(2,1)} %finish.3.refs_0_), channel_id=1, source_target_pairs={{0,2},{1,3},{2,4},{3,5},{4,6},{5,7},{6,0},{7,1},{8,10},{9,11},{10,... | collective-permute-start | bytes 1179656 | tf_op jit(solution)/shard_map/ppermute | solution.py:398
  181.5 11.4 %all-gather.11.cloned.1.call-done.far = bf16[768,1024]{1,0:T(8,128)(2,1)} async-done(((bf16[192,1024]{1,0:T(8,128)(2,1)}), bf16[768,1024]{1,0:T(8,128)(2,1)}) %all-gather.11.cloned.1.call-update) | async-done | bytes 1572880 | tf_op jit(solution)/shard_map/all_gather | solution.py:437
  192.9 10.0 %output.1 = bf16[1024,1536]{1,0:T(8,128)(2,1)} custom-call(bf16[1024,1536]{1,0:T(8,128)(2,1)} %bitcast.42, bf16[768,1024]{1,0:T(8,128)(2,1)} %all-gather.9.cloned.1.call-done.near, bf16[768,1024]{1,0:T(8,128)(2,1)} %all-gather.11.cloned.1.call-done.far, bf16[768,1536]{1,0:T(8,128)(2,1)} %all-gather.5.cloned.1.call-done.near_weight, ...), custom_call_target="tpu_custom_call" | custom-call | flops 10000000000 | bytes 12000000 | tf_op jit(solution)/shard_map/output/pallas_call | solution.py:312
  206.1 2.8 %assemble.1 = bf16[1024,1536]{1,0:T(8,128)(2,1)} custom-call(s32[8]{0:T(128)S(1)} %stack.32.places, bf16[128,1536]{1,0:T(8,128)(2,1)S(1)} %copy-done, bf16[128,1536]{1,0:T(8,128)(2,1)S(1)} %collective-permute-done.12.refs_1_, bf16[128,1536]{1,0:T(8,128)(2,1)S(1)} %collective-permute-done.13.refs_2_, bf16[128,1536]{1,0:T(8,128)(2,1)S(1)} %collective-permute-done.14.refs_3_, ...), custom_call_target="tpu_custom_call" | custom-call | bytes 6000000 | tf_op jit(solution)/shard_map/assemble/pallas_call | solution.py:381
  (86 shorter events, 26.4 us)
Async XLA Ops:
  7.2 58.9 %all-gather.5.cloned.1.call-start = ((), (), s32[]{:S(2)}) async-start(), calls=%async_computation.2 | async-start | bytes 2949120 | tf_op jit(solution)/shard_map/all_gather | solution.py:437
  7.9 87.3 %all-gather.7.cloned.1.call-start = ((), (), s32[]{:S(2)}) async-start(), calls=%async_computation.3 | async-start | bytes 2949120 | tf_op jit(solution)/shard_map/all_gather | solution.py:437
  7.9 8.8 %copy-start.8 = (bf16[192,1536]{1,0:T(8,128)(2,1)S(1)}, bf16[192,1536]{1,0:T(8,128)(2,1)}, u32[]{:S(2)}) copy-start(bf16[192,1536]{1,0:T(8,128)(2,1)} %out_w.1) | copy-start | bytes 1769476
  8.0 26.4 %copy-start.16 = (s32[2,2048]{1,0:T(2,128)S(1)}, s32[2,2048]{1,0:T(2,128)}, u32[]{:S(2)}) copy-start(s32[2,2048]{1,0:T(2,128)} %param.15) | copy-start | bytes 49156
  8.0 26.4 %copy-start.17 = (s32[2]{0:T(128)S(1)}, s32[2]{0:T(128)}, u32[]{:S(2)}) copy-start(s32[2]{0:T(128)} %lengths.1) | copy-start | bytes 28
  16.7 16.7 %collective-permute-start.2 = (bf16[192,1536]{1,0:T(8,128)(2,1)S(1)}, bf16[192,1536]{1,0:T(8,128)(2,1)S(1)}, u32[]{:S(2)}, u32[]{:S(2)}) collective-permute-start(bf16[192,1536]{1,0:T(8,128)(2,1)S(1)} %copy-done.8), channel_id=1, source_target_pairs={{0,1},{1,0},{2,3},{3,2},{4,5},{5,4},{6,7},{7,6},{8,9},{9,8},{10,11... | collective-permute-start | bytes 1769480 | tf_op jit(solution)/shard_map/ppermute | solution.py:398
  17.2 12.7 %collective-permute-start = (bf16[384,512]{1,0:T(8,128)(2,1)}, bf16[384,512]{1,0:T(8,128)(2,1)S(1)}, u32[]{:S(2)}, u32[]{:S(2)}) collective-permute-start(bf16[384,512]{1,0:T(8,128)(2,1)} %get-tuple-element.48), channel_id=1, source_target_pairs={{0,8},{8,16},{16,24},{1,9},{9,17},{17,25},{2,10},{10,18},{18,26},{... | collective-permute-start | bytes 1179656 | tf_op jit(solution)/shard_map/ppermute | solution.py:468
  20.6 12.4 %collective-permute-start.1 = (bf16[384,512]{1,0:T(8,128)(2,1)}, bf16[384,512]{1,0:T(8,128)(2,1)S(1)}, u32[]{:S(2)}, u32[]{:S(2)}) collective-permute-start(bf16[384,512]{1,0:T(8,128)(2,1)} %get-tuple-element.49), channel_id=1, source_target_pairs={{8,0},{16,8},{24,16},{9,1},{17,9},{25,17},{10,2},{18,10},{26,18},{... | collective-permute-start | bytes 1179656 | tf_op jit(solution)/shard_map/ppermute | solution.py:469
  34.3 147.1 %all-gather.9.cloned.1.call-start = ((), (), s32[]{:S(2)}) async-start(), calls=%async_computation.4 | async-start | bytes 1966080 | tf_op jit(solution)/shard_map/all_gather | solution.py:437
  44.9 15.3 %collective-permute-start.3 = (bf16[384,256]{1,0:T(8,128)(2,1)}, bf16[384,256]{1,0:T(8,128)(2,1)S(1)}, u32[]{:S(2)}, u32[]{:S(2)}) collective-permute-start(bf16[384,256]{1,0:T(8,128)(2,1)} %get-tuple-element.61), channel_id=1, source_target_pairs={{0,8},{8,16},{16,24},{1,9},{9,17},{17,25},{2,10},{10,18},{18,26},{... | collective-permute-start | bytes 589832 | tf_op jit(solution)/shard_map/ppermute | solution.py:481
  48.3 11.9 %collective-permute-start.4 = (bf16[384,256]{1,0:T(8,128)(2,1)}, bf16[384,256]{1,0:T(8,128)(2,1)S(1)}, u32[]{:S(2)}, u32[]{:S(2)}) collective-permute-start(bf16[384,256]{1,0:T(8,128)(2,1)} %get-tuple-element.62), channel_id=1, source_target_pairs={{8,0},{16,8},{24,16},{9,1},{17,9},{25,17},{10,2},{18,10},{26,18},{... | collective-permute-start | bytes 589832 | tf_op jit(solution)/shard_map/ppermute | solution.py:480
  66.0 11.9 %copy-start.18 = (bf16[384,256]{1,0:T(8,128)(2,1)S(1)}, bf16[384,256]{1,0:T(8,128)(2,1)}, u32[]{:S(2)}) copy-start(bf16[384,256]{1,0:T(8,128)(2,1)} %get-tuple-element.67) | copy-start | bytes 589828
  66.0 14.4 %copy-start.10 = (bf16[192,1024]{1,0:T(8,128)(2,1)S(1)}, bf16[192,1024]{1,0:T(8,128)(2,1)}, u32[]{:S(2)}) copy-start(bf16[192,1024]{1,0:T(8,128)(2,1)} %get-tuple-element.68.rest_8_) | copy-start | bytes 1179652
  66.1 30.5 %all-to-all-start = ((bf16[8,64,1536]{2,1,0:T(8,128)(2,1)}), bf16[8,64,1536]{2,1,0:T(8,128)(2,1)S(1)}, u32[]{:S(2)}, u32[]{:S(2)}) async-start(bf16[8,64,1536]{2,1,0:T(8,128)(2,1)} %bitcast.47), calls=%async_computation | async-start | bytes 3145728 | tf_op jit(solution)/shard_map/all_to_all | solution.py:407
  74.5 118.4 %all-gather.11.cloned.1.call-start = ((), (), s32[]{:S(2)}) async-start(), calls=%async_computation.5 | async-start | bytes 1966080 | tf_op jit(solution)/shard_map/all_gather | solution.py:437
  74.5 7.6 %collective-permute-start.5 = (bf16[384,256]{1,0:T(8,128)(2,1)S(1)}, bf16[384,256]{1,0:T(8,128)(2,1)S(1)}, u32[]{:S(2)}, u32[]{:S(2)}) collective-permute-start(bf16[384,256]{1,0:T(8,128)(2,1)S(1)} %copy-done.19), channel_id=1, source_target_pairs={{0,8},{8,16},{16,24},{1,9},{9,17},{17,25},{2,10},{10,18},{18,26},{... | collective-permute-start | bytes 589832 | tf_op jit(solution)/shard_map/ppermute | solution.py:481
  77.9 7.6 %collective-permute-start.6 = (bf16[384,256]{1,0:T(8,128)(2,1)S(1)}, bf16[384,256]{1,0:T(8,128)(2,1)S(1)}, u32[]{:S(2)}, u32[]{:S(2)}) collective-permute-start(bf16[384,256]{1,0:T(8,128)(2,1)S(1)} %copy-done.18), channel_id=1, source_target_pairs={{8,0},{16,8},{24,16},{9,1},{17,9},{25,17},{10,2},{18,10},{26,18},{... | collective-permute-start | bytes 589832 | tf_op jit(solution)/shard_map/ppermute | solution.py:480
  80.4 21.9 %collective-permute-start.11 = (bf16[192,1024]{1,0:T(8,128)(2,1)S(1)}, bf16[192,1024]{1,0:T(8,128)(2,1)S(1)}, u32[]{:S(2)}, u32[]{:S(2)}) collective-permute-start(bf16[192,1024]{1,0:T(8,128)(2,1)S(1)} %copy-done.10), channel_id=1, source_target_pairs={{0,1},{1,0},{2,3},{3,2},{4,5},{5,4},{6,7},{7,6},{8,9},{9,8},{10,11... | collective-permute-start | bytes 1179656 | tf_op jit(solution)/shard_map/ppermute | solution.py:398
  96.6 12.2 %collective-permute-start.7 = (bf16[4,2,96,768]{3,2,1,0:T(8,128)(2,1)}, bf16[4,2,96,768]{3,2,1,0:T(8,128)(2,1)}, u32[]{:S(2)}, u32[]{:S(2)}) collective-permute-start(bf16[4,2,96,768]{3,2,1,0:T(8,128)(2,1)} %get-tuple-element.73), channel_id=1, source_target_pairs={{0,32},{32,0},{64,96},{96,64},{1,33},{33,1},{65,97},{97,65},{2,34}... | collective-permute-start | bytes 3538952 | tf_op jit(solution)/shard_map/ppermute | solution.py:415
  103.1 34.1 %all-to-all-start.1 = ((bf16[8,64,1536]{2,1,0:T(8,128)(2,1)}), bf16[8,64,1536]{2,1,0:T(8,128)(2,1)S(1)}, u32[]{:S(2)}, u32[]{:S(2)}) async-start(bf16[8,64,1536]{2,1,0:T(8,128)(2,1)} %bitcast.46), calls=%async_computation.1 | async-start | bytes 3145728 | tf_op jit(solution)/shard_map/all_to_all | solution.py:407
  111.9 11.6 %collective-permute-start.10 = (bf16[2,96,768]{2,1,0:T(8,128)(2,1)S(1)}, bf16[2,96,768]{2,1,0:T(8,128)(2,1)S(1)}, u32[]{:S(2)}, u32[]{:S(2)}) collective-permute-start(bf16[2,96,768]{2,1,0:T(8,128)(2,1)S(1)} %get-tuple-element.88), channel_id=1, source_target_pairs={{0,16},{8,24},{16,0},{24,8},{1,17},{9,25},{17,1},{25,9},{2,18},{10... | collective-permute-start | bytes 884744 | tf_op jit(solution)/shard_map/ppermute | solution.py:423
  114.0 14.2 %collective-permute-start.9 = (bf16[2,96,768]{2,1,0:T(8,128)(2,1)S(1)}, bf16[2,96,768]{2,1,0:T(8,128)(2,1)S(1)}, u32[]{:S(2)}, u32[]{:S(2)}) collective-permute-start(bf16[2,96,768]{2,1,0:T(8,128)(2,1)S(1)} %get-tuple-element.89), channel_id=1, source_target_pairs={{0,24},{8,0},{16,8},{24,16},{1,25},{9,1},{17,9},{25,17},{2,26},{10... | collective-permute-start | bytes 884744 | tf_op jit(solution)/shard_map/ppermute | solution.py:423
  115.5 12.9 %collective-permute-start.8 = (bf16[2,96,768]{2,1,0:T(8,128)(2,1)S(1)}, bf16[2,96,768]{2,1,0:T(8,128)(2,1)S(1)}, u32[]{:S(2)}, u32[]{:S(2)}) collective-permute-start(bf16[2,96,768]{2,1,0:T(8,128)(2,1)S(1)} %get-tuple-element.87), channel_id=1, source_target_pairs={{0,8},{8,16},{16,24},{24,0},{1,9},{9,17},{17,25},{25,1},{2,10},{10... | collective-permute-start | bytes 884744 | tf_op jit(solution)/shard_map/ppermute | solution.py:423
  141.1 16.2 %collective-permute-start.12 = (bf16[128,1536]{1,0:T(8,128)(2,1)}, bf16[128,1536]{1,0:T(8,128)(2,1)S(1)}, u32[]{:S(2)}, u32[]{:S(2)}) collective-permute-start(bf16[128,1536]{1,0:T(8,128)(2,1)} %finish.3.refs_0_), channel_id=1, source_target_pairs={{0,5},{1,4},{2,7},{3,6},{4,1},{5,0},{6,3},{7,2},{8,13},{9,12},{10,... | collective-permute-start | bytes 1179656 | tf_op jit(solution)/shard_map/ppermute | solution.py:398
  141.9 36.6 %collective-permute-start.13 = (bf16[128,1536]{1,0:T(8,128)(2,1)}, bf16[128,1536]{1,0:T(8,128)(2,1)S(1)}, u32[]{:S(2)}, u32[]{:S(2)}) collective-permute-start(bf16[128,1536]{1,0:T(8,128)(2,1)} %finish.3.refs_0_), channel_id=1, source_target_pairs={{0,4},{1,5},{2,6},{3,7},{4,0},{5,1},{6,2},{7,3},{8,12},{9,13},{10,... | collective-permute-start | bytes 1179656 | tf_op jit(solution)/shard_map/ppermute | solution.py:398
  144.6 61.5 %copy-start = (bf16[128,1536]{1,0:T(8,128)(2,1)S(1)}, bf16[128,1536]{1,0:T(8,128)(2,1)}, u32[]{:S(2)}) copy-start(bf16[128,1536]{1,0:T(8,128)(2,1)} %finish.3.refs_0_) | copy-start | bytes 1179652
  144.6 59.3 %collective-permute-start.14 = (bf16[128,1536]{1,0:T(8,128)(2,1)}, bf16[128,1536]{1,0:T(8,128)(2,1)S(1)}, u32[]{:S(2)}, u32[]{:S(2)}) collective-permute-start(bf16[128,1536]{1,0:T(8,128)(2,1)} %finish.3.refs_0_), channel_id=1, source_target_pairs={{0,7},{1,6},{2,1},{3,0},{4,3},{5,2},{6,5},{7,4},{8,15},{9,14},{10,... | collective-permute-start | bytes 1179656 | tf_op jit(solution)/shard_map/ppermute | solution.py:398
  148.4 57.7 %collective-permute-start.15 = (bf16[128,1536]{1,0:T(8,128)(2,1)}, bf16[128,1536]{1,0:T(8,128)(2,1)S(1)}, u32[]{:S(2)}, u32[]{:S(2)}) collective-permute-start(bf16[128,1536]{1,0:T(8,128)(2,1)} %finish.3.refs_0_), channel_id=1, source_target_pairs={{0,3},{1,2},{2,5},{3,4},{4,7},{5,6},{6,1},{7,0},{8,11},{9,10},{10,... | collective-permute-start | bytes 1179656 | tf_op jit(solution)/shard_map/ppermute | solution.py:398
  149.1 57.0 %collective-permute-start.16 = (bf16[128,1536]{1,0:T(8,128)(2,1)}, bf16[128,1536]{1,0:T(8,128)(2,1)S(1)}, u32[]{:S(2)}, u32[]{:S(2)}) collective-permute-start(bf16[128,1536]{1,0:T(8,128)(2,1)} %finish.3.refs_0_), channel_id=1, source_target_pairs={{0,1},{1,0},{2,3},{3,2},{4,5},{5,4},{6,7},{7,6},{8,9},{9,8},{10,11... | collective-permute-start | bytes 1179656 | tf_op jit(solution)/shard_map/ppermute | solution.py:398
  157.3 48.8 %collective-permute-start.17 = (bf16[128,1536]{1,0:T(8,128)(2,1)}, bf16[128,1536]{1,0:T(8,128)(2,1)S(1)}, u32[]{:S(2)}, u32[]{:S(2)}) collective-permute-start(bf16[128,1536]{1,0:T(8,128)(2,1)} %finish.3.refs_0_), channel_id=1, source_target_pairs={{0,6},{1,7},{2,0},{3,1},{4,2},{5,3},{6,4},{7,5},{8,14},{9,15},{10,... | collective-permute-start | bytes 1179656 | tf_op jit(solution)/shard_map/ppermute | solution.py:398
  178.5 27.6 %collective-permute-start.18 = (bf16[128,1536]{1,0:T(8,128)(2,1)}, bf16[128,1536]{1,0:T(8,128)(2,1)S(1)}, u32[]{:S(2)}, u32[]{:S(2)}) collective-permute-start(bf16[128,1536]{1,0:T(8,128)(2,1)} %finish.3.refs_0_), channel_id=1, source_target_pairs={{0,2},{1,3},{2,4},{3,5},{4,6},{5,7},{6,0},{7,1},{8,10},{9,11},{10,... | collective-permute-start | bytes 1179656 | tf_op jit(solution)/shard_map/ppermute | solution.py:398
  203.9 6.0 %collective-permute-start.19 = (bf16[96,768]{1,0:T(8,128)(2,1)S(1)}, bf16[96,768]{1,0:T(8,128)(2,1)S(1)}, u32[]{:S(2)}, u32[]{:S(2)}) collective-permute-start(bf16[96,768]{1,0:T(8,128)(2,1)S(1)} %fusion.5), channel_id=1, source_target_pairs={{0,64},{32,96},{64,0},{96,32},{1,65},{33,97},{65,1},{97,33},{2,66}... | collective-permute-start | bytes 442376 | tf_op jit(solution)/shard_map/ppermute | solution.py:431
  (14 other events, 42.9 us)
Sparse Core Ops, SparseCore 0:
  9.7 35.4 all-gather.4
  46.8 44.0 all-gather.6
  92.5 43.6 all-gather.8
  138.3 54.5 all-gather.10

commit v13 on v12

--- a/solution.py
+++ b/solution.py
@@ -297,30 +297,41 @@
     )(core, normed, cotangent, *pieces)
 
 
-def output_body(tok, near, far, near_weight, far_weight, out):
-    total = dot_nn(near[...].T, near_weight[...]) + dot_nn(far[...].T, far_weight[...])
-    out[...] = (tok[...].astype(F32) + total).astype(BF16)
-
-
-def output_rows(tokens, near, far, near_weight, far_weight):
+def output_body(tok, near, far, *refs):
+    weights, (out, stacks) = refs[:4], refs[4:]
+    core = lax.axis_index("batch") & 1
+    half = weights[0].shape[0] // 4
+    total = tok[...].astype(F32)
+    for index, weight in enumerate(weights):
+        offset = core if index < 2 else 1 - core
+        source = (near, far)[index % 2]
+        for z in range(4):
+            place = pl.multiple_of((2 * z + offset) * half, half)
+            stacks[index, z * half : (z + 1) * half, :] = source[pl.ds(place, half), :]
+        total = total + dot_nn(stacks[index].T, weight[...])
+    out[...] = total.astype(BF16)
+
+
+def output_rows(tokens, near, far, weights):
     rows, model = tokens.shape
-    depth = near.shape[0]
+    depth = weights[0].shape[0]
     block = 2 * CTX
     by_row = pl.BlockSpec((block, model), lambda i: (i, 0))
-    by_col = pl.BlockSpec((depth, block), lambda i: (0, i))
+    by_col = pl.BlockSpec((2 * depth, block), lambda i: (0, i))
     full = pl.BlockSpec((depth, model), lambda i: (0, 0))
     return pl.pallas_call(
         output_body,
         grid=(rows // block,),
-        in_specs=[by_row, by_col, by_col, full, full],
+        in_specs=[by_row, by_col, by_col] + [full] * 4,
         out_specs=by_row,
         out_shape=jax.ShapeDtypeStruct((rows, model), BF16),
+        scratch_shapes=[pltpu.VMEM((4, depth, block), BF16)],
         compiler_params=params(),
         cost_estimate=pl.CostEstimate(
             flops=10000000000, bytes_accessed=12000000, transcendentals=0
         ),
         name="output",
-    )(tokens, near, far, near_weight, far_weight)
+    )(tokens, near, far, *weights)
 
 
 def finish_body(place, gain, tok, cot, parts, *refs):
@@ -448,7 +459,8 @@
     weight = qkv_weight.transpose(1, 2, 0).reshape(3 * width, model)
     tie = lax.optimization_barrier
     core = lax.axis_index("batch") & 1
-    near_out = over_z(out_weight)
+    half_out = lax.dynamic_slice_in_dim(out_weight, core * (width // 2), width // 2, 0)
+    near_out = over_z(half_out)
 
     flat_tokens = tokens.reshape(rows, model)
     flat_cot = cotangent.reshape(rows, model)
@@ -465,10 +477,10 @@
     size = lax.axis_size("frames")
     up = [(i, i + 1) for i in range(size - 1)]
     down = [(i + 1, i) for i in range(size - 1)]
+    late_out, kv_first = tie((half_out, kv_first))
+    peer_out = to_peer(late_out, (0, 1))
     before = lax.ppermute(kv_last, "frames", up)
     after = lax.ppermute(kv_first, "frames", down)
-    late_out, _ = tie((out_weight, kv_first))
-    peer_out = to_peer(late_out, (0, 1))
     before, after, peer_out = tie((before, after, peer_out))
     far_out = over_z(peer_out)
 
@@ -491,10 +503,10 @@
     mixed, second_back = tie((mixed[0], second_back))
     near_mixed = over_z(mixed)
     peer_mixed = to_peer(mixed, (0, 1))
-    first[0], second_back, near_out = tie((first[0], second_back, near_out))
+    first[0], second_back, far_out, near_out = tie((first[0], second_back, far_out, near_out))
     sent, kept = weight_grads(scalar(core), normed, flat_cot, first + second + [mixed])
     second_parts = to_all(second_back)
-    first[0], sent, second_parts, far_out = tie((first[0], sent, second_parts, far_out))
+    first[0], sent, second_parts = tie((first[0], sent, second_parts))
     first_back = split(back_rows(*first[:4], weight))
     first_back, peer_mixed = tie((first_back, peer_mixed))
     far_mixed = over_z(peer_mixed)
@@ -509,7 +521,10 @@
     sums, first_parts = tie((sums, first_parts))
     piece = ending(0, first_parts, piece)
     pieces = [to_peer(piece, shift) for shift in SHIFTS]
-    output = output_rows(flat_tokens, near_mixed, far_mixed, near_out, far_out)
+    own = [near_out, far_out]
+    output = output_rows(
+        flat_tokens, near_mixed, far_mixed, own + [core_swap(array) for array in own]
+    )
     pieces[0], output = tie((pieces[0], output))
     places = jnp.stack([me] + [peer_index(me, shift, -1) for shift in SHIFTS]).astype(jnp.int32)
     grad_tokens = assemble(places, [piece] + pieces)

time: 219 us -> 206 us (0.941)
  waiting for transfers between devices: 69.2 us -> 38.2 us
  starting transfers between devices: 56.1 us -> 71.1 us
    ppermute x9, starting transfers between devices: 17.7 us -> 32.2 us  [to_peer(): return lax.ppermute(array, 'chan', pairs)]
    all_gather x4, waiting for transfers between devices: 11.5 us -> 0.04 us  [over_z(): return lax.all_gather(array, 'chan', axis_index_groups=groups, tiled=True)]
    ppermute x9, waiting for transfers between devices: 23.6 us -> 14.7 us  [to_peer(): return lax.ppermute(array, 'chan', pairs)]
    ppermute x1, waiting for transfers between devices: 6.8 us -> 0.01 us  [shards(): before = lax.ppermute(kv_last, 'frames', up)]
    ppermute x1, waiting for transfers between devices: 3.12 us -> 0.42 us  [shards(): after = lax.ppermute(kv_first, 'frames', down)]
  transfers between devices with their start and end apart: 26 -> 28, of which waited for: 14 -> 10; matrix products, arithmetic and copies ran while one was open for 3% -> 3% of each run, Pallas kernels for 30% -> 33%
where the time goes in v13:
time: 206 us; the launch traced here: 204 us
  starting transfers between devices  71.1 us (35%)
  Pallas kernels  67 us (33%)
  waiting for transfers between devices  38.2 us (19%)
  between operations  14.1 us (7%)
  local copies, waits for them, and re-layouts  10.1 us (5%)
  other arithmetic  3.63 us (2%)
    ppermute x9, starting transfers between devices, to_peer(): return lax.ppermute(array, 'chan', pairs)  32.2 us
    pallas_call x2, Pallas kernels, attention(): pl.pallas_call(attention_body, grid=(1,), in_specs=[by_rec(width, frames)...  18.3 us
    ppermute x9, waiting for transfers between devices, to_peer(): return lax.ppermute(array, 'chan', pairs)  14.7 us
    all_to_all x2, starting transfers between devices, to_all(): return lax.all_to_all(array, 'chan', 0, 0, tiled=True)  14.4 us
    pallas_call x1, Pallas kernels, output_rows(): pl.pallas_call(output_body, grid=(rows // block,), in_specs=[by_row, by_c...  11.6 us
    pallas_call x2, Pallas kernels, back_rows(): pl.pallas_call(back_body, grid=(model // tile,), in_specs=[full(width, ro...  10.8 us
    ppermute x3, waiting for transfers between devices, frame_sums(): got = lax.ppermute(sent, 'frames', [(i, (i + shift) % 4) for i in range(4)])  9.76 us
    pallas_call x1, Pallas kernels, weight_grads(): pl.pallas_call(weight_grads_body, grid_spec=pltpu.PrefetchScalarGridSpec(...  8.97 us
  transfers between devices with their start and end apart: 28, of which 10 were waited for; matrix products, arithmetic and copies ran while one was open for 3% of the time, Pallas kernels for 33%

profile of v13, /device:TPU:18, one launch (start us, length us, event | category | flops | bytes accessed | tf_op | source)
XLA Modules:
  0.0 204.1 jit_solution(3571400784108441943)
XLA Ops:
  9.0 8.8 %project.1 = (bf16[1024,1536]{1,0:T(8,128)(2,1)}, bf16[192,1024]{1,0:T(8,128)(2,1)}, bf16[384,1024]{1,0:T(8,128)(2,1)}, bf16[192,1024]{1,0:T(8,128)(2,1)}, bf16[...) custom-call(s32[2]{0:T(128)} %lengths.1, bf16[1024,1536]{1,0:T(8,128)(2,1)} %bitcast.39, ...), custom_call_target="tpu_custom_call" | custom-call | flops 2400000000 | bytes 15000000 | tf_op jit(solution)/shard_map/project/pallas_call | solution.py:70
  17.8 3.4 %collective-permute-start = (bf16[384,512]{1,0:T(8,128)(2,1)}, bf16[384,512]{1,0:T(8,128)(2,1)S(1)}, u32[]{:S(2)}, u32[]{:S(2)}) collective-permute-start(bf16[384,512]{1,0:T(8,128)(2,1)} %get-tuple-element.49), channel_id=1, source_target_pairs={{0,8},{8,16},{16,24},{1,9},{9,17},{17,25},{2,10},{10,18},{18,26},{... | collective-permute-start | bytes 1179656 | tf_op jit(solution)/shard_map/ppermute | solution.py:482
  21.2 2.5 %collective-permute-start.1 = (bf16[384,512]{1,0:T(8,128)(2,1)}, bf16[384,512]{1,0:T(8,128)(2,1)S(1)}, u32[]{:S(2)}, u32[]{:S(2)}) collective-permute-start(bf16[384,512]{1,0:T(8,128)(2,1)} %get-tuple-element.51), channel_id=1, source_target_pairs={{8,0},{16,8},{24,16},{9,1},{17,9},{25,17},{10,2},{18,10},{26,18},{... | collective-permute-start | bytes 1179656 | tf_op jit(solution)/shard_map/ppermute | solution.py:483
  24.1 9.4 %collective-permute-done.2 = bf16[96,1536]{1,0:T(8,128)(2,1)S(1)} collective-permute-done((bf16[96,1536]{1,0:T(8,128)(2,1)S(1)}, bf16[96,1536]{1,0:T(8,128)(2,1)S(1)}, u32[]{:S(2)}, u32[]{:S(2)}) %collective-permute-start.2) | collective-permute-done | bytes 294944 | tf_op jit(solution)/shard_map/ppermute | solution.py:409
  35.6 9.1 %attention.2 = (bf16[192,512]{1,0:T(8,128)(2,1)}, bf16[192,512]{1,0:T(8,128)(2,1)}, f32[384,512]{1,0:T(8,128)}, bf16[384,256]{1,0:T(8,128)(2,1)}, bf16[384,256]{1,0:T(8,128)(2,1)}) custom-call(bf16[192,1024]{1,0:T(8,128)(2,1)} %get-tuple-element.47.q, bf16[384,1024]{1,0:T(8,128)(2,1)} %get-tuple-element.48.kv, bf16[384,512]{1,0:T(8,128)(2,1)} %copy-done.5, ...), custom_call_target="tpu_custom_call" | custom-call | flops 1000 | bytes 1000 | tf_op jit(solution)/shard_map/attention/pallas_call | solution.py:158
  44.7 3.4 %collective-permute-start.3 = (bf16[384,256]{1,0:T(8,128)(2,1)}, bf16[384,256]{1,0:T(8,128)(2,1)S(1)}, u32[]{:S(2)}, u32[]{:S(2)}) collective-permute-start(bf16[384,256]{1,0:T(8,128)(2,1)} %get-tuple-element.63), channel_id=1, source_target_pairs={{0,8},{8,16},{16,24},{1,9},{9,17},{17,25},{2,10},{10,18},{18,26},{... | collective-permute-start | bytes 589832 | tf_op jit(solution)/shard_map/ppermute | solution.py:493
  48.0 2.7 %collective-permute-start.4 = (bf16[384,256]{1,0:T(8,128)(2,1)}, bf16[384,256]{1,0:T(8,128)(2,1)S(1)}, u32[]{:S(2)}, u32[]{:S(2)}) collective-permute-start(bf16[384,256]{1,0:T(8,128)(2,1)} %get-tuple-element.64), channel_id=1, source_target_pairs={{8,0},{16,8},{24,16},{9,1},{17,9},{25,17},{10,2},{18,10},{26,18},{... | collective-permute-start | bytes 589832 | tf_op jit(solution)/shard_map/ppermute | solution.py:492
  50.7 9.2 %attention.3 = (bf16[192,1024]{1,0:T(8,128)(2,1)}, bf16[192,512]{1,0:T(8,128)(2,1)}, f32[384,512]{1,0:T(8,128)}, bf16[384,256]{1,0:T(8,128)(2,1)}, bf16[384,256]{1,0:T(8,128)(2,1)}) custom-call(bf16[192,1024]{1,0:T(8,128)(2,1)} %get-tuple-element.47.q, bf16[384,1024]{1,0:T(8,128)(2,1)} %get-tuple-element.48.kv, bf16[384,512]{1,0:T(8,128)(2,1)} %copy-done.5, ...), custom_call_target="tpu_custom_call" | custom-call | flops 1000 | bytes 1000 | tf_op jit(solution)/shard_map/attention/pallas_call | solution.py:158
  60.7 5.1 %back.2 = bf16[512,1536]{1,0:T(8,128)(2,1)} custom-call(bf16[192,512]{1,0:T(8,128)(2,1)} %get-tuple-element.61.dq.rest_4_, f32[384,512]{1,0:T(8,128)} %get-tuple-element.62.own.rest_5_, bf16[384,256]{1,0:T(8,128)(2,1)} %copy-done.12, bf16[384,256]{1,0:T(8,128)(2,1)} %copy-done.13, bf16[576,1536]{1,0:T(8,128)(2,1)} %bitcast.44), custom_call_target="tpu_custom_call" | custom-call | flops 900000000 | bytes 4000000 | tf_op jit(solution)/shard_map/back/pallas_call | solution.py:215
  65.9 8.4 %all-to-all-start = ((bf16[8,64,1536]{2,1,0:T(8,128)(2,1)}), bf16[8,64,1536]{2,1,0:T(8,128)(2,1)S(1)}, u32[]{:S(2)}, u32[]{:S(2)}) async-start(bf16[8,64,1536]{2,1,0:T(8,128)(2,1)} %bitcast.47), calls=%async_computation | async-start | bytes 3145728 | tf_op jit(solution)/shard_map/all_to_all | solution.py:418
  74.3 3.4 %collective-permute-start.5 = (bf16[384,256]{1,0:T(8,128)(2,1)S(1)}, bf16[384,256]{1,0:T(8,128)(2,1)S(1)}, u32[]{:S(2)}, u32[]{:S(2)}) collective-permute-start(bf16[384,256]{1,0:T(8,128)(2,1)S(1)} %copy-done.19), channel_id=1, source_target_pairs={{0,8},{8,16},{16,24},{1,9},{9,17},{17,25},{2,10},{10,18},{18,26},{... | collective-permute-start | bytes 589832 | tf_op jit(solution)/shard_map/ppermute | solution.py:493
  77.7 2.5 %collective-permute-start.6 = (bf16[384,256]{1,0:T(8,128)(2,1)S(1)}, bf16[384,256]{1,0:T(8,128)(2,1)S(1)}, u32[]{:S(2)}, u32[]{:S(2)}) collective-permute-start(bf16[384,256]{1,0:T(8,128)(2,1)S(1)} %copy-done.18), channel_id=1, source_target_pairs={{8,0},{16,8},{24,16},{9,1},{17,9},{25,17},{10,2},{18,10},{26,18},{... | collective-permute-start | bytes 589832 | tf_op jit(solution)/shard_map/ppermute | solution.py:492
  81.9 3.4 %collective-permute-done.6.rest_3_.right = bf16[384,256]{1,0:T(8,128)(2,1)S(1)} collective-permute-done((bf16[384,256]{1,0:T(8,128)(2,1)S(1)}, bf16[384,256]{1,0:T(8,128)(2,1)S(1)}, u32[]{:S(2)}, u32[]{:S(2)}) %collective-permute-start.6) | collective-permute-done | bytes 196640 | tf_op jit(solution)/shard_map/ppermute | solution.py:492
  86.0 9.0 %weight_grads.1 = (bf16[4,2,96,768]{3,2,1,0:T(8,128)(2,1)}, bf16[4,2,96,768]{3,2,1,0:T(8,128)(2,1)}) custom-call(s32[1]{0:T(128)} %bitcast.core, bf16[1024,1536]{1,0:T(8,128)(2,1)} %get-tuple-element.46.normed, bf16[1024,1536]{1,0:T(8,128)(2,1)} %bitcast.36, bf16[192,512]{1,0:T(8,128)(2,1)} %get-tuple-element.76.rest_0_.dq, ...), custom_call_target="tpu_custom_call" | custom-call | flops 10000000000 | bytes 12000000 | tf_op jit(solution)/shard_map/weight_grads/pallas_call | solution.py:274
  94.9 4.6 %all-to-all-done.parts = bf16[8,64,1536]{2,1,0:T(8,128)(2,1)S(1)} async-done(((bf16[8,64,1536]{2,1,0:T(8,128)(2,1)}), bf16[8,64,1536]{2,1,0:T(8,128)(2,1)S(1)}, u32[]{:S(2)}, u32[]{:S(2)}) %all-to-all-start) | async-done | bytes 1572896 | tf_op jit(solution)/shard_map/all_to_all | solution.py:418
  99.5 5.7 %back.3 = bf16[512,1536]{1,0:T(8,128)(2,1)} custom-call(bf16[192,512]{1,0:T(8,128)(2,1)} %get-tuple-element.76.rest_0_.dq, f32[384,512]{1,0:T(8,128)} %get-tuple-element.68.rest_1_.own, bf16[384,256]{1,0:T(8,128)(2,1)} %copy-done.14, bf16[384,256]{1,0:T(8,128)(2,1)} %copy-done.15, bf16[576,1536]{1,0:T(8,128)(2,1)} %bitcast.45), custom_call_target="tpu_custom_call" | custom-call | flops 900000000 | bytes 4000000 | tf_op jit(solution)/shard_map/back/pallas_call | solution.py:215
  106.0 5.9 %all-to-all-start.1 = ((bf16[8,64,1536]{2,1,0:T(8,128)(2,1)}), bf16[8,64,1536]{2,1,0:T(8,128)(2,1)S(1)}, u32[]{:S(2)}, u32[]{:S(2)}) async-start(bf16[8,64,1536]{2,1,0:T(8,128)(2,1)} %bitcast.46), calls=%async_computation.1 | async-start | bytes 3145728 | tf_op jit(solution)/shard_map/all_to_all | solution.py:418
  115.5 2.2 %collective-permute-start.10 = (bf16[2,96,768]{2,1,0:T(8,128)(2,1)S(1)}, bf16[2,96,768]{2,1,0:T(8,128)(2,1)S(1)}, u32[]{:S(2)}, u32[]{:S(2)}) collective-permute-start(bf16[2,96,768]{2,1,0:T(8,128)(2,1)S(1)} %get-tuple-element.90), channel_id=1, source_target_pairs={{0,16},{8,24},{16,0},{24,8},{1,17},{9,25},{17,1},{25,9},{2,18},{10... | collective-permute-start | bytes 884744 | tf_op jit(solution)/shard_map/ppermute | solution.py:434
  119.7 2.9 %finish.2.refs_0_ = bf16[64,1536]{1,0:T(8,128)(2,1)} custom-call(s32[1]{0:T(128)} %bitcast.13.place, f32[1536]{0:T(1024)} %gain.5, bf16[1024,1536]{1,0:T(8,128)(2,1)} %bitcast.40, bf16[1024,1536]{1,0:T(8,128)(2,1)} %bitcast.37, bf16[8,64,1536]{2,1,0:T(8,128)(2,1)} %copy-done.2), custom_call_target="tpu_custom_call" | custom-call | flops 10000000 | bytes 3000000 | tf_op jit(solution)/shard_map/finish/pallas_call | solution.py:356
  122.5 4.4 %collective-permute-done.10 = bf16[2,96,768]{2,1,0:T(8,128)(2,1)S(1)} collective-permute-done((bf16[2,96,768]{2,1,0:T(8,128)(2,1)S(1)}, bf16[2,96,768]{2,1,0:T(8,128)(2,1)S(1)}, u32[]{:S(2)}, u32[]{:S(2)}) %collective-permute-start.10) | collective-permute-done | bytes 294944 | tf_op jit(solution)/shard_map/ppermute | solution.py:434
  127.0 5.3 %collective-permute-done.9 = bf16[2,96,768]{2,1,0:T(8,128)(2,1)S(1)} collective-permute-done((bf16[2,96,768]{2,1,0:T(8,128)(2,1)S(1)}, bf16[2,96,768]{2,1,0:T(8,128)(2,1)S(1)}, u32[]{:S(2)}, u32[]{:S(2)}) %collective-permute-start.9) | collective-permute-done | bytes 294944 | tf_op jit(solution)/shard_map/ppermute | solution.py:434
  132.3 2.0 fusion.1
  134.3 3.3 %all-to-all-done.1.parts = bf16[8,64,1536]{2,1,0:T(8,128)(2,1)S(1)} async-done(((bf16[8,64,1536]{2,1,0:T(8,128)(2,1)}), bf16[8,64,1536]{2,1,0:T(8,128)(2,1)S(1)}, u32[]{:S(2)}, u32[]{:S(2)}) %all-to-all-start.1) | async-done | bytes 1572896 | tf_op jit(solution)/shard_map/all_to_all | solution.py:418
  138.8 2.9 %finish.3.refs_0_ = bf16[128,1536]{1,0:T(8,128)(2,1)} custom-call(s32[1]{0:T(128)} %bitcast.12.place, f32[1536]{0:T(1024)} %gain.5, bf16[1024,1536]{1,0:T(8,128)(2,1)} %bitcast.41, bf16[1024,1536]{1,0:T(8,128)(2,1)} %bitcast.38, bf16[8,64,1536]{2,1,0:T(8,128)(2,1)} %copy-done.1, bf16[64,1536]{1,0:T(8,128)(2,1)} %finish.2.refs_0_), custom_call_target="tpu_custom_call" | custom-call | flops 10000000 | bytes 3000000 | tf_op jit(solution)/shard_map/finish/pallas_call | solution.py:356
  141.7 2.4 %collective-permute-start.15 = (bf16[128,1536]{1,0:T(8,128)(2,1)}, bf16[128,1536]{1,0:T(8,128)(2,1)S(1)}, u32[]{:S(2)}, u32[]{:S(2)}) collective-permute-start(bf16[128,1536]{1,0:T(8,128)(2,1)} %finish.3.refs_0_), channel_id=1, source_target_pairs={{0,4},{1,5},{2,6},{3,7},{4,0},{5,1},{6,2},{7,3},{8,12},{9,13},{10,... | collective-permute-start | bytes 1179656 | tf_op jit(solution)/shard_map/ppermute | solution.py:409
  144.0 6.2 %collective-permute-start.16 = (bf16[128,1536]{1,0:T(8,128)(2,1)}, bf16[128,1536]{1,0:T(8,128)(2,1)S(1)}, u32[]{:S(2)}, u32[]{:S(2)}) collective-permute-start(bf16[128,1536]{1,0:T(8,128)(2,1)} %finish.3.refs_0_), channel_id=1, source_target_pairs={{0,7},{1,6},{2,1},{3,0},{4,3},{5,2},{6,5},{7,4},{8,15},{9,14},{10,... | collective-permute-start | bytes 1179656 | tf_op jit(solution)/shard_map/ppermute | solution.py:409
  150.2 2.4 %collective-permute-start.18 = (bf16[128,1536]{1,0:T(8,128)(2,1)}, bf16[128,1536]{1,0:T(8,128)(2,1)S(1)}, u32[]{:S(2)}, u32[]{:S(2)}) collective-permute-start(bf16[128,1536]{1,0:T(8,128)(2,1)} %finish.3.refs_0_), channel_id=1, source_target_pairs={{0,1},{1,0},{2,3},{3,2},{4,5},{5,4},{6,7},{7,6},{8,9},{9,8},{10,11... | collective-permute-start | bytes 1179656 | tf_op jit(solution)/shard_map/ppermute | solution.py:409
  152.6 5.3 %collective-permute-done.12.refs_1_ = bf16[128,1536]{1,0:T(8,128)(2,1)S(1)} collective-permute-done((bf16[128,1536]{1,0:T(8,128)(2,1)}, bf16[128,1536]{1,0:T(8,128)(2,1)S(1)}, u32[]{:S(2)}, u32[]{:S(2)}) %collective-permute-start.12) | collective-permute-done | bytes 393248 | tf_op jit(solution)/shard_map/ppermute | solution.py:409
  157.9 5.6 %collective-permute-start.19 = (bf16[128,1536]{1,0:T(8,128)(2,1)}, bf16[128,1536]{1,0:T(8,128)(2,1)S(1)}, u32[]{:S(2)}, u32[]{:S(2)}) collective-permute-start(bf16[128,1536]{1,0:T(8,128)(2,1)} %finish.3.refs_0_), channel_id=1, source_target_pairs={{0,6},{1,7},{2,0},{3,1},{4,2},{5,3},{6,4},{7,5},{8,14},{9,15},{10,... | collective-permute-start | bytes 1179656 | tf_op jit(solution)/shard_map/ppermute | solution.py:409
  163.6 15.1 %collective-permute-start.20 = (bf16[128,1536]{1,0:T(8,128)(2,1)}, bf16[128,1536]{1,0:T(8,128)(2,1)S(1)}, u32[]{:S(2)}, u32[]{:S(2)}) collective-permute-start(bf16[128,1536]{1,0:T(8,128)(2,1)} %finish.3.refs_0_), channel_id=1, source_target_pairs={{0,2},{1,3},{2,4},{3,5},{4,6},{5,7},{6,0},{7,1},{8,10},{9,11},{10,... | collective-permute-start | bytes 1179656 | tf_op jit(solution)/shard_map/ppermute | solution.py:409
  178.6 11.6 %output.1 = bf16[1024,1536]{1,0:T(8,128)(2,1)} custom-call(bf16[1024,1536]{1,0:T(8,128)(2,1)} %bitcast.42, bf16[768,1024]{1,0:T(8,128)(2,1)} %all-gather.9.cloned.1.call-done.near, bf16[768,1024]{1,0:T(8,128)(2,1)} %all-gather.11.cloned.1.call-done.far, bf16[384,1536]{1,0:T(8,128)(2,1)} %all-gather.7.cloned.1.call-done.refs_0_, ...), custom_call_target="tpu_custom_call" | custom-call | flops 10000000000 | bytes 12000000 | tf_op jit(solution)/shard_map/output/pallas_call | solution.py:322
  193.3 2.8 %assemble.1 = bf16[1024,1536]{1,0:T(8,128)(2,1)} custom-call(s32[8]{0:T(128)S(1)} %stack.32.places, bf16[128,1536]{1,0:T(8,128)(2,1)S(1)} %copy-done, bf16[128,1536]{1,0:T(8,128)(2,1)S(1)} %collective-permute-done.12.refs_1_, bf16[128,1536]{1,0:T(8,128)(2,1)S(1)} %collective-permute-done.15.refs_2_, bf16[128,1536]{1,0:T(8,128)(2,1)S(1)} %collective-permute-done.16.refs_3_, ...), custom_call_target="tpu_custom_call" | custom-call | bytes 6000000 | tf_op jit(solution)/shard_map/assemble/pallas_call | solution.py:392
  (91 shorter events, 19.4 us)
Async XLA Ops:
  7.2 58.7 %all-gather.7.cloned.1.call-start = ((), (), s32[]{:S(2)}) async-start(), calls=%async_computation.3 | async-start | bytes 1474560 | tf_op jit(solution)/shard_map/all_gather | solution.py:448
  8.9 56.9 %all-gather.5.cloned.1.call-start = ((), (), s32[]{:S(2)}) async-start(), calls=%async_computation.2 | async-start | bytes 1474560 | tf_op jit(solution)/shard_map/all_gather | solution.py:448
  9.0 14.7 %copy-start.7 = (bf16[96,1536]{1,0:T(8,128)(2,1)S(1)}, bf16[96,1536]{1,0:T(8,128)(2,1)}, u32[]{:S(2)}) copy-start(bf16[96,1536]{1,0:T(8,128)(2,1)} %constant_dynamic-slice_fusion) | copy-start | bytes 884740
  9.0 25.3 %copy-start.16 = (s32[2,2048]{1,0:T(2,128)S(1)}, s32[2,2048]{1,0:T(2,128)}, u32[]{:S(2)}) copy-start(s32[2,2048]{1,0:T(2,128)} %param.15) | copy-start | bytes 49156
  9.0 25.2 %copy-start.17 = (s32[2]{0:T(128)S(1)}, s32[2]{0:T(128)}, u32[]{:S(2)}) copy-start(s32[2]{0:T(128)} %lengths.1) | copy-start | bytes 28
  17.8 15.7 %collective-permute-start = (bf16[384,512]{1,0:T(8,128)(2,1)}, bf16[384,512]{1,0:T(8,128)(2,1)S(1)}, u32[]{:S(2)}, u32[]{:S(2)}) collective-permute-start(bf16[384,512]{1,0:T(8,128)(2,1)} %get-tuple-element.49), channel_id=1, source_target_pairs={{0,8},{8,16},{16,24},{1,9},{9,17},{17,25},{2,10},{10,18},{18,26},{... | collective-permute-start | bytes 1179656 | tf_op jit(solution)/shard_map/ppermute | solution.py:482
  21.2 12.7 %collective-permute-start.1 = (bf16[384,512]{1,0:T(8,128)(2,1)}, bf16[384,512]{1,0:T(8,128)(2,1)S(1)}, u32[]{:S(2)}, u32[]{:S(2)}) collective-permute-start(bf16[384,512]{1,0:T(8,128)(2,1)} %get-tuple-element.51), channel_id=1, source_target_pairs={{8,0},{16,8},{24,16},{9,1},{17,9},{25,17},{10,2},{18,10},{26,18},{... | collective-permute-start | bytes 1179656 | tf_op jit(solution)/shard_map/ppermute | solution.py:483
  23.7 9.8 %collective-permute-start.2 = (bf16[96,1536]{1,0:T(8,128)(2,1)S(1)}, bf16[96,1536]{1,0:T(8,128)(2,1)S(1)}, u32[]{:S(2)}, u32[]{:S(2)}) collective-permute-start(bf16[96,1536]{1,0:T(8,128)(2,1)S(1)} %copy-done.7), channel_id=1, source_target_pairs={{0,1},{1,0},{2,3},{3,2},{4,5},{5,4},{6,7},{7,6},{8,9},{9,8},{10,11... | collective-permute-start | bytes 884744 | tf_op jit(solution)/shard_map/ppermute | solution.py:409
  34.2 144.5 %all-gather.9.cloned.1.call-start = ((), (), s32[]{:S(2)}) async-start(), calls=%async_computation.4 | async-start | bytes 1966080 | tf_op jit(solution)/shard_map/all_gather | solution.py:448
  44.7 15.2 %collective-permute-start.3 = (bf16[384,256]{1,0:T(8,128)(2,1)}, bf16[384,256]{1,0:T(8,128)(2,1)S(1)}, u32[]{:S(2)}, u32[]{:S(2)}) collective-permute-start(bf16[384,256]{1,0:T(8,128)(2,1)} %get-tuple-element.63), channel_id=1, source_target_pairs={{0,8},{8,16},{16,24},{1,9},{9,17},{17,25},{2,10},{10,18},{18,26},{... | collective-permute-start | bytes 589832 | tf_op jit(solution)/shard_map/ppermute | solution.py:493
  48.0 11.9 %collective-permute-start.4 = (bf16[384,256]{1,0:T(8,128)(2,1)}, bf16[384,256]{1,0:T(8,128)(2,1)S(1)}, u32[]{:S(2)}, u32[]{:S(2)}) collective-permute-start(bf16[384,256]{1,0:T(8,128)(2,1)} %get-tuple-element.64), channel_id=1, source_target_pairs={{8,0},{16,8},{24,16},{9,1},{17,9},{25,17},{10,2},{18,10},{26,18},{... | collective-permute-start | bytes 589832 | tf_op jit(solution)/shard_map/ppermute | solution.py:492
  65.9 33.6 %all-to-all-start = ((bf16[8,64,1536]{2,1,0:T(8,128)(2,1)}), bf16[8,64,1536]{2,1,0:T(8,128)(2,1)S(1)}, u32[]{:S(2)}, u32[]{:S(2)}) async-start(bf16[8,64,1536]{2,1,0:T(8,128)(2,1)} %bitcast.47), calls=%async_computation | async-start | bytes 3145728 | tf_op jit(solution)/shard_map/all_to_all | solution.py:418
  74.3 104.3 %all-gather.11.cloned.1.call-start = ((), (), s32[]{:S(2)}) async-start(), calls=%async_computation.5 | async-start | bytes 1966080 | tf_op jit(solution)/shard_map/all_gather | solution.py:448
  74.3 7.6 %collective-permute-start.5 = (bf16[384,256]{1,0:T(8,128)(2,1)S(1)}, bf16[384,256]{1,0:T(8,128)(2,1)S(1)}, u32[]{:S(2)}, u32[]{:S(2)}) collective-permute-start(bf16[384,256]{1,0:T(8,128)(2,1)S(1)} %copy-done.19), channel_id=1, source_target_pairs={{0,8},{8,16},{16,24},{1,9},{9,17},{17,25},{2,10},{10,18},{18,26},{... | collective-permute-start | bytes 589832 | tf_op jit(solution)/shard_map/ppermute | solution.py:493
  77.7 7.6 %collective-permute-start.6 = (bf16[384,256]{1,0:T(8,128)(2,1)S(1)}, bf16[384,256]{1,0:T(8,128)(2,1)S(1)}, u32[]{:S(2)}, u32[]{:S(2)}) collective-permute-start(bf16[384,256]{1,0:T(8,128)(2,1)S(1)} %copy-done.18), channel_id=1, source_target_pairs={{8,0},{16,8},{24,16},{9,1},{17,9},{25,17},{10,2},{18,10},{26,18},{... | collective-permute-start | bytes 589832 | tf_op jit(solution)/shard_map/ppermute | solution.py:492
  80.2 25.0 %collective-permute-start.11 = (bf16[192,1024]{1,0:T(8,128)(2,1)S(1)}, bf16[192,1024]{1,0:T(8,128)(2,1)S(1)}, u32[]{:S(2)}, u32[]{:S(2)}) collective-permute-start(bf16[192,1024]{1,0:T(8,128)(2,1)S(1)} %copy-done.9), channel_id=1, source_target_pairs={{0,1},{1,0},{2,3},{3,2},{4,5},{5,4},{6,7},{7,6},{8,9},{9,8},{10,11... | collective-permute-start | bytes 1179656 | tf_op jit(solution)/shard_map/ppermute | solution.py:409
  99.5 12.9 %collective-permute-start.7 = (bf16[4,2,96,768]{3,2,1,0:T(8,128)(2,1)}, bf16[4,2,96,768]{3,2,1,0:T(8,128)(2,1)}, u32[]{:S(2)}, u32[]{:S(2)}) collective-permute-start(bf16[4,2,96,768]{3,2,1,0:T(8,128)(2,1)} %get-tuple-element.75), channel_id=1, source_target_pairs={{0,32},{32,0},{64,96},{96,64},{1,33},{33,1},{65,97},{97,65},{2,34}... | collective-permute-start | bytes 3538952 | tf_op jit(solution)/shard_map/ppermute | solution.py:426
  106.0 31.6 %all-to-all-start.1 = ((bf16[8,64,1536]{2,1,0:T(8,128)(2,1)}), bf16[8,64,1536]{2,1,0:T(8,128)(2,1)S(1)}, u32[]{:S(2)}, u32[]{:S(2)}) async-start(bf16[8,64,1536]{2,1,0:T(8,128)(2,1)} %bitcast.46), calls=%async_computation.1 | async-start | bytes 3145728 | tf_op jit(solution)/shard_map/all_to_all | solution.py:418
  111.9 38.3 %collective-permute-start.13 = (bf16[384,1536]{1,0:T(8,128)(2,1)}, bf16[384,1536]{1,0:T(8,128)(2,1)}, u32[]{:S(2)}, u32[]{:S(2)}) collective-permute-start(bf16[384,1536]{1,0:T(8,128)(2,1)} %all-gather.7.cloned.1.call-done.refs_0_), channel_id=1, source_target_pairs={{0,32},{32,0},{64,96},{96,64},{1,33},{33,1},{65,97},{97,65},{2,34}... | collective-permute-start | bytes 3538952 | tf_op jit(solution)/shard_map/ppermute | solution.py:426
  111.9 38.3 %collective-permute-start.14 = (bf16[384,1536]{1,0:T(8,128)(2,1)}, bf16[384,1536]{1,0:T(8,128)(2,1)}, u32[]{:S(2)}, u32[]{:S(2)}) collective-permute-start(bf16[384,1536]{1,0:T(8,128)(2,1)} %all-gather.5.cloned.1.call-done.refs_1_), channel_id=1, source_target_pairs={{0,32},{32,0},{64,96},{96,64},{1,33},{33,1},{65,97},{97,65},{2,34}... | collective-permute-start | bytes 3538952 | tf_op jit(solution)/shard_map/ppermute | solution.py:426
  115.5 11.5 %collective-permute-start.10 = (bf16[2,96,768]{2,1,0:T(8,128)(2,1)S(1)}, bf16[2,96,768]{2,1,0:T(8,128)(2,1)S(1)}, u32[]{:S(2)}, u32[]{:S(2)}) collective-permute-start(bf16[2,96,768]{2,1,0:T(8,128)(2,1)S(1)} %get-tuple-element.90), channel_id=1, source_target_pairs={{0,16},{8,24},{16,0},{24,8},{1,17},{9,25},{17,1},{25,9},{2,18},{10... | collective-permute-start | bytes 884744 | tf_op jit(solution)/shard_map/ppermute | solution.py:434
  117.6 14.6 %collective-permute-start.9 = (bf16[2,96,768]{2,1,0:T(8,128)(2,1)S(1)}, bf16[2,96,768]{2,1,0:T(8,128)(2,1)S(1)}, u32[]{:S(2)}, u32[]{:S(2)}) collective-permute-start(bf16[2,96,768]{2,1,0:T(8,128)(2,1)S(1)} %get-tuple-element.91), channel_id=1, source_target_pairs={{0,24},{8,0},{16,8},{24,16},{1,25},{9,1},{17,9},{25,17},{2,26},{10... | collective-permute-start | bytes 884744 | tf_op jit(solution)/shard_map/ppermute | solution.py:434
  119.1 13.3 %collective-permute-start.8 = (bf16[2,96,768]{2,1,0:T(8,128)(2,1)S(1)}, bf16[2,96,768]{2,1,0:T(8,128)(2,1)S(1)}, u32[]{:S(2)}, u32[]{:S(2)}) collective-permute-start(bf16[2,96,768]{2,1,0:T(8,128)(2,1)S(1)} %get-tuple-element.89), channel_id=1, source_target_pairs={{0,8},{8,16},{16,24},{24,0},{1,9},{9,17},{17,25},{25,1},{2,10},{10... | collective-permute-start | bytes 884744 | tf_op jit(solution)/shard_map/ppermute | solution.py:434
  141.7 16.3 %collective-permute-start.12 = (bf16[128,1536]{1,0:T(8,128)(2,1)}, bf16[128,1536]{1,0:T(8,128)(2,1)S(1)}, u32[]{:S(2)}, u32[]{:S(2)}) collective-permute-start(bf16[128,1536]{1,0:T(8,128)(2,1)} %finish.3.refs_0_), channel_id=1, source_target_pairs={{0,5},{1,4},{2,7},{3,6},{4,1},{5,0},{6,3},{7,2},{8,13},{9,12},{10,... | collective-permute-start | bytes 1179656 | tf_op jit(solution)/shard_map/ppermute | solution.py:409
  141.7 21.9 %collective-permute-start.15 = (bf16[128,1536]{1,0:T(8,128)(2,1)}, bf16[128,1536]{1,0:T(8,128)(2,1)S(1)}, u32[]{:S(2)}, u32[]{:S(2)}) collective-permute-start(bf16[128,1536]{1,0:T(8,128)(2,1)} %finish.3.refs_0_), channel_id=1, source_target_pairs={{0,4},{1,5},{2,6},{3,7},{4,0},{5,1},{6,2},{7,3},{8,12},{9,13},{10,... | collective-permute-start | bytes 1179656 | tf_op jit(solution)/shard_map/ppermute | solution.py:409
  144.0 49.3 %copy-start = (bf16[128,1536]{1,0:T(8,128)(2,1)S(1)}, bf16[128,1536]{1,0:T(8,128)(2,1)}, u32[]{:S(2)}) copy-start(bf16[128,1536]{1,0:T(8,128)(2,1)} %finish.3.refs_0_) | copy-start | bytes 1179652
  144.0 47.2 %collective-permute-start.16 = (bf16[128,1536]{1,0:T(8,128)(2,1)}, bf16[128,1536]{1,0:T(8,128)(2,1)S(1)}, u32[]{:S(2)}, u32[]{:S(2)}) collective-permute-start(bf16[128,1536]{1,0:T(8,128)(2,1)} %finish.3.refs_0_), channel_id=1, source_target_pairs={{0,7},{1,6},{2,1},{3,0},{4,3},{5,2},{6,5},{7,4},{8,15},{9,14},{10,... | collective-permute-start | bytes 1179656 | tf_op jit(solution)/shard_map/ppermute | solution.py:409
  150.2 43.1 %collective-permute-start.17 = (bf16[128,1536]{1,0:T(8,128)(2,1)}, bf16[128,1536]{1,0:T(8,128)(2,1)S(1)}, u32[]{:S(2)}, u32[]{:S(2)}) collective-permute-start(bf16[128,1536]{1,0:T(8,128)(2,1)} %finish.3.refs_0_), channel_id=1, source_target_pairs={{0,3},{1,2},{2,5},{3,4},{4,7},{5,6},{6,1},{7,0},{8,11},{9,10},{10,... | collective-permute-start | bytes 1179656 | tf_op jit(solution)/shard_map/ppermute | solution.py:409
  150.2 43.1 %collective-permute-start.18 = (bf16[128,1536]{1,0:T(8,128)(2,1)}, bf16[128,1536]{1,0:T(8,128)(2,1)S(1)}, u32[]{:S(2)}, u32[]{:S(2)}) collective-permute-start(bf16[128,1536]{1,0:T(8,128)(2,1)} %finish.3.refs_0_), channel_id=1, source_target_pairs={{0,1},{1,0},{2,3},{3,2},{4,5},{5,4},{6,7},{7,6},{8,9},{9,8},{10,11... | collective-permute-start | bytes 1179656 | tf_op jit(solution)/shard_map/ppermute | solution.py:409
  157.9 35.4 %collective-permute-start.19 = (bf16[128,1536]{1,0:T(8,128)(2,1)}, bf16[128,1536]{1,0:T(8,128)(2,1)S(1)}, u32[]{:S(2)}, u32[]{:S(2)}) collective-permute-start(bf16[128,1536]{1,0:T(8,128)(2,1)} %finish.3.refs_0_), channel_id=1, source_target_pairs={{0,6},{1,7},{2,0},{3,1},{4,2},{5,3},{6,4},{7,5},{8,14},{9,15},{10,... | collective-permute-start | bytes 1179656 | tf_op jit(solution)/shard_map/ppermute | solution.py:409
  163.6 29.8 %collective-permute-start.20 = (bf16[128,1536]{1,0:T(8,128)(2,1)}, bf16[128,1536]{1,0:T(8,128)(2,1)S(1)}, u32[]{:S(2)}, u32[]{:S(2)}) collective-permute-start(bf16[128,1536]{1,0:T(8,128)(2,1)} %finish.3.refs_0_), channel_id=1, source_target_pairs={{0,2},{1,3},{2,4},{3,5},{4,6},{5,7},{6,0},{7,1},{8,10},{9,11},{10,... | collective-permute-start | bytes 1179656 | tf_op jit(solution)/shard_map/ppermute | solution.py:409
  191.3 5.2 %collective-permute-start.21 = (bf16[96,768]{1,0:T(8,128)(2,1)S(1)}, bf16[96,768]{1,0:T(8,128)(2,1)S(1)}, u32[]{:S(2)}, u32[]{:S(2)}) collective-permute-start(bf16[96,768]{1,0:T(8,128)(2,1)S(1)} %fusion.5), channel_id=1, source_target_pairs={{0,64},{32,96},{64,0},{96,32},{1,65},{33,97},{65,1},{97,33},{2,66}... | collective-permute-start | bytes 442376 | tf_op jit(solution)/shard_map/ppermute | solution.py:442
  (16 other events, 63.4 us)
Sparse Core Ops, SparseCore 0:
  9.7 26.7 all-gather.6
  38.1 25.0 all-gather.4
  65.9 39.3 all-gather.8
  107.4 37.4 all-gather.10

commit v14 on v13

--- a/solution.py
+++ b/solution.py
@@ -10,7 +10,7 @@
 EPS = 1e-05
 NEG = -1e30
 
-SHIFTS = ((2, 1), (2, 0), (3, 1), (1, 1), (0, 1), (3, 0), (1, 0))
+SHIFTS = ((2, 1), (3, 1), (1, 1), (0, 1))
 
 F32 = jnp.float32
 BF16 = jnp.bfloat16
@@ -346,6 +346,8 @@
     out[:chunk, :] = grad.astype(BF16)
     if len(refs) > 1:
         out[chunk:, :] = refs[0][...]
+        copies = refs[1]
+        copies[...] = jnp.broadcast_to(out[...][None], copies.shape)
 
 
 def finish(place, tokens, cotangent, gain, parts, *later):
@@ -365,40 +367,47 @@
                 pl.BlockSpec((count, chunk, model), lambda i, p: (0, 0, 0)),
             ]
             + [whole(chunk)] * len(later),
-            out_specs=whole(rows),
+            out_specs=[pl.BlockSpec((4, rows, model), lambda i, p: (0, 0, 0))] * len(later)
+            + [whole(rows)],
         ),
-        out_shape=jax.ShapeDtypeStruct((rows, model), BF16),
+        out_shape=[jax.ShapeDtypeStruct((4, rows, model), BF16)] * len(later)
+        + [jax.ShapeDtypeStruct((rows, model), BF16)],
         compiler_params=params(),
         cost_estimate=pl.CostEstimate(flops=10000000, bytes_accessed=3000000, transcendentals=0),
         name="finish",
     )(place, gain, tokens, cotangent, parts, *later)
 
 
-def assemble_body(places, *refs):
+def assemble_body(places, near, *refs):
     pieces, out = refs[:-1], refs[-1]
-    chunk = pieces[0].shape[0] // 2
+    chunk = near.shape[1] // 2
     half = out.shape[0] // 2
-    for index, piece in enumerate(pieces):
+    blocks = [near.at[z] for z in range(near.shape[0])] + list(pieces)
+    for index, block in enumerate(blocks):
         for rec in range(2):
             place = pl.multiple_of(rec * half + places[index] * chunk, chunk)
-            out[pl.ds(place, chunk), :] = piece[rec * chunk : (rec + 1) * chunk, :]
-
-
-def assemble(places, pieces):
-    chunk, model = pieces[0].shape
-    count = len(pieces)
+            out[pl.ds(place, chunk), :] = block[rec * chunk : (rec + 1) * chunk, :]
+
+
+def assemble(places, near, pieces):
+    depth, chunk, model = near.shape
+    rows = 2 * depth * chunk
     tile = 512
     by_col = lambda n: pl.BlockSpec((n, tile), lambda i: (0, i))
     return pl.pallas_call(
         assemble_body,
         grid=(model // tile,),
-        in_specs=[pl.BlockSpec(memory_space=pltpu.SMEM)] + [by_col(chunk)] * count,
-        out_specs=by_col(count * chunk),
-        out_shape=jax.ShapeDtypeStruct((count * chunk, model), BF16),
+        in_specs=[
+            pl.BlockSpec(memory_space=pltpu.SMEM),
+            pl.BlockSpec((depth, chunk, tile), lambda i: (0, 0, i)),
+        ]
+        + [by_col(chunk)] * len(pieces),
+        out_specs=by_col(rows),
+        out_shape=jax.ShapeDtypeStruct((rows, model), BF16),
         compiler_params=params(16),
         cost_estimate=pl.CostEstimate(flops=0, bytes_accessed=6000000, transcendentals=0),
         name="assemble",
-    )(places, *pieces)
+    )(places, near, *pieces)
 
 
 def to_peer(array, shift):
@@ -516,18 +525,21 @@
         scalar(rec * count + me), flat_tokens, flat_cot, norm_gain, *refs
     )
     second_parts, first_back = tie((second_parts, first_back))
-    piece = ending(1, second_parts)
+    (piece,) = ending(1, second_parts)
     sums = frame_sums(kept.astype(F32) + core_swap(sent).astype(F32))
     sums, first_parts = tie((sums, first_parts))
-    piece = ending(0, first_parts, piece)
+    copies, piece = ending(0, first_parts, piece)
+    rings = [[0, 2, 4, 6], [1, 3, 5, 7]]
+    near = lax.all_to_all(copies, "chan", 0, 0, axis_index_groups=rings, tiled=True)
     pieces = [to_peer(piece, shift) for shift in SHIFTS]
     own = [near_out, far_out]
     output = output_rows(
         flat_tokens, near_mixed, far_mixed, own + [core_swap(array) for array in own]
     )
     pieces[0], output = tie((pieces[0], output))
-    places = jnp.stack([me] + [peer_index(me, shift, -1) for shift in SHIFTS]).astype(jnp.int32)
-    grad_tokens = assemble(places, [piece] + pieces)
+    places = [2 * z + (me & 1) for z in range(4)]
+    places = jnp.stack(places + [peer_index(me, shift, -1) for shift in SHIFTS])
+    grad_tokens = assemble(places.astype(jnp.int32), near, pieces)
     sums, output = tie((sums, output))
     own_sums, got_sums = row_sums(sums)
     grad_proj = (own_sums + got_sums.astype(F32)).reshape(-1, 4, width)

time: 206 us -> 201 us (0.976)
  starting transfers between devices: 71.1 us -> 53.9 us
  waiting for transfers between devices: 38.2 us -> 48 us
    ppermute x9 -> x6, starting transfers between devices: 32.2 us -> 12.8 us  [to_peer(): return lax.ppermute(array, 'chan', pairs)]
    ppermute x9 -> x6, waiting for transfers between devices: 14.7 us -> 19.3 us  [to_peer(): return lax.ppermute(array, 'chan', pairs)]
    ppermute x1, waiting for transfers between devices: 0.34 us -> 4.48 us  [row_sums(): got = lax.ppermute(sent, 'batch', [(0, 2), (1, 3), (2, 0), (3, 1)])]
    all_to_all x0 -> x1, starting transfers between devices: none -> 3.69 us  [shards(): lax.all_to_all(copies, 'chan', 0, 0, axis_index_groups=rings, tiled=True)]
    unnamed x40 -> x38, local copies, waits for them, and re-layouts: 5.08 us -> 5.48 us
  transfers between devices with their start and end apart: 28 -> 26, of which waited for: 10 -> 11; matrix products, arithmetic and copies ran while one was open for 3% -> 4% of each run, Pallas kernels for 33% -> 33%
where the time goes in v14:
time: 201 us; the launch traced here: 199 us
  Pallas kernels  67.5 us (34%)
  starting transfers between devices  53.9 us (27%)
  waiting for transfers between devices  48 us (24%)
  between operations  14.1 us (7%)
  local copies, waits for them, and re-layouts  10.5 us (5%)
  other arithmetic  4.69 us (2%)
    ppermute x6, waiting for transfers between devices, to_peer(): return lax.ppermute(array, 'chan', pairs)  19.3 us
    pallas_call x2, Pallas kernels, attention(): pl.pallas_call(attention_body, grid=(1,), in_specs=[by_rec(width, frames)...  18.3 us
    all_to_all x2, starting transfers between devices, to_all(): return lax.all_to_all(array, 'chan', 0, 0, tiled=True)  14.4 us
    ppermute x6, starting transfers between devices, to_peer(): return lax.ppermute(array, 'chan', pairs)  12.8 us
    pallas_call x1, Pallas kernels, output_rows(): pl.pallas_call(output_body, grid=(rows // block,), in_specs=[by_row, by_c...  11.6 us
    pallas_call x2, Pallas kernels, back_rows(): pl.pallas_call(back_body, grid=(model // tile,), in_specs=[full(width, ro...  10.7 us
    ppermute x3, waiting for transfers between devices, frame_sums(): got = lax.ppermute(sent, 'frames', [(i, (i + shift) % 4) for i in range(4)])  9.81 us
    pallas_call x1, Pallas kernels, weight_grads(): pl.pallas_call(weight_grads_body, grid_spec=pltpu.PrefetchScalarGridSpec(...  9.01 us
  transfers between devices with their start and end apart: 26, of which 11 were waited for; matrix products, arithmetic and copies ran while one was open for 4% of the time, Pallas kernels for 33%

profile of v14, /device:TPU:18, one launch (start us, length us, event | category | flops | bytes accessed | tf_op | source)
XLA Modules:
  0.0 198.7 jit_solution(1855025465383488890)
XLA Ops:
  9.0 8.7 %project.1 = (bf16[1024,1536]{1,0:T(8,128)(2,1)}, bf16[192,1024]{1,0:T(8,128)(2,1)}, bf16[384,1024]{1,0:T(8,128)(2,1)}, bf16[192,1024]{1,0:T(8,128)(2,1)}, bf16[...) custom-call(s32[2]{0:T(128)} %lengths.1, bf16[1024,1536]{1,0:T(8,128)(2,1)} %bitcast.40, ...), custom_call_target="tpu_custom_call" | custom-call | flops 2400000000 | bytes 15000000 | tf_op jit(solution)/shard_map/project/pallas_call | solution.py:70
  17.8 2.4 %collective-permute-start.1 = (bf16[384,512]{1,0:T(8,128)(2,1)}, bf16[384,512]{1,0:T(8,128)(2,1)S(1)}, u32[]{:S(2)}, u32[]{:S(2)}) collective-permute-start(bf16[384,512]{1,0:T(8,128)(2,1)} %get-tuple-element.53), channel_id=1, source_target_pairs={{8,0},{16,8},{24,16},{9,1},{17,9},{25,17},{10,2},{18,10},{26,18},{... | collective-permute-start | bytes 1179656 | tf_op jit(solution)/shard_map/ppermute | solution.py:492
  20.2 3.4 %collective-permute-start = (bf16[384,512]{1,0:T(8,128)(2,1)}, bf16[384,512]{1,0:T(8,128)(2,1)S(1)}, u32[]{:S(2)}, u32[]{:S(2)}) collective-permute-start(bf16[384,512]{1,0:T(8,128)(2,1)} %get-tuple-element.51), channel_id=1, source_target_pairs={{0,8},{8,16},{16,24},{1,9},{9,17},{17,25},{2,10},{10,18},{18,26},{... | collective-permute-start | bytes 1179656 | tf_op jit(solution)/shard_map/ppermute | solution.py:491
  24.0 9.4 %collective-permute-done.2 = bf16[96,1536]{1,0:T(8,128)(2,1)S(1)} collective-permute-done((bf16[96,1536]{1,0:T(8,128)(2,1)S(1)}, bf16[96,1536]{1,0:T(8,128)(2,1)S(1)}, u32[]{:S(2)}, u32[]{:S(2)}) %collective-permute-start.2) | collective-permute-done | bytes 294944 | tf_op jit(solution)/shard_map/ppermute | solution.py:418
  35.5 9.1 %attention.2 = (bf16[192,512]{1,0:T(8,128)(2,1)}, bf16[192,512]{1,0:T(8,128)(2,1)}, f32[384,512]{1,0:T(8,128)}, bf16[384,256]{1,0:T(8,128)(2,1)}, bf16[384,256]{1,0:T(8,128)(2,1)}) custom-call(bf16[192,1024]{1,0:T(8,128)(2,1)} %get-tuple-element.49.q, bf16[384,1024]{1,0:T(8,128)(2,1)} %get-tuple-element.50.kv, bf16[384,512]{1,0:T(8,128)(2,1)} %copy-done.4, ...), custom_call_target="tpu_custom_call" | custom-call | flops 1000 | bytes 1000 | tf_op jit(solution)/shard_map/attention/pallas_call | solution.py:158
  44.6 3.4 %collective-permute-start.3 = (bf16[384,256]{1,0:T(8,128)(2,1)}, bf16[384,256]{1,0:T(8,128)(2,1)S(1)}, u32[]{:S(2)}, u32[]{:S(2)}) collective-permute-start(bf16[384,256]{1,0:T(8,128)(2,1)} %get-tuple-element.65), channel_id=1, source_target_pairs={{0,8},{8,16},{16,24},{1,9},{9,17},{17,25},{2,10},{10,18},{18,26},{... | collective-permute-start | bytes 589832 | tf_op jit(solution)/shard_map/ppermute | solution.py:502
  48.0 2.6 %collective-permute-start.4 = (bf16[384,256]{1,0:T(8,128)(2,1)}, bf16[384,256]{1,0:T(8,128)(2,1)S(1)}, u32[]{:S(2)}, u32[]{:S(2)}) collective-permute-start(bf16[384,256]{1,0:T(8,128)(2,1)} %get-tuple-element.66), channel_id=1, source_target_pairs={{8,0},{16,8},{24,16},{9,1},{17,9},{25,17},{10,2},{18,10},{26,18},{... | collective-permute-start | bytes 589832 | tf_op jit(solution)/shard_map/ppermute | solution.py:501
  50.7 9.2 %attention.3 = (bf16[192,1024]{1,0:T(8,128)(2,1)}, bf16[192,512]{1,0:T(8,128)(2,1)}, f32[384,512]{1,0:T(8,128)}, bf16[384,256]{1,0:T(8,128)(2,1)}, bf16[384,256]{1,0:T(8,128)(2,1)}) custom-call(bf16[192,1024]{1,0:T(8,128)(2,1)} %get-tuple-element.49.q, bf16[384,1024]{1,0:T(8,128)(2,1)} %get-tuple-element.50.kv, bf16[384,512]{1,0:T(8,128)(2,1)} %copy-done.4, ...), custom_call_target="tpu_custom_call" | custom-call | flops 1000 | bytes 1000 | tf_op jit(solution)/shard_map/attention/pallas_call | solution.py:158
  60.6 5.1 %back.2 = bf16[512,1536]{1,0:T(8,128)(2,1)} custom-call(bf16[192,512]{1,0:T(8,128)(2,1)} %get-tuple-element.63.dq.rest_4_, f32[384,512]{1,0:T(8,128)} %get-tuple-element.64.own.rest_5_, bf16[384,256]{1,0:T(8,128)(2,1)} %copy-done.10, bf16[384,256]{1,0:T(8,128)(2,1)} %copy-done.11, bf16[576,1536]{1,0:T(8,128)(2,1)} %bitcast.45), custom_call_target="tpu_custom_call" | custom-call | flops 900000000 | bytes 4000000 | tf_op jit(solution)/shard_map/back/pallas_call | solution.py:215
  65.8 8.4 %all-to-all-start = ((bf16[8,64,1536]{2,1,0:T(8,128)(2,1)}), bf16[8,64,1536]{2,1,0:T(8,128)(2,1)S(1)}, u32[]{:S(2)}, u32[]{:S(2)}) async-start(bf16[8,64,1536]{2,1,0:T(8,128)(2,1)} %bitcast.48), calls=%async_computation | async-start | bytes 3145728 | tf_op jit(solution)/shard_map/all_to_all | solution.py:427
  74.3 3.4 %collective-permute-start.5 = (bf16[384,256]{1,0:T(8,128)(2,1)S(1)}, bf16[384,256]{1,0:T(8,128)(2,1)S(1)}, u32[]{:S(2)}, u32[]{:S(2)}) collective-permute-start(bf16[384,256]{1,0:T(8,128)(2,1)S(1)} %copy-done.18), channel_id=1, source_target_pairs={{0,8},{8,16},{16,24},{1,9},{9,17},{17,25},{2,10},{10,18},{18,26},{... | collective-permute-start | bytes 589832 | tf_op jit(solution)/shard_map/ppermute | solution.py:502
  77.7 2.4 %collective-permute-start.6 = (bf16[384,256]{1,0:T(8,128)(2,1)S(1)}, bf16[384,256]{1,0:T(8,128)(2,1)S(1)}, u32[]{:S(2)}, u32[]{:S(2)}) collective-permute-start(bf16[384,256]{1,0:T(8,128)(2,1)S(1)} %copy-done.17), channel_id=1, source_target_pairs={{8,0},{16,8},{24,16},{9,1},{17,9},{25,17},{10,2},{18,10},{26,18},{... | collective-permute-start | bytes 589832 | tf_op jit(solution)/shard_map/ppermute | solution.py:501
  81.8 3.4 %collective-permute-done.6.rest_3_.right = bf16[384,256]{1,0:T(8,128)(2,1)S(1)} collective-permute-done((bf16[384,256]{1,0:T(8,128)(2,1)S(1)}, bf16[384,256]{1,0:T(8,128)(2,1)S(1)}, u32[]{:S(2)}, u32[]{:S(2)}) %collective-permute-start.6) | collective-permute-done | bytes 196640 | tf_op jit(solution)/shard_map/ppermute | solution.py:501
  86.0 9.0 %weight_grads.1 = (bf16[4,2,96,768]{3,2,1,0:T(8,128)(2,1)}, bf16[4,2,96,768]{3,2,1,0:T(8,128)(2,1)}) custom-call(s32[1]{0:T(128)} %bitcast.core, bf16[1024,1536]{1,0:T(8,128)(2,1)} %get-tuple-element.48.normed, bf16[1024,1536]{1,0:T(8,128)(2,1)} %bitcast.37, bf16[192,512]{1,0:T(8,128)(2,1)} %get-tuple-element.78.rest_0_.dq, ...), custom_call_target="tpu_custom_call" | custom-call | flops 10000000000 | bytes 12000000 | tf_op jit(solution)/shard_map/weight_grads/pallas_call | solution.py:274
  95.0 4.5 %all-to-all-done.parts = bf16[8,64,1536]{2,1,0:T(8,128)(2,1)S(1)} async-done(((bf16[8,64,1536]{2,1,0:T(8,128)(2,1)}), bf16[8,64,1536]{2,1,0:T(8,128)(2,1)S(1)}, u32[]{:S(2)}, u32[]{:S(2)}) %all-to-all-start) | async-done | bytes 1572896 | tf_op jit(solution)/shard_map/all_to_all | solution.py:427
  99.4 5.7 %back.3 = bf16[512,1536]{1,0:T(8,128)(2,1)} custom-call(bf16[192,512]{1,0:T(8,128)(2,1)} %get-tuple-element.78.rest_0_.dq, f32[384,512]{1,0:T(8,128)} %get-tuple-element.70.rest_1_.own, bf16[384,256]{1,0:T(8,128)(2,1)} %copy-done.12, bf16[384,256]{1,0:T(8,128)(2,1)} %copy-done.13, bf16[576,1536]{1,0:T(8,128)(2,1)} %bitcast.46), custom_call_target="tpu_custom_call" | custom-call | flops 900000000 | bytes 4000000 | tf_op jit(solution)/shard_map/back/pallas_call | solution.py:215
  106.0 5.9 %all-to-all-start.1 = ((bf16[8,64,1536]{2,1,0:T(8,128)(2,1)}), bf16[8,64,1536]{2,1,0:T(8,128)(2,1)S(1)}, u32[]{:S(2)}, u32[]{:S(2)}) async-start(bf16[8,64,1536]{2,1,0:T(8,128)(2,1)} %bitcast.47), calls=%async_computation.1 | async-start | bytes 3145728 | tf_op jit(solution)/shard_map/all_to_all | solution.py:427
  117.1 2.3 %collective-permute-start.9 = (bf16[2,96,768]{2,1,0:T(8,128)(2,1)S(1)}, bf16[2,96,768]{2,1,0:T(8,128)(2,1)S(1)}, u32[]{:S(2)}, u32[]{:S(2)}) collective-permute-start(bf16[2,96,768]{2,1,0:T(8,128)(2,1)S(1)} %get-tuple-element.95), channel_id=1, source_target_pairs={{0,24},{8,0},{16,8},{24,16},{1,25},{9,1},{17,9},{25,17},{2,26},{10... | collective-permute-start | bytes 884744 | tf_op jit(solution)/shard_map/ppermute | solution.py:443
  119.4 2.8 %finish.2.refs_0_ = bf16[64,1536]{1,0:T(8,128)(2,1)} custom-call(s32[1]{0:T(128)} %bitcast.13.place, f32[1536]{0:T(1024)} %gain.5, bf16[1024,1536]{1,0:T(8,128)(2,1)} %bitcast.41, bf16[1024,1536]{1,0:T(8,128)(2,1)} %bitcast.38, bf16[8,64,1536]{2,1,0:T(8,128)(2,1)} %copy-done), custom_call_target="tpu_custom_call" | custom-call | flops 10000000 | bytes 3000000 | tf_op jit(solution)/shard_map/finish/pallas_call | solution.py:358
  122.2 3.2 %collective-permute-done.8 = bf16[2,96,768]{2,1,0:T(8,128)(2,1)S(1)} collective-permute-done((bf16[2,96,768]{2,1,0:T(8,128)(2,1)S(1)}, bf16[2,96,768]{2,1,0:T(8,128)(2,1)S(1)}, u32[]{:S(2)}, u32[]{:S(2)}) %collective-permute-start.8) | collective-permute-done | bytes 294944 | tf_op jit(solution)/shard_map/ppermute | solution.py:443
  125.4 3.0 %collective-permute-done.10 = bf16[2,96,768]{2,1,0:T(8,128)(2,1)S(1)} collective-permute-done((bf16[2,96,768]{2,1,0:T(8,128)(2,1)S(1)}, bf16[2,96,768]{2,1,0:T(8,128)(2,1)S(1)}, u32[]{:S(2)}, u32[]{:S(2)}) %collective-permute-start.10) | collective-permute-done | bytes 294944 | tf_op jit(solution)/shard_map/ppermute | solution.py:443
  128.5 3.5 %collective-permute-done.9 = bf16[2,96,768]{2,1,0:T(8,128)(2,1)S(1)} collective-permute-done((bf16[2,96,768]{2,1,0:T(8,128)(2,1)S(1)}, bf16[2,96,768]{2,1,0:T(8,128)(2,1)S(1)}, u32[]{:S(2)}, u32[]{:S(2)}) %collective-permute-start.9) | collective-permute-done | bytes 294944 | tf_op jit(solution)/shard_map/ppermute | solution.py:443
  132.0 2.0 %fusion.1 = f32[2,96,768]{2,1,0:T(8,128)} fusion(bf16[2,96,768]{2,1,0:T(8,128)(2,1)S(1)} %collective-permute-done.10, bf16[2,96,768]{2,1,0:T(8,128)(2,1)S(1)} %collective-permute-done.9, bf16[2,96,768]{2,1,0:T(8,128)(2,1)S(1)} %collective-permute-done.8, f32[4,2,96,768]{3,2,1,0:T(8,128)} %copy-done.2, s32[]{:T(128)S(6)} %select_n.37), kind=kLoop, calls=%fused_computation.3 | loop fusion | flops 884736 | bytes 2064388 | tf_op jit(solution)/shard_map/add | solution.py:444
  134.0 3.5 %all-to-all-done.1.parts = bf16[8,64,1536]{2,1,0:T(8,128)(2,1)S(1)} async-done(((bf16[8,64,1536]{2,1,0:T(8,128)(2,1)}), bf16[8,64,1536]{2,1,0:T(8,128)(2,1)S(1)}, u32[]{:S(2)}, u32[]{:S(2)}) %all-to-all-start.1) | async-done | bytes 1572896 | tf_op jit(solution)/shard_map/all_to_all | solution.py:427
  138.7 3.5 %finish.3 = (bf16[4,128,1536]{2,1,0:T(8,128)(2,1)}, bf16[128,1536]{1,0:T(8,128)(2,1)}) custom-call(s32[1]{0:T(128)} %bitcast.12.place, f32[1536]{0:T(1024)} %gain.5, bf16[1024,1536]{1,0:T(8,128)(2,1)} %bitcast.42, bf16[1024,1536]{1,0:T(8,128)(2,1)} %bitcast.39, bf16[8,64,1536]{2,1,0:T(8,128)(2,1)} %copy-done.1, bf16[64,1536]{1,0:T(8,128)(2,1)} %finish.2.refs_0_), custom_call_target="tpu_custom_call" | custom-call | flops 10000000 | bytes 3000000 | tf_op jit(solution)/shard_map/finish/pallas_call | solution.py:358
  142.2 5.8 %collective-permute-start.16 = (bf16[128,1536]{1,0:T(8,128)(2,1)}, bf16[128,1536]{1,0:T(8,128)(2,1)S(1)}, u32[]{:S(2)}, u32[]{:S(2)}) collective-permute-start(bf16[128,1536]{1,0:T(8,128)(2,1)} %get-tuple-element.84), channel_id=1, source_target_pairs={{0,3},{1,2},{2,5},{3,4},{4,7},{5,6},{6,1},{7,0},{8,11},{9,10},{10,... | collective-permute-start | bytes 1179656 | tf_op jit(solution)/shard_map/ppermute | solution.py:418
  148.7 3.7 %all-to-all-start.2 = ((bf16[4,128,1536]{2,1,0:T(8,128)(2,1)}), bf16[4,128,1536]{2,1,0:T(8,128)(2,1)S(1)}, u32[]{:S(2)}, u32[]{:S(2)}) async-start(bf16[4,128,1536]{2,1,0:T(8,128)(2,1)} %get-tuple-element.90), calls=%async_computation.2 | async-start | bytes 3145728 | tf_op jit(solution)/shard_map/all_to_all | solution.py:533
  152.5 5.6 %collective-permute-start.12 = (bf16[128,1536]{1,0:T(8,128)(2,1)S(1)}, bf16[128,1536]{1,0:T(8,128)(2,1)S(1)}, u32[]{:S(2)}, u32[]{:S(2)}) collective-permute-start(bf16[128,1536]{1,0:T(8,128)(2,1)S(1)} %copy-done.16), channel_id=1, source_target_pairs={{0,5},{1,4},{2,7},{3,6},{4,1},{5,0},{6,3},{7,2},{8,13},{9,12},{10,... | collective-permute-start | bytes 1179656 | tf_op jit(solution)/shard_map/ppermute | solution.py:418
  158.1 11.6 %output.1 = bf16[1024,1536]{1,0:T(8,128)(2,1)} custom-call(bf16[1024,1536]{1,0:T(8,128)(2,1)} %bitcast.43, bf16[768,1024]{1,0:T(8,128)(2,1)} %all-gather.9.cloned.1.call-done.near, bf16[768,1024]{1,0:T(8,128)(2,1)} %all-gather.11.cloned.1.call-done.far, bf16[384,1536]{1,0:T(8,128)(2,1)} %all-gather.7.cloned.1.call-done.refs_0_, ...), custom_call_target="tpu_custom_call" | custom-call | flops 10000000000 | bytes 12000000 | tf_op jit(solution)/shard_map/output/pallas_call | solution.py:322
  169.7 9.9 %collective-permute-done.12.refs_0_ = bf16[128,1536]{1,0:T(8,128)(2,1)S(1)} collective-permute-done((bf16[128,1536]{1,0:T(8,128)(2,1)S(1)}, bf16[128,1536]{1,0:T(8,128)(2,1)S(1)}, u32[]{:S(2)}, u32[]{:S(2)}) %collective-permute-start.12) | collective-permute-done | bytes 393248 | tf_op jit(solution)/shard_map/ppermute | solution.py:418
  181.5 4.5 %collective-permute-done.18 = bf16[96,768]{1,0:T(8,128)(2,1)} collective-permute-done((bf16[96,768]{1,0:T(8,128)(2,1)S(1)}, bf16[96,768]{1,0:T(8,128)(2,1)}, u32[]{:S(2)}, u32[]{:S(2)}) %collective-permute-start.18) | collective-permute-done | bytes 147488 | tf_op jit(solution)/shard_map/ppermute | solution.py:451
  189.4 2.8 %assemble.1 = bf16[1024,1536]{1,0:T(8,128)(2,1)} custom-call(s32[8]{0:T(128)S(1)} %stack.35.places, bf16[4,128,1536]{2,1,0:T(8,128)(2,1)S(1)} %all-to-all-done.2.near, bf16[128,1536]{1,0:T(8,128)(2,1)S(1)} %collective-permute-done.12.refs_0_, bf16[128,1536]{1,0:T(8,128)(2,1)S(1)} %collective-permute-done.15.refs_1_, ...), custom_call_target="tpu_custom_call" | custom-call | bytes 6000000 | tf_op jit(solution)/shard_map/assemble/pallas_call | solution.py:397
  (85 shorter events, 20.6 us)
Async XLA Ops:
  7.2 58.6 %all-gather.7.cloned.1.call-start = ((), (), s32[]{:S(2)}) async-start(), calls=%async_computation.4 | async-start | bytes 1474560 | tf_op jit(solution)/shard_map/all_gather | solution.py:457
  8.9 56.9 %all-gather.5.cloned.1.call-start = ((), (), s32[]{:S(2)}) async-start(), calls=%async_computation.3 | async-start | bytes 1474560 | tf_op jit(solution)/shard_map/all_gather | solution.py:457
  9.0 14.6 %copy-start.5 = (bf16[96,1536]{1,0:T(8,128)(2,1)S(1)}, bf16[96,1536]{1,0:T(8,128)(2,1)}, u32[]{:S(2)}) copy-start(bf16[96,1536]{1,0:T(8,128)(2,1)} %constant_dynamic-slice_fusion) | copy-start | bytes 884740
  9.0 25.2 %copy-start.14 = (s32[2,2048]{1,0:T(2,128)S(1)}, s32[2,2048]{1,0:T(2,128)}, u32[]{:S(2)}) copy-start(s32[2,2048]{1,0:T(2,128)} %param.15) | copy-start | bytes 49156
  9.0 25.8 %copy-start.15 = (s32[2]{0:T(128)S(1)}, s32[2]{0:T(128)}, u32[]{:S(2)}) copy-start(s32[2]{0:T(128)} %lengths.1) | copy-start | bytes 28
  17.8 15.6 %collective-permute-start.1 = (bf16[384,512]{1,0:T(8,128)(2,1)}, bf16[384,512]{1,0:T(8,128)(2,1)S(1)}, u32[]{:S(2)}, u32[]{:S(2)}) collective-permute-start(bf16[384,512]{1,0:T(8,128)(2,1)} %get-tuple-element.53), channel_id=1, source_target_pairs={{8,0},{16,8},{24,16},{9,1},{17,9},{25,17},{10,2},{18,10},{26,18},{... | collective-permute-start | bytes 1179656 | tf_op jit(solution)/shard_map/ppermute | solution.py:492
  20.2 13.2 %collective-permute-start = (bf16[384,512]{1,0:T(8,128)(2,1)}, bf16[384,512]{1,0:T(8,128)(2,1)S(1)}, u32[]{:S(2)}, u32[]{:S(2)}) collective-permute-start(bf16[384,512]{1,0:T(8,128)(2,1)} %get-tuple-element.51), channel_id=1, source_target_pairs={{0,8},{8,16},{16,24},{1,9},{9,17},{17,25},{2,10},{10,18},{18,26},{... | collective-permute-start | bytes 1179656 | tf_op jit(solution)/shard_map/ppermute | solution.py:491
  23.6 9.8 %collective-permute-start.2 = (bf16[96,1536]{1,0:T(8,128)(2,1)S(1)}, bf16[96,1536]{1,0:T(8,128)(2,1)S(1)}, u32[]{:S(2)}, u32[]{:S(2)}) collective-permute-start(bf16[96,1536]{1,0:T(8,128)(2,1)S(1)} %copy-done.5), channel_id=1, source_target_pairs={{0,1},{1,0},{2,3},{3,2},{4,5},{5,4},{6,7},{7,6},{8,9},{9,8},{10,11... | collective-permute-start | bytes 884744 | tf_op jit(solution)/shard_map/ppermute | solution.py:418
  34.2 123.9 %all-gather.9.cloned.1.call-start = ((), (), s32[]{:S(2)}) async-start(), calls=%async_computation.5 | async-start | bytes 1966080 | tf_op jit(solution)/shard_map/all_gather | solution.py:457
  44.6 15.3 %collective-permute-start.3 = (bf16[384,256]{1,0:T(8,128)(2,1)}, bf16[384,256]{1,0:T(8,128)(2,1)S(1)}, u32[]{:S(2)}, u32[]{:S(2)}) collective-permute-start(bf16[384,256]{1,0:T(8,128)(2,1)} %get-tuple-element.65), channel_id=1, source_target_pairs={{0,8},{8,16},{16,24},{1,9},{9,17},{17,25},{2,10},{10,18},{18,26},{... | collective-permute-start | bytes 589832 | tf_op jit(solution)/shard_map/ppermute | solution.py:502
  48.0 11.9 %collective-permute-start.4 = (bf16[384,256]{1,0:T(8,128)(2,1)}, bf16[384,256]{1,0:T(8,128)(2,1)S(1)}, u32[]{:S(2)}, u32[]{:S(2)}) collective-permute-start(bf16[384,256]{1,0:T(8,128)(2,1)} %get-tuple-element.66), channel_id=1, source_target_pairs={{8,0},{16,8},{24,16},{9,1},{17,9},{25,17},{10,2},{18,10},{26,18},{... | collective-permute-start | bytes 589832 | tf_op jit(solution)/shard_map/ppermute | solution.py:501
  65.8 8.5 %copy-start.18 = (bf16[384,256]{1,0:T(8,128)(2,1)S(1)}, bf16[384,256]{1,0:T(8,128)(2,1)}, u32[]{:S(2)}) copy-start(bf16[384,256]{1,0:T(8,128)(2,1)} %get-tuple-element.71) | copy-start | bytes 589828
  65.8 11.9 %copy-start.17 = (bf16[384,256]{1,0:T(8,128)(2,1)S(1)}, bf16[384,256]{1,0:T(8,128)(2,1)}, u32[]{:S(2)}) copy-start(bf16[384,256]{1,0:T(8,128)(2,1)} %get-tuple-element.72) | copy-start | bytes 589828
  65.8 14.4 %copy-start.7 = (bf16[192,1024]{1,0:T(8,128)(2,1)S(1)}, bf16[192,1024]{1,0:T(8,128)(2,1)}, u32[]{:S(2)}) copy-start(bf16[192,1024]{1,0:T(8,128)(2,1)} %get-tuple-element.73.rest_8_) | copy-start | bytes 1179652
  65.8 33.6 %all-to-all-start = ((bf16[8,64,1536]{2,1,0:T(8,128)(2,1)}), bf16[8,64,1536]{2,1,0:T(8,128)(2,1)S(1)}, u32[]{:S(2)}, u32[]{:S(2)}) async-start(bf16[8,64,1536]{2,1,0:T(8,128)(2,1)} %bitcast.48), calls=%async_computation | async-start | bytes 3145728 | tf_op jit(solution)/shard_map/all_to_all | solution.py:427
  74.3 83.8 %all-gather.11.cloned.1.call-start = ((), (), s32[]{:S(2)}) async-start(), calls=%async_computation.6 | async-start | bytes 1966080 | tf_op jit(solution)/shard_map/all_gather | solution.py:457
  74.3 7.6 %collective-permute-start.5 = (bf16[384,256]{1,0:T(8,128)(2,1)S(1)}, bf16[384,256]{1,0:T(8,128)(2,1)S(1)}, u32[]{:S(2)}, u32[]{:S(2)}) collective-permute-start(bf16[384,256]{1,0:T(8,128)(2,1)S(1)} %copy-done.18), channel_id=1, source_target_pairs={{0,8},{8,16},{16,24},{1,9},{9,17},{17,25},{2,10},{10,18},{18,26},{... | collective-permute-start | bytes 589832 | tf_op jit(solution)/shard_map/ppermute | solution.py:502
  77.7 7.6 %collective-permute-start.6 = (bf16[384,256]{1,0:T(8,128)(2,1)S(1)}, bf16[384,256]{1,0:T(8,128)(2,1)S(1)}, u32[]{:S(2)}, u32[]{:S(2)}) collective-permute-start(bf16[384,256]{1,0:T(8,128)(2,1)S(1)} %copy-done.17), channel_id=1, source_target_pairs={{8,0},{16,8},{24,16},{9,1},{17,9},{25,17},{10,2},{18,10},{26,18},{... | collective-permute-start | bytes 589832 | tf_op jit(solution)/shard_map/ppermute | solution.py:501
  80.2 25.0 %collective-permute-start.11 = (bf16[192,1024]{1,0:T(8,128)(2,1)S(1)}, bf16[192,1024]{1,0:T(8,128)(2,1)S(1)}, u32[]{:S(2)}, u32[]{:S(2)}) collective-permute-start(bf16[192,1024]{1,0:T(8,128)(2,1)S(1)} %copy-done.7), channel_id=1, source_target_pairs={{0,1},{1,0},{2,3},{3,2},{4,5},{5,4},{6,7},{7,6},{8,9},{9,8},{10,11... | collective-permute-start | bytes 1179656 | tf_op jit(solution)/shard_map/ppermute | solution.py:418
  105.9 6.6 %collective-permute-start.7 = (bf16[4,2,96,768]{3,2,1,0:T(8,128)(2,1)}, bf16[4,2,96,768]{3,2,1,0:T(8,128)(2,1)}, u32[]{:S(2)}, u32[]{:S(2)}) collective-permute-start(bf16[4,2,96,768]{3,2,1,0:T(8,128)(2,1)} %get-tuple-element.77), channel_id=1, source_target_pairs={{0,32},{32,0},{64,96},{96,64},{1,33},{33,1},{65,97},{97,65},{2,34}... | collective-permute-start | bytes 3538952 | tf_op jit(solution)/shard_map/ppermute | solution.py:435
  106.0 31.6 %all-to-all-start.1 = ((bf16[8,64,1536]{2,1,0:T(8,128)(2,1)}), bf16[8,64,1536]{2,1,0:T(8,128)(2,1)S(1)}, u32[]{:S(2)}, u32[]{:S(2)}) async-start(bf16[8,64,1536]{2,1,0:T(8,128)(2,1)} %bitcast.47), calls=%async_computation.1 | async-start | bytes 3145728 | tf_op jit(solution)/shard_map/all_to_all | solution.py:427
  111.9 40.5 %collective-permute-start.13 = (bf16[384,1536]{1,0:T(8,128)(2,1)}, bf16[384,1536]{1,0:T(8,128)(2,1)}, u32[]{:S(2)}, u32[]{:S(2)}) collective-permute-start(bf16[384,1536]{1,0:T(8,128)(2,1)} %all-gather.7.cloned.1.call-done.refs_0_), channel_id=1, source_target_pairs={{0,32},{32,0},{64,96},{96,64},{1,33},{33,1},{65,97},{97,65},{2,34}... | collective-permute-start | bytes 3538952 | tf_op jit(solution)/shard_map/ppermute | solution.py:435
  112.0 46.2 %collective-permute-start.14 = (bf16[384,1536]{1,0:T(8,128)(2,1)}, bf16[384,1536]{1,0:T(8,128)(2,1)}, u32[]{:S(2)}, u32[]{:S(2)}) collective-permute-start(bf16[384,1536]{1,0:T(8,128)(2,1)} %all-gather.5.cloned.1.call-done.refs_1_), channel_id=1, source_target_pairs={{0,32},{32,0},{64,96},{96,64},{1,33},{33,1},{65,97},{97,65},{2,34}... | collective-permute-start | bytes 3538952 | tf_op jit(solution)/shard_map/ppermute | solution.py:435
  115.5 9.9 %collective-permute-start.8 = (bf16[2,96,768]{2,1,0:T(8,128)(2,1)S(1)}, bf16[2,96,768]{2,1,0:T(8,128)(2,1)S(1)}, u32[]{:S(2)}, u32[]{:S(2)}) collective-permute-start(bf16[2,96,768]{2,1,0:T(8,128)(2,1)S(1)} %get-tuple-element.93), channel_id=1, source_target_pairs={{0,8},{8,16},{16,24},{24,0},{1,9},{9,17},{17,25},{25,1},{2,10},{10... | collective-permute-start | bytes 884744 | tf_op jit(solution)/shard_map/ppermute | solution.py:443
  117.1 11.4 %collective-permute-start.10 = (bf16[2,96,768]{2,1,0:T(8,128)(2,1)S(1)}, bf16[2,96,768]{2,1,0:T(8,128)(2,1)S(1)}, u32[]{:S(2)}, u32[]{:S(2)}) collective-permute-start(bf16[2,96,768]{2,1,0:T(8,128)(2,1)S(1)} %get-tuple-element.94), channel_id=1, source_target_pairs={{0,16},{8,24},{16,0},{24,8},{1,17},{9,25},{17,1},{25,9},{2,18},{10... | collective-permute-start | bytes 884744 | tf_op jit(solution)/shard_map/ppermute | solution.py:443
  117.1 15.0 %collective-permute-start.9 = (bf16[2,96,768]{2,1,0:T(8,128)(2,1)S(1)}, bf16[2,96,768]{2,1,0:T(8,128)(2,1)S(1)}, u32[]{:S(2)}, u32[]{:S(2)}) collective-permute-start(bf16[2,96,768]{2,1,0:T(8,128)(2,1)S(1)} %get-tuple-element.95), channel_id=1, source_target_pairs={{0,24},{8,0},{16,8},{24,16},{1,25},{9,1},{17,9},{25,17},{2,26},{10... | collective-permute-start | bytes 884744 | tf_op jit(solution)/shard_map/ppermute | solution.py:443
  142.2 45.9 %collective-permute-start.17 = (bf16[128,1536]{1,0:T(8,128)(2,1)}, bf16[128,1536]{1,0:T(8,128)(2,1)S(1)}, u32[]{:S(2)}, u32[]{:S(2)}) collective-permute-start(bf16[128,1536]{1,0:T(8,128)(2,1)} %get-tuple-element.84), channel_id=1, source_target_pairs={{0,1},{1,0},{2,3},{3,2},{4,5},{5,4},{6,7},{7,6},{8,9},{9,8},{10,11... | collective-permute-start | bytes 1179656 | tf_op jit(solution)/shard_map/ppermute | solution.py:418
  142.2 45.9 %collective-permute-start.16 = (bf16[128,1536]{1,0:T(8,128)(2,1)}, bf16[128,1536]{1,0:T(8,128)(2,1)S(1)}, u32[]{:S(2)}, u32[]{:S(2)}) collective-permute-start(bf16[128,1536]{1,0:T(8,128)(2,1)} %get-tuple-element.84), channel_id=1, source_target_pairs={{0,3},{1,2},{2,5},{3,4},{4,7},{5,6},{6,1},{7,0},{8,11},{9,10},{10,... | collective-permute-start | bytes 1179656 | tf_op jit(solution)/shard_map/ppermute | solution.py:418
  147.9 40.2 %collective-permute-start.15 = (bf16[128,1536]{1,0:T(8,128)(2,1)}, bf16[128,1536]{1,0:T(8,128)(2,1)S(1)}, u32[]{:S(2)}, u32[]{:S(2)}) collective-permute-start(bf16[128,1536]{1,0:T(8,128)(2,1)} %get-tuple-element.84), channel_id=1, source_target_pairs={{0,7},{1,6},{2,1},{3,0},{4,3},{5,2},{6,5},{7,4},{8,15},{9,14},{10,... | collective-permute-start | bytes 1179656 | tf_op jit(solution)/shard_map/ppermute | solution.py:418
  148.7 40.7 %all-to-all-start.2 = ((bf16[4,128,1536]{2,1,0:T(8,128)(2,1)}), bf16[4,128,1536]{2,1,0:T(8,128)(2,1)S(1)}, u32[]{:S(2)}, u32[]{:S(2)}) async-start(bf16[4,128,1536]{2,1,0:T(8,128)(2,1)} %get-tuple-element.90), calls=%async_computation.2 | async-start | bytes 3145728 | tf_op jit(solution)/shard_map/all_to_all | solution.py:533
  152.5 27.2 %collective-permute-start.12 = (bf16[128,1536]{1,0:T(8,128)(2,1)S(1)}, bf16[128,1536]{1,0:T(8,128)(2,1)S(1)}, u32[]{:S(2)}, u32[]{:S(2)}) collective-permute-start(bf16[128,1536]{1,0:T(8,128)(2,1)S(1)} %copy-done.16), channel_id=1, source_target_pairs={{0,5},{1,4},{2,7},{3,6},{4,1},{5,0},{6,3},{7,2},{8,13},{9,12},{10,... | collective-permute-start | bytes 1179656 | tf_op jit(solution)/shard_map/ppermute | solution.py:418
  180.7 5.3 %collective-permute-start.18 = (bf16[96,768]{1,0:T(8,128)(2,1)S(1)}, bf16[96,768]{1,0:T(8,128)(2,1)}, u32[]{:S(2)}, u32[]{:S(2)}) collective-permute-start(bf16[96,768]{1,0:T(8,128)(2,1)S(1)} %fusion.5), channel_id=1, source_target_pairs={{0,64},{32,96},{64,0},{96,32},{1,65},{33,97},{65,1},{97,33},{2,66}... | collective-permute-start | bytes 442376 | tf_op jit(solution)/shard_map/ppermute | solution.py:451
  (13 other events, 29.8 us)
Sparse Core Ops, SparseCore 0:
  9.7 26.7 all-gather.6
  38.1 25.0 all-gather.4
  65.9 39.3 all-gather.8
  107.3 37.9 all-gather.10

commit v15 on v14

--- a/solution.py
+++ b/solution.py
@@ -540,8 +540,8 @@
     places = [2 * z + (me & 1) for z in range(4)]
     places = jnp.stack(places + [peer_index(me, shift, -1) for shift in SHIFTS])
     grad_tokens = assemble(places.astype(jnp.int32), near, pieces)
-    sums, output = tie((sums, output))
     own_sums, got_sums = row_sums(sums)
+    got_sums, output = tie((got_sums, output))
     grad_proj = (own_sums + got_sums.astype(F32)).reshape(-1, 4, width)
     shape = (recs, frames, model)
     return (output.reshape(shape), grad_tokens.reshape(shape), grad_proj)

time: 201 us -> 205 us (1.020)
  the two profiles are of different devices: /device:TPU:18 before, /device:TPU:110 now
where the time goes in v15:
time: 205 us; the launch traced here: 204 us
  Pallas kernels  67.7 us (33%)
  starting transfers between devices  63 us (31%)
  waiting for transfers between devices  43.7 us (21%)
  between operations  14.1 us (7%)
  local copies, waits for them, and re-layouts  10.5 us (5%)
  other arithmetic  4.72 us (2%)
    ppermute x1, waiting for transfers between devices, row_sums(): got = lax.ppermute(sent, 'batch', [(0, 2), (1, 3), (2, 0), (3, 1)])  22.4 us
    ppermute x6, starting transfers between devices, to_peer(): return lax.ppermute(array, 'chan', pairs)  19.6 us
    pallas_call x2, Pallas kernels, attention(): pl.pallas_call(attention_body, grid=(1,), in_specs=[by_rec(width, frames)...  18.4 us
    all_to_all x2, starting transfers between devices, to_all(): return lax.all_to_all(array, 'chan', 0, 0, tiled=True)  14.5 us
    pallas_call x1, Pallas kernels, output_rows(): pl.pallas_call(output_body, grid=(rows // block,), in_specs=[by_row, by_c...  11.6 us
    pallas_call x2, Pallas kernels, back_rows(): pl.pallas_call(back_body, grid=(model // tile,), in_specs=[full(width, ro...  10.7 us
    ppermute x2, starting transfers between devices, shards(): right = lax.ppermute(dbefore, 'frames', down)  9.3 us
    ppermute x3, waiting for transfers between devices, frame_sums(): got = lax.ppermute(sent, 'frames', [(i, (i + shift) % 4) for i in range(4)])  9.18 us
  transfers between devices with their start and end apart: 26, of which 7 were waited for; matrix products, arithmetic and copies ran while one was open for 4% of the time, Pallas kernels for 32%

profile of v15, /device:TPU:110, one launch (start us, length us, event | category | flops | bytes accessed | tf_op | source)
XLA Modules:
  0.0 203.7 jit_solution(9376309543590300715)
XLA Ops:
  7.2 1.7 constant_dynamic-slice_fusion
  9.0 8.8 %project.1 = (bf16[1024,1536]{1,0:T(8,128)(2,1)}, bf16[192,1024]{1,0:T(8,128)(2,1)}, bf16[384,1024]{1,0:T(8,128)(2,1)}, bf16[192,1024]{1,0:T(8,128)(2,1)}, bf16[...) custom-call(s32[2]{0:T(128)} %lengths.1, bf16[1024,1536]{1,0:T(8,128)(2,1)} %bitcast.40, ...), custom_call_target="tpu_custom_call" | custom-call | flops 2400000000 | bytes 15000000 | tf_op jit(solution)/shard_map/project/pallas_call | solution.py:70
  17.8 1.3 collective-permute-start
  19.1 4.6 %collective-permute-start.1 = (bf16[384,512]{1,0:T(8,128)(2,1)}, bf16[384,512]{1,0:T(8,128)(2,1)S(1)}, u32[]{:S(2)}, u32[]{:S(2)}) collective-permute-start(bf16[384,512]{1,0:T(8,128)(2,1)} %get-tuple-element.53), channel_id=1, source_target_pairs={{8,0},{16,8},{24,16},{9,1},{17,9},{25,17},{10,2},{18,10},{26,18},{... | collective-permute-start | bytes 1179656 | tf_op jit(solution)/shard_map/ppermute | solution.py:492
  23.7 2.4 %collective-permute-start.2 = (bf16[96,1536]{1,0:T(8,128)(2,1)S(1)}, bf16[96,1536]{1,0:T(8,128)(2,1)S(1)}, u32[]{:S(2)}, u32[]{:S(2)}) collective-permute-start(bf16[96,1536]{1,0:T(8,128)(2,1)S(1)} %copy-done.5), channel_id=1, source_target_pairs={{0,1},{1,0},{2,3},{3,2},{4,5},{5,4},{6,7},{7,6},{8,9},{9,8},{10,11... | collective-permute-start | bytes 884744 | tf_op jit(solution)/shard_map/ppermute | solution.py:418
  26.0 7.4 %collective-permute-done.2 = bf16[96,1536]{1,0:T(8,128)(2,1)S(1)} collective-permute-done((bf16[96,1536]{1,0:T(8,128)(2,1)S(1)}, bf16[96,1536]{1,0:T(8,128)(2,1)S(1)}, u32[]{:S(2)}, u32[]{:S(2)}) %collective-permute-start.2) | collective-permute-done | bytes 294944 | tf_op jit(solution)/shard_map/ppermute | solution.py:418
  35.6 9.1 %attention.2 = (bf16[192,512]{1,0:T(8,128)(2,1)}, bf16[192,512]{1,0:T(8,128)(2,1)}, f32[384,512]{1,0:T(8,128)}, bf16[384,256]{1,0:T(8,128)(2,1)}, bf16[384,256]{1,0:T(8,128)(2,1)}) custom-call(bf16[192,1024]{1,0:T(8,128)(2,1)} %get-tuple-element.49.q, bf16[384,1024]{1,0:T(8,128)(2,1)} %get-tuple-element.50.kv, bf16[384,512]{1,0:T(8,128)(2,1)} %copy-done.3, ...), custom_call_target="tpu_custom_call" | custom-call | flops 1000 | bytes 1000 | tf_op jit(solution)/shard_map/attention/pallas_call | solution.py:158
  46.0 4.7 %collective-permute-start.4 = (bf16[384,256]{1,0:T(8,128)(2,1)}, bf16[384,256]{1,0:T(8,128)(2,1)S(1)}, u32[]{:S(2)}, u32[]{:S(2)}) collective-permute-start(bf16[384,256]{1,0:T(8,128)(2,1)} %get-tuple-element.66), channel_id=1, source_target_pairs={{8,0},{16,8},{24,16},{9,1},{17,9},{25,17},{10,2},{18,10},{26,18},{... | collective-permute-start | bytes 589832 | tf_op jit(solution)/shard_map/ppermute | solution.py:501
  50.7 9.2 %attention.3 = (bf16[192,1024]{1,0:T(8,128)(2,1)}, bf16[192,512]{1,0:T(8,128)(2,1)}, f32[384,512]{1,0:T(8,128)}, bf16[384,256]{1,0:T(8,128)(2,1)}, bf16[384,256]{1,0:T(8,128)(2,1)}) custom-call(bf16[192,1024]{1,0:T(8,128)(2,1)} %get-tuple-element.49.q, bf16[384,1024]{1,0:T(8,128)(2,1)} %get-tuple-element.50.kv, bf16[384,512]{1,0:T(8,128)(2,1)} %copy-done.3, ...), custom_call_target="tpu_custom_call" | custom-call | flops 1000 | bytes 1000 | tf_op jit(solution)/shard_map/attention/pallas_call | solution.py:158
  60.7 5.1 %back.2 = bf16[512,1536]{1,0:T(8,128)(2,1)} custom-call(bf16[192,512]{1,0:T(8,128)(2,1)} %get-tuple-element.63.dq.rest_4_, f32[384,512]{1,0:T(8,128)} %get-tuple-element.64.own.rest_5_, bf16[384,256]{1,0:T(8,128)(2,1)} %copy-done.10, bf16[384,256]{1,0:T(8,128)(2,1)} %copy-done.11, bf16[576,1536]{1,0:T(8,128)(2,1)} %bitcast.45), custom_call_target="tpu_custom_call" | custom-call | flops 900000000 | bytes 4000000 | tf_op jit(solution)/shard_map/back/pallas_call | solution.py:215
  65.9 6.4 %all-to-all-start = ((bf16[8,64,1536]{2,1,0:T(8,128)(2,1)}), bf16[8,64,1536]{2,1,0:T(8,128)(2,1)S(1)}, u32[]{:S(2)}, u32[]{:S(2)}) async-start(bf16[8,64,1536]{2,1,0:T(8,128)(2,1)} %bitcast.48), calls=%async_computation | async-start | bytes 3145728 | tf_op jit(solution)/shard_map/all_to_all | solution.py:427
  73.6 4.6 %collective-permute-start.6 = (bf16[384,256]{1,0:T(8,128)(2,1)S(1)}, bf16[384,256]{1,0:T(8,128)(2,1)S(1)}, u32[]{:S(2)}, u32[]{:S(2)}) collective-permute-start(bf16[384,256]{1,0:T(8,128)(2,1)S(1)} %copy-done.16), channel_id=1, source_target_pairs={{8,0},{16,8},{24,16},{9,1},{17,9},{25,17},{10,2},{18,10},{26,18},{... | collective-permute-start | bytes 589832 | tf_op jit(solution)/shard_map/ppermute | solution.py:501
  78.2 3.0 %collective-permute-start.11 = (bf16[192,1024]{1,0:T(8,128)(2,1)S(1)}, bf16[192,1024]{1,0:T(8,128)(2,1)S(1)}, u32[]{:S(2)}, u32[]{:S(2)}) collective-permute-start(bf16[192,1024]{1,0:T(8,128)(2,1)S(1)} %copy-done.7), channel_id=1, source_target_pairs={{0,1},{1,0},{2,3},{3,2},{4,5},{5,4},{6,7},{7,6},{8,9},{9,8},{10,11... | collective-permute-start | bytes 1179656 | tf_op jit(solution)/shard_map/ppermute | solution.py:418
  82.0 9.0 %weight_grads.1 = (bf16[4,2,96,768]{3,2,1,0:T(8,128)(2,1)}, bf16[4,2,96,768]{3,2,1,0:T(8,128)(2,1)}) custom-call(s32[1]{0:T(128)} %bitcast.core, bf16[1024,1536]{1,0:T(8,128)(2,1)} %get-tuple-element.48.normed, bf16[1024,1536]{1,0:T(8,128)(2,1)} %bitcast.37, bf16[192,512]{1,0:T(8,128)(2,1)} %get-tuple-element.78.rest_0_.dq, ...), custom_call_target="tpu_custom_call" | custom-call | flops 10000000000 | bytes 12000000 | tf_op jit(solution)/shard_map/weight_grads/pallas_call | solution.py:274
  91.0 4.3 %all-to-all-done.parts = bf16[8,64,1536]{2,1,0:T(8,128)(2,1)S(1)} async-done(((bf16[8,64,1536]{2,1,0:T(8,128)(2,1)}), bf16[8,64,1536]{2,1,0:T(8,128)(2,1)S(1)}, u32[]{:S(2)}, u32[]{:S(2)}) %all-to-all-start) | async-done | bytes 1572896 | tf_op jit(solution)/shard_map/all_to_all | solution.py:427
  95.4 5.7 %back.3 = bf16[512,1536]{1,0:T(8,128)(2,1)} custom-call(bf16[192,512]{1,0:T(8,128)(2,1)} %get-tuple-element.78.rest_0_.dq, f32[384,512]{1,0:T(8,128)} %get-tuple-element.70.rest_1_.own, bf16[384,256]{1,0:T(8,128)(2,1)} %copy-done.12, bf16[384,256]{1,0:T(8,128)(2,1)} %copy-done.13, bf16[576,1536]{1,0:T(8,128)(2,1)} %bitcast.46), custom_call_target="tpu_custom_call" | custom-call | flops 900000000 | bytes 4000000 | tf_op jit(solution)/shard_map/back/pallas_call | solution.py:215
  101.9 8.1 %all-to-all-start.1 = ((bf16[8,64,1536]{2,1,0:T(8,128)(2,1)}), bf16[8,64,1536]{2,1,0:T(8,128)(2,1)S(1)}, u32[]{:S(2)}, u32[]{:S(2)}) async-start(bf16[8,64,1536]{2,1,0:T(8,128)(2,1)} %bitcast.47), calls=%async_computation.1 | async-start | bytes 3145728 | tf_op jit(solution)/shard_map/all_to_all | solution.py:427
  110.5 1.5 convert_add_fusion
  112.1 1.4 copy-done.2
  113.6 1.5 collective-permute-start.10
  115.0 3.2 %collective-permute-start.8 = (bf16[2,96,768]{2,1,0:T(8,128)(2,1)S(1)}, bf16[2,96,768]{2,1,0:T(8,128)(2,1)S(1)}, u32[]{:S(2)}, u32[]{:S(2)}) collective-permute-start(bf16[2,96,768]{2,1,0:T(8,128)(2,1)S(1)} %get-tuple-element.93), channel_id=1, source_target_pairs={{0,8},{8,16},{16,24},{24,0},{1,9},{9,17},{17,25},{25,1},{2,10},{10... | collective-permute-start | bytes 884744 | tf_op jit(solution)/shard_map/ppermute | solution.py:443
  118.3 2.9 %finish.2.refs_0_ = bf16[64,1536]{1,0:T(8,128)(2,1)} custom-call(s32[1]{0:T(128)} %bitcast.14.place, f32[1536]{0:T(1024)} %gain.5, bf16[1024,1536]{1,0:T(8,128)(2,1)} %bitcast.41, bf16[1024,1536]{1,0:T(8,128)(2,1)} %bitcast.38, bf16[8,64,1536]{2,1,0:T(8,128)(2,1)} %copy-done), custom_call_target="tpu_custom_call" | custom-call | flops 10000000 | bytes 3000000 | tf_op jit(solution)/shard_map/finish/pallas_call | solution.py:358
  121.2 3.9 %collective-permute-done.10 = bf16[2,96,768]{2,1,0:T(8,128)(2,1)S(1)} collective-permute-done((bf16[2,96,768]{2,1,0:T(8,128)(2,1)S(1)}, bf16[2,96,768]{2,1,0:T(8,128)(2,1)S(1)}, u32[]{:S(2)}, u32[]{:S(2)}) %collective-permute-start.10) | collective-permute-done | bytes 294944 | tf_op jit(solution)/shard_map/ppermute | solution.py:443
  125.1 5.3 %collective-permute-done.9 = bf16[2,96,768]{2,1,0:T(8,128)(2,1)S(1)} collective-permute-done((bf16[2,96,768]{2,1,0:T(8,128)(2,1)S(1)}, bf16[2,96,768]{2,1,0:T(8,128)(2,1)S(1)}, u32[]{:S(2)}, u32[]{:S(2)}) %collective-permute-start.9) | collective-permute-done | bytes 294944 | tf_op jit(solution)/shard_map/ppermute | solution.py:443
  130.4 2.1 %fusion.1 = f32[2,96,768]{2,1,0:T(8,128)} fusion(bf16[2,96,768]{2,1,0:T(8,128)(2,1)S(1)} %collective-permute-done.10, bf16[2,96,768]{2,1,0:T(8,128)(2,1)S(1)} %collective-permute-done.9, bf16[2,96,768]{2,1,0:T(8,128)(2,1)S(1)} %collective-permute-done.8, f32[4,2,96,768]{3,2,1,0:T(8,128)} %copy-done.2, s32[]{:T(128)S(6)} %select_n.37), kind=kLoop, calls=%fused_computation.3 | loop fusion | flops 884736 | bytes 2064388 | tf_op jit(solution)/shard_map/add | solution.py:444
  133.7 3.5 %finish.3 = (bf16[4,128,1536]{2,1,0:T(8,128)(2,1)}, bf16[128,1536]{1,0:T(8,128)(2,1)}) custom-call(s32[1]{0:T(128)} %bitcast.13.place, f32[1536]{0:T(1024)} %gain.5, bf16[1024,1536]{1,0:T(8,128)(2,1)} %bitcast.42, bf16[1024,1536]{1,0:T(8,128)(2,1)} %bitcast.39, bf16[8,64,1536]{2,1,0:T(8,128)(2,1)} %copy-done.1, bf16[64,1536]{1,0:T(8,128)(2,1)} %finish.2.refs_0_), custom_call_target="tpu_custom_call" | custom-call | flops 10000000 | bytes 3000000 | tf_op jit(solution)/shard_map/finish/pallas_call | solution.py:358
  137.3 8.5 %collective-permute-start.13 = (bf16[128,1536]{1,0:T(8,128)(2,1)}, bf16[128,1536]{1,0:T(8,128)(2,1)S(1)}, u32[]{:S(2)}, u32[]{:S(2)}) collective-permute-start(bf16[128,1536]{1,0:T(8,128)(2,1)} %get-tuple-element.84), channel_id=1, source_target_pairs={{0,5},{1,4},{2,7},{3,6},{4,1},{5,0},{6,3},{7,2},{8,13},{9,12},{10,... | collective-permute-start | bytes 1179656 | tf_op jit(solution)/shard_map/ppermute | solution.py:418
  145.8 5.6 %collective-permute-start.17 = (bf16[128,1536]{1,0:T(8,128)(2,1)}, bf16[128,1536]{1,0:T(8,128)(2,1)S(1)}, u32[]{:S(2)}, u32[]{:S(2)}) collective-permute-start(bf16[128,1536]{1,0:T(8,128)(2,1)} %get-tuple-element.84), channel_id=1, source_target_pairs={{0,3},{1,2},{2,5},{3,4},{4,7},{5,6},{6,1},{7,0},{8,11},{9,10},{10,... | collective-permute-start | bytes 1179656 | tf_op jit(solution)/shard_map/ppermute | solution.py:418
  151.4 4.5 %all-to-all-start.2 = ((bf16[4,128,1536]{2,1,0:T(8,128)(2,1)}), bf16[4,128,1536]{2,1,0:T(8,128)(2,1)S(1)}, u32[]{:S(2)}, u32[]{:S(2)}) async-start(bf16[4,128,1536]{2,1,0:T(8,128)(2,1)} %get-tuple-element.90), calls=%async_computation.2 | async-start | bytes 3145728 | tf_op jit(solution)/shard_map/all_to_all | solution.py:533
  158.2 11.6 %output.1 = bf16[1024,1536]{1,0:T(8,128)(2,1)} custom-call(bf16[1024,1536]{1,0:T(8,128)(2,1)} %bitcast.43, bf16[768,1024]{1,0:T(8,128)(2,1)} %all-gather.9.cloned.1.call-done.near, bf16[768,1024]{1,0:T(8,128)(2,1)} %all-gather.11.cloned.1.call-done.far, bf16[384,1536]{1,0:T(8,128)(2,1)} %all-gather.7.cloned.1.call-done.refs_0_, ...), custom_call_target="tpu_custom_call" | custom-call | flops 10000000000 | bytes 12000000 | tf_op jit(solution)/shard_map/output/pallas_call | solution.py:322
  169.9 22.4 %collective-permute-done.12 = bf16[96,768]{1,0:T(8,128)(2,1)} collective-permute-done((bf16[96,768]{1,0:T(8,128)(2,1)S(1)}, bf16[96,768]{1,0:T(8,128)(2,1)}, u32[]{:S(2)}, u32[]{:S(2)}) %collective-permute-start.12) | collective-permute-done | bytes 147488 | tf_op jit(solution)/shard_map/ppermute | solution.py:451
  194.4 2.8 %assemble.1 = bf16[1024,1536]{1,0:T(8,128)(2,1)} custom-call(s32[8]{0:T(128)S(1)} %stack.35.places, bf16[4,128,1536]{2,1,0:T(8,128)(2,1)S(1)} %all-to-all-done.2.near, bf16[128,1536]{1,0:T(8,128)(2,1)S(1)} %collective-permute-done.13.refs_0_, bf16[128,1536]{1,0:T(8,128)(2,1)S(1)} %collective-permute-done.16.refs_1_, ...), custom_call_target="tpu_custom_call" | custom-call | bytes 6000000 | tf_op jit(solution)/shard_map/assemble/pallas_call | solution.py:397
  (83 shorter events, 13.6 us)
Async XLA Ops:
  7.2 58.7 %all-gather.7.cloned.1.call-start = ((), (), s32[]{:S(2)}) async-start(), calls=%async_computation.4 | async-start | bytes 1474560 | tf_op jit(solution)/shard_map/all_gather | solution.py:457
  8.9 57.0 %all-gather.5.cloned.1.call-start = ((), (), s32[]{:S(2)}) async-start(), calls=%async_computation.3 | async-start | bytes 1474560 | tf_op jit(solution)/shard_map/all_gather | solution.py:457
  9.0 14.7 %copy-start.5 = (bf16[96,1536]{1,0:T(8,128)(2,1)S(1)}, bf16[96,1536]{1,0:T(8,128)(2,1)}, u32[]{:S(2)}) copy-start(bf16[96,1536]{1,0:T(8,128)(2,1)} %constant_dynamic-slice_fusion) | copy-start | bytes 884740
  9.0 25.3 %copy-start.14 = (s32[2,2048]{1,0:T(2,128)S(1)}, s32[2,2048]{1,0:T(2,128)}, u32[]{:S(2)}) copy-start(s32[2,2048]{1,0:T(2,128)} %param.15) | copy-start | bytes 49156
  9.0 25.3 %copy-start.15 = (s32[2]{0:T(128)S(1)}, s32[2]{0:T(128)}, u32[]{:S(2)}) copy-start(s32[2]{0:T(128)} %lengths.1) | copy-start | bytes 28
  17.8 15.7 %collective-permute-start = (bf16[384,512]{1,0:T(8,128)(2,1)}, bf16[384,512]{1,0:T(8,128)(2,1)S(1)}, u32[]{:S(2)}, u32[]{:S(2)}) collective-permute-start(bf16[384,512]{1,0:T(8,128)(2,1)} %get-tuple-element.51), channel_id=1, source_target_pairs={{0,8},{8,16},{16,24},{1,9},{9,17},{17,25},{2,10},{10,18},{18,26},{... | collective-permute-start | bytes 1179656 | tf_op jit(solution)/shard_map/ppermute | solution.py:491
  19.1 14.4 %collective-permute-start.1 = (bf16[384,512]{1,0:T(8,128)(2,1)}, bf16[384,512]{1,0:T(8,128)(2,1)S(1)}, u32[]{:S(2)}, u32[]{:S(2)}) collective-permute-start(bf16[384,512]{1,0:T(8,128)(2,1)} %get-tuple-element.53), channel_id=1, source_target_pairs={{8,0},{16,8},{24,16},{9,1},{17,9},{25,17},{10,2},{18,10},{26,18},{... | collective-permute-start | bytes 1179656 | tf_op jit(solution)/shard_map/ppermute | solution.py:492
  23.7 9.8 %collective-permute-start.2 = (bf16[96,1536]{1,0:T(8,128)(2,1)S(1)}, bf16[96,1536]{1,0:T(8,128)(2,1)S(1)}, u32[]{:S(2)}, u32[]{:S(2)}) collective-permute-start(bf16[96,1536]{1,0:T(8,128)(2,1)S(1)} %copy-done.5), channel_id=1, source_target_pairs={{0,1},{1,0},{2,3},{3,2},{4,5},{5,4},{6,7},{7,6},{8,9},{9,8},{10,11... | collective-permute-start | bytes 884744 | tf_op jit(solution)/shard_map/ppermute | solution.py:418
  34.2 124.1 %all-gather.9.cloned.1.call-start = ((), (), s32[]{:S(2)}) async-start(), calls=%async_computation.5 | async-start | bytes 1966080 | tf_op jit(solution)/shard_map/all_gather | solution.py:457
  44.7 15.3 %collective-permute-start.3 = (bf16[384,256]{1,0:T(8,128)(2,1)}, bf16[384,256]{1,0:T(8,128)(2,1)S(1)}, u32[]{:S(2)}, u32[]{:S(2)}) collective-permute-start(bf16[384,256]{1,0:T(8,128)(2,1)} %get-tuple-element.65), channel_id=1, source_target_pairs={{0,8},{8,16},{16,24},{1,9},{9,17},{17,25},{2,10},{10,18},{18,26},{... | collective-permute-start | bytes 589832 | tf_op jit(solution)/shard_map/ppermute | solution.py:502
  46.0 14.0 %collective-permute-start.4 = (bf16[384,256]{1,0:T(8,128)(2,1)}, bf16[384,256]{1,0:T(8,128)(2,1)S(1)}, u32[]{:S(2)}, u32[]{:S(2)}) collective-permute-start(bf16[384,256]{1,0:T(8,128)(2,1)} %get-tuple-element.66), channel_id=1, source_target_pairs={{8,0},{16,8},{24,16},{9,1},{17,9},{25,17},{10,2},{18,10},{26,18},{... | collective-permute-start | bytes 589832 | tf_op jit(solution)/shard_map/ppermute | solution.py:501
  65.8 7.8 %copy-start.16 = (bf16[384,256]{1,0:T(8,128)(2,1)S(1)}, bf16[384,256]{1,0:T(8,128)(2,1)}, u32[]{:S(2)}) copy-start(bf16[384,256]{1,0:T(8,128)(2,1)} %get-tuple-element.72) | copy-start | bytes 589828
  65.8 12.3 %copy-start.7 = (bf16[192,1024]{1,0:T(8,128)(2,1)S(1)}, bf16[192,1024]{1,0:T(8,128)(2,1)}, u32[]{:S(2)}) copy-start(bf16[192,1024]{1,0:T(8,128)(2,1)} %get-tuple-element.73.rest_8_) | copy-start | bytes 1179652
  65.9 29.5 %all-to-all-start = ((bf16[8,64,1536]{2,1,0:T(8,128)(2,1)}), bf16[8,64,1536]{2,1,0:T(8,128)(2,1)S(1)}, u32[]{:S(2)}, u32[]{:S(2)}) async-start(bf16[8,64,1536]{2,1,0:T(8,128)(2,1)} %bitcast.48), calls=%async_computation | async-start | bytes 3145728 | tf_op jit(solution)/shard_map/all_to_all | solution.py:427
  72.3 86.0 %all-gather.11.cloned.1.call-start = ((), (), s32[]{:S(2)}) async-start(), calls=%async_computation.6 | async-start | bytes 1966080 | tf_op jit(solution)/shard_map/all_gather | solution.py:457
  72.3 8.9 %collective-permute-start.5 = (bf16[384,256]{1,0:T(8,128)(2,1)S(1)}, bf16[384,256]{1,0:T(8,128)(2,1)S(1)}, u32[]{:S(2)}, u32[]{:S(2)}) collective-permute-start(bf16[384,256]{1,0:T(8,128)(2,1)S(1)} %copy-done.17), channel_id=1, source_target_pairs={{0,8},{8,16},{16,24},{1,9},{9,17},{17,25},{2,10},{10,18},{18,26},{... | collective-permute-start | bytes 589832 | tf_op jit(solution)/shard_map/ppermute | solution.py:502
  73.6 7.7 %collective-permute-start.6 = (bf16[384,256]{1,0:T(8,128)(2,1)S(1)}, bf16[384,256]{1,0:T(8,128)(2,1)S(1)}, u32[]{:S(2)}, u32[]{:S(2)}) collective-permute-start(bf16[384,256]{1,0:T(8,128)(2,1)S(1)} %copy-done.16), channel_id=1, source_target_pairs={{8,0},{16,8},{24,16},{9,1},{17,9},{25,17},{10,2},{18,10},{26,18},{... | collective-permute-start | bytes 589832 | tf_op jit(solution)/shard_map/ppermute | solution.py:501
  78.2 22.8 %collective-permute-start.11 = (bf16[192,1024]{1,0:T(8,128)(2,1)S(1)}, bf16[192,1024]{1,0:T(8,128)(2,1)S(1)}, u32[]{:S(2)}, u32[]{:S(2)}) collective-permute-start(bf16[192,1024]{1,0:T(8,128)(2,1)S(1)} %copy-done.7), channel_id=1, source_target_pairs={{0,1},{1,0},{2,3},{3,2},{4,5},{5,4},{6,7},{7,6},{8,9},{9,8},{10,11... | collective-permute-start | bytes 1179656 | tf_op jit(solution)/shard_map/ppermute | solution.py:418
  101.8 8.7 %copy-start.6 = (bf16[4,2,96,768]{3,2,1,0:T(8,128)(2,1)S(1)}, bf16[4,2,96,768]{3,2,1,0:T(8,128)(2,1)}, u32[]{:S(2)}) copy-start(bf16[4,2,96,768]{3,2,1,0:T(8,128)(2,1)} %get-tuple-element.74) | copy-start | bytes 3538948
  101.8 8.7 %collective-permute-start.7 = (bf16[4,2,96,768]{3,2,1,0:T(8,128)(2,1)}, bf16[4,2,96,768]{3,2,1,0:T(8,128)(2,1)}, u32[]{:S(2)}, u32[]{:S(2)}) collective-permute-start(bf16[4,2,96,768]{3,2,1,0:T(8,128)(2,1)} %get-tuple-element.77), channel_id=1, source_target_pairs={{0,32},{32,0},{64,96},{96,64},{1,33},{33,1},{65,97},{97,65},{2,34}... | collective-permute-start | bytes 3538952 | tf_op jit(solution)/shard_map/ppermute | solution.py:435
  101.9 30.7 %all-to-all-start.1 = ((bf16[8,64,1536]{2,1,0:T(8,128)(2,1)}), bf16[8,64,1536]{2,1,0:T(8,128)(2,1)S(1)}, u32[]{:S(2)}, u32[]{:S(2)}) async-start(bf16[8,64,1536]{2,1,0:T(8,128)(2,1)} %bitcast.47), calls=%async_computation.1 | async-start | bytes 3145728 | tf_op jit(solution)/shard_map/all_to_all | solution.py:427
  110.0 46.9 %collective-permute-start.14 = (bf16[384,1536]{1,0:T(8,128)(2,1)}, bf16[384,1536]{1,0:T(8,128)(2,1)}, u32[]{:S(2)}, u32[]{:S(2)}) collective-permute-start(bf16[384,1536]{1,0:T(8,128)(2,1)} %all-gather.7.cloned.1.call-done.refs_0_), channel_id=1, source_target_pairs={{0,32},{32,0},{64,96},{96,64},{1,33},{33,1},{65,97},{97,65},{2,34}... | collective-permute-start | bytes 3538952 | tf_op jit(solution)/shard_map/ppermute | solution.py:435
  110.0 47.0 %collective-permute-start.15 = (bf16[384,1536]{1,0:T(8,128)(2,1)}, bf16[384,1536]{1,0:T(8,128)(2,1)}, u32[]{:S(2)}, u32[]{:S(2)}) collective-permute-start(bf16[384,1536]{1,0:T(8,128)(2,1)} %all-gather.5.cloned.1.call-done.refs_1_), channel_id=1, source_target_pairs={{0,32},{32,0},{64,96},{96,64},{1,33},{33,1},{65,97},{97,65},{2,34}... | collective-permute-start | bytes 3538952 | tf_op jit(solution)/shard_map/ppermute | solution.py:435
  113.6 11.5 %collective-permute-start.10 = (bf16[2,96,768]{2,1,0:T(8,128)(2,1)S(1)}, bf16[2,96,768]{2,1,0:T(8,128)(2,1)S(1)}, u32[]{:S(2)}, u32[]{:S(2)}) collective-permute-start(bf16[2,96,768]{2,1,0:T(8,128)(2,1)S(1)} %get-tuple-element.94), channel_id=1, source_target_pairs={{0,16},{8,24},{16,0},{24,8},{1,17},{9,25},{17,1},{25,9},{2,18},{10... | collective-permute-start | bytes 884744 | tf_op jit(solution)/shard_map/ppermute | solution.py:443
  115.0 15.4 %collective-permute-start.9 = (bf16[2,96,768]{2,1,0:T(8,128)(2,1)S(1)}, bf16[2,96,768]{2,1,0:T(8,128)(2,1)S(1)}, u32[]{:S(2)}, u32[]{:S(2)}) collective-permute-start(bf16[2,96,768]{2,1,0:T(8,128)(2,1)S(1)} %get-tuple-element.95), channel_id=1, source_target_pairs={{0,24},{8,0},{16,8},{24,16},{1,25},{9,1},{17,9},{25,17},{2,26},{10... | collective-permute-start | bytes 884744 | tf_op jit(solution)/shard_map/ppermute | solution.py:443
  115.0 15.4 %collective-permute-start.8 = (bf16[2,96,768]{2,1,0:T(8,128)(2,1)S(1)}, bf16[2,96,768]{2,1,0:T(8,128)(2,1)S(1)}, u32[]{:S(2)}, u32[]{:S(2)}) collective-permute-start(bf16[2,96,768]{2,1,0:T(8,128)(2,1)S(1)} %get-tuple-element.93), channel_id=1, source_target_pairs={{0,8},{8,16},{16,24},{24,0},{1,9},{9,17},{17,25},{25,1},{2,10},{10... | collective-permute-start | bytes 884744 | tf_op jit(solution)/shard_map/ppermute | solution.py:443
  137.3 32.6 %collective-permute-start.13 = (bf16[128,1536]{1,0:T(8,128)(2,1)}, bf16[128,1536]{1,0:T(8,128)(2,1)S(1)}, u32[]{:S(2)}, u32[]{:S(2)}) collective-permute-start(bf16[128,1536]{1,0:T(8,128)(2,1)} %get-tuple-element.84), channel_id=1, source_target_pairs={{0,5},{1,4},{2,7},{3,6},{4,1},{5,0},{6,3},{7,2},{8,13},{9,12},{10,... | collective-permute-start | bytes 1179656 | tf_op jit(solution)/shard_map/ppermute | solution.py:418
  145.8 48.6 %collective-permute-start.16 = (bf16[128,1536]{1,0:T(8,128)(2,1)}, bf16[128,1536]{1,0:T(8,128)(2,1)S(1)}, u32[]{:S(2)}, u32[]{:S(2)}) collective-permute-start(bf16[128,1536]{1,0:T(8,128)(2,1)} %get-tuple-element.84), channel_id=1, source_target_pairs={{0,7},{1,6},{2,1},{3,0},{4,3},{5,2},{6,5},{7,4},{8,15},{9,14},{10,... | collective-permute-start | bytes 1179656 | tf_op jit(solution)/shard_map/ppermute | solution.py:418
  145.8 48.6 %collective-permute-start.17 = (bf16[128,1536]{1,0:T(8,128)(2,1)}, bf16[128,1536]{1,0:T(8,128)(2,1)S(1)}, u32[]{:S(2)}, u32[]{:S(2)}) collective-permute-start(bf16[128,1536]{1,0:T(8,128)(2,1)} %get-tuple-element.84), channel_id=1, source_target_pairs={{0,3},{1,2},{2,5},{3,4},{4,7},{5,6},{6,1},{7,0},{8,11},{9,10},{10,... | collective-permute-start | bytes 1179656 | tf_op jit(solution)/shard_map/ppermute | solution.py:418
  151.4 43.0 %all-to-all-start.2 = ((bf16[4,128,1536]{2,1,0:T(8,128)(2,1)}), bf16[4,128,1536]{2,1,0:T(8,128)(2,1)S(1)}, u32[]{:S(2)}, u32[]{:S(2)}) async-start(bf16[4,128,1536]{2,1,0:T(8,128)(2,1)} %get-tuple-element.90), calls=%async_computation.2 | async-start | bytes 3145728 | tf_op jit(solution)/shard_map/all_to_all | solution.py:533
  156.9 37.5 %collective-permute-start.18 = (bf16[128,1536]{1,0:T(8,128)(2,1)}, bf16[128,1536]{1,0:T(8,128)(2,1)S(1)}, u32[]{:S(2)}, u32[]{:S(2)}) collective-permute-start(bf16[128,1536]{1,0:T(8,128)(2,1)} %get-tuple-element.84), channel_id=1, source_target_pairs={{0,1},{1,0},{2,3},{3,2},{4,5},{5,4},{6,7},{7,6},{8,9},{9,8},{10,11... | collective-permute-start | bytes 1179656 | tf_op jit(solution)/shard_map/ppermute | solution.py:418
  157.0 35.3 %collective-permute-start.12 = (bf16[96,768]{1,0:T(8,128)(2,1)S(1)}, bf16[96,768]{1,0:T(8,128)(2,1)}, u32[]{:S(2)}, u32[]{:S(2)}) collective-permute-start(bf16[96,768]{1,0:T(8,128)(2,1)S(1)} %fusion.5), channel_id=1, source_target_pairs={{0,64},{32,96},{64,0},{96,32},{1,65},{33,97},{65,1},{97,33},{2,66}... | collective-permute-start | bytes 442376 | tf_op jit(solution)/shard_map/ppermute | solution.py:451
  (12 other events, 23.2 us)
Sparse Core Ops, SparseCore 0:
  9.7 24.4 all-gather.6
  35.9 25.0 all-gather.4
  65.9 36.1 all-gather.8
  104.3 38.1 all-gather.10
